TPU v7x, 32 devices: a whole 2x2x4 slice. The times are simulated.
32 devices in a mesh: aisle: 8 (over y, x, core), span: 4 (over z).
Axes of the slice: x: 2, y: 2, z: 4, core: 2. Of those that a mesh axis runs over, the one named last changes fastest.
Arguments:
- room_pops: float32 [19, 32, 16, 512], P(None, 'aisle', 'span'), may hold values from 0.5 to 1.5
- plenum_pops: float32 [19, 32, 16, 128], P(None, 'aisle', 'span'), may hold values from 0.5 to 1.5
- tile_cell: int32 [256], P('aisle'), may hold values from 0 to 15
- tile_owner: int32 [256, 1], P('aisle'), may hold values from 0 to 3; in each aligned block of 8 rows (0 to 7, 8 to 15, ...) at most 4 rows name the same one
- tile_class: int32 [256], P('aisle'), may hold values from 0 to 3
Outputs:
- room_next: float32 [19, 32, 16, 512], P(None, 'aisle', 'span')
- plenum_next: float32 [19, 32, 16, 128], P(None, 'aisle', 'span')
Inputs may be any that keep to these rules, and one draw needn't show every extreme that they name: `tile_owner`: among the 8 rows of each aligned block of rows, at most 4 name the same owner, and exactly 4 do in some blocks.
All inputs are finite; a program needn't handle non-finite values.
Results may differ from a plain program's by a relative error of at most 0.00005.
Values sent between devices are 32-bit elements; how exact they have to be, the bound alone decides.
No kernel may reach another device: no remote copies, remote signals or barrier semaphores. Data moves between devices by JAX's collectives and lax.ppermute only.
A program may use at most 64 MiB of HBM per device.

v0:
```python
import jax
import jax.numpy as jnp
from jax import lax
from jax.sharding import PartitionSpec as P

VELOCITIES = [
    (0, 0, 0),
    (1, 0, 0),
    (-1, 0, 0),
    (0, 1, 0),
    (0, -1, 0),
    (0, 0, 1),
    (0, 0, -1),
    (1, 1, 0),
    (-1, -1, 0),
    (1, -1, 0),
    (-1, 1, 0),
    (1, 0, 1),
    (-1, 0, -1),
    (1, 0, -1),
    (-1, 0, 1),
    (0, 1, 1),
    (0, -1, -1),
    (0, 1, -1),
    (0, -1, 1),
]
WEIGHTS = [1.0 / 3.0] + [1.0 / 18.0] * 6 + [1.0 / 36.0] * 12
UPWARD = [5, 11, 14, 15, 18]
OMEGA = 1.25


def passed_along(value, axis, by):
    count = lax.axis_size(axis)
    return lax.ppermute(value, axis, [(i, (i + by) % count) for i in range(count)])


def passed_along_2(value, axis, by):
    count = lax.axis_size(axis)
    pairs = [(i, i + by) for i in range(count) if 0 <= i + by < count]
    return lax.ppermute(value, axis, pairs)


def collide(pops):
    weights = jnp.array(WEIGHTS, jnp.float32).reshape(19, 1, 1, 1)
    vel = jnp.array(VELOCITIES, jnp.float32)
    weighted = pops * weights
    rho = jnp.sum(weighted, axis=0)
    moment = jnp.tensordot(vel.T, weighted, axes=1, precision=lax.Precision.HIGHEST)
    speed = moment / rho
    usq = jnp.sum(speed * speed, axis=0)
    along = jnp.tensordot(vel, speed, axes=1, precision=lax.Precision.HIGHEST)
    equil = rho * (1.0 + 3.0 * along + 4.5 * along * along - 1.5 * usq)
    return pops - OMEGA * (pops - equil)


def plane(field, where, axis):
    return lax.index_in_dim(field, where, axis=axis, keepdims=False)


def enter(field, incoming, sign, axis):
    size = field.shape[axis]
    entry = jnp.expand_dims(incoming, axis)
    if sign == 1:
        return jnp.concatenate([entry, lax.slice_in_dim(field, 0, size - 1, axis=axis)], axis=axis)
    return jnp.concatenate([lax.slice_in_dim(field, 1, size, axis=axis), entry], axis=axis)


def clamp_height(field, sign):
    size = field.shape[2]
    if sign == 1:
        return jnp.concatenate([field[:, :, :1], field[:, :, : size - 1]], axis=2)
    if sign == -1:
        return jnp.concatenate([field[:, :, 1:], field[:, :, size - 1 :]], axis=2)
    return field


def move_aisle(room_list, plen_list):
    ups = [q for q in range(19) if VELOCITIES[q][0] == 1]
    downs = [q for q in range(19) if VELOCITIES[q][0] == -1]
    got_up = passed_along(
        (
            jnp.stack([plane(room_list[q], -1, 0) for q in ups], 0),
            jnp.stack([plane(plen_list[q], -1, 0) for q in ups], 0),
        ),
        "aisle",
        1,
    )
    got_down = passed_along(
        (
            jnp.stack([plane(room_list[q], 0, 0) for q in downs], 0),
            jnp.stack([plane(plen_list[q], 0, 0) for q in downs], 0),
        ),
        "aisle",
        -1,
    )
    for slot, q in enumerate(ups):
        room_list[q] = enter(room_list[q], got_up[0][slot], 1, 0)
        plen_list[q] = enter(plen_list[q], got_up[1][slot], 1, 0)
    for slot, q in enumerate(downs):
        room_list[q] = enter(room_list[q], got_down[0][slot], -1, 0)
        plen_list[q] = enter(plen_list[q], got_down[1][slot], -1, 0)
    return (room_list, plen_list)


def move_span(room_list, plen_list):
    ups = [q for q in range(19) if VELOCITIES[q][1] == 1]
    downs = [q for q in range(19) if VELOCITIES[q][1] == -1]
    here = lax.axis_index("span")
    first = here == 0
    last = here == lax.axis_size("span") - 1
    got_up = passed_along_2(
        (
            jnp.stack([plane(room_list[q], -1, 1) for q in ups], 0),
            jnp.stack([plane(plen_list[q], -1, 1) for q in ups], 0),
        ),
        "span",
        1,
    )
    got_down = passed_along_2(
        (
            jnp.stack([plane(room_list[q], 0, 1) for q in downs], 0),
            jnp.stack([plane(plen_list[q], 0, 1) for q in downs], 0),
        ),
        "span",
        -1,
    )
    for slot, q in enumerate(ups):
        room_in = jnp.where(first, plane(room_list[q], 0, 1), got_up[0][slot])
        plen_in = jnp.where(first, plane(plen_list[q], 0, 1), got_up[1][slot])
        room_list[q] = enter(room_list[q], room_in, 1, 1)
        plen_list[q] = enter(plen_list[q], plen_in, 1, 1)
    for slot, q in enumerate(downs):
        room_in = jnp.where(last, plane(room_list[q], -1, 1), got_down[0][slot])
        plen_in = jnp.where(last, plane(plen_list[q], -1, 1), got_down[1][slot])
        room_list[q] = enter(room_list[q], room_in, -1, 1)
        plen_list[q] = enter(plen_list[q], plen_in, -1, 1)
    return (room_list, plen_list)


def jet_inflow(plenum_post, tile_cell, tile_owner, tile_class):
    n_span = lax.axis_size("span")
    here = lax.axis_index("span")
    cells_a, cells_s, height = (plenum_post.shape[1], plenum_post.shape[2], plenum_post.shape[3])
    cells = cells_a * cells_s
    columns = jnp.stack([plenum_post[q] for q in UPWARD], 0)
    columns = jnp.transpose(columns, (1, 2, 0, 3)).reshape(cells, 5 * height)
    rows = tile_cell.shape[0]
    per_brick = rows // n_span
    owner_all = tile_owner[:, 0]
    open_area = 0.15 * (tile_class.astype(jnp.float32) + 1.0)
    source = jnp.arange(rows, dtype=jnp.int32) // per_brick
    mine = owner_all == here
    cell_hot = (tile_cell[:, None] == jnp.arange(cells, dtype=jnp.int32)[None, :]).astype(
        jnp.float32
    )
    gathered = lax.all_gather(columns, "span", axis=0, tiled=True)
    weighted = cell_hot * (open_area * mine.astype(jnp.float32))[:, None]
    position = source * cells + tile_cell
    pos_hot = (position[:, None] == jnp.arange(n_span * cells, dtype=jnp.int32)[None, :]).astype(
        jnp.float32
    )
    mixing = jnp.dot(weighted.T, pos_hot, precision=lax.Precision.HIGHEST)
    inflow = jnp.dot(mixing, gathered, precision=lax.Precision.HIGHEST)
    inflow = inflow.reshape(cells_a, cells_s, 5, height)
    return jnp.transpose(inflow, (2, 0, 1, 3))


def shards(room_pops, plenum_pops, tile_cell, tile_owner, tile_class):
    plenum_post = collide(plenum_pops)
    inflow = jet_inflow(plenum_post, tile_cell, tile_owner, tile_class)
    room_post = collide(room_pops)
    room_list = [room_post[q] for q in range(19)]
    plen_list = [plenum_post[q] for q in range(19)]
    room_list, plen_list = move_aisle(room_list, plen_list)
    room_list, plen_list = move_span(room_list, plen_list)
    height = plenum_pops.shape[3]
    for q in range(19):
        room_list[q] = clamp_height(room_list[q], VELOCITIES[q][2])
        plen_list[q] = clamp_height(plen_list[q], VELOCITIES[q][2])
    for slot, q in enumerate(UPWARD):
        room_list[q] = room_list[q].at[:, :, :height].add(inflow[slot])
    return (jnp.stack(room_list, 0), jnp.stack(plen_list, 0))


def solution(mesh):
    return jax.shard_map(
        shards,
        mesh=mesh,
        in_specs=(
            P(None, "aisle", "span", None),
            P(None, "aisle", "span", None),
            P("aisle"),
            P("aisle", None),
            P("aisle"),
        ),
        out_specs=(P(None, "aisle", "span", None), P(None, "aisle", "span", None)),
        check_vma=False,
    )
```

profile of v0, /device:TPU:0, one launch (start us, length us, event | category | flops | bytes accessed | tf_op | source)
XLA Modules:
  0.0 53.9 jit_solution(10825893586372022893)
XLA Ops:
  0.6 0.6 %copy-done.3 = f32[19]{0:T(128)S(1)} copy-done((f32[19]{0:T(128)S(1)}, f32[19]{0:T(128)}, u32[]{:S(2)}) %copy-start.3) | copy-done | bytes 100
  1.3 1.3 %fusion.101 = (f32[4,4,512]{2,1,0:T(4,128)S(1)}, f32[19,4,4,512]{3,2,1,0:T(4,128)S(1)}) fusion(f32[19,4,4,512]{3,2,1,0:T(4,128)} %param.19, f32[19]{0:T(128)S(1)} %copy-done.3), kind=kLoop, calls=%fused_computation.362 | loop fusion | flops 303104 | bytes 1278028 | tf_op jit(solution)/shard_map/reduce_sum | solution.py:47
  2.6 0.7 %copy-done.9 = f32[19,3,1,1]{0,1,3,2:T(4,128)S(1)} copy-done((f32[19,3,1,1]{0,1,3,2:T(4,128)S(1)}, f32[19,3,1,1]{0,1,3,2:T(4,128)}, u32[]{:S(2)}) %copy-start.9) | copy-done | bytes 252
  3.3 1.1 %multiply_reduce_fusion = (f32[4,4,512]{2,1,0:T(4,128)S(1)}, f32[3,4,4,512]{3,0,2,1:T(4,128)S(1)}) fusion(f32[4,4,512]{2,1,0:T(4,128)S(1)} %get-tuple-element.64, f32[19,3,1,1]{0,1,3,2:T(4,128)S(1)} %copy-done.9, f32[19,4,4,512]{3,2,1,0:T(4,128)S(1)} %get-tuple-element.65), kind=kOutput, calls=%fused_computation.21 | convolution fusion | flops 5668864 | bytes 786660 | tf_op jit(solution)/shard_map/dot_general | solution.py:48
  4.4 1.3 %copy_subtract_fusion.1 = f32[19,4,4,512]{3,0,2,1:T(8,128)S(1)} fusion(f32[19,4,4,512]{3,2,1,0:T(4,128)S(1)} %copy-done, f32[19,3,1,1]{0,1,3,2:T(4,128)S(1)} %copy-done.9, f32[3,4,4,512]{3,0,2,1:T(4,128)S(1)} %get-tuple-element.169, f32[4,4,512]{2,1,0:T(4,128)S(1)} %broadcast_multiply_fusion.2, f32[4,4,512]{2,1,0:T(4,128)S(1)} %get-tuple-element.64), kind=kOutput, calls=%fused_computation.6 | convolution fusion | flops 7159808 | bytes 1409252 | tf_op jit(solution)/shard_map/dot_general | solution.py:51
  5.7 0.1 fusion.104
  5.8 0.5 collective-permute-start
  6.4 3.0 %collective-permute-start.1 = (f32[5,4,512]{2,1,0:T(4,128)S(1)}, f32[5,4,512]{2,1,0:T(4,128)S(1)}, u32[]{:S(2)}, u32[]{:S(2)}) collective-permute-start(f32[5,4,512]{2,1,0:T(4,128)S(1)} %constant_dynamic-update-slice_fusion.5), channel_id=1, source_target_pairs={{0,28},{4,0},{8,4},{12,8},{16,12},{20,16},{24,20},{28,24},{1,29},{... | collective-permute-start | bytes 122888 | tf_op jit(solution)/shard_map/ppermute | solution.py:34
  9.3 0.1 fusion.100
  9.4 0.3 multiply_reduce_fusion.1
  9.8 0.5 copy_subtract_fusion.3
  10.3 0.1 collective-permute-start.4
  10.4 2.7 %collective-permute-start.5 = (f32[5,4,128]{2,0,1:T(8,128)S(1)}, f32[5,4,128]{2,0,1:T(8,128)S(1)}, u32[]{:S(2)}, u32[]{:S(2)}) collective-permute-start(f32[5,4,128]{2,0,1:T(8,128)S(1)} %stack.183), channel_id=1, source_target_pairs={{0,28},{4,0},{8,4},{12,8},{16,12},{20,16},{24,20},{28,24},{1,29},{... | collective-permute-start | bytes 30728 | tf_op jit(solution)/shard_map/ppermute | solution.py:34
  13.1 0.2 fusion.103
  13.3 0.2 fusion.102
  13.5 0.1 fusion.106
  13.8 0.6 %copy-done.8 = s32[32]{0:T(128)S(1)} copy-done((s32[32]{0:T(128)S(1)}, s32[32]{0:T(128)}, u32[]{:S(2)}) %copy-start.8) | copy-done | bytes 152
  14.5 14.5 %all_gather.3 = f32[64,640]{1,0:T(8,128)S(1)} all-gather(f32[16,640]{1,0:T(8,128)S(1)} %bitcast.557), channel_id=1, replica_groups=mesh['aisle'=8,'span'=4] {'span'}, dimensions={0}, use_global_device_ids=true | all-gather | bytes 204800 | tf_op jit(solution)/shard_map/all_gather | solution.py:156
  29.1 0.6 %copy-done.5 = s32[32,1]{0,1:T(1,128)S(1)} copy-done((s32[32,1]{0,1:T(1,128)S(1)}, s32[32,1]{0,1:T(1,128)}, u32[]{:S(2)}) %copy-start.5) | copy-done | bytes 152
  29.8 0.0 copy-done.6
  29.8 0.3 fusion.37
  30.0 0.2 fusion.111
  30.3 0.1 fusion.28
  30.5 0.1 slice.1222
  30.5 0.1 slice.1221
  30.7 0.1 slice.1311
  30.7 0.1 slice.1310
  31.2 3.4 %collective-permute-start.6 = (f32[5,4,128]{2,1,0:T(4,128)S(1)}, f32[5,4,128]{2,1,0:T(4,128)S(1)}, u32[]{:S(2)}, u32[]{:S(2)}) collective-permute-start(f32[5,4,128]{2,1,0:T(4,128)S(1)} %constant_dynamic-update-slice_fusion.29), channel_id=1, source_target_pairs={{0,1},{1,2},{2,3},{4,5},{5,6},{6,7},{8,9},{9,10},{10,11},{12,13},{... | collective-permute-start | bytes 30728 | tf_op jit(solution)/shard_map/ppermute | solution.py:40
  34.6 1.3 %collective-permute-start.7 = (f32[5,4,128]{2,1,0:T(4,128)S(1)}, f32[5,4,128]{2,1,0:T(4,128)S(1)}, u32[]{:S(2)}, u32[]{:S(2)}) collective-permute-start(f32[5,4,128]{2,1,0:T(4,128)S(1)} %constant_dynamic-update-slice_fusion.34), channel_id=1, source_target_pairs={{1,0},{2,1},{3,2},{5,4},{6,5},{7,6},{9,8},{10,9},{11,10},{13,12},{... | collective-permute-start | bytes 30728 | tf_op jit(solution)/shard_map/ppermute | solution.py:40
  36.0 0.1 fusion.47
  36.0 0.1 fusion.43
  36.2 0.1 fusion.62
  36.3 3.9 %collective-permute-done.7 = f32[5,4,128]{2,1,0:T(4,128)S(1)} collective-permute-done((f32[5,4,128]{2,1,0:T(4,128)S(1)}, f32[5,4,128]{2,1,0:T(4,128)S(1)}, u32[]{:S(2)}, u32[]{:S(2)}) %collective-permute-start.7) | collective-permute-done | bytes 10272 | tf_op jit(solution)/shard_map/ppermute | solution.py:40
  40.2 0.1 fusion.39
  40.4 0.1 constant_dynamic-update-slice_fusion.52
  40.5 0.1 constant_dynamic-update-slice_fusion.51
  40.6 0.1 constant_dynamic-update-slice_fusion.46
  40.7 0.1 constant_dynamic-update-slice_fusion.43
  40.8 0.1 fusion.51
  41.0 0.7 %slice-done = f32[1,4,128]{2,1,0:T(4,128)S(1)} async-done(((f32[5,4,128]{2,1,0:T(4,128)}), f32[1,4,128]{2,1,0:T(4,128)S(1)}, s32[]{:S(2)}) %slice-start) | async-done | bytes 2072 | tf_op jit(solution)/shard_map/slice | solution.py:134
  41.7 0.1 constant_dynamic-update-slice_fusion.39
  41.8 0.1 fusion.121
  41.8 0.1 fusion.31
  42.0 0.1 fusion.120
  42.0 0.4 copy-done.7
  42.4 0.1 fusion.32
  42.6 0.1 stack.156
  42.7 2.9 %collective-permute-start.2 = (f32[5,4,512]{2,0,1:T(8,128)S(1)}, f32[5,4,512]{2,0,1:T(8,128)S(1)}, u32[]{:S(2)}, u32[]{:S(2)}) collective-permute-start(f32[5,4,512]{2,0,1:T(8,128)S(1)} %stack.156), channel_id=1, source_target_pairs={{0,1},{1,2},{2,3},{4,5},{5,6},{6,7},{8,9},{9,10},{10,11},{12,13},{... | collective-permute-start | bytes 122888 | tf_op jit(solution)/shard_map/ppermute | solution.py:40
  45.5 0.1 stack.158
  45.6 1.3 %collective-permute-start.3 = (f32[5,4,512]{2,0,1:T(8,128)S(1)}, f32[5,4,512]{2,0,1:T(8,128)S(1)}, u32[]{:S(2)}, u32[]{:S(2)}) collective-permute-start(f32[5,4,512]{2,0,1:T(8,128)S(1)} %stack.158), channel_id=1, source_target_pairs={{1,0},{2,1},{3,2},{5,4},{6,5},{7,6},{9,8},{10,9},{11,10},{13,12},{... | collective-permute-start | bytes 122888 | tf_op jit(solution)/shard_map/ppermute | solution.py:40
  46.9 0.1 fusion.16
  47.0 0.1 fusion.12
  47.1 4.6 %collective-permute-done.3 = f32[5,4,512]{2,0,1:T(8,128)S(1)} collective-permute-done((f32[5,4,512]{2,0,1:T(8,128)S(1)}, f32[5,4,512]{2,0,1:T(8,128)S(1)}, u32[]{:S(2)}, u32[]{:S(2)}) %collective-permute-start.3) | collective-permute-done | bytes 40992 | tf_op jit(solution)/shard_map/ppermute | solution.py:40
  51.8 0.1 broadcast_select_fusion
  51.8 0.1 fusion.123
  52.0 0.1 fusion.29
  52.1 0.1 broadcast_select_fusion.5
  52.1 0.1 fusion.122
  52.2 0.1 fusion.30
  52.4 0.1 fusion.73
  52.5 0.1 constant_dynamic-update-slice_fusion.22
  52.8 0.1 fusion.24
  52.9 0.1 fusion.20
  53.1 0.8 %copy-done.4 = f32[19,4,4,512]{3,2,1,0:T(4,128)} copy-done((f32[19,4,4,512]{3,2,1,0:T(4,128)}, f32[19,4,4,512]{3,2,1,0:T(4,128)S(1)}, u32[]{:S(2)}) %copy-start.4) | copy-done | bytes 622616
  (150 shorter events, 1.5 us)
Async XLA Ops:
  0.6 0.7 %copy-start.3 = (f32[19]{0:T(128)S(1)}, f32[19]{0:T(128)}, u32[]{:S(2)}) copy-start(f32[19]{0:T(128)} %constant.163.clone) | copy-start | bytes 232
  2.6 0.7 %copy-start.9 = (f32[19,3,1,1]{0,1,3,2:T(4,128)S(1)}, f32[19,3,1,1]{0,1,3,2:T(4,128)}, u32[]{:S(2)}) copy-start(f32[19,3,1,1]{0,1,3,2:T(4,128)} %constant.167) | copy-start | bytes 688
  3.3 1.1 %copy-start = (f32[19,4,4,512]{3,2,1,0:T(4,128)S(1)}, f32[19,4,4,512]{3,2,1,0:T(4,128)}, u32[]{:S(2)}) copy-start(f32[19,4,4,512]{3,2,1,0:T(4,128)} %param.19) | copy-start | bytes 1867780
  5.7 3.7 %copy-start.1 = (f32[19,4,4,128]{3,2,1,0:T(4,128)S(1)}, f32[19,4,4,128]{3,2,1,0:T(4,128)}, u32[]{:S(2)}) copy-start(f32[19,4,4,128]{3,2,1,0:T(4,128)} %param.20) | copy-start | bytes 466948
  5.8 36.1 %collective-permute-start = (f32[5,4,512]{2,1,0:T(4,128)S(1)}, f32[5,4,512]{2,1,0:T(4,128)S(1)}, u32[]{:S(2)}, u32[]{:S(2)}) collective-permute-start(f32[5,4,512]{2,1,0:T(4,128)S(1)} %constant_dynamic-update-slice_fusion), channel_id=1, source_target_pairs={{0,4},{4,8},{8,12},{12,16},{16,20},{20,24},{24,28},{28,0},{1,5},{5... | collective-permute-start | bytes 122888 | tf_op jit(solution)/shard_map/ppermute | solution.py:34
  6.4 35.4 %collective-permute-start.1 = (f32[5,4,512]{2,1,0:T(4,128)S(1)}, f32[5,4,512]{2,1,0:T(4,128)S(1)}, u32[]{:S(2)}, u32[]{:S(2)}) collective-permute-start(f32[5,4,512]{2,1,0:T(4,128)S(1)} %constant_dynamic-update-slice_fusion.5), channel_id=1, source_target_pairs={{0,28},{4,0},{8,4},{12,8},{16,12},{20,16},{24,20},{28,24},{1,29},{... | collective-permute-start | bytes 122888 | tf_op jit(solution)/shard_map/ppermute | solution.py:34
  10.3 20.8 %collective-permute-start.4 = (f32[5,4,128]{2,0,1:T(8,128)S(1)}, f32[5,4,128]{2,0,1:T(8,128)S(1)}, u32[]{:S(2)}, u32[]{:S(2)}) collective-permute-start(f32[5,4,128]{2,0,1:T(8,128)S(1)} %stack.181), channel_id=1, source_target_pairs={{0,4},{4,8},{8,12},{12,16},{16,20},{20,24},{24,28},{28,0},{1,5},{5... | collective-permute-start | bytes 30728 | tf_op jit(solution)/shard_map/ppermute | solution.py:34
  10.4 20.7 %collective-permute-start.5 = (f32[5,4,128]{2,0,1:T(8,128)S(1)}, f32[5,4,128]{2,0,1:T(8,128)S(1)}, u32[]{:S(2)}, u32[]{:S(2)}) collective-permute-start(f32[5,4,128]{2,0,1:T(8,128)S(1)} %stack.183), channel_id=1, source_target_pairs={{0,28},{4,0},{8,4},{12,8},{16,12},{20,16},{24,20},{28,24},{1,29},{... | collective-permute-start | bytes 30728 | tf_op jit(solution)/shard_map/ppermute | solution.py:34
  13.8 0.7 %copy-start.8 = (s32[32]{0:T(128)S(1)}, s32[32]{0:T(128)}, u32[]{:S(2)}) copy-start(s32[32]{0:T(128)} %param.21) | copy-start | bytes 388
  29.1 0.7 %copy-start.5 = (s32[32,1]{0,1:T(1,128)S(1)}, s32[32,1]{0,1:T(1,128)}, u32[]{:S(2)}) copy-start(s32[32,1]{0,1:T(1,128)} %param.22) | copy-start | bytes 388
  29.1 0.7 %copy-start.6 = (s32[32]{0:T(128)S(1)}, s32[32]{0:T(128)}, u32[]{:S(2)}) copy-start(s32[32]{0:T(128)} %param.23) | copy-start | bytes 388
  31.2 5.0 %collective-permute-start.6 = (f32[5,4,128]{2,1,0:T(4,128)S(1)}, f32[5,4,128]{2,1,0:T(4,128)S(1)}, u32[]{:S(2)}, u32[]{:S(2)}) collective-permute-start(f32[5,4,128]{2,1,0:T(4,128)S(1)} %constant_dynamic-update-slice_fusion.29), channel_id=1, source_target_pairs={{0,1},{1,2},{2,3},{4,5},{5,6},{6,7},{8,9},{9,10},{10,11},{12,13},{... | collective-permute-start | bytes 30728 | tf_op jit(solution)/shard_map/ppermute | solution.py:40
  34.6 5.6 %collective-permute-start.7 = (f32[5,4,128]{2,1,0:T(4,128)S(1)}, f32[5,4,128]{2,1,0:T(4,128)S(1)}, u32[]{:S(2)}, u32[]{:S(2)}) collective-permute-start(f32[5,4,128]{2,1,0:T(4,128)S(1)} %constant_dynamic-update-slice_fusion.34), channel_id=1, source_target_pairs={{1,0},{2,1},{3,2},{5,4},{6,5},{7,6},{9,8},{10,9},{11,10},{13,12},{... | collective-permute-start | bytes 30728 | tf_op jit(solution)/shard_map/ppermute | solution.py:40
  40.2 0.7 %copy-start.2 = (f32[5,4,128]{2,1,0:T(4,128)}, f32[5,4,128]{2,1,0:T(4,128)S(1)}, u32[]{:S(2)}) copy-start(f32[5,4,128]{2,1,0:T(4,128)S(1)} %collective-permute-done.7) | copy-start | bytes 30724
  40.9 0.7 %slice-start = ((f32[5,4,128]{2,1,0:T(4,128)}), f32[1,4,128]{2,1,0:T(4,128)S(1)}, s32[]{:S(2)}) async-start(f32[5,4,128]{2,1,0:T(4,128)} %copy-done.2), calls=%async_computation | async-start | bytes 4096 | tf_op jit(solution)/shard_map/slice | solution.py:134
  41.7 0.7 %copy-start.7 = (f32[19,4,4,128]{3,2,1,0:T(4,128)}, f32[19,4,4,128]{3,2,1,0:T(4,128)S(1)}, u32[]{:S(2)}) copy-start(f32[19,4,4,128]{3,2,1,0:T(4,128)S(1)} %constant_dynamic-update-slice_fusion.39) | copy-start | bytes 466948
  42.7 9.4 %collective-permute-start.2 = (f32[5,4,512]{2,0,1:T(8,128)S(1)}, f32[5,4,512]{2,0,1:T(8,128)S(1)}, u32[]{:S(2)}, u32[]{:S(2)}) collective-permute-start(f32[5,4,512]{2,0,1:T(8,128)S(1)} %stack.156), channel_id=1, source_target_pairs={{0,1},{1,2},{2,3},{4,5},{5,6},{6,7},{8,9},{9,10},{10,11},{12,13},{... | collective-permute-start | bytes 122888 | tf_op jit(solution)/shard_map/ppermute | solution.py:40
  45.6 6.2 %collective-permute-start.3 = (f32[5,4,512]{2,0,1:T(8,128)S(1)}, f32[5,4,512]{2,0,1:T(8,128)S(1)}, u32[]{:S(2)}, u32[]{:S(2)}) collective-permute-start(f32[5,4,512]{2,0,1:T(8,128)S(1)} %stack.158), channel_id=1, source_target_pairs={{1,0},{2,1},{3,2},{5,4},{6,5},{7,6},{9,8},{10,9},{11,10},{13,12},{... | collective-permute-start | bytes 122888 | tf_op jit(solution)/shard_map/ppermute | solution.py:40
  53.1 0.8 %copy-start.4 = (f32[19,4,4,512]{3,2,1,0:T(4,128)}, f32[19,4,4,512]{3,2,1,0:T(4,128)S(1)}, u32[]{:S(2)}) copy-start(f32[19,4,4,512]{3,2,1,0:T(4,128)S(1)} %constant_dynamic-update-slice_fusion.10) | copy-start | bytes 1867780
where the time goes:
time: 54.3 us; the launch traced here: 53.9 us
  starting transfers between devices  15.1 us (28%)
  blocking collectives  14.5 us (27%)
  waiting for transfers between devices  8.57 us (16%)
  local copies, waits for them, and re-layouts  6.2 us (11%)
  other arithmetic  4.32 us (8%)
  matrix products  3.58 us (7%)
  between operations  1.66 us (3%)
    all_gather x1, blocking collectives, jet_inflow(): gathered = lax.all_gather(columns, 'span', axis=0, tiled=True)  14.5 us
    ppermute x4, starting transfers between devices, passed_along_2(): return lax.ppermute(value, axis, pairs)  8.85 us
    ppermute x4, waiting for transfers between devices, passed_along_2(): return lax.ppermute(value, axis, pairs)  8.56 us
    ppermute x4, starting transfers between devices, passed_along(): lax.ppermute(value, axis, [(i, (i + by) % count) for i in range(count)])  6.21 us
    unnamed x62, local copies, waits for them, and re-layouts  4.15 us
    dot_general x2, matrix products, collide(): along = jnp.tensordot(vel, speed, axes=1, precision=lax.Precision.HIGHEST)  1.74 us
    reduce_sum x2, other arithmetic, collide(): rho = jnp.sum(weighted, axis=0)  1.39 us
    dot_general x2, matrix products, collide(): jnp.tensordot(vel.T, weighted, axes=1, precision=lax.Precision.HIGHEST)  1.37 us
  transfers between devices with their start and end apart: 8, of which 2 were waited for; matrix products, arithmetic and copies ran while one was open for 9% of the time, Pallas kernels for 0%

commit v1 on v0

v1 whole, which is shorter than its diff:
```python
import functools

import jax
import jax.numpy as jnp
from jax import lax
from jax.experimental import pallas as pl
from jax.experimental.pallas import tpu as pltpu
from jax.sharding import PartitionSpec as P

VELOCITIES = [
    (0, 0, 0),
    (1, 0, 0),
    (-1, 0, 0),
    (0, 1, 0),
    (0, -1, 0),
    (0, 0, 1),
    (0, 0, -1),
    (1, 1, 0),
    (-1, -1, 0),
    (1, -1, 0),
    (-1, 1, 0),
    (1, 0, 1),
    (-1, 0, -1),
    (1, 0, -1),
    (-1, 0, 1),
    (0, 1, 1),
    (0, -1, -1),
    (0, 1, -1),
    (0, -1, 1),
]
UPWARD = [5, 11, 14, 15, 18]
OMEGA = 1.25
CAP = 4
X_UP = [q for q in range(19) if VELOCITIES[q][0] == 1]
X_DOWN = [q for q in range(19) if VELOCITIES[q][0] == -1]
Y_UP = [q for q in range(19) if VELOCITIES[q][1] == 1]
Y_DOWN = [q for q in range(19) if VELOCITIES[q][1] == -1]
F32 = jnp.float32
VMEM = pl.BlockSpec(memory_space=pltpu.VMEM)
HBM = pl.BlockSpec(memory_space=pltpu.HBM)


def collide(g):
    total = lambda i: g[i] + g[i + 1]
    apart = lambda i: g[i] - g[i + 1]
    dx, dy, dz = apart(1), apart(3), apart(5)
    d7, d9, d11, d13, d15, d17 = (apart(i) for i in (7, 9, 11, 13, 15, 17))
    edges = (total(7) + total(9)) + (total(11) + total(13)) + (total(15) + total(17))
    faces = total(1) + total(3) + total(5)
    rho = g[0] * (1.0 / 3.0) + faces * (1.0 / 18.0) + edges * (1.0 / 36.0)
    mx = dx * (1.0 / 18.0) + ((d7 + d9) + (d11 + d13)) * (1.0 / 36.0)
    my = dy * (1.0 / 18.0) + ((d7 - d9) + (d15 + d17)) * (1.0 / 36.0)
    mz = dz * (1.0 / 18.0) + ((d11 - d13) + (d15 - d17)) * (1.0 / 36.0)
    inv = 1.0 / rho
    base = OMEGA * rho - (1.5 * OMEGA) * inv * (mx * mx + my * my + mz * mz)
    square = (4.5 * OMEGA) * inv
    out = [None] * 19
    out[0] = base + (1.0 - OMEGA) * g[0]
    along = {1: mx, 3: my, 5: mz, 7: mx + my, 9: mx - my, 11: mx + mz, 13: mx - mz, 15: my + mz, 17: my - mz}
    for i, c in along.items():
        even = base + square * c * c
        odd = (3.0 * OMEGA) * c
        out[i] = (even + odd) + (1.0 - OMEGA) * g[i]
        out[i + 1] = (even - odd) + (1.0 - OMEGA) * g[i + 1]
    return out


def raised(value, cz):
    if cz == 0:
        return value
    size = value.shape[-1]
    lane = lax.broadcasted_iota(jnp.int32, value.shape, value.ndim - 1)
    if cz == 1:
        return jnp.where(lane == 0, value, pltpu.roll(value, 1, value.ndim - 1))
    return jnp.where(lane == size - 1, value, pltpu.roll(value, size - 1, value.ndim - 1))


def collide_kernel(sizes, relayed, room_in, plen_in, cell_in, owner_in, class_in, room_post, plen_post, swap_a, swap_b, *rest):
    ca, cs, hr, hp, n_span, per_brick = sizes
    jets = rest[:-7]
    columns, room_buf, plen_buf, cells, owners, classes, sems = rest[-7:]
    copies = [pltpu.make_async_copy(src, dst, sems.at[i]) for i, (src, dst) in enumerate(
        ((plen_in, plen_buf), (cell_in, cells), (owner_in, owners), (class_in, classes), (room_in, room_buf)))]
    for copy in copies:
        copy.start()
    for part in jets:
        part[...] = jnp.zeros_like(part)
    copies[0].wait()
    for x in range(ca):
        for h in range(0, hp, 128):
            post = collide([plen_buf[q, x, :, h : h + 128] for q in range(19)])
            for q in range(19):
                plen_post[q, x, :, h : h + 128] = post[q]
            for k, q in enumerate(UPWARD):
                for y in range(cs):
                    columns[x * cs + y, :, k * hp + h : k * hp + h + 128] = post[q][y : y + 1]
    for copy in copies[1:4]:
        copy.wait()
    here = lax.axis_index("span")
    first = here * per_brick

    def send_jet(i, carry):
        t = first + i
        owner, cell = owners[t, 0], cells[t]
        share = 0.15 * (classes[t].astype(F32) + 1.0)
        slot = lax.fori_loop(0, i, lambda j, n: n + (owners[first + j, 0] == owner).astype(jnp.int32), 0)
        column = share * columns[cell]
        if not relayed:
            jets[0][owner, slot] = column
            return carry
        apart = owner ^ here

        @pl.when(apart < 2)
        def _():
            jets[0][apart, slot] = column

        @pl.when(apart >= 2)
        def _():
            jets[1][apart - 2, slot] = column

        return carry

    lax.fori_loop(0, per_brick, send_jet, 0)
    copies[4].wait()

    def room_plane(x, carry):
        for h in range(0, hr, 128):
            post = collide([room_buf[q, x, :, h : h + 128] for q in range(19)])
            for q in range(19):
                room_post[q, x, :, h : h + 128] = post[q]
        return carry

    lax.fori_loop(0, ca, room_plane, 0)
    even = lax.axis_index("aisle") % 2 == 0
    for k in range(5):
        up, down = X_UP[k], X_DOWN[k]
        for source, low, high in ((room_post, 0, hr), (plen_post, hr, hr + hp)):
            rising = raised(source[up, ca - 1], VELOCITIES[up][2])
            falling = raised(source[down, 0], VELOCITIES[down][2])
            swap_a[k, :, low:high] = jnp.where(even, rising, falling)
            swap_b[k, :, low:high] = jnp.where(even, falling, rising)


def local_kernel(sizes, room_post, plen_post, cell_in, owner_in, room_part, plen_part, span_up, span_down, places):
    ca, cs, hr, hp, n_span, per_brick = sizes
    for source, dest, low, high in ((plen_post, plen_part, hr, hr + hp), (room_post, room_part, 0, hr)):
        for q in range(19):
            cx, cy, cz = VELOCITIES[q]
            for x in range(ca):
                if not 0 <= x - cx < ca:
                    continue
                value = raised(source[q, x - cx], cz)
                if cy == 1:
                    span_up[Y_UP.index(q), x : x + 1, low:high] = value[cs - 1 : cs]
                    dest[q, x, 0:1] = value[0:1]
                    dest[q, x, 1:cs] = value[: cs - 1]
                elif cy == -1:
                    span_down[Y_DOWN.index(q), x : x + 1, low:high] = value[0:1]
                    dest[q, x, cs - 1 : cs] = value[cs - 1 : cs]
                    dest[q, x, : cs - 1] = value[1:cs]
                else:
                    dest[q, x] = value
    places[...] = jnp.zeros_like(places)
    here = lax.axis_index("span")
    row = lax.broadcasted_iota(jnp.int32, (cs, 128), 0)

    def brick(b, carry):
        def place(i, slot):
            t = b * per_brick + i
            mine = owner_in[t, 0] == here

            @pl.when(mine)
            def _():
                cell = cell_in[t]
                places[b * CAP + slot, cell // cs] = (row == cell % cs).astype(F32)

            return slot + mine.astype(jnp.int32)

        lax.fori_loop(0, per_brick, place, 0)
        return carry

    lax.fori_loop(0, n_span, brick, 0)


def corner_rows(ca, cs, even, got_a, got_b, rows):
    for q, plane, y in ((7, Y_UP, cs - 1), (10, Y_UP, cs - 1), (8, Y_DOWN, 0), (9, Y_DOWN, 0)):
        if VELOCITIES[q][0] == 1:
            k, x = X_UP.index(q), 0
            row = jnp.where(even, got_b[k, y : y + 1], got_a[k, y : y + 1])
        else:
            k, x = X_DOWN.index(q), ca - 1
            row = jnp.where(even, got_a[k, y : y + 1], got_b[k, y : y + 1])
        rows(plane, q, x, row)


def pack_kernel(sizes, relayed, got_a, got_b, span_up, span_down, *rest):
    ca, cs, hr, hp, n_span, per_brick = sizes
    if relayed:
        jets, got_jets, cross_a, cross_b = rest
    else:
        cross_a, cross_b = rest
    here = lax.axis_index("span")
    even = lax.axis_index("aisle") % 2 == 0
    low = here % 2 == 0
    for k in range(5):
        rising, falling = span_up[k], span_down[k]
        cross_a[k] = jnp.where(low, rising, falling)
        cross_b[k] = jnp.where(low, falling, rising)

    def rows(plane, q, x, row):
        k = plane.index(q)

        @pl.when(low == (plane is Y_UP))
        def _():
            cross_a[k, x : x + 1] = row

        @pl.when(low != (plane is Y_UP))
        def _():
            cross_b[k, x : x + 1] = row

    corner_rows(ca, cs, even, got_a, got_b, rows)
    if relayed:
        for s in range(CAP):
            cross_a[5, s : s + 1] = jets[1, s]
            cross_a[6, s : s + 1] = got_jets[1, s]


def jet_sums(sizes, start, places, bricks, put):
    ca, cs, hr, hp, n_span, per_brick = sizes
    for x in range(ca):
        marks = [[places[b * CAP + s, x] for s in range(CAP)] for b, _ in bricks]
        for k in range(5):
            for h in range(0, hp, 128):
                total = start(k, x, h)
                for (_, jet), brick_marks in zip(bricks, marks):
                    for s in range(CAP):
                        total = total + brick_marks[s] * jet(s, k * hp + h)
                put(k, x, h, total)


def aisle_kernel(sizes, relayed, room_in, plen_in, got_a, got_b, jets, got_jets, places, room, plen, inflow):
    ca, cs, hr, hp, n_span, per_brick = sizes
    even = lax.axis_index("aisle") % 2 == 0
    here = lax.axis_index("span")
    for k in range(5):
        for q, x, first, second in ((X_UP[k], 0, got_b, got_a), (X_DOWN[k], ca - 1, got_a, got_b)):
            cy = VELOCITIES[q][1]
            for dest, low, high in ((plen, hr, hr + hp), (room, 0, hr)):
                value = jnp.where(even, first[k, :, low:high], second[k, :, low:high])
                if cy == 1:
                    dest[q, x, 0:1] = value[0:1]
                    dest[q, x, 1:cs] = value[: cs - 1]
                elif cy == -1:
                    dest[q, x, cs - 1 : cs] = value[cs - 1 : cs]
                    dest[q, x, : cs - 1] = value[1:cs]
                else:
                    dest[q, x] = value

    def put(k, x, h, total):
        inflow[k, x, :, h : h + 128] = total

    if relayed:
        own = (here, lambda s, h: jets[0, s, :, h : h + 128])
        second = (here ^ 2, lambda s, h: got_jets[0, s, :, h : h + 128])
        jet_sums(sizes, lambda k, x, h: jnp.zeros((cs, 128), F32), places, [own, second], put)
    else:
        inflow[...] = jnp.zeros_like(inflow)

        def brick(b, carry):
            one = (b, lambda s, h: got_jets[b, s, :, h : h + 128])
            jet_sums(sizes, lambda k, x, h: inflow[k, x, :, h : h + 128], places, [one], put)
            return carry

        lax.fori_loop(0, n_span, brick, 0)


def finish_kernel(sizes, relayed, room_in, plen_in, got_a, got_b, places, inflow, room, plen, room_out, plen_out, sems):
    ca, cs, hr, hp, n_span, per_brick = sizes
    here = lax.axis_index("span")
    low = here % 2 == 0

    def enter(got, up):
        planes, y = (Y_UP, 0) if up else (Y_DOWN, cs - 1)
        for k, q in enumerate(planes):
            for x in range(ca):
                plen[q, x, y : y + 1] = got[k, x : x + 1, hr : hr + hp]
                room[q, x, y : y + 1] = got[k, x : x + 1, 0:hr]

    @pl.when(low)
    def _():
        enter(got_a, False)

    @pl.when(jnp.logical_not(low))
    def _():
        enter(got_a, True)

    @pl.when(jnp.logical_and(low, here > 0))
    def _():
        enter(got_b, True)

    @pl.when(jnp.logical_and(jnp.logical_not(low), here < n_span - 1))
    def _():
        enter(got_b, False)

    plen_copy = pltpu.make_async_copy(plen, plen_out, sems.at[0])
    plen_copy.start()
    bricks = []
    if relayed:
        bricks = [(here ^ 1, lambda s, h: got_a[5, s : s + 1, h : h + 128]),
                  (here ^ 3, lambda s, h: got_a[6, s : s + 1, h : h + 128])]

    def put(k, x, h, total):
        room[UPWARD[k], x, :, h : h + 128] = total

    jet_sums(sizes, lambda k, x, h: room[UPWARD[k], x, :, h : h + 128] + inflow[k, x, :, h : h + 128], places, bricks, put)
    room_copy = pltpu.make_async_copy(room, room_out, sems.at[1])
    room_copy.start()
    plen_copy.wait()
    room_copy.wait()


def call(kernel, outs, in_specs, out_specs=None, scratch=(), aliases={}, flops=100_000, moved=1_000_000):
    return pl.pallas_call(
        kernel,
        out_shape=outs,
        in_specs=in_specs,
        out_specs=[VMEM] * len(outs) if out_specs is None else out_specs,
        scratch_shapes=list(scratch),
        input_output_aliases=aliases,
        cost_estimate=pl.CostEstimate(flops=flops, bytes_accessed=moved, transcendentals=0),
        compiler_params=pltpu.CompilerParams(vmem_limit_bytes=40 * 2**20),
    )


def swap(value, axis, odd, wraps):
    count = lax.axis_size(axis)
    pairs = []
    for i in range(count):
        j = (i ^ 1) if not odd else (i + 1 if i % 2 else i - 1)
        if wraps or 0 <= j < count:
            pairs.append((i, j % count))
    return lax.ppermute(value, axis, pairs)


def shards(room_pops, plenum_pops, tile_cell, tile_owner, tile_class):
    n_span = lax.axis_size("span")
    _, ca, cs, hr = room_pops.shape
    hp = plenum_pops.shape[3]
    rows = tile_cell.shape[0]
    per_brick = rows // n_span
    sizes = (ca, cs, hr, hp, n_span, per_brick)
    relayed = n_span == 4
    near = pltpu.VMEM
    room_shape, plen_shape = room_pops.shape, plenum_pops.shape
    halo_x, halo_y = (5, cs, hr + hp), (5, ca, hr + hp)
    smem = pl.BlockSpec(memory_space=pltpu.SMEM)

    jets_shape = (2 if relayed else n_span, CAP, 1, 5 * hp)
    room_post, plen_post, swap_a, swap_b, *jets = call(
        functools.partial(collide_kernel, sizes, relayed),
        [near(room_shape, F32), near(plen_shape, F32), near(halo_x, F32), near(halo_x, F32)]
        + [near(jets_shape, F32)] * (2 if relayed else 1),
        [HBM] * 5,
        scratch=[pltpu.VMEM((ca * cs, 1, 5 * hp), F32), pltpu.VMEM(room_shape, F32), pltpu.VMEM(plen_shape, F32),
                 pltpu.SMEM((rows,), jnp.int32), pltpu.SMEM((rows, 1), jnp.int32), pltpu.SMEM((rows,), jnp.int32),
                 pltpu.SemaphoreType.DMA((5,))],
    )(room_pops, plenum_pops, tile_cell, tile_owner, tile_class)

    got_a = swap(swap_a, "aisle", False, True)
    got_b = swap(swap_b, "aisle", True, True)
    if relayed:
        got_jets = lax.ppermute(jets[1], "span", [(i, i ^ 2) for i in range(4)])
    else:
        got_jets = lax.all_to_all(jets[0], "span", 0, 0, tiled=True)

    room_part, plen_part, span_up, span_down, places = call(
        functools.partial(local_kernel, sizes),
        [near(room_shape, F32), near(plen_shape, F32), near(halo_y, F32), near(halo_y, F32),
         near((n_span * CAP, ca, cs, 128), F32)],
        [VMEM, VMEM, smem, smem],
    )(room_post, plen_post, tile_cell, tile_owner)

    cross_a_shape = (7, ca, hr + hp) if relayed else halo_y
    cross_a, cross_b = call(
        functools.partial(pack_kernel, sizes, relayed),
        [near(cross_a_shape, F32), near(halo_y, F32)],
        [VMEM] * (6 if relayed else 4),
    )(got_a, got_b, span_up, span_down, *((jets[0], got_jets) if relayed else ()))

    in_a = swap(cross_a, "span", False, False)
    in_b = swap(cross_b, "span", True, False)
    room_part, plen_part, inflow = call(
        functools.partial(aisle_kernel, sizes, relayed),
        [near(room_shape, F32), near(plen_shape, F32), near((5, ca, cs, hp), F32)],
        [VMEM] * 7,
        aliases={0: 0, 1: 1},
    )(room_part, plen_part, got_a, got_b, jets[0], got_jets, places)

    _, _, room_next, plenum_next = call(
        functools.partial(finish_kernel, sizes, relayed),
        [near(room_shape, F32), near(plen_shape, F32), jax.ShapeDtypeStruct(room_shape, F32),
         jax.ShapeDtypeStruct(plen_shape, F32)],
        [VMEM] * 6,
        out_specs=[VMEM, VMEM, HBM, HBM],
        scratch=[pltpu.SemaphoreType.DMA((2,))],
        aliases={0: 0, 1: 1},
    )(room_part, plen_part, in_a, in_b, places, inflow)
    return room_next, plenum_next


def solution(mesh):
    return jax.shard_map(
        shards,
        mesh=mesh,
        in_specs=(
            P(None, "aisle", "span", None),
            P(None, "aisle", "span", None),
            P("aisle"),
            P("aisle", None),
            P("aisle"),
        ),
        out_specs=(P(None, "aisle", "span", None), P(None, "aisle", "span", None)),
        check_vma=False,
    )
```

time: 54.3 us -> 21.7 us (0.40)
  the two profiles are of different devices: /device:TPU:0 before, /device:TPU:16 now
where the time goes in v1:
time: 21.7 us; the launch traced here: 21.5 us
  waiting for transfers between devices  6.72 us (31%)
  starting transfers between devices  6.6 us (30%)
  Pallas kernels  4.69 us (22%)
  local copies, waits for them, and re-layouts  2.74 us (13%)
  between operations  0.71 us (3%)
    ppermute x4, starting transfers between devices, swap(): return lax.ppermute(value, axis, pairs)  6.27 us
    ppermute x4, waiting for transfers between devices, swap(): return lax.ppermute(value, axis, pairs)  4.01 us
    unnamed x9, local copies, waits for them, and re-layouts  2.74 us
    ppermute x1, waiting for transfers between devices, shards(): got_jets = lax.ppermute(jets[1], 'span', [(i, i ^ 2) for i in range(4)])  2.71 us
    pallas_call x1, Pallas kernels, shards(): call(functools.partial(collide_kernel, sizes, relayed), [near(room_shape,...  1.98 us
    pallas_call x1, Pallas kernels, shards(): call(functools.partial(local_kernel, sizes), [near(room_shape, F32), near...  1.63 us
    pallas_call x1, Pallas kernels, shards(): call(functools.partial(finish_kernel, sizes, relayed), [near(room_shape,...  0.95 us
  transfers between devices with their start and end apart: 5, of which 2 were waited for; matrix products, arithmetic and copies ran while one was open for 0% of the time, Pallas kernels for 8%

profile of v1, /device:TPU:16, one launch (start us, length us, event | category | flops | bytes accessed | tf_op | source)
XLA Modules:
  0.0 21.5 jit_solution(11589617493263080184)
XLA Ops:
  0.6 0.0 copy-start.2
  0.6 0.0 copy-start.3
  0.7 0.7 %copy.11.owner_in = s32[32,1]{1,0:T(8,128)S(1)} copy(s32[32,1]{0,1:T(1,128)} %param.8) | data formatting | bytes 256 | tf_op args[3]
  1.4 0.0 copy-done.2
  1.4 0.0 copy-done.3
  1.4 0.0 copy-start
  1.4 1.1 %copy-done = f32[19,4,4,512]{3,2,1,0:T(4,128)S(1)} copy-done((f32[19,4,4,512]{3,2,1,0:T(4,128)S(1)}, f32[19,4,4,512]{3,2,1,0:T(4,128)}, u32[]{:S(2)}) %copy-start) | copy-done | bytes 622616
  2.5 0.0 copy-start.1
  2.5 0.9 %copy-done.1 = f32[19,4,4,128]{3,2,1,0:T(4,128)S(1)} copy-done((f32[19,4,4,128]{3,2,1,0:T(4,128)S(1)}, f32[19,4,4,128]{3,2,1,0:T(4,128)}, u32[]{:S(2)}) %copy-start.1) | copy-done | bytes 155672
  3.4 2.0 %shard_map.68 = (f32[19,4,4,512]{3,2,1,0:T(4,128)S(1)}, f32[19,4,4,128]{3,2,1,0:T(4,128)S(1)}, f32[5,4,640]{2,1,0:T(4,128)S(1)}, f32[5,4,640]{2,1,0:T(4,128)S(1)...) custom-call(f32[19,4,4,512]{3,2,1,0:T(4,128)S(1)} %copy-done, f32[19,4,4,128]{3,2,1,0:T(4,128)S(1)} %copy-done.1, ...), custom_call_target="tpu_custom_call" | custom-call | flops 100000 | bytes 1000000 | tf_op jit(solution)/shard_map/pallas_call | solution.py:359
  5.4 0.1 collective-permute-start
  5.5 2.5 %collective-permute-start.1 = (f32[5,4,640]{2,1,0:T(4,128)S(1)}, f32[5,4,640]{2,1,0:T(4,128)S(1)}, u32[]{:S(2)}, u32[]{:S(2)}) collective-permute-start(f32[5,4,640]{2,1,0:T(4,128)S(1)} %get-tuple-element.25), channel_id=1, source_target_pairs={{0,28},{4,8},{8,4},{12,16},{16,12},{20,24},{24,20},{28,0},{1,29},{... | collective-permute-start | bytes 153608 | tf_op jit(solution)/shard_map/ppermute | solution.py:342
  8.0 0.3 %collective-permute-start.2 = (f32[2,4,1,640]{3,2,1,0:T(1,128)S(1)}, f32[2,4,1,640]{3,2,1,0:T(1,128)S(1)}, u32[]{:S(2)}, u32[]{:S(2)}) collective-permute-start(f32[2,4,1,640]{3,2,1,0:T(1,128)S(1)} %get-tuple-element.27), channel_id=1, source_target_pairs={{0,2},{1,3},{2,0},{3,1},{4,6},{5,7},{6,4},{7,5},{8,10},{9,11},{10,... | collective-permute-start | bytes 61448 | tf_op jit(solution)/shard_map/ppermute | solution.py:372
  8.4 1.6 %shard_map.69 = (f32[19,4,4,512]{3,2,1,0:T(4,128)S(1)}, f32[19,4,4,128]{3,2,1,0:T(4,128)S(1)}, f32[5,4,640]{2,1,0:T(4,128)S(1)}, f32[5,4,640]{2,1,0:T(4,128)S(1)}, f32[16,4,4,128]{3,2,1,0:T(4,128)S(1)}) custom-call(f32[19,4,4,512]{3,2,1,0:T(4,128)S(1)} %get-tuple-element.20.room_post, f32[19,4,4,128]{3,2,1,0:T(4,128)S(1)} %get-tuple-element.21.plen_post, ...), custom_call_target="tpu_custom_call" | custom-call | flops 100000 | bytes 1000000 | tf_op jit(solution)/shard_map/pallas_call | solution.py:376
  10.0 2.7 %collective-permute-done.2.got_jets.rest_1_ = f32[2,4,1,640]{3,2,1,0:T(1,128)S(1)} collective-permute-done((f32[2,4,1,640]{3,2,1,0:T(1,128)S(1)}, f32[2,4,1,640]{3,2,1,0:T(1,128)S(1)}, u32[]{:S(2)}, u32[]{:S(2)}) %collective-permute-start.2) | collective-permute-done | bytes 20512 | tf_op jit(solution)/shard_map/ppermute | solution.py:372
  12.7 0.0 collective-permute-done.got_a
  12.7 0.0 collective-permute-done.1.got_b
  12.8 1.7 %collective-permute-start.3 = (f32[7,4,640]{2,1,0:T(4,128)S(1)}, f32[7,4,640]{2,1,0:T(4,128)S(1)}, u32[]{:S(2)}, u32[]{:S(2)}) collective-permute-start(f32[7,4,640]{2,1,0:T(4,128)S(1)} %get-tuple-element.33), channel_id=1, source_target_pairs={{0,1},{1,0},{2,3},{3,2},{4,5},{5,4},{6,7},{7,6},{8,9},{9,8},{10,11... | collective-permute-start | bytes 215048 | tf_op jit(solution)/shard_map/ppermute | solution.py:342
  14.5 1.9 %collective-permute-start.4 = (f32[5,4,640]{2,1,0:T(4,128)S(1)}, f32[5,4,640]{2,1,0:T(4,128)S(1)}, u32[]{:S(2)}, u32[]{:S(2)}) collective-permute-start(f32[5,4,640]{2,1,0:T(4,128)S(1)} %get-tuple-element.34), channel_id=1, source_target_pairs={{1,2},{2,1},{5,6},{6,5},{9,10},{10,9},{13,14},{14,13},{17,18},{18,... | collective-permute-start | bytes 153608 | tf_op jit(solution)/shard_map/ppermute | solution.py:342
  16.4 0.1 shard_map.70
  16.5 4.0 %collective-permute-done.4.got_b = f32[5,4,640]{2,1,0:T(4,128)S(1)} collective-permute-done((f32[5,4,640]{2,1,0:T(4,128)S(1)}, f32[5,4,640]{2,1,0:T(4,128)S(1)}, u32[]{:S(2)}, u32[]{:S(2)}) %collective-permute-start.4) | collective-permute-done | bytes 51232 | tf_op jit(solution)/shard_map/ppermute | solution.py:342
  20.5 0.0 collective-permute-done.3.got_a
  20.5 1.0 %shard_map.72 = (f32[19,4,4,512]{3,2,1,0:T(4,128)S(1)}, f32[19,4,4,128]{3,2,1,0:T(4,128)S(1)}, f32[19,4,4,512]{3,2,1,0:T(4,128)}, f32[19,4,4,128]{3,2,1,0:T(4,128)}) custom-call(f32[19,4,4,512]{3,2,1,0:T(4,128)S(1)} %get-tuple-element.29.room_in, f32[19,4,4,128]{3,2,1,0:T(4,128)S(1)} %get-tuple-element.30.plen_in, ...), custom_call_target="tpu_custom_call", output_to_operand_aliasing={{0}: (0, {}), {1}: (1, {})} | custom-call | flops 100000 | bytes 1000000 | tf_op jit(solution)/shard_map/pallas_call | solution.py:399
  (1 shorter events, 0.0 us)
Async XLA Ops:
  0.6 0.8 %copy-start.2 = (s32[32]{0:T(128)S(1)}, s32[32]{0:T(128)}, u32[]{:S(2)}) copy-start(s32[32]{0:T(128)} %cell_in.3) | copy-start | bytes 388
  0.6 0.8 %copy-start.3 = (s32[32]{0:T(128)S(1)}, s32[32]{0:T(128)}, u32[]{:S(2)}) copy-start(s32[32]{0:T(128)} %class_in.1) | copy-start | bytes 388
  1.4 1.1 %copy-start = (f32[19,4,4,512]{3,2,1,0:T(4,128)S(1)}, f32[19,4,4,512]{3,2,1,0:T(4,128)}, u32[]{:S(2)}) copy-start(f32[19,4,4,512]{3,2,1,0:T(4,128)} %room_in.1) | copy-start | bytes 1867780
  2.5 0.9 %copy-start.1 = (f32[19,4,4,128]{3,2,1,0:T(4,128)S(1)}, f32[19,4,4,128]{3,2,1,0:T(4,128)}, u32[]{:S(2)}) copy-start(f32[19,4,4,128]{3,2,1,0:T(4,128)} %plen_in.1) | copy-start | bytes 466948
  5.4 7.3 %collective-permute-start = (f32[5,4,640]{2,1,0:T(4,128)S(1)}, f32[5,4,640]{2,1,0:T(4,128)S(1)}, u32[]{:S(2)}, u32[]{:S(2)}) collective-permute-start(f32[5,4,640]{2,1,0:T(4,128)S(1)} %get-tuple-element.24), channel_id=1, source_target_pairs={{0,4},{4,0},{8,12},{12,8},{16,20},{20,16},{24,28},{28,24},{1,5},{5... | collective-permute-start | bytes 153608 | tf_op jit(solution)/shard_map/ppermute | solution.py:342
  5.5 7.2 %collective-permute-start.1 = (f32[5,4,640]{2,1,0:T(4,128)S(1)}, f32[5,4,640]{2,1,0:T(4,128)S(1)}, u32[]{:S(2)}, u32[]{:S(2)}) collective-permute-start(f32[5,4,640]{2,1,0:T(4,128)S(1)} %get-tuple-element.25), channel_id=1, source_target_pairs={{0,28},{4,8},{8,4},{12,16},{16,12},{20,24},{24,20},{28,0},{1,29},{... | collective-permute-start | bytes 153608 | tf_op jit(solution)/shard_map/ppermute | solution.py:342
  8.0 4.7 %collective-permute-start.2 = (f32[2,4,1,640]{3,2,1,0:T(1,128)S(1)}, f32[2,4,1,640]{3,2,1,0:T(1,128)S(1)}, u32[]{:S(2)}, u32[]{:S(2)}) collective-permute-start(f32[2,4,1,640]{3,2,1,0:T(1,128)S(1)} %get-tuple-element.27), channel_id=1, source_target_pairs={{0,2},{1,3},{2,0},{3,1},{4,6},{5,7},{6,4},{7,5},{8,10},{9,11},{10,... | collective-permute-start | bytes 61448 | tf_op jit(solution)/shard_map/ppermute | solution.py:372
  12.8 7.7 %collective-permute-start.3 = (f32[7,4,640]{2,1,0:T(4,128)S(1)}, f32[7,4,640]{2,1,0:T(4,128)S(1)}, u32[]{:S(2)}, u32[]{:S(2)}) collective-permute-start(f32[7,4,640]{2,1,0:T(4,128)S(1)} %get-tuple-element.33), channel_id=1, source_target_pairs={{0,1},{1,0},{2,3},{3,2},{4,5},{5,4},{6,7},{7,6},{8,9},{9,8},{10,11... | collective-permute-start | bytes 215048 | tf_op jit(solution)/shard_map/ppermute | solution.py:342
  14.5 6.0 %collective-permute-start.4 = (f32[5,4,640]{2,1,0:T(4,128)S(1)}, f32[5,4,640]{2,1,0:T(4,128)S(1)}, u32[]{:S(2)}, u32[]{:S(2)}) collective-permute-start(f32[5,4,640]{2,1,0:T(4,128)S(1)} %get-tuple-element.34), channel_id=1, source_target_pairs={{1,2},{2,1},{5,6},{6,5},{9,10},{10,9},{13,14},{14,13},{17,18},{18,... | collective-permute-start | bytes 153608 | tf_op jit(solution)/shard_map/ppermute | solution.py:342

commit v2 on v1

--- a/solution.py
+++ b/solution.py
@@ -101,9 +101,9 @@
 
     def send_jet(i, carry):
         t = first + i
-        owner, cell = owners[t, 0], cells[t]
+        owner, cell = owners[t], cells[t]
         share = 0.15 * (classes[t].astype(F32) + 1.0)
-        slot = lax.fori_loop(0, i, lambda j, n: n + (owners[first + j, 0] == owner).astype(jnp.int32), 0)
+        slot = lax.fori_loop(0, i, lambda j, n: n + (owners[first + j] == owner).astype(jnp.int32), 0)
         column = share * columns[cell]
         if not relayed:
             jets[0][owner, slot] = column
@@ -167,7 +167,7 @@
     def brick(b, carry):
         def place(i, slot):
             t = b * per_brick + i
-            mine = owner_in[t, 0] == here
+            mine = owner_in[t] == here
 
             @pl.when(mine)
             def _():
@@ -350,6 +350,8 @@
     per_brick = rows // n_span
     sizes = (ca, cs, hr, hp, n_span, per_brick)
     relayed = n_span == 4
+    tile_owner = tile_owner.reshape(rows)
+    far = lambda value: pltpu.with_memory_space_constraint(value, pltpu.HBM)
     near = pltpu.VMEM
     room_shape, plen_shape = room_pops.shape, plenum_pops.shape
     halo_x, halo_y = (5, cs, hr + hp), (5, ca, hr + hp)
@@ -362,9 +364,9 @@
         + [near(jets_shape, F32)] * (2 if relayed else 1),
         [HBM] * 5,
         scratch=[pltpu.VMEM((ca * cs, 1, 5 * hp), F32), pltpu.VMEM(room_shape, F32), pltpu.VMEM(plen_shape, F32),
-                 pltpu.SMEM((rows,), jnp.int32), pltpu.SMEM((rows, 1), jnp.int32), pltpu.SMEM((rows,), jnp.int32),
+                 pltpu.SMEM((rows,), jnp.int32), pltpu.SMEM((rows,), jnp.int32), pltpu.SMEM((rows,), jnp.int32),
                  pltpu.SemaphoreType.DMA((5,))],
-    )(room_pops, plenum_pops, tile_cell, tile_owner, tile_class)
+    )(far(room_pops), far(plenum_pops), far(tile_cell), far(tile_owner), far(tile_class))
 
     got_a = swap(swap_a, "aisle", False, True)
     got_b = swap(swap_b, "aisle", True, True)

time: 21.7 us -> 18.9 us (0.87)
  local copies, waits for them, and re-layouts: 2.74 us -> 0.67 us
  waiting for transfers between devices: 6.72 us -> 6.31 us
    unnamed x9 -> x4, local copies, waits for them, and re-layouts: 2.74 us -> 0.67 us
    ppermute x1, waiting for transfers between devices: 2.71 us -> 2.3 us  [shards(): got_jets = lax.ppermute(jets[1], 'span', [(i, i ^ 2) for i in range(4)])]
    pallas_call x1, Pallas kernels: 1.63 us -> 1.37 us  [shards(): call(functools.partial(local_kernel, sizes), [near(room_shape, F32), near...]
where the time goes in v2:
time: 18.9 us; the launch traced here: 18.8 us
  starting transfers between devices  6.6 us (35%)
  waiting for transfers between devices  6.31 us (33%)
  Pallas kernels  4.5 us (24%)
  between operations  0.68 us (4%)
  local copies, waits for them, and re-layouts  0.67 us (4%)
    ppermute x4, starting transfers between devices, swap(): return lax.ppermute(value, axis, pairs)  6.27 us
    ppermute x4, waiting for transfers between devices, swap(): return lax.ppermute(value, axis, pairs)  4.01 us
    ppermute x1, waiting for transfers between devices, shards(): got_jets = lax.ppermute(jets[1], 'span', [(i, i ^ 2) for i in range(4)])  2.3 us
    pallas_call x1, Pallas kernels, shards(): call(functools.partial(collide_kernel, sizes, relayed), [near(room_shape,...  2.06 us
    pallas_call x1, Pallas kernels, shards(): call(functools.partial(local_kernel, sizes), [near(room_shape, F32), near...  1.37 us
    pallas_call x1, Pallas kernels, shards(): call(functools.partial(finish_kernel, sizes, relayed), [near(room_shape,...  0.95 us
    unnamed x4, local copies, waits for them, and re-layouts  0.67 us
  transfers between devices with their start and end apart: 5, of which 2 were waited for; matrix products, arithmetic and copies ran while one was open for 0% of the time, Pallas kernels for 8%

profile of v2, /device:TPU:16, one launch (start us, length us, event | category | flops | bytes accessed | tf_op | source)
XLA Modules:
  0.0 18.8 jit_solution(11190357024894532356)
XLA Ops:
  0.6 2.1 %shard_map.68 = (f32[19,4,4,512]{3,2,1,0:T(4,128)S(1)}, f32[19,4,4,128]{3,2,1,0:T(4,128)S(1)}, f32[5,4,640]{2,1,0:T(4,128)S(1)}, f32[5,4,640]{2,1,0:T(4,128)S(1)...) custom-call(f32[19,4,4,512]{3,2,1,0:T(4,128)} %room_in.1, f32[19,4,4,128]{3,2,1,0:T(4,128)} %plen_in.1, ...), custom_call_target="tpu_custom_call" | custom-call | flops 100000 | bytes 1000000 | tf_op jit(solution)/shard_map/pallas_call | solution.py:361
  2.7 0.1 collective-permute-start
  2.8 2.5 %collective-permute-start.1 = (f32[5,4,640]{2,1,0:T(4,128)S(1)}, f32[5,4,640]{2,1,0:T(4,128)S(1)}, u32[]{:S(2)}, u32[]{:S(2)}) collective-permute-start(f32[5,4,640]{2,1,0:T(4,128)S(1)} %get-tuple-element.25), channel_id=1, source_target_pairs={{0,28},{4,8},{8,4},{12,16},{16,12},{20,24},{24,20},{28,0},{1,29},{... | collective-permute-start | bytes 153608 | tf_op jit(solution)/shard_map/ppermute | solution.py:342
  5.3 0.3 %collective-permute-start.2 = (f32[2,4,1,640]{3,2,1,0:T(1,128)S(1)}, f32[2,4,1,640]{3,2,1,0:T(1,128)S(1)}, u32[]{:S(2)}, u32[]{:S(2)}) collective-permute-start(f32[2,4,1,640]{3,2,1,0:T(1,128)S(1)} %get-tuple-element.27), channel_id=1, source_target_pairs={{0,2},{1,3},{2,0},{3,1},{4,6},{5,7},{6,4},{7,5},{8,10},{9,11},{10,... | collective-permute-start | bytes 61448 | tf_op jit(solution)/shard_map/ppermute | solution.py:374
  5.7 0.0 copy-start
  5.7 0.0 copy-start.1
  5.7 0.7 %copy-done = s32[32]{0:T(128)S(1)} copy-done((s32[32]{0:T(128)S(1)}, s32[32]{0:T(128)}, u32[]{:S(2)}) %copy-start) | copy-done | bytes 152
  6.3 0.0 copy-done.1
  6.3 1.4 %shard_map.69 = (f32[19,4,4,512]{3,2,1,0:T(4,128)S(1)}, f32[19,4,4,128]{3,2,1,0:T(4,128)S(1)}, f32[5,4,640]{2,1,0:T(4,128)S(1)}, f32[5,4,640]{2,1,0:T(4,128)S(1)}, f32[16,4,4,128]{3,2,1,0:T(4,128)S(1)}) custom-call(f32[19,4,4,512]{3,2,1,0:T(4,128)S(1)} %get-tuple-element.20.room_post, f32[19,4,4,128]{3,2,1,0:T(4,128)S(1)} %get-tuple-element.21.plen_post, ...), custom_call_target="tpu_custom_call" | custom-call | flops 100000 | bytes 1000000 | tf_op jit(solution)/shard_map/pallas_call | solution.py:378
  7.7 2.3 %collective-permute-done.2.got_jets.rest_1_ = f32[2,4,1,640]{3,2,1,0:T(1,128)S(1)} collective-permute-done((f32[2,4,1,640]{3,2,1,0:T(1,128)S(1)}, f32[2,4,1,640]{3,2,1,0:T(1,128)S(1)}, u32[]{:S(2)}, u32[]{:S(2)}) %collective-permute-start.2) | collective-permute-done | bytes 20512 | tf_op jit(solution)/shard_map/ppermute | solution.py:374
  10.0 0.0 collective-permute-done.got_a
  10.0 0.0 collective-permute-done.1.got_b
  10.1 1.7 %collective-permute-start.3 = (f32[7,4,640]{2,1,0:T(4,128)S(1)}, f32[7,4,640]{2,1,0:T(4,128)S(1)}, u32[]{:S(2)}, u32[]{:S(2)}) collective-permute-start(f32[7,4,640]{2,1,0:T(4,128)S(1)} %get-tuple-element.33), channel_id=1, source_target_pairs={{0,1},{1,0},{2,3},{3,2},{4,5},{5,4},{6,7},{7,6},{8,9},{9,8},{10,11... | collective-permute-start | bytes 215048 | tf_op jit(solution)/shard_map/ppermute | solution.py:342
  11.8 1.9 %collective-permute-start.4 = (f32[5,4,640]{2,1,0:T(4,128)S(1)}, f32[5,4,640]{2,1,0:T(4,128)S(1)}, u32[]{:S(2)}, u32[]{:S(2)}) collective-permute-start(f32[5,4,640]{2,1,0:T(4,128)S(1)} %get-tuple-element.34), channel_id=1, source_target_pairs={{1,2},{2,1},{5,6},{6,5},{9,10},{10,9},{13,14},{14,13},{17,18},{18,... | collective-permute-start | bytes 153608 | tf_op jit(solution)/shard_map/ppermute | solution.py:342
  13.7 0.1 shard_map.70
  13.8 4.0 %collective-permute-done.4.got_b = f32[5,4,640]{2,1,0:T(4,128)S(1)} collective-permute-done((f32[5,4,640]{2,1,0:T(4,128)S(1)}, f32[5,4,640]{2,1,0:T(4,128)S(1)}, u32[]{:S(2)}, u32[]{:S(2)}) %collective-permute-start.4) | collective-permute-done | bytes 51232 | tf_op jit(solution)/shard_map/ppermute | solution.py:342
  17.8 0.0 collective-permute-done.3.got_a
  17.8 0.9 %shard_map.72 = (f32[19,4,4,512]{3,2,1,0:T(4,128)S(1)}, f32[19,4,4,128]{3,2,1,0:T(4,128)S(1)}, f32[19,4,4,512]{3,2,1,0:T(4,128)}, f32[19,4,4,128]{3,2,1,0:T(4,128)}) custom-call(f32[19,4,4,512]{3,2,1,0:T(4,128)S(1)} %get-tuple-element.29.room_in, f32[19,4,4,128]{3,2,1,0:T(4,128)S(1)} %get-tuple-element.30.plen_in, ...), custom_call_target="tpu_custom_call", output_to_operand_aliasing={{0}: (0, {}), {1}: (1, {})} | custom-call | flops 100000 | bytes 1000000 | tf_op jit(solution)/shard_map/pallas_call | solution.py:401
  (1 shorter events, 0.0 us)
Async XLA Ops:
  2.7 7.3 %collective-permute-start = (f32[5,4,640]{2,1,0:T(4,128)S(1)}, f32[5,4,640]{2,1,0:T(4,128)S(1)}, u32[]{:S(2)}, u32[]{:S(2)}) collective-permute-start(f32[5,4,640]{2,1,0:T(4,128)S(1)} %get-tuple-element.24), channel_id=1, source_target_pairs={{0,4},{4,0},{8,12},{12,8},{16,20},{20,16},{24,28},{28,24},{1,5},{5... | collective-permute-start | bytes 153608 | tf_op jit(solution)/shard_map/ppermute | solution.py:342
  2.8 7.2 %collective-permute-start.1 = (f32[5,4,640]{2,1,0:T(4,128)S(1)}, f32[5,4,640]{2,1,0:T(4,128)S(1)}, u32[]{:S(2)}, u32[]{:S(2)}) collective-permute-start(f32[5,4,640]{2,1,0:T(4,128)S(1)} %get-tuple-element.25), channel_id=1, source_target_pairs={{0,28},{4,8},{8,4},{12,16},{16,12},{20,24},{24,20},{28,0},{1,29},{... | collective-permute-start | bytes 153608 | tf_op jit(solution)/shard_map/ppermute | solution.py:342
  5.3 4.7 %collective-permute-start.2 = (f32[2,4,1,640]{3,2,1,0:T(1,128)S(1)}, f32[2,4,1,640]{3,2,1,0:T(1,128)S(1)}, u32[]{:S(2)}, u32[]{:S(2)}) collective-permute-start(f32[2,4,1,640]{3,2,1,0:T(1,128)S(1)} %get-tuple-element.27), channel_id=1, source_target_pairs={{0,2},{1,3},{2,0},{3,1},{4,6},{5,7},{6,4},{7,5},{8,10},{9,11},{10,... | collective-permute-start | bytes 61448 | tf_op jit(solution)/shard_map/ppermute | solution.py:374
  5.7 0.7 %copy-start = (s32[32]{0:T(128)S(1)}, s32[32]{0:T(128)}, u32[]{:S(2)}) copy-start(s32[32]{0:T(128)} %cell_in.3) | copy-start | bytes 388
  5.7 0.7 %copy-start.1 = (s32[32,1]{0,1:T(1,128)S(1)}, s32[32,1]{0,1:T(1,128)}, u32[]{:S(2)}) copy-start(s32[32,1]{0,1:T(1,128)} %param.8) | copy-start | bytes 388
  10.1 7.7 %collective-permute-start.3 = (f32[7,4,640]{2,1,0:T(4,128)S(1)}, f32[7,4,640]{2,1,0:T(4,128)S(1)}, u32[]{:S(2)}, u32[]{:S(2)}) collective-permute-start(f32[7,4,640]{2,1,0:T(4,128)S(1)} %get-tuple-element.33), channel_id=1, source_target_pairs={{0,1},{1,0},{2,3},{3,2},{4,5},{5,4},{6,7},{7,6},{8,9},{9,8},{10,11... | collective-permute-start | bytes 215048 | tf_op jit(solution)/shard_map/ppermute | solution.py:342
  11.8 6.0 %collective-permute-start.4 = (f32[5,4,640]{2,1,0:T(4,128)S(1)}, f32[5,4,640]{2,1,0:T(4,128)S(1)}, u32[]{:S(2)}, u32[]{:S(2)}) collective-permute-start(f32[5,4,640]{2,1,0:T(4,128)S(1)} %get-tuple-element.34), channel_id=1, source_target_pairs={{1,2},{2,1},{5,6},{6,5},{9,10},{10,9},{13,14},{14,13},{17,18},{18,... | collective-permute-start | bytes 153608 | tf_op jit(solution)/shard_map/ppermute | solution.py:342

commit v3 on v2

v3 whole, which is shorter than its diff:
```python
import functools

import jax
import jax.numpy as jnp
from jax import lax
from jax.experimental import pallas as pl
from jax.experimental.pallas import tpu as pltpu
from jax.sharding import PartitionSpec as P

VELOCITIES = [
    (0, 0, 0),
    (1, 0, 0),
    (-1, 0, 0),
    (0, 1, 0),
    (0, -1, 0),
    (0, 0, 1),
    (0, 0, -1),
    (1, 1, 0),
    (-1, -1, 0),
    (1, -1, 0),
    (-1, 1, 0),
    (1, 0, 1),
    (-1, 0, -1),
    (1, 0, -1),
    (-1, 0, 1),
    (0, 1, 1),
    (0, -1, -1),
    (0, 1, -1),
    (0, -1, 1),
]
UPWARD = [5, 11, 14, 15, 18]
OMEGA = 1.25
CAP = 4
X_UP = [q for q in range(19) if VELOCITIES[q][0] == 1]
X_DOWN = [q for q in range(19) if VELOCITIES[q][0] == -1]
Y_UP = [q for q in range(19) if VELOCITIES[q][1] == 1]
Y_DOWN = [q for q in range(19) if VELOCITIES[q][1] == -1]
F32 = jnp.float32
LANES = 128
VMEM = pl.BlockSpec(memory_space=pltpu.VMEM)
HBM = pl.BlockSpec(memory_space=pltpu.HBM)


def collide(g):
    total = lambda i: g[i] + g[i + 1]
    apart = lambda i: g[i] - g[i + 1]
    dx, dy, dz = apart(1), apart(3), apart(5)
    d7, d9, d11, d13, d15, d17 = (apart(i) for i in (7, 9, 11, 13, 15, 17))
    edges = (total(7) + total(9)) + (total(11) + total(13)) + (total(15) + total(17))
    faces = total(1) + total(3) + total(5)
    rho = g[0] * (1.0 / 3.0) + faces * (1.0 / 18.0) + edges * (1.0 / 36.0)
    mx = dx * (1.0 / 18.0) + ((d7 + d9) + (d11 + d13)) * (1.0 / 36.0)
    my = dy * (1.0 / 18.0) + ((d7 - d9) + (d15 + d17)) * (1.0 / 36.0)
    mz = dz * (1.0 / 18.0) + ((d11 - d13) + (d15 - d17)) * (1.0 / 36.0)
    inv = 1.0 / rho
    base = OMEGA * rho - (1.5 * OMEGA) * inv * (mx * mx + my * my + mz * mz)
    square = (4.5 * OMEGA) * inv
    out = [None] * 19
    out[0] = base + (1.0 - OMEGA) * g[0]
    along = {1: mx, 3: my, 5: mz, 7: mx + my, 9: mx - my, 11: mx + mz, 13: mx - mz, 15: my + mz, 17: my - mz}
    for i, c in along.items():
        even = base + square * c * c
        odd = (3.0 * OMEGA) * c
        out[i] = (even + odd) + (1.0 - OMEGA) * g[i]
        out[i + 1] = (even - odd) + (1.0 - OMEGA) * g[i + 1]
    return out


def raised(value, cz, rows):
    if cz == 0:
        return value
    lane = lax.broadcasted_iota(jnp.int32, value.shape, 1)
    row = lax.broadcasted_iota(jnp.int32, value.shape, 0)
    total = value.shape[0]
    shift, edge = (1, 0) if cz == 1 else (LANES - 1, LANES - 1)
    turned = pltpu.roll(value, shift, 1)
    if rows == total:
        return jnp.where(lane == edge, value, turned)
    carried = pltpu.roll(turned, rows if cz == 1 else total - rows, 0)
    clamped = row < rows if cz == 1 else row >= total - rows
    return jnp.where(lane == edge, jnp.where(clamped, value, carried), turned)


def crossed(value, cy, cs):
    if cy == 0:
        return value
    row = lax.broadcasted_iota(jnp.int32, value.shape, 0) % cs
    turned = pltpu.roll(value, 1 if cy == 1 else value.shape[0] - 1, 0)
    return jnp.where(row == (0 if cy == 1 else cs - 1), value, turned)


def turned_to(value, source, dest):
    shift = (dest - source) % value.shape[0]
    return value if shift == 0 else pltpu.roll(value, shift, 0)


def plenum_kernel(sizes, relayed, room_in, plen_in, cell_in, owner_in, class_in, room_near, plen_post, *rest):
    ca, cs, blocks, n_span, per_brick = sizes
    jets = rest[:-6]
    columns, plen_buf, cells, owners, classes, sems = rest[-6:]
    copies = [pltpu.make_async_copy(src, dst, sems.at[i]) for i, (src, dst) in enumerate(
        ((plen_in, plen_buf), (cell_in, cells), (owner_in, owners), (class_in, classes), (room_in, room_near)))]
    for copy in copies:
        copy.start()
    for part in jets:
        part[...] = jnp.zeros_like(part)
    copies[0].wait()
    for r in range(0, ca * cs, 8):
        post = collide([plen_buf[q, r : r + 8] for q in range(19)])
        for q in range(19):
            plen_post[q, r : r + 8] = post[q]
        for k, q in enumerate(UPWARD):
            for y in range(8):
                columns[r + y, :, k * LANES : (k + 1) * LANES] = post[q][y : y + 1]
    for copy in copies[1:4]:
        copy.wait()
    here = lax.axis_index("span")
    first = here * per_brick

    def send_jet(i, carry):
        t = first + i
        owner = owners[t]
        share = 0.15 * (classes[t].astype(F32) + 1.0)
        slot = lax.fori_loop(0, i, lambda j, n: n + (owners[first + j] == owner).astype(jnp.int32), 0)
        column = share * columns[cells[t]]
        if not relayed:
            jets[0][owner, slot] = column
            return carry
        apart = owner ^ here

        @pl.when(apart < 2)
        def _():
            jets[0][apart, slot] = column

        @pl.when(apart >= 2)
        def _():
            jets[1][apart - 2, slot] = column

        return carry

    lax.fori_loop(0, per_brick, send_jet, 0)
    copies[4].wait()


def room_kernel(sizes, room_near, plen_post, room_post, swap_a, swap_b):
    ca, cs, blocks, n_span, per_brick = sizes
    rows = blocks * cs

    def plane(x, carry):
        for r in range(0, rows, 8):
            post = collide([room_near[q, x, r : r + 8] for q in range(19)])
            for q in range(19):
                room_post[q, x, r : r + 8] = post[q]
        return carry

    lax.fori_loop(0, ca, plane, 0)
    even = lax.axis_index("aisle") % 2 == 0
    for k in range(5):
        up, down = X_UP[k], X_DOWN[k]
        rising = raised(room_post[up, ca - 1], VELOCITIES[up][2], cs)
        falling = raised(room_post[down, 0], VELOCITIES[down][2], cs)
        swap_a[k * rows : (k + 1) * rows] = jnp.where(even, rising, falling)
        swap_b[k * rows : (k + 1) * rows] = jnp.where(even, falling, rising)
        rising = raised(plen_post[up, (ca - 1) * cs : ca * cs], VELOCITIES[up][2], cs)
        falling = raised(plen_post[down, 0:cs], VELOCITIES[down][2], cs)
        low = 5 * rows + k * cs
        swap_a[low : low + cs] = jnp.where(even, rising, falling)
        swap_b[low : low + cs] = jnp.where(even, falling, rising)


def local_kernel(sizes, room_post, plen_post, cell_in, owner_in, room_part, plen_part, span_up, span_down, places,
                 cells, owners, sems):
    ca, cs, blocks, n_span, per_brick = sizes
    rows = blocks * cs
    copies = [pltpu.make_async_copy(src, dst, sems.at[i]) for i, (src, dst) in enumerate(
        ((cell_in, cells), (owner_in, owners)))]
    for copy in copies:
        copy.start()
    group = lax.broadcasted_iota(jnp.int32, (rows, LANES), 0) % cs
    for q in range(19):
        cx, cy, cz = VELOCITIES[q]
        edge = cs - 1 if cy == 1 else 0
        span, planes = (span_up, Y_UP) if cy == 1 else (span_down, Y_DOWN)
        packed = None
        for x in range(ca):
            if not 0 <= x - cx < ca:
                continue
            value = raised(room_post[q, x - cx], cz, cs)
            room_part[q, x] = crossed(value, cy, cs)
            if cy:
                ready = turned_to(value, edge, x)
                packed = ready if packed is None else jnp.where(group == x, ready, packed)
        value = raised(plen_post[q], cz, ca * cs)
        if cx == 1:
            value = pltpu.roll(value, cs, 0)
        elif cx == -1:
            value = pltpu.roll(value, ca * cs - cs, 0)
        plen_part[q] = crossed(value, cy, cs)
        if cy:
            k = planes.index(q)
            span[k * rows : (k + 1) * rows] = packed
            for x in range(ca):
                to = 5 * rows + k * ca + x
                span[to : to + 1] = value[x * cs + edge : x * cs + edge + 1]
    places[...] = jnp.zeros_like(places)
    here = lax.axis_index("span")
    row = lax.broadcasted_iota(jnp.int32, (ca * cs, LANES), 0)
    for copy in copies:
        copy.wait()

    def brick(b, carry):
        def place(i, slot):
            t = b * per_brick + i
            mine = owners[t] == here

            @pl.when(mine)
            def _():
                places[b * CAP + slot] = (row == cells[t]).astype(F32)

            return slot + mine.astype(jnp.int32)

        lax.fori_loop(0, per_brick, place, 0)
        return carry

    lax.fori_loop(0, n_span, brick, 0)


def pack_kernel(sizes, relayed, got_a, got_b, span_up, span_down, *rest):
    ca, cs, blocks, n_span, per_brick = sizes
    rows = blocks * cs
    if relayed:
        jets, got_jets, cross_a, cross_b = rest
    else:
        cross_a, cross_b = rest
    even = lax.axis_index("aisle") % 2 == 0
    low = lax.axis_index("span") % 2 == 0
    halo = span_up.shape[0]
    group = lax.broadcasted_iota(jnp.int32, (rows, LANES), 0) % cs

    def corner(q, low, high):
        if VELOCITIES[q][0] == 1:
            k = X_UP.index(q)
            return jnp.where(even, got_b[low(k) : high(k)], got_a[low(k) : high(k)])
        k = X_DOWN.index(q)
        return jnp.where(even, got_a[low(k) : high(k)], got_b[low(k) : high(k)])

    for k in range(5):
        sides = []
        for span, planes, edge in ((span_up, Y_UP, cs - 1), (span_down, Y_DOWN, 0)):
            q = planes[k]
            value = span[k * rows : (k + 1) * rows]
            if VELOCITIES[q][0]:
                x = 0 if VELOCITIES[q][0] == 1 else ca - 1
                came = corner(q, lambda k: k * rows, lambda k: (k + 1) * rows)
                value = jnp.where(group == x, turned_to(came, edge, x), value)
            sides.append(value)
        cross_a[k * rows : (k + 1) * rows] = jnp.where(low, sides[0], sides[1])
        cross_b[k * rows : (k + 1) * rows] = jnp.where(low, sides[1], sides[0])
    for r in range(5 * rows, halo, 8):
        rising, falling = span_up[r : r + 8], span_down[r : r + 8]
        cross_a[r : r + 8] = jnp.where(low, rising, falling)
        cross_b[r : r + 8] = jnp.where(low, falling, rising)
    for planes, edge in ((Y_UP, cs - 1), (Y_DOWN, 0)):
        for k, q in enumerate(planes):
            if VELOCITIES[q][0]:
                x = 0 if VELOCITIES[q][0] == 1 else ca - 1
                at = lambda k: 5 * rows + k * cs + edge
                came = corner(q, at, lambda k: at(k) + 1)
                to = 5 * rows + k * ca + x

                @pl.when(low == (planes is Y_UP))
                def _():
                    cross_a[to : to + 1] = came

                @pl.when(low != (planes is Y_UP))
                def _():
                    cross_b[to : to + 1] = came

    if relayed:
        for b, source in enumerate((jets, got_jets)):
            for s in range(CAP):
                for k in range(5):
                    to = halo + (b * CAP + s) * 5 + k
                    cross_a[to : to + 1] = source[1, s, :, k * LANES : (k + 1) * LANES]


def jet_sums(start, places, bricks):
    sums = [start(k) for k in range(5)]
    for b, jet in bricks:
        for s in range(CAP):
            marks = places[b * CAP + s]
            sums = [total + marks * jet(s, k) for k, total in enumerate(sums)]
    return sums


def aisle_kernel(sizes, relayed, room_in, plen_in, got_a, got_b, jets, got_jets, places, room, plen, inflow):
    ca, cs, blocks, n_span, per_brick = sizes
    rows = blocks * cs
    even = lax.axis_index("aisle") % 2 == 0
    here = lax.axis_index("span")
    for k in range(5):
        for q, x, first, second in ((X_UP[k], 0, got_b, got_a), (X_DOWN[k], ca - 1, got_a, got_b)):
            cy = VELOCITIES[q][1]
            low, high = k * rows, (k + 1) * rows
            room[q, x] = crossed(jnp.where(even, first[low:high], second[low:high]), cy, cs)
            low = 5 * rows + k * cs
            value = jnp.where(even, first[low : low + cs], second[low : low + cs])
            at = x * cs
            if cy == 1:
                plen[q, at : at + 1] = value[0:1]
                plen[q, at + 1 : at + cs] = value[: cs - 1]
            elif cy == -1:
                plen[q, at + cs - 1 : at + cs] = value[cs - 1 : cs]
                plen[q, at : at + cs - 1] = value[1:cs]
            else:
                plen[q, at : at + cs] = value

    def put(sums):
        for k in range(5):
            inflow[k] = sums[k]

    def reader(source, b):
        return lambda s, k: source[b, s, :, k * LANES : (k + 1) * LANES]

    if relayed:
        put(jet_sums(lambda k: jnp.zeros((ca * cs, LANES), F32), places,
                     [(here, reader(jets, 0)), (here ^ 2, reader(got_jets, 0))]))
    else:
        inflow[...] = jnp.zeros_like(inflow)

        def brick(b, carry):
            put(jet_sums(lambda k: inflow[k], places, [(b, reader(got_jets, b))]))
            return carry

        lax.fori_loop(0, n_span, brick, 0)


def finish_kernel(sizes, relayed, room_in, plen_in, got_a, got_b, places, inflow, room, plen, room_out, plen_out, sems):
    ca, cs, blocks, n_span, per_brick = sizes
    rows = blocks * cs
    here = lax.axis_index("span")
    low = here % 2 == 0
    halo = 5 * (rows + cs)
    halo = halo + -halo % 8
    group = lax.broadcasted_iota(jnp.int32, (rows, LANES), 0) % cs

    def enter(got, up):
        planes, y = (Y_UP, 0) if up else (Y_DOWN, cs - 1)
        for k, q in enumerate(planes):
            came = got[k * rows : (k + 1) * rows]
            for x in range(ca):
                room[q, x] = jnp.where(group == y, turned_to(came, x, y), room[q, x])
                at = 5 * rows + k * ca + x
                plen[q, x * cs + y : x * cs + y + 1] = got[at : at + 1]

    @pl.when(low)
    def _():
        enter(got_a, False)

    @pl.when(jnp.logical_not(low))
    def _():
        enter(got_a, True)

    @pl.when(jnp.logical_and(low, here > 0))
    def _():
        enter(got_b, True)

    @pl.when(jnp.logical_and(jnp.logical_not(low), here < n_span - 1))
    def _():
        enter(got_b, False)

    plen_copy = pltpu.make_async_copy(plen, plen_out, sems.at[0])
    plen_copy.start()
    bricks = []
    if relayed:
        def reader(b):
            return lambda s, k: got_a[halo + (b * CAP + s) * 5 + k : halo + (b * CAP + s) * 5 + k + 1]

        bricks = [(here ^ 1, reader(0)), (here ^ 3, reader(1))]
    sums = jet_sums(lambda k: inflow[k], places, bricks)
    for k, q in enumerate(UPWARD):
        for x in range(ca):
            room[q, x, 0:cs] = room[q, x, 0:cs] + sums[k][x * cs : (x + 1) * cs]
    room_copy = pltpu.make_async_copy(room, room_out, sems.at[1])
    room_copy.start()
    plen_copy.wait()
    room_copy.wait()


def call(kernel, outs, in_specs, out_specs=None, scratch=(), aliases={}, flops=100_000, moved=1_000_000):
    return pl.pallas_call(
        kernel,
        out_shape=outs,
        in_specs=in_specs,
        out_specs=[VMEM] * len(outs) if out_specs is None else out_specs,
        scratch_shapes=list(scratch),
        input_output_aliases=aliases,
        cost_estimate=pl.CostEstimate(flops=flops, bytes_accessed=moved, transcendentals=0),
        compiler_params=pltpu.CompilerParams(vmem_limit_bytes=40 * 2**20),
    )


def swap(value, axis, odd, wraps):
    count = lax.axis_size(axis)
    pairs = []
    for i in range(count):
        j = (i ^ 1) if not odd else (i + 1 if i % 2 else i - 1)
        if wraps or 0 <= j < count:
            pairs.append((i, j % count))
    return lax.ppermute(value, axis, pairs)


def shards(room_pops, plenum_pops, tile_cell, tile_owner, tile_class):
    n_span = lax.axis_size("span")
    _, ca, cs, hr = room_pops.shape
    hp = plenum_pops.shape[3]
    blocks = hr // LANES
    rows = blocks * cs
    tiles = tile_cell.shape[0]
    sizes = (ca, cs, blocks, n_span, tiles // n_span)
    relayed = n_span == 4
    near = lambda shape: pltpu.VMEM(shape, F32)
    far = lambda value: pltpu.with_memory_space_constraint(value, pltpu.HBM)
    room_shape, plen_shape = (19, ca, rows, LANES), (19, ca * cs, LANES)
    halo = 5 * (rows + cs)
    halo = halo + -halo % 8
    room = far(room_pops.reshape(19, ca, cs, blocks, LANES).transpose(0, 1, 3, 2, 4).reshape(room_shape))
    plen = far(plenum_pops.reshape(plen_shape))
    tile_cell, tile_owner, tile_class = far(tile_cell), far(tile_owner.reshape(tiles)), far(tile_class)
    numbers = pltpu.SMEM((tiles,), jnp.int32)

    jets_shape = (2 if relayed else n_span, CAP, 1, 5 * hp)
    room_near, plen_post, *jets = call(
        functools.partial(plenum_kernel, sizes, relayed),
        [near(room_shape), near(plen_shape)] + [near(jets_shape)] * (2 if relayed else 1),
        [HBM] * 5,
        scratch=[pltpu.VMEM((ca * cs, 1, 5 * hp), F32), pltpu.VMEM(plen_shape, F32), numbers, numbers, numbers,
                 pltpu.SemaphoreType.DMA((5,))],
    )(room, plen, tile_cell, tile_owner, tile_class)
    if relayed:
        got_jets = lax.ppermute(jets[1], "span", [(i, i ^ 2) for i in range(4)])
    else:
        got_jets = lax.all_to_all(jets[0], "span", 0, 0, tiled=True)

    room_post, swap_a, swap_b = call(
        functools.partial(room_kernel, sizes),
        [near(room_shape), near((halo, LANES)), near((halo, LANES))],
        [VMEM] * 2,
    )(room_near, plen_post)
    got_a = swap(swap_a, "aisle", False, True)
    got_b = swap(swap_b, "aisle", True, True)

    room_part, plen_part, span_up, span_down, places = call(
        functools.partial(local_kernel, sizes),
        [near(room_shape), near(plen_shape), near((halo, LANES)), near((halo, LANES)),
         near((n_span * CAP, ca * cs, LANES))],
        [VMEM, VMEM, HBM, HBM],
        scratch=[numbers, numbers, pltpu.SemaphoreType.DMA((2,))],
    )(room_post, plen_post, tile_cell, tile_owner)

    cross_shape = (halo + 2 * CAP * 5, LANES) if relayed else (halo, LANES)
    cross_a, cross_b = call(
        functools.partial(pack_kernel, sizes, relayed),
        [near(cross_shape), near((halo, LANES))],
        [VMEM] * (6 if relayed else 4),
    )(got_a, got_b, span_up, span_down, *((jets[0], got_jets) if relayed else ()))

    in_b = swap(cross_b, "span", True, False)
    in_a = swap(cross_a, "span", False, False)
    room_part, plen_part, inflow = call(
        functools.partial(aisle_kernel, sizes, relayed),
        [near(room_shape), near(plen_shape), near((5, ca * cs, LANES))],
        [VMEM] * 7,
        aliases={0: 0, 1: 1},
    )(room_part, plen_part, got_a, got_b, jets[0], got_jets, places)

    _, _, room_next, plenum_next = call(
        functools.partial(finish_kernel, sizes, relayed),
        [near(room_shape), near(plen_shape), jax.ShapeDtypeStruct(room_shape, F32),
         jax.ShapeDtypeStruct(plen_shape, F32)],
        [VMEM] * 6,
        out_specs=[VMEM, VMEM, HBM, HBM],
        scratch=[pltpu.SemaphoreType.DMA((2,))],
        aliases={0: 0, 1: 1},
    )(room_part, plen_part, in_a, in_b, places, inflow)
    room_next = room_next.reshape(19, ca, blocks, cs, LANES).transpose(0, 1, 3, 2, 4).reshape(room_pops.shape)
    return room_next, plenum_next.reshape(plenum_pops.shape)


def solution(mesh):
    return jax.shard_map(
        shards,
        mesh=mesh,
        in_specs=(
            P(None, "aisle", "span", None),
            P(None, "aisle", "span", None),
            P("aisle"),
            P("aisle", None),
            P("aisle"),
        ),
        out_specs=(P(None, "aisle", "span", None), P(None, "aisle", "span", None)),
        check_vma=False,
    )
```

time: 18.9 us -> 18.7 us (0.989)
  waiting for transfers between devices: 6.31 us -> 7.19 us
  local copies, waits for them, and re-layouts: 0.67 us -> 0 us
  Pallas kernels: 4.5 us -> 4.03 us
    ppermute x1, waiting for transfers between devices: 2.3 us -> 3.13 us  [shards(): got_jets = lax.ppermute(jets[1], 'span', [(i, i ^ 2) for i in range(4)])]
    unnamed x4 -> x0, local copies, waits for them, and re-layouts: 0.67 us -> none
    pallas_call x5 -> x6, Pallas kernels: 4.5 us -> 4.03 us  [the longest x1 1.45 us: shards(): call(functools.partial(plenum_kernel, sizes, relayed), [near(room_shape),...]
  transfers between devices with their start and end apart: 5 -> 5, of which waited for: 2 -> 2; matrix products, arithmetic and copies ran while one was open for 0% -> 0% of each run, Pallas kernels for 8% -> 7%
where the time goes in v3:
time: 18.7 us; the launch traced here: 18.5 us
  waiting for transfers between devices  7.19 us (38%)
  starting transfers between devices  6.6 us (35%)
  Pallas kernels  4.03 us (22%)
  between operations  0.69 us (4%)
    ppermute x4, starting transfers between devices, swap(): return lax.ppermute(value, axis, pairs)  6.26 us
    ppermute x4, waiting for transfers between devices, swap(): return lax.ppermute(value, axis, pairs)  4.06 us
    ppermute x1, waiting for transfers between devices, shards(): got_jets = lax.ppermute(jets[1], 'span', [(i, i ^ 2) for i in range(4)])  3.13 us
    pallas_call x1, Pallas kernels, shards(): call(functools.partial(plenum_kernel, sizes, relayed), [near(room_shape),...  1.45 us
    pallas_call x1, Pallas kernels, shards(): call(functools.partial(local_kernel, sizes), [near(room_shape), near(plen...  1.21 us
    pallas_call x1, Pallas kernels, shards(): call(functools.partial(finish_kernel, sizes, relayed), [near(room_shape),...  0.95 us
  transfers between devices with their start and end apart: 5, of which 2 were waited for; matrix products, arithmetic and copies ran while one was open for 0% of the time, Pallas kernels for 7%

profile of v3, /device:TPU:16, one launch (start us, length us, event | category | flops | bytes accessed | tf_op | source)
XLA Modules:
  0.0 18.5 jit_solution(15628460112267696436)
XLA Ops:
  0.6 1.4 %shard_map.68 = (f32[19,4,16,128]{3,2,1,0:T(8,128)S(1)}, f32[19,16,128]{2,1,0:T(8,128)S(1)}, f32[2,4,1,640]{3,2,1,0:T(1,128)S(1)}, f32[2,4,1,640]{3,2,1,0:T(1,128)S(1)}) custom-call(f32[19,4,16,128]{3,2,1,0:T(8,128)} %bitcast.13, f32[19,16,128]{2,1,0:T(8,128)} %bitcast.14, s32[32]{0:T(128)} %cell_in.3, s32[32]{0:T(128)} %bitcast.15, s32[32]{0:T(128)} %class_in.1), custom_call_target="tpu_custom_call" | custom-call | flops 100000 | bytes 1000000 | tf_op jit(solution)/shard_map/pallas_call | solution.py:433
  2.1 0.3 %shard_map.69 = (f32[19,4,16,128]{3,2,1,0:T(8,128)S(1)}, f32[104,128]{1,0:T(8,128)S(1)}, f32[104,128]{1,0:T(8,128)S(1)}) custom-call(f32[19,4,16,128]{3,2,1,0:T(8,128)S(1)} %get-tuple-element.21.room_near, f32[19,16,128]{2,1,0:T(8,128)S(1)} %get-tuple-element.22.plen_post), custom_call_target="tpu_custom_call" | custom-call | flops 100000 | bytes 1000000 | tf_op jit(solution)/shard_map/pallas_call | solution.py:445
  2.4 0.1 collective-permute-start
  2.5 2.5 %collective-permute-start.1 = (f32[104,128]{1,0:T(8,128)S(1)}, f32[104,128]{1,0:T(8,128)S(1)}, u32[]{:S(2)}, u32[]{:S(2)}) collective-permute-start(f32[104,128]{1,0:T(8,128)S(1)} %get-tuple-element.27), channel_id=1, source_target_pairs={{0,28},{4,8},{8,4},{12,16},{16,12},{20,24},{24,20},{28,0},{1,29},{... | collective-permute-start | bytes 159752 | tf_op jit(solution)/shard_map/ppermute | solution.py:410
  5.0 0.3 %collective-permute-start.2 = (f32[2,4,1,640]{3,2,1,0:T(1,128)S(1)}, f32[2,4,1,640]{3,2,1,0:T(1,128)S(1)}, u32[]{:S(2)}, u32[]{:S(2)}) collective-permute-start(f32[2,4,1,640]{3,2,1,0:T(1,128)S(1)} %get-tuple-element.29), channel_id=1, source_target_pairs={{0,2},{1,3},{2,0},{3,1},{4,6},{5,7},{6,4},{7,5},{8,10},{9,11},{10,... | collective-permute-start | bytes 61448 | tf_op jit(solution)/shard_map/ppermute | solution.py:441
  5.4 1.2 %shard_map.70 = (f32[19,4,16,128]{3,2,1,0:T(8,128)S(1)}, f32[19,16,128]{2,1,0:T(8,128)S(1)}, f32[104,128]{1,0:T(8,128)S(1)}, f32[104,128]{1,0:T(8,128)S(1)}, f32[16,16,128]{2,1,0:T(8,128)S(1)}) custom-call(f32[19,4,16,128]{3,2,1,0:T(8,128)S(1)} %get-tuple-element.23.room_post, f32[19,16,128]{2,1,0:T(8,128)S(1)} %get-tuple-element.22.plen_post, s32[32]{0:T(128)} %cell_in.3, ...), custom_call_target="tpu_custom_call" | custom-call | flops 100000 | bytes 1000000 | tf_op jit(solution)/shard_map/pallas_call | solution.py:453
  6.6 3.1 %collective-permute-done.2.got_jets.rest_1_ = f32[2,4,1,640]{3,2,1,0:T(1,128)S(1)} collective-permute-done((f32[2,4,1,640]{3,2,1,0:T(1,128)S(1)}, f32[2,4,1,640]{3,2,1,0:T(1,128)S(1)}, u32[]{:S(2)}, u32[]{:S(2)}) %collective-permute-start.2) | collective-permute-done | bytes 20512 | tf_op jit(solution)/shard_map/ppermute | solution.py:441
  9.7 0.0 collective-permute-done.got_a
  9.7 0.0 collective-permute-done.1.got_b
  9.8 1.7 %collective-permute-start.3 = (f32[144,128]{1,0:T(8,128)S(1)}, f32[144,128]{1,0:T(8,128)S(1)}, u32[]{:S(2)}, u32[]{:S(2)}) collective-permute-start(f32[144,128]{1,0:T(8,128)S(1)} %get-tuple-element.35), channel_id=1, source_target_pairs={{0,1},{1,0},{2,3},{3,2},{4,5},{5,4},{6,7},{7,6},{8,9},{9,8},{10,11... | collective-permute-start | bytes 221192 | tf_op jit(solution)/shard_map/ppermute | solution.py:410
  11.5 1.9 %collective-permute-start.4 = (f32[104,128]{1,0:T(8,128)S(1)}, f32[104,128]{1,0:T(8,128)S(1)}, u32[]{:S(2)}, u32[]{:S(2)}) collective-permute-start(f32[104,128]{1,0:T(8,128)S(1)} %get-tuple-element.36), channel_id=1, source_target_pairs={{1,2},{2,1},{5,6},{6,5},{9,10},{10,9},{13,14},{14,13},{17,18},{18,... | collective-permute-start | bytes 159752 | tf_op jit(solution)/shard_map/ppermute | solution.py:410
  13.5 4.0 %collective-permute-done.4.got_b = f32[104,128]{1,0:T(8,128)S(1)} collective-permute-done((f32[104,128]{1,0:T(8,128)S(1)}, f32[104,128]{1,0:T(8,128)S(1)}, u32[]{:S(2)}, u32[]{:S(2)}) %collective-permute-start.4) | collective-permute-done | bytes 53280 | tf_op jit(solution)/shard_map/ppermute | solution.py:410
  17.6 0.0 collective-permute-done.3.got_a
  17.6 0.9 %shard_map.73 = (f32[19,4,16,128]{3,2,1,0:T(8,128)S(1)}, f32[19,16,128]{2,1,0:T(8,128)S(1)}, f32[19,4,16,128]{3,2,1,0:T(8,128)}, f32[19,16,128]{2,1,0:T(8,128)}) custom-call(f32[19,4,16,128]{3,2,1,0:T(8,128)S(1)} %get-tuple-element.31.room_in, f32[19,16,128]{2,1,0:T(8,128)S(1)} %get-tuple-element.32.plen_in, ...), custom_call_target="tpu_custom_call", output_to_operand_aliasing={{0}: (0, {}), {1}: (1, {})} | custom-call | flops 100000 | bytes 1000000 | tf_op jit(solution)/shard_map/pallas_call | solution.py:477
  (2 shorter events, 0.1 us)
Async XLA Ops:
  2.4 7.3 %collective-permute-start = (f32[104,128]{1,0:T(8,128)S(1)}, f32[104,128]{1,0:T(8,128)S(1)}, u32[]{:S(2)}, u32[]{:S(2)}) collective-permute-start(f32[104,128]{1,0:T(8,128)S(1)} %get-tuple-element.26), channel_id=1, source_target_pairs={{0,4},{4,0},{8,12},{12,8},{16,20},{20,16},{24,28},{28,24},{1,5},{5... | collective-permute-start | bytes 159752 | tf_op jit(solution)/shard_map/ppermute | solution.py:410
  2.5 7.2 %collective-permute-start.1 = (f32[104,128]{1,0:T(8,128)S(1)}, f32[104,128]{1,0:T(8,128)S(1)}, u32[]{:S(2)}, u32[]{:S(2)}) collective-permute-start(f32[104,128]{1,0:T(8,128)S(1)} %get-tuple-element.27), channel_id=1, source_target_pairs={{0,28},{4,8},{8,4},{12,16},{16,12},{20,24},{24,20},{28,0},{1,29},{... | collective-permute-start | bytes 159752 | tf_op jit(solution)/shard_map/ppermute | solution.py:410
  5.0 4.7 %collective-permute-start.2 = (f32[2,4,1,640]{3,2,1,0:T(1,128)S(1)}, f32[2,4,1,640]{3,2,1,0:T(1,128)S(1)}, u32[]{:S(2)}, u32[]{:S(2)}) collective-permute-start(f32[2,4,1,640]{3,2,1,0:T(1,128)S(1)} %get-tuple-element.29), channel_id=1, source_target_pairs={{0,2},{1,3},{2,0},{3,1},{4,6},{5,7},{6,4},{7,5},{8,10},{9,11},{10,... | collective-permute-start | bytes 61448 | tf_op jit(solution)/shard_map/ppermute | solution.py:441
  9.8 7.8 %collective-permute-start.3 = (f32[144,128]{1,0:T(8,128)S(1)}, f32[144,128]{1,0:T(8,128)S(1)}, u32[]{:S(2)}, u32[]{:S(2)}) collective-permute-start(f32[144,128]{1,0:T(8,128)S(1)} %get-tuple-element.35), channel_id=1, source_target_pairs={{0,1},{1,0},{2,3},{3,2},{4,5},{5,4},{6,7},{7,6},{8,9},{9,8},{10,11... | collective-permute-start | bytes 221192 | tf_op jit(solution)/shard_map/ppermute | solution.py:410
  11.5 6.0 %collective-permute-start.4 = (f32[104,128]{1,0:T(8,128)S(1)}, f32[104,128]{1,0:T(8,128)S(1)}, u32[]{:S(2)}, u32[]{:S(2)}) collective-permute-start(f32[104,128]{1,0:T(8,128)S(1)} %get-tuple-element.36), channel_id=1, source_target_pairs={{1,2},{2,1},{5,6},{6,5},{9,10},{10,9},{13,14},{14,13},{17,18},{18,... | collective-permute-start | bytes 159752 | tf_op jit(solution)/shard_map/ppermute | solution.py:410

commit v4 on v3

--- a/solution.py
+++ b/solution.py
@@ -94,16 +94,23 @@
     return value if shift == 0 else pltpu.roll(value, shift, 0)
 
 
+def repeat(count, body, start):
+    if count > 8:
+        return lax.fori_loop(0, count, body, start)
+    for i in range(count):
+        start = body(i, start)
+    return start
+
+
 def plenum_kernel(sizes, relayed, room_in, plen_in, cell_in, owner_in, class_in, room_near, plen_post, *rest):
     ca, cs, blocks, n_span, per_brick = sizes
-    jets = rest[:-6]
-    columns, plen_buf, cells, owners, classes, sems = rest[-6:]
+    jets = rest[:-7]
+    columns, dealt, plen_buf, cells, owners, classes, sems = rest[-7:]
     copies = [pltpu.make_async_copy(src, dst, sems.at[i]) for i, (src, dst) in enumerate(
         ((plen_in, plen_buf), (cell_in, cells), (owner_in, owners), (class_in, classes), (room_in, room_near)))]
     for copy in copies:
         copy.start()
-    for part in jets:
-        part[...] = jnp.zeros_like(part)
+    dealt[...] = jnp.zeros_like(dealt)
     copies[0].wait()
     for r in range(0, ca * cs, 8):
         post = collide([plen_buf[q, r : r + 8] for q in range(19)])
@@ -121,24 +128,20 @@
         t = first + i
         owner = owners[t]
         share = 0.15 * (classes[t].astype(F32) + 1.0)
-        slot = lax.fori_loop(0, i, lambda j, n: n + (owners[first + j] == owner).astype(jnp.int32), 0)
-        column = share * columns[cells[t]]
-        if not relayed:
-            jets[0][owner, slot] = column
-            return carry
-        apart = owner ^ here
-
-        @pl.when(apart < 2)
-        def _():
-            jets[0][apart, slot] = column
-
-        @pl.when(apart >= 2)
-        def _():
-            jets[1][apart - 2, slot] = column
-
+        same = lambda j, n: n + (owners[first + j] == owner).astype(jnp.int32)
+        slot = repeat(i, same, 0) if relayed else lax.fori_loop(0, i, same, 0)
+        to = (owner ^ here if relayed else owner) * CAP + slot
+        dealt[to] = share * columns[cells[t]]
         return carry
 
-    lax.fori_loop(0, per_brick, send_jet, 0)
+    if relayed:
+        for i in range(per_brick):
+            send_jet(i, 0)
+    else:
+        lax.fori_loop(0, per_brick, send_jet, 0)
+    for part, jet in enumerate(jets):
+        many = jet.shape[0]
+        jet[...] = dealt[part * many : (part + 1) * many]
     copies[4].wait()
 
 
@@ -168,8 +171,17 @@
         swap_b[low : low + cs] = jnp.where(even, falling, rising)
 
 
-def local_kernel(sizes, room_post, plen_post, cell_in, owner_in, room_part, plen_part, span_up, span_down, places,
-                 cells, owners, sems):
+def jet_sums(start, places, bricks):
+    sums = [start(k) for k in range(5)]
+    for b, jet in bricks:
+        for s in range(CAP):
+            marks = places[b * CAP + s]
+            sums = [total + marks * jet(s, k) for k, total in enumerate(sums)]
+    return sums
+
+
+def local_kernel(sizes, relayed, room_post, plen_post, jets, got_jets, cell_in, owner_in, room_part, plen_part, span_up,
+                 span_down, places, inflow, cells, owners, sems):
     ca, cs, blocks, n_span, per_brick = sizes
     rows = blocks * cs
     copies = [pltpu.make_async_copy(src, dst, sems.at[i]) for i, (src, dst) in enumerate(
@@ -202,7 +214,7 @@
             for x in range(ca):
                 to = 5 * rows + k * ca + x
                 span[to : to + 1] = value[x * cs + edge : x * cs + edge + 1]
-    places[...] = jnp.zeros_like(places)
+    places[0 : n_span * CAP] = jnp.zeros((n_span * CAP, ca * cs, LANES), F32)
     here = lax.axis_index("span")
     row = lax.broadcasted_iota(jnp.int32, (ca * cs, LANES), 0)
     for copy in copies:
@@ -212,17 +224,32 @@
         def place(i, slot):
             t = b * per_brick + i
             mine = owners[t] == here
-
-            @pl.when(mine)
-            def _():
-                places[b * CAP + slot] = (row == cells[t]).astype(F32)
-
+            places[jnp.where(mine, b * CAP + slot, n_span * CAP)] = (row == cells[t]).astype(F32)
             return slot + mine.astype(jnp.int32)
 
-        lax.fori_loop(0, per_brick, place, 0)
+        repeat(per_brick, place, 0)
         return carry
 
-    lax.fori_loop(0, n_span, brick, 0)
+    repeat(n_span, brick, 0)
+
+    def put(sums):
+        for k in range(5):
+            inflow[k] = sums[k]
+
+    def reader(source, b):
+        return lambda s, k: source[b * CAP + s, :, k * LANES : (k + 1) * LANES]
+
+    if relayed:
+        put(jet_sums(lambda k: jnp.zeros((ca * cs, LANES), F32), places,
+                     [(here, reader(jets, 0)), (here ^ 2, reader(got_jets, 0))]))
+    else:
+        inflow[...] = jnp.zeros_like(inflow)
+
+        def add_brick(b, carry):
+            put(jet_sums(lambda k: inflow[k], places, [(b, reader(got_jets, b))]))
+            return carry
+
+        lax.fori_loop(0, n_span, add_brick, 0)
 
 
 def pack_kernel(sizes, relayed, got_a, got_b, span_up, span_down, *rest):
@@ -281,23 +308,13 @@
             for s in range(CAP):
                 for k in range(5):
                     to = halo + (b * CAP + s) * 5 + k
-                    cross_a[to : to + 1] = source[1, s, :, k * LANES : (k + 1) * LANES]
-
-
-def jet_sums(start, places, bricks):
-    sums = [start(k) for k in range(5)]
-    for b, jet in bricks:
-        for s in range(CAP):
-            marks = places[b * CAP + s]
-            sums = [total + marks * jet(s, k) for k, total in enumerate(sums)]
-    return sums
-
-
-def aisle_kernel(sizes, relayed, room_in, plen_in, got_a, got_b, jets, got_jets, places, room, plen, inflow):
+                    cross_a[to : to + 1] = source[CAP + s, :, k * LANES : (k + 1) * LANES]
+
+
+def aisle_kernel(sizes, room_in, plen_in, got_a, got_b, room, plen):
     ca, cs, blocks, n_span, per_brick = sizes
     rows = blocks * cs
     even = lax.axis_index("aisle") % 2 == 0
-    here = lax.axis_index("span")
     for k in range(5):
         for q, x, first, second in ((X_UP[k], 0, got_b, got_a), (X_DOWN[k], ca - 1, got_a, got_b)):
             cy = VELOCITIES[q][1]
@@ -315,25 +332,6 @@
             else:
                 plen[q, at : at + cs] = value
 
-    def put(sums):
-        for k in range(5):
-            inflow[k] = sums[k]
-
-    def reader(source, b):
-        return lambda s, k: source[b, s, :, k * LANES : (k + 1) * LANES]
-
-    if relayed:
-        put(jet_sums(lambda k: jnp.zeros((ca * cs, LANES), F32), places,
-                     [(here, reader(jets, 0)), (here ^ 2, reader(got_jets, 0))]))
-    else:
-        inflow[...] = jnp.zeros_like(inflow)
-
-        def brick(b, carry):
-            put(jet_sums(lambda k: inflow[k], places, [(b, reader(got_jets, b))]))
-            return carry
-
-        lax.fori_loop(0, n_span, brick, 0)
-
 
 def finish_kernel(sizes, relayed, room_in, plen_in, got_a, got_b, places, inflow, room, plen, room_out, plen_out, sems):
     ca, cs, blocks, n_span, per_brick = sizes
@@ -343,6 +341,24 @@
     halo = 5 * (rows + cs)
     halo = halo + -halo % 8
     group = lax.broadcasted_iota(jnp.int32, (rows, LANES), 0) % cs
+    spans = [[], [], []]
+    for q in range(19):
+        stage = 2 if q in UPWARD else 1 if VELOCITIES[q][1] else 0
+        if spans[stage] and spans[stage][-1][1] == q:
+            spans[stage][-1][1] = q + 1
+        else:
+            spans[stage].append([q, q + 1])
+    copies, sem = [], 1
+    for stage in spans:
+        copies.append([])
+        for low_q, high_q in stage:
+            copies[-1].append(pltpu.make_async_copy(room.at[low_q:high_q], room_out.at[low_q:high_q], sems.at[sem]))
+            sem = sem + 1
+    copies[1].append(pltpu.make_async_copy(plen, plen_out, sems.at[0]))
+
+    def put_out(stage):
+        for copy in copies[stage]:
+            copy.start()
 
     def enter(got, up):
         planes, y = (Y_UP, 0) if up else (Y_DOWN, cs - 1)
@@ -353,6 +369,8 @@
                 at = 5 * rows + k * ca + x
                 plen[q, x * cs + y : x * cs + y + 1] = got[at : at + 1]
 
+    put_out(0)
+
     @pl.when(low)
     def _():
         enter(got_a, False)
@@ -369,8 +387,7 @@
     def _():
         enter(got_b, False)
 
-    plen_copy = pltpu.make_async_copy(plen, plen_out, sems.at[0])
-    plen_copy.start()
+    put_out(1)
     bricks = []
     if relayed:
         def reader(b):
@@ -381,10 +398,10 @@
     for k, q in enumerate(UPWARD):
         for x in range(ca):
             room[q, x, 0:cs] = room[q, x, 0:cs] + sums[k][x * cs : (x + 1) * cs]
-    room_copy = pltpu.make_async_copy(room, room_out, sems.at[1])
-    room_copy.start()
-    plen_copy.wait()
-    room_copy.wait()
+    put_out(2)
+    for group in copies:
+        for copy in group:
+            copy.wait()
 
 
 def call(kernel, outs, in_specs, out_specs=None, scratch=(), aliases={}, flops=100_000, moved=1_000_000):
@@ -429,12 +446,12 @@
     tile_cell, tile_owner, tile_class = far(tile_cell), far(tile_owner.reshape(tiles)), far(tile_class)
     numbers = pltpu.SMEM((tiles,), jnp.int32)
 
-    jets_shape = (2 if relayed else n_span, CAP, 1, 5 * hp)
+    jets_shape = ((2 if relayed else n_span) * CAP, 1, 5 * hp)
     room_near, plen_post, *jets = call(
         functools.partial(plenum_kernel, sizes, relayed),
         [near(room_shape), near(plen_shape)] + [near(jets_shape)] * (2 if relayed else 1),
         [HBM] * 5,
-        scratch=[pltpu.VMEM((ca * cs, 1, 5 * hp), F32), pltpu.VMEM(plen_shape, F32), numbers, numbers, numbers,
+        scratch=[pltpu.VMEM((ca * cs, 1, 5 * hp), F32), near((n_span * CAP, 1, 5 * hp)), near(plen_shape), numbers, numbers, numbers,
                  pltpu.SemaphoreType.DMA((5,))],
     )(room, plen, tile_cell, tile_owner, tile_class)
     if relayed:
@@ -450,13 +467,14 @@
     got_a = swap(swap_a, "aisle", False, True)
     got_b = swap(swap_b, "aisle", True, True)
 
-    room_part, plen_part, span_up, span_down, places = call(
-        functools.partial(local_kernel, sizes),
+    room_part, plen_part, span_up, span_down, places, inflow = call(
+        functools.partial(local_kernel, sizes, relayed),
         [near(room_shape), near(plen_shape), near((halo, LANES)), near((halo, LANES)),
-         near((n_span * CAP, ca * cs, LANES))],
-        [VMEM, VMEM, HBM, HBM],
+         near((n_span * CAP + 1, ca * cs, LANES)), near((5, ca * cs, LANES))],
+        [VMEM, VMEM, VMEM, VMEM, HBM, HBM],
         scratch=[numbers, numbers, pltpu.SemaphoreType.DMA((2,))],
-    )(room_post, plen_post, tile_cell, tile_owner)
+        flops=10**9,
+    )(room_post, plen_post, jets[0], got_jets, tile_cell, tile_owner)
 
     cross_shape = (halo + 2 * CAP * 5, LANES) if relayed else (halo, LANES)
     cross_a, cross_b = call(
@@ -467,12 +485,12 @@
 
     in_b = swap(cross_b, "span", True, False)
     in_a = swap(cross_a, "span", False, False)
-    room_part, plen_part, inflow = call(
-        functools.partial(aisle_kernel, sizes, relayed),
-        [near(room_shape), near(plen_shape), near((5, ca * cs, LANES))],
-        [VMEM] * 7,
+    room_part, plen_part = call(
+        functools.partial(aisle_kernel, sizes),
+        [near(room_shape), near(plen_shape)],
+        [VMEM] * 4,
         aliases={0: 0, 1: 1},
-    )(room_part, plen_part, got_a, got_b, jets[0], got_jets, places)
+    )(room_part, plen_part, got_a, got_b)
 
     _, _, room_next, plenum_next = call(
         functools.partial(finish_kernel, sizes, relayed),
@@ -480,7 +498,7 @@
          jax.ShapeDtypeStruct(plen_shape, F32)],
         [VMEM] * 6,
         out_specs=[VMEM, VMEM, HBM, HBM],
-        scratch=[pltpu.SemaphoreType.DMA((2,))],
+        scratch=[pltpu.SemaphoreType.DMA((20,))],
         aliases={0: 0, 1: 1},
     )(room_part, plen_part, in_a, in_b, places, inflow)
     room_next = room_next.reshape(19, ca, blocks, cs, LANES).transpose(0, 1, 3, 2, 4).reshape(room_pops.shape)

time: 18.7 us -> 17.5 us (0.936)
  the two profiles are of different devices: /device:TPU:16 before, /device:TPU:12 now
where the time goes in v4:
time: 17.5 us; the launch traced here: 17.3 us
  starting transfers between devices  7.25 us (41%)
  waiting for transfers between devices  5.91 us (34%)
  Pallas kernels  3.43 us (20%)
  between operations  0.7 us (4%)
    ppermute x4, waiting for transfers between devices, swap(): return lax.ppermute(value, axis, pairs)  5.76 us
    ppermute x4, starting transfers between devices, swap(): return lax.ppermute(value, axis, pairs)  4.59 us
    ppermute x1, starting transfers between devices, shards(): got_jets = lax.ppermute(jets[1], 'span', [(i, i ^ 2) for i in range(4)])  2.65 us
    pallas_call x1, Pallas kernels, shards(): call(functools.partial(plenum_kernel, sizes, relayed), [near(room_shape),...  1.21 us
    pallas_call x1, Pallas kernels, shards(): call(functools.partial(finish_kernel, sizes, relayed), [near(room_shape),...  1.04 us
    pallas_call x1, Pallas kernels, shards(): call(functools.partial(local_kernel, sizes, relayed), [near(room_shape),...  0.79 us
  transfers between devices with their start and end apart: 5, of which 3 were waited for; matrix products, arithmetic and copies ran while one was open for 0% of the time, Pallas kernels for 7%

profile of v4, /device:TPU:12, one launch (start us, length us, event | category | flops | bytes accessed | tf_op | source)
XLA Modules:
  0.0 17.3 jit_solution(1992610660153467281)
XLA Ops:
  0.6 1.2 %shard_map.68 = (f32[19,4,16,128]{3,2,1,0:T(8,128)S(1)}, f32[19,16,128]{2,1,0:T(8,128)S(1)}, f32[8,1,640]{2,1,0:T(1,128)S(1)}, f32[8,1,640]{2,1,0:T(1,128)S(1)}) custom-call(f32[19,4,16,128]{3,2,1,0:T(8,128)} %bitcast.13, f32[19,16,128]{2,1,0:T(8,128)} %bitcast.14, s32[32]{0:T(128)} %cell_in.3, s32[32]{0:T(128)} %bitcast.15, s32[32]{0:T(128)} %class_in.1), custom_call_target="tpu_custom_call" | custom-call | flops 100000 | bytes 1000000 | tf_op jit(solution)/shard_map/pallas_call | solution.py:450
  1.8 2.7 %collective-permute-start = (f32[8,1,640]{2,1,0:T(1,128)S(1)}, f32[8,1,640]{2,1,0:T(1,128)S(1)}, u32[]{:S(2)}, u32[]{:S(2)}) collective-permute-start(f32[8,1,640]{2,1,0:T(1,128)S(1)} %get-tuple-element.25), channel_id=1, source_target_pairs={{0,2},{1,3},{2,0},{3,1},{4,6},{5,7},{6,4},{7,5},{8,10},{9,11},{10,... | collective-permute-start | bytes 61448 | tf_op jit(solution)/shard_map/ppermute | solution.py:458
  4.5 0.3 %shard_map.69 = (f32[19,4,16,128]{3,2,1,0:T(8,128)S(1)}, f32[104,128]{1,0:T(8,128)S(1)}, f32[104,128]{1,0:T(8,128)S(1)}) custom-call(f32[19,4,16,128]{3,2,1,0:T(8,128)S(1)} %get-tuple-element.21.room_near, f32[19,16,128]{2,1,0:T(8,128)S(1)} %get-tuple-element.22.plen_post), custom_call_target="tpu_custom_call" | custom-call | flops 100000 | bytes 1000000 | tf_op jit(solution)/shard_map/pallas_call | solution.py:462
  4.8 0.1 collective-permute-start.1
  4.9 1.5 %collective-permute-start.2 = (f32[104,128]{1,0:T(8,128)S(1)}, f32[104,128]{1,0:T(8,128)S(1)}, u32[]{:S(2)}, u32[]{:S(2)}) collective-permute-start(f32[104,128]{1,0:T(8,128)S(1)} %get-tuple-element.29), channel_id=1, source_target_pairs={{0,28},{4,8},{8,4},{12,16},{16,12},{20,24},{24,20},{28,0},{1,29},{... | collective-permute-start | bytes 159752 | tf_op jit(solution)/shard_map/ppermute | solution.py:427
  6.4 0.1 collective-permute-done.got_jets.rest_1_
  6.6 0.8 %shard_map.70 = (f32[19,4,16,128]{3,2,1,0:T(8,128)S(1)}, f32[19,16,128]{2,1,0:T(8,128)S(1)}, f32[104,128]{1,0:T(8,128)S(1)}, f32[104,128]{1,0:T(8,128)S(1)}, f32...) custom-call(f32[19,4,16,128]{3,2,1,0:T(8,128)S(1)} %get-tuple-element.23.room_post, ...), custom_call_target="tpu_custom_call" | custom-call | flops 1000000000 | bytes 1000000 | tf_op jit(solution)/shard_map/pallas_call | solution.py:470
  7.4 0.0 collective-permute-done.1.got_a
  7.4 2.3 %collective-permute-done.2.got_b = f32[104,128]{1,0:T(8,128)S(1)} collective-permute-done((f32[104,128]{1,0:T(8,128)S(1)}, f32[104,128]{1,0:T(8,128)S(1)}, u32[]{:S(2)}, u32[]{:S(2)}) %collective-permute-start.2) | collective-permute-done | bytes 53280 | tf_op jit(solution)/shard_map/ppermute | solution.py:427
  9.7 0.5 %collective-permute-start.3 = (f32[144,128]{1,0:T(8,128)S(1)}, f32[144,128]{1,0:T(8,128)S(1)}, u32[]{:S(2)}, u32[]{:S(2)}) collective-permute-start(f32[144,128]{1,0:T(8,128)S(1)} %get-tuple-element.34), channel_id=1, source_target_pairs={{0,1},{1,0},{2,3},{3,2},{4,5},{5,4},{6,7},{7,6},{8,9},{9,8},{10,11... | collective-permute-start | bytes 221192 | tf_op jit(solution)/shard_map/ppermute | solution.py:427
  10.2 2.5 %collective-permute-start.4 = (f32[104,128]{1,0:T(8,128)S(1)}, f32[104,128]{1,0:T(8,128)S(1)}, u32[]{:S(2)}, u32[]{:S(2)}) collective-permute-start(f32[104,128]{1,0:T(8,128)S(1)} %get-tuple-element.35), channel_id=1, source_target_pairs={{1,2},{2,1},{5,6},{6,5},{9,10},{10,9},{13,14},{14,13},{17,18},{18,... | collective-permute-start | bytes 159752 | tf_op jit(solution)/shard_map/ppermute | solution.py:427
  12.7 3.5 %collective-permute-done.4.got_b = f32[104,128]{1,0:T(8,128)S(1)} collective-permute-done((f32[104,128]{1,0:T(8,128)S(1)}, f32[104,128]{1,0:T(8,128)S(1)}, u32[]{:S(2)}, u32[]{:S(2)}) %collective-permute-start.4) | collective-permute-done | bytes 53280 | tf_op jit(solution)/shard_map/ppermute | solution.py:427
  16.2 0.0 collective-permute-done.3.got_a
  16.2 1.0 %shard_map.73 = (f32[19,4,16,128]{3,2,1,0:T(8,128)S(1)}, f32[19,16,128]{2,1,0:T(8,128)S(1)}, f32[19,4,16,128]{3,2,1,0:T(8,128)}, f32[19,16,128]{2,1,0:T(8,128)}) custom-call(f32[19,4,16,128]{3,2,1,0:T(8,128)S(1)} %get-tuple-element.30.room_in, f32[19,16,128]{2,1,0:T(8,128)S(1)} %get-tuple-element.31.plen_in, ...), custom_call_target="tpu_custom_call", output_to_operand_aliasing={{0}: (0, {}), {1}: (1, {})} | custom-call | flops 100000 | bytes 1000000 | tf_op jit(solution)/shard_map/pallas_call | solution.py:495
  (2 shorter events, 0.1 us)
Async XLA Ops:
  1.8 4.7 %collective-permute-start = (f32[8,1,640]{2,1,0:T(1,128)S(1)}, f32[8,1,640]{2,1,0:T(1,128)S(1)}, u32[]{:S(2)}, u32[]{:S(2)}) collective-permute-start(f32[8,1,640]{2,1,0:T(1,128)S(1)} %get-tuple-element.25), channel_id=1, source_target_pairs={{0,2},{1,3},{2,0},{3,1},{4,6},{5,7},{6,4},{7,5},{8,10},{9,11},{10,... | collective-permute-start | bytes 61448 | tf_op jit(solution)/shard_map/ppermute | solution.py:458
  4.8 2.6 %collective-permute-start.1 = (f32[104,128]{1,0:T(8,128)S(1)}, f32[104,128]{1,0:T(8,128)S(1)}, u32[]{:S(2)}, u32[]{:S(2)}) collective-permute-start(f32[104,128]{1,0:T(8,128)S(1)} %get-tuple-element.28), channel_id=1, source_target_pairs={{0,4},{4,0},{8,12},{12,8},{16,20},{20,16},{24,28},{28,24},{1,5},{5... | collective-permute-start | bytes 159752 | tf_op jit(solution)/shard_map/ppermute | solution.py:427
  4.9 4.7 %collective-permute-start.2 = (f32[104,128]{1,0:T(8,128)S(1)}, f32[104,128]{1,0:T(8,128)S(1)}, u32[]{:S(2)}, u32[]{:S(2)}) collective-permute-start(f32[104,128]{1,0:T(8,128)S(1)} %get-tuple-element.29), channel_id=1, source_target_pairs={{0,28},{4,8},{8,4},{12,16},{16,12},{20,24},{24,20},{28,0},{1,29},{... | collective-permute-start | bytes 159752 | tf_op jit(solution)/shard_map/ppermute | solution.py:427
  9.7 6.5 %collective-permute-start.3 = (f32[144,128]{1,0:T(8,128)S(1)}, f32[144,128]{1,0:T(8,128)S(1)}, u32[]{:S(2)}, u32[]{:S(2)}) collective-permute-start(f32[144,128]{1,0:T(8,128)S(1)} %get-tuple-element.34), channel_id=1, source_target_pairs={{0,1},{1,0},{2,3},{3,2},{4,5},{5,4},{6,7},{7,6},{8,9},{9,8},{10,11... | collective-permute-start | bytes 221192 | tf_op jit(solution)/shard_map/ppermute | solution.py:427
  10.2 6.0 %collective-permute-start.4 = (f32[104,128]{1,0:T(8,128)S(1)}, f32[104,128]{1,0:T(8,128)S(1)}, u32[]{:S(2)}, u32[]{:S(2)}) collective-permute-start(f32[104,128]{1,0:T(8,128)S(1)} %get-tuple-element.35), channel_id=1, source_target_pairs={{1,2},{2,1},{5,6},{6,5},{9,10},{10,9},{13,14},{14,13},{17,18},{18,... | collective-permute-start | bytes 159752 | tf_op jit(solution)/shard_map/ppermute | solution.py:427

commit v5 on v3

--- a/solution.py
+++ b/solution.py
@@ -94,16 +94,23 @@
     return value if shift == 0 else pltpu.roll(value, shift, 0)
 
 
+def repeat(count, body, start):
+    if count > 8:
+        return lax.fori_loop(0, count, body, start)
+    for i in range(count):
+        start = body(i, start)
+    return start
+
+
 def plenum_kernel(sizes, relayed, room_in, plen_in, cell_in, owner_in, class_in, room_near, plen_post, *rest):
     ca, cs, blocks, n_span, per_brick = sizes
-    jets = rest[:-6]
-    columns, plen_buf, cells, owners, classes, sems = rest[-6:]
+    jets = rest[:-7]
+    columns, dealt, plen_buf, cells, owners, classes, sems = rest[-7:]
     copies = [pltpu.make_async_copy(src, dst, sems.at[i]) for i, (src, dst) in enumerate(
         ((plen_in, plen_buf), (cell_in, cells), (owner_in, owners), (class_in, classes), (room_in, room_near)))]
     for copy in copies:
         copy.start()
-    for part in jets:
-        part[...] = jnp.zeros_like(part)
+    dealt[...] = jnp.zeros_like(dealt)
     copies[0].wait()
     for r in range(0, ca * cs, 8):
         post = collide([plen_buf[q, r : r + 8] for q in range(19)])
@@ -121,24 +128,20 @@
         t = first + i
         owner = owners[t]
         share = 0.15 * (classes[t].astype(F32) + 1.0)
-        slot = lax.fori_loop(0, i, lambda j, n: n + (owners[first + j] == owner).astype(jnp.int32), 0)
-        column = share * columns[cells[t]]
-        if not relayed:
-            jets[0][owner, slot] = column
-            return carry
-        apart = owner ^ here
-
-        @pl.when(apart < 2)
-        def _():
-            jets[0][apart, slot] = column
-
-        @pl.when(apart >= 2)
-        def _():
-            jets[1][apart - 2, slot] = column
-
+        same = lambda j, n: n + (owners[first + j] == owner).astype(jnp.int32)
+        slot = repeat(i, same, 0) if relayed else lax.fori_loop(0, i, same, 0)
+        to = (owner ^ here if relayed else owner) * CAP + slot
+        dealt[to] = share * columns[cells[t]]
         return carry
 
-    lax.fori_loop(0, per_brick, send_jet, 0)
+    if relayed:
+        for i in range(per_brick):
+            send_jet(i, 0)
+    else:
+        lax.fori_loop(0, per_brick, send_jet, 0)
+    for part, jet in enumerate(jets):
+        many = jet.shape[0]
+        jet[...] = dealt[part * many : (part + 1) * many]
     copies[4].wait()
 
 
@@ -166,6 +169,15 @@
         low = 5 * rows + k * cs
         swap_a[low : low + cs] = jnp.where(even, rising, falling)
         swap_b[low : low + cs] = jnp.where(even, falling, rising)
+
+
+def jet_sums(start, places, bricks):
+    sums = [start(k) for k in range(5)]
+    for b, jet in bricks:
+        for s in range(CAP):
+            marks = places[b * CAP + s]
+            sums = [total + marks * jet(s, k) for k, total in enumerate(sums)]
+    return sums
 
 
 def local_kernel(sizes, room_post, plen_post, cell_in, owner_in, room_part, plen_part, span_up, span_down, places,
@@ -202,7 +214,7 @@
             for x in range(ca):
                 to = 5 * rows + k * ca + x
                 span[to : to + 1] = value[x * cs + edge : x * cs + edge + 1]
-    places[...] = jnp.zeros_like(places)
+    places[0 : n_span * CAP] = jnp.zeros((n_span * CAP, ca * cs, LANES), F32)
     here = lax.axis_index("span")
     row = lax.broadcasted_iota(jnp.int32, (ca * cs, LANES), 0)
     for copy in copies:
@@ -212,17 +224,13 @@
         def place(i, slot):
             t = b * per_brick + i
             mine = owners[t] == here
-
-            @pl.when(mine)
-            def _():
-                places[b * CAP + slot] = (row == cells[t]).astype(F32)
-
+            places[jnp.where(mine, b * CAP + slot, n_span * CAP)] = (row == cells[t]).astype(F32)
             return slot + mine.astype(jnp.int32)
 
-        lax.fori_loop(0, per_brick, place, 0)
+        repeat(per_brick, place, 0)
         return carry
 
-    lax.fori_loop(0, n_span, brick, 0)
+    repeat(n_span, brick, 0)
 
 
 def pack_kernel(sizes, relayed, got_a, got_b, span_up, span_down, *rest):
@@ -281,23 +289,13 @@
             for s in range(CAP):
                 for k in range(5):
                     to = halo + (b * CAP + s) * 5 + k
-                    cross_a[to : to + 1] = source[1, s, :, k * LANES : (k + 1) * LANES]
-
-
-def jet_sums(start, places, bricks):
-    sums = [start(k) for k in range(5)]
-    for b, jet in bricks:
-        for s in range(CAP):
-            marks = places[b * CAP + s]
-            sums = [total + marks * jet(s, k) for k, total in enumerate(sums)]
-    return sums
+                    cross_a[to : to + 1] = source[CAP + s, :, k * LANES : (k + 1) * LANES]
 
 
 def aisle_kernel(sizes, relayed, room_in, plen_in, got_a, got_b, jets, got_jets, places, room, plen, inflow):
     ca, cs, blocks, n_span, per_brick = sizes
     rows = blocks * cs
     even = lax.axis_index("aisle") % 2 == 0
-    here = lax.axis_index("span")
     for k in range(5):
         for q, x, first, second in ((X_UP[k], 0, got_b, got_a), (X_DOWN[k], ca - 1, got_a, got_b)):
             cy = VELOCITIES[q][1]
@@ -314,13 +312,14 @@
                 plen[q, at : at + cs - 1] = value[1:cs]
             else:
                 plen[q, at : at + cs] = value
+    here = lax.axis_index("span")
 
     def put(sums):
         for k in range(5):
             inflow[k] = sums[k]
 
     def reader(source, b):
-        return lambda s, k: source[b, s, :, k * LANES : (k + 1) * LANES]
+        return lambda s, k: source[b * CAP + s, :, k * LANES : (k + 1) * LANES]
 
     if relayed:
         put(jet_sums(lambda k: jnp.zeros((ca * cs, LANES), F32), places,
@@ -328,11 +327,11 @@
     else:
         inflow[...] = jnp.zeros_like(inflow)
 
-        def brick(b, carry):
+        def add_brick(b, carry):
             put(jet_sums(lambda k: inflow[k], places, [(b, reader(got_jets, b))]))
             return carry
 
-        lax.fori_loop(0, n_span, brick, 0)
+        lax.fori_loop(0, n_span, add_brick, 0)
 
 
 def finish_kernel(sizes, relayed, room_in, plen_in, got_a, got_b, places, inflow, room, plen, room_out, plen_out, sems):
@@ -343,7 +342,6 @@
     halo = 5 * (rows + cs)
     halo = halo + -halo % 8
     group = lax.broadcasted_iota(jnp.int32, (rows, LANES), 0) % cs
-
     def enter(got, up):
         planes, y = (Y_UP, 0) if up else (Y_DOWN, cs - 1)
         for k, q in enumerate(planes):
@@ -429,12 +427,12 @@
     tile_cell, tile_owner, tile_class = far(tile_cell), far(tile_owner.reshape(tiles)), far(tile_class)
     numbers = pltpu.SMEM((tiles,), jnp.int32)
 
-    jets_shape = (2 if relayed else n_span, CAP, 1, 5 * hp)
+    jets_shape = ((2 if relayed else n_span) * CAP, 1, 5 * hp)
     room_near, plen_post, *jets = call(
         functools.partial(plenum_kernel, sizes, relayed),
         [near(room_shape), near(plen_shape)] + [near(jets_shape)] * (2 if relayed else 1),
         [HBM] * 5,
-        scratch=[pltpu.VMEM((ca * cs, 1, 5 * hp), F32), pltpu.VMEM(plen_shape, F32), numbers, numbers, numbers,
+        scratch=[pltpu.VMEM((ca * cs, 1, 5 * hp), F32), near((n_span * CAP, 1, 5 * hp)), near(plen_shape), numbers, numbers, numbers,
                  pltpu.SemaphoreType.DMA((5,))],
     )(room, plen, tile_cell, tile_owner, tile_class)
     if relayed:
@@ -444,18 +442,19 @@
 
     room_post, swap_a, swap_b = call(
         functools.partial(room_kernel, sizes),
-        [near(room_shape), near((halo, LANES)), near((halo, LANES))],
+        [near(room_shape), near((halo + 8, LANES)), near((halo, LANES))],
         [VMEM] * 2,
     )(room_near, plen_post)
+    got_b = swap(swap_b, "aisle", True, True)
     got_a = swap(swap_a, "aisle", False, True)
-    got_b = swap(swap_b, "aisle", True, True)
 
     room_part, plen_part, span_up, span_down, places = call(
         functools.partial(local_kernel, sizes),
         [near(room_shape), near(plen_shape), near((halo, LANES)), near((halo, LANES)),
-         near((n_span * CAP, ca * cs, LANES))],
+         near((n_span * CAP + 1, ca * cs, LANES))],
         [VMEM, VMEM, HBM, HBM],
         scratch=[numbers, numbers, pltpu.SemaphoreType.DMA((2,))],
+        flops=10**9,
     )(room_post, plen_post, tile_cell, tile_owner)
 
     cross_shape = (halo + 2 * CAP * 5, LANES) if relayed else (halo, LANES)
@@ -472,6 +471,7 @@
         [near(room_shape), near(plen_shape), near((5, ca * cs, LANES))],
         [VMEM] * 7,
         aliases={0: 0, 1: 1},
+        flops=10**9,
     )(room_part, plen_part, got_a, got_b, jets[0], got_jets, places)
 
     _, _, room_next, plenum_next = call(

time: 18.7 us -> 18.3 us (0.979)
  the two profiles are of different devices: /device:TPU:16 before, /device:TPU:0 now
where the time goes in v5:
time: 18.3 us; the launch traced here: 18.2 us
  starting transfers between devices  9.33 us (51%)
  waiting for transfers between devices  4.81 us (26%)
  Pallas kernels  3.32 us (18%)
  between operations  0.69 us (4%)
    ppermute x4, starting transfers between devices, swap(): return lax.ppermute(value, axis, pairs)  5.23 us
    ppermute x4, waiting for transfers between devices, swap(): return lax.ppermute(value, axis, pairs)  4.81 us
    ppermute x1, starting transfers between devices, shards(): got_jets = lax.ppermute(jets[1], 'span', [(i, i ^ 2) for i in range(4)])  4.1 us
    pallas_call x1, Pallas kernels, shards(): call(functools.partial(plenum_kernel, sizes, relayed), [near(room_shape),...  1.21 us
    pallas_call x1, Pallas kernels, shards(): call(functools.partial(finish_kernel, sizes, relayed), [near(room_shape),...  0.93 us
    pallas_call x1, Pallas kernels, shards(): call(functools.partial(local_kernel, sizes), [near(room_shape), near(plen...  0.77 us
  transfers between devices with their start and end apart: 5, of which 2 were waited for; matrix products, arithmetic and copies ran while one was open for 0% of the time, Pallas kernels for 6%

profile of v5, /device:TPU:0, one launch (start us, length us, event | category | flops | bytes accessed | tf_op | source)
XLA Modules:
  0.0 18.2 jit_solution(8266363959445271021)
XLA Ops:
  0.6 1.2 %shard_map.68 = (f32[19,4,16,128]{3,2,1,0:T(8,128)S(1)}, f32[19,16,128]{2,1,0:T(8,128)S(1)}, f32[8,1,640]{2,1,0:T(1,128)S(1)}, f32[8,1,640]{2,1,0:T(1,128)S(1)}) custom-call(f32[19,4,16,128]{3,2,1,0:T(8,128)} %bitcast.13, f32[19,16,128]{2,1,0:T(8,128)} %bitcast.14, s32[32]{0:T(128)} %cell_in.3, s32[32]{0:T(128)} %bitcast.15, s32[32]{0:T(128)} %class_in.1), custom_call_target="tpu_custom_call" | custom-call | flops 100000 | bytes 1000000 | tf_op jit(solution)/shard_map/pallas_call | solution.py:431
  1.8 4.1 %collective-permute-start.2 = (f32[8,1,640]{2,1,0:T(1,128)S(1)}, f32[8,1,640]{2,1,0:T(1,128)S(1)}, u32[]{:S(2)}, u32[]{:S(2)}) collective-permute-start(f32[8,1,640]{2,1,0:T(1,128)S(1)} %get-tuple-element.29), channel_id=1, source_target_pairs={{0,2},{1,3},{2,0},{3,1},{4,6},{5,7},{6,4},{7,5},{8,10},{9,11},{10,... | collective-permute-start | bytes 61448 | tf_op jit(solution)/shard_map/ppermute | solution.py:439
  5.9 0.3 %shard_map.69 = (f32[19,4,16,128]{3,2,1,0:T(8,128)S(1)}, f32[112,128]{1,0:T(8,128)S(1)}, f32[104,128]{1,0:T(8,128)S(1)}) custom-call(f32[19,4,16,128]{3,2,1,0:T(8,128)S(1)} %get-tuple-element.21.room_near, f32[19,16,128]{2,1,0:T(8,128)S(1)} %get-tuple-element.22.plen_post), custom_call_target="tpu_custom_call" | custom-call | flops 100000 | bytes 1000000 | tf_op jit(solution)/shard_map/pallas_call | solution.py:443
  6.3 1.7 %collective-permute-start.1 = (f32[104,128]{1,0:T(8,128)S(1)}, f32[104,128]{1,0:T(8,128)S(1)}, u32[]{:S(2)}, u32[]{:S(2)}) collective-permute-start(f32[104,128]{1,0:T(8,128)S(1)} %get-tuple-element.27), channel_id=1, source_target_pairs={{0,28},{4,8},{8,4},{12,16},{16,12},{20,24},{24,20},{28,0},{1,29},{... | collective-permute-start | bytes 159752 | tf_op jit(solution)/shard_map/ppermute | solution.py:408
  8.0 0.0 collective-permute-start
  8.0 0.8 %shard_map.70 = (f32[19,4,16,128]{3,2,1,0:T(8,128)S(1)}, f32[19,16,128]{2,1,0:T(8,128)S(1)}, f32[104,128]{1,0:T(8,128)S(1)}, f32[104,128]{1,0:T(8,128)S(1)}, f32[17,16,128]{2,1,0:T(8,128)S(1)}) custom-call(f32[19,4,16,128]{3,2,1,0:T(8,128)S(1)} %get-tuple-element.23.room_post, f32[19,16,128]{2,1,0:T(8,128)S(1)} %get-tuple-element.22.plen_post, s32[32]{0:T(128)} %cell_in.3, ...), custom_call_target="tpu_custom_call" | custom-call | flops 1000000000 | bytes 1000000 | tf_op jit(solution)/shard_map/pallas_call | solution.py:451
  8.7 0.0 collective-permute-done.2.got_jets.rest_1_
  8.7 2.5 %collective-permute-done.1.got_b = f32[104,128]{1,0:T(8,128)S(1)} collective-permute-done((f32[104,128]{1,0:T(8,128)S(1)}, f32[104,128]{1,0:T(8,128)S(1)}, u32[]{:S(2)}, u32[]{:S(2)}) %collective-permute-start.1) | collective-permute-done | bytes 53280 | tf_op jit(solution)/shard_map/ppermute | solution.py:408
  11.3 0.0 collective-permute-done.got_a
  11.3 0.7 %collective-permute-start.4 = (f32[104,128]{1,0:T(8,128)S(1)}, f32[104,128]{1,0:T(8,128)S(1)}, u32[]{:S(2)}, u32[]{:S(2)}) collective-permute-start(f32[104,128]{1,0:T(8,128)S(1)} %get-tuple-element.36), channel_id=1, source_target_pairs={{1,2},{2,1},{5,6},{6,5},{9,10},{10,9},{13,14},{14,13},{17,18},{18,... | collective-permute-start | bytes 159752 | tf_op jit(solution)/shard_map/ppermute | solution.py:408
  12.0 2.9 %collective-permute-start.3 = (f32[144,128]{1,0:T(8,128)S(1)}, f32[144,128]{1,0:T(8,128)S(1)}, u32[]{:S(2)}, u32[]{:S(2)}) collective-permute-start(f32[144,128]{1,0:T(8,128)S(1)} %get-tuple-element.35), channel_id=1, source_target_pairs={{0,1},{1,0},{2,3},{3,2},{4,5},{5,4},{6,7},{7,6},{8,9},{9,8},{10,11... | collective-permute-start | bytes 221192 | tf_op jit(solution)/shard_map/ppermute | solution.py:408
  14.9 0.0 collective-permute-done.4.got_b
  14.9 2.3 %collective-permute-done.3.got_a = f32[144,128]{1,0:T(8,128)S(1)} collective-permute-done((f32[144,128]{1,0:T(8,128)S(1)}, f32[144,128]{1,0:T(8,128)S(1)}, u32[]{:S(2)}, u32[]{:S(2)}) %collective-permute-start.3) | collective-permute-done | bytes 73760 | tf_op jit(solution)/shard_map/ppermute | solution.py:408
  17.2 0.9 %shard_map.73 = (f32[19,4,16,128]{3,2,1,0:T(8,128)S(1)}, f32[19,16,128]{2,1,0:T(8,128)S(1)}, f32[19,4,16,128]{3,2,1,0:T(8,128)}, f32[19,16,128]{2,1,0:T(8,128)}) custom-call(f32[19,4,16,128]{3,2,1,0:T(8,128)S(1)} %get-tuple-element.31.room_in, f32[19,16,128]{2,1,0:T(8,128)S(1)} %get-tuple-element.32.plen_in, ...), custom_call_target="tpu_custom_call", output_to_operand_aliasing={{0}: (0, {}), {1}: (1, {})} | custom-call | flops 100000 | bytes 1000000 | tf_op jit(solution)/shard_map/pallas_call | solution.py:477
  (2 shorter events, 0.1 us)
Async XLA Ops:
  1.8 6.9 %collective-permute-start.2 = (f32[8,1,640]{2,1,0:T(1,128)S(1)}, f32[8,1,640]{2,1,0:T(1,128)S(1)}, u32[]{:S(2)}, u32[]{:S(2)}) collective-permute-start(f32[8,1,640]{2,1,0:T(1,128)S(1)} %get-tuple-element.29), channel_id=1, source_target_pairs={{0,2},{1,3},{2,0},{3,1},{4,6},{5,7},{6,4},{7,5},{8,10},{9,11},{10,... | collective-permute-start | bytes 61448 | tf_op jit(solution)/shard_map/ppermute | solution.py:439
  6.3 5.0 %collective-permute-start.1 = (f32[104,128]{1,0:T(8,128)S(1)}, f32[104,128]{1,0:T(8,128)S(1)}, u32[]{:S(2)}, u32[]{:S(2)}) collective-permute-start(f32[104,128]{1,0:T(8,128)S(1)} %get-tuple-element.27), channel_id=1, source_target_pairs={{0,28},{4,8},{8,4},{12,16},{16,12},{20,24},{24,20},{28,0},{1,29},{... | collective-permute-start | bytes 159752 | tf_op jit(solution)/shard_map/ppermute | solution.py:408
  8.0 3.3 %collective-permute-start = (f32[112,128]{1,0:T(8,128)S(1)}, f32[112,128]{1,0:T(8,128)S(1)}, u32[]{:S(2)}, u32[]{:S(2)}) collective-permute-start(f32[112,128]{1,0:T(8,128)S(1)} %get-tuple-element.26), channel_id=1, source_target_pairs={{0,4},{4,0},{8,12},{12,8},{16,20},{20,16},{24,28},{28,24},{1,5},{5... | collective-permute-start | bytes 172040 | tf_op jit(solution)/shard_map/ppermute | solution.py:408
  11.3 3.6 %collective-permute-start.4 = (f32[104,128]{1,0:T(8,128)S(1)}, f32[104,128]{1,0:T(8,128)S(1)}, u32[]{:S(2)}, u32[]{:S(2)}) collective-permute-start(f32[104,128]{1,0:T(8,128)S(1)} %get-tuple-element.36), channel_id=1, source_target_pairs={{1,2},{2,1},{5,6},{6,5},{9,10},{10,9},{13,14},{14,13},{17,18},{18,... | collective-permute-start | bytes 159752 | tf_op jit(solution)/shard_map/ppermute | solution.py:408
  12.0 5.2 %collective-permute-start.3 = (f32[144,128]{1,0:T(8,128)S(1)}, f32[144,128]{1,0:T(8,128)S(1)}, u32[]{:S(2)}, u32[]{:S(2)}) collective-permute-start(f32[144,128]{1,0:T(8,128)S(1)} %get-tuple-element.35), channel_id=1, source_target_pairs={{0,1},{1,0},{2,3},{3,2},{4,5},{5,4},{6,7},{7,6},{8,9},{9,8},{10,11... | collective-permute-start | bytes 221192 | tf_op jit(solution)/shard_map/ppermute | solution.py:408

commit v6 on v5

--- a/solution.py
+++ b/solution.py
@@ -403,8 +403,7 @@
     pairs = []
     for i in range(count):
         j = (i ^ 1) if not odd else (i + 1 if i % 2 else i - 1)
-        if wraps or 0 <= j < count:
-            pairs.append((i, j % count))
+        pairs.append((i, j % count if wraps or 0 <= j < count else i))
     return lax.ppermute(value, axis, pairs)
 
 

time: 18.3 us -> 18.3 us (level)
  no operation moved by 1% of the time
where the time goes in v6:
time: 18.3 us; the launch traced here: 18.2 us
  starting transfers between devices  9.33 us (51%)
  waiting for transfers between devices  4.81 us (26%)
  Pallas kernels  3.32 us (18%)
  between operations  0.69 us (4%)
    ppermute x4, starting transfers between devices, swap(): return lax.ppermute(value, axis, pairs)  5.23 us
    ppermute x4, waiting for transfers between devices, swap(): return lax.ppermute(value, axis, pairs)  4.81 us
    ppermute x1, starting transfers between devices, shards(): got_jets = lax.ppermute(jets[1], 'span', [(i, i ^ 2) for i in range(4)])  4.1 us
    pallas_call x1, Pallas kernels, shards(): call(functools.partial(plenum_kernel, sizes, relayed), [near(room_shape),...  1.21 us
    pallas_call x1, Pallas kernels, shards(): call(functools.partial(finish_kernel, sizes, relayed), [near(room_shape),...  0.93 us
    pallas_call x1, Pallas kernels, shards(): call(functools.partial(local_kernel, sizes), [near(room_shape), near(plen...  0.77 us
  transfers between devices with their start and end apart: 5, of which 2 were waited for; matrix products, arithmetic and copies ran while one was open for 0% of the time, Pallas kernels for 6%

profile of v6, /device:TPU:0, one launch (start us, length us, event | category | flops | bytes accessed | tf_op | source)
XLA Modules:
  0.0 18.2 jit_solution(3733560409344051537)
XLA Ops:
  0.6 1.2 %shard_map.68 = (f32[19,4,16,128]{3,2,1,0:T(8,128)S(1)}, f32[19,16,128]{2,1,0:T(8,128)S(1)}, f32[8,1,640]{2,1,0:T(1,128)S(1)}, f32[8,1,640]{2,1,0:T(1,128)S(1)}) custom-call(f32[19,4,16,128]{3,2,1,0:T(8,128)} %bitcast.13, f32[19,16,128]{2,1,0:T(8,128)} %bitcast.14, s32[32]{0:T(128)} %cell_in.3, s32[32]{0:T(128)} %bitcast.15, s32[32]{0:T(128)} %class_in.1), custom_call_target="tpu_custom_call" | custom-call | flops 100000 | bytes 1000000 | tf_op jit(solution)/shard_map/pallas_call | solution.py:430
  1.8 4.1 %collective-permute-start.2 = (f32[8,1,640]{2,1,0:T(1,128)S(1)}, f32[8,1,640]{2,1,0:T(1,128)S(1)}, u32[]{:S(2)}, u32[]{:S(2)}) collective-permute-start(f32[8,1,640]{2,1,0:T(1,128)S(1)} %get-tuple-element.29), channel_id=1, source_target_pairs={{0,2},{1,3},{2,0},{3,1},{4,6},{5,7},{6,4},{7,5},{8,10},{9,11},{10,... | collective-permute-start | bytes 61448 | tf_op jit(solution)/shard_map/ppermute | solution.py:438
  5.9 0.3 %shard_map.69 = (f32[19,4,16,128]{3,2,1,0:T(8,128)S(1)}, f32[112,128]{1,0:T(8,128)S(1)}, f32[104,128]{1,0:T(8,128)S(1)}) custom-call(f32[19,4,16,128]{3,2,1,0:T(8,128)S(1)} %get-tuple-element.21.room_near, f32[19,16,128]{2,1,0:T(8,128)S(1)} %get-tuple-element.22.plen_post), custom_call_target="tpu_custom_call" | custom-call | flops 100000 | bytes 1000000 | tf_op jit(solution)/shard_map/pallas_call | solution.py:442
  6.3 1.7 %collective-permute-start.1 = (f32[104,128]{1,0:T(8,128)S(1)}, f32[104,128]{1,0:T(8,128)S(1)}, u32[]{:S(2)}, u32[]{:S(2)}) collective-permute-start(f32[104,128]{1,0:T(8,128)S(1)} %get-tuple-element.27), channel_id=1, source_target_pairs={{0,28},{4,8},{8,4},{12,16},{16,12},{20,24},{24,20},{28,0},{1,29},{... | collective-permute-start | bytes 159752 | tf_op jit(solution)/shard_map/ppermute | solution.py:407
  8.0 0.0 collective-permute-start
  8.0 0.8 %shard_map.70 = (f32[19,4,16,128]{3,2,1,0:T(8,128)S(1)}, f32[19,16,128]{2,1,0:T(8,128)S(1)}, f32[104,128]{1,0:T(8,128)S(1)}, f32[104,128]{1,0:T(8,128)S(1)}, f32[17,16,128]{2,1,0:T(8,128)S(1)}) custom-call(f32[19,4,16,128]{3,2,1,0:T(8,128)S(1)} %get-tuple-element.23.room_post, f32[19,16,128]{2,1,0:T(8,128)S(1)} %get-tuple-element.22.plen_post, s32[32]{0:T(128)} %cell_in.3, ...), custom_call_target="tpu_custom_call" | custom-call | flops 1000000000 | bytes 1000000 | tf_op jit(solution)/shard_map/pallas_call | solution.py:450
  8.7 0.0 collective-permute-done.2.got_jets.rest_1_
  8.7 2.5 %collective-permute-done.1.got_b = f32[104,128]{1,0:T(8,128)S(1)} collective-permute-done((f32[104,128]{1,0:T(8,128)S(1)}, f32[104,128]{1,0:T(8,128)S(1)}, u32[]{:S(2)}, u32[]{:S(2)}) %collective-permute-start.1) | collective-permute-done | bytes 53280 | tf_op jit(solution)/shard_map/ppermute | solution.py:407
  11.3 0.0 collective-permute-done.got_a
  11.3 0.7 %collective-permute-start.4 = (f32[104,128]{1,0:T(8,128)S(1)}, f32[104,128]{1,0:T(8,128)S(1)}, u32[]{:S(2)}, u32[]{:S(2)}) collective-permute-start(f32[104,128]{1,0:T(8,128)S(1)} %get-tuple-element.36), channel_id=1, source_target_pairs={{0,0},{1,2},{2,1},{3,3},{4,4},{5,6},{6,5},{7,7},{8,8},{9,10},{10,9... | collective-permute-start | bytes 159752 | tf_op jit(solution)/shard_map/ppermute | solution.py:407
  12.0 2.9 %collective-permute-start.3 = (f32[144,128]{1,0:T(8,128)S(1)}, f32[144,128]{1,0:T(8,128)S(1)}, u32[]{:S(2)}, u32[]{:S(2)}) collective-permute-start(f32[144,128]{1,0:T(8,128)S(1)} %get-tuple-element.35), channel_id=1, source_target_pairs={{0,1},{1,0},{2,3},{3,2},{4,5},{5,4},{6,7},{7,6},{8,9},{9,8},{10,11... | collective-permute-start | bytes 221192 | tf_op jit(solution)/shard_map/ppermute | solution.py:407
  14.9 0.0 collective-permute-done.4.got_b
  14.9 2.3 %collective-permute-done.3.got_a = f32[144,128]{1,0:T(8,128)S(1)} collective-permute-done((f32[144,128]{1,0:T(8,128)S(1)}, f32[144,128]{1,0:T(8,128)S(1)}, u32[]{:S(2)}, u32[]{:S(2)}) %collective-permute-start.3) | collective-permute-done | bytes 73760 | tf_op jit(solution)/shard_map/ppermute | solution.py:407
  17.2 0.9 %shard_map.73 = (f32[19,4,16,128]{3,2,1,0:T(8,128)S(1)}, f32[19,16,128]{2,1,0:T(8,128)S(1)}, f32[19,4,16,128]{3,2,1,0:T(8,128)}, f32[19,16,128]{2,1,0:T(8,128)}) custom-call(f32[19,4,16,128]{3,2,1,0:T(8,128)S(1)} %get-tuple-element.31.room_in, f32[19,16,128]{2,1,0:T(8,128)S(1)} %get-tuple-element.32.plen_in, ...), custom_call_target="tpu_custom_call", output_to_operand_aliasing={{0}: (0, {}), {1}: (1, {})} | custom-call | flops 100000 | bytes 1000000 | tf_op jit(solution)/shard_map/pallas_call | solution.py:476
  (2 shorter events, 0.1 us)
Async XLA Ops:
  1.8 6.9 %collective-permute-start.2 = (f32[8,1,640]{2,1,0:T(1,128)S(1)}, f32[8,1,640]{2,1,0:T(1,128)S(1)}, u32[]{:S(2)}, u32[]{:S(2)}) collective-permute-start(f32[8,1,640]{2,1,0:T(1,128)S(1)} %get-tuple-element.29), channel_id=1, source_target_pairs={{0,2},{1,3},{2,0},{3,1},{4,6},{5,7},{6,4},{7,5},{8,10},{9,11},{10,... | collective-permute-start | bytes 61448 | tf_op jit(solution)/shard_map/ppermute | solution.py:438
  6.3 5.0 %collective-permute-start.1 = (f32[104,128]{1,0:T(8,128)S(1)}, f32[104,128]{1,0:T(8,128)S(1)}, u32[]{:S(2)}, u32[]{:S(2)}) collective-permute-start(f32[104,128]{1,0:T(8,128)S(1)} %get-tuple-element.27), channel_id=1, source_target_pairs={{0,28},{4,8},{8,4},{12,16},{16,12},{20,24},{24,20},{28,0},{1,29},{... | collective-permute-start | bytes 159752 | tf_op jit(solution)/shard_map/ppermute | solution.py:407
  8.0 3.3 %collective-permute-start = (f32[112,128]{1,0:T(8,128)S(1)}, f32[112,128]{1,0:T(8,128)S(1)}, u32[]{:S(2)}, u32[]{:S(2)}) collective-permute-start(f32[112,128]{1,0:T(8,128)S(1)} %get-tuple-element.26), channel_id=1, source_target_pairs={{0,4},{4,0},{8,12},{12,8},{16,20},{20,16},{24,28},{28,24},{1,5},{5... | collective-permute-start | bytes 172040 | tf_op jit(solution)/shard_map/ppermute | solution.py:407
  11.3 3.6 %collective-permute-start.4 = (f32[104,128]{1,0:T(8,128)S(1)}, f32[104,128]{1,0:T(8,128)S(1)}, u32[]{:S(2)}, u32[]{:S(2)}) collective-permute-start(f32[104,128]{1,0:T(8,128)S(1)} %get-tuple-element.36), channel_id=1, source_target_pairs={{0,0},{1,2},{2,1},{3,3},{4,4},{5,6},{6,5},{7,7},{8,8},{9,10},{10,9... | collective-permute-start | bytes 159752 | tf_op jit(solution)/shard_map/ppermute | solution.py:407
  12.0 5.2 %collective-permute-start.3 = (f32[144,128]{1,0:T(8,128)S(1)}, f32[144,128]{1,0:T(8,128)S(1)}, u32[]{:S(2)}, u32[]{:S(2)}) collective-permute-start(f32[144,128]{1,0:T(8,128)S(1)} %get-tuple-element.35), channel_id=1, source_target_pairs={{0,1},{1,0},{2,3},{3,2},{4,5},{5,4},{6,7},{7,6},{8,9},{9,8},{10,11... | collective-permute-start | bytes 221192 | tf_op jit(solution)/shard_map/ppermute | solution.py:407

commit v7 on v6

--- a/solution.py
+++ b/solution.py
@@ -398,13 +398,21 @@
     )
 
 
-def swap(value, axis, odd, wraps):
-    count = lax.axis_size(axis)
+def swap_aisle(value, odd):
+    count = lax.axis_size("aisle")
+    pairs = [(i, (i ^ 1 if not odd else i + 1 if i % 2 else i - 1) % count) for i in range(count)]
+    return lax.ppermute(value, "aisle", pairs)
+
+
+def swap_span(value, odd):
+    count = lax.axis_size("span")
     pairs = []
-    for i in range(count):
-        j = (i ^ 1) if not odd else (i + 1 if i % 2 else i - 1)
-        pairs.append((i, j % count if wraps or 0 <= j < count else i))
-    return lax.ppermute(value, axis, pairs)
+    for a in range(lax.axis_size("aisle")):
+        for s in range(count):
+            t = s ^ 1 if not odd else s + 1 if s % 2 else s - 1
+            b, t = (a, t) if 0 <= t < count else (a ^ 1, s)
+            pairs.append((a * count + s, b * count + t))
+    return lax.ppermute(value, ("aisle", "span"), pairs)
 
 
 def shards(room_pops, plenum_pops, tile_cell, tile_owner, tile_class):
@@ -444,8 +452,8 @@
         [near(room_shape), near((halo + 8, LANES)), near((halo, LANES))],
         [VMEM] * 2,
     )(room_near, plen_post)
-    got_b = swap(swap_b, "aisle", True, True)
-    got_a = swap(swap_a, "aisle", False, True)
+    got_b = swap_aisle(swap_b, True)
+    got_a = swap_aisle(swap_a, False)
 
     room_part, plen_part, span_up, span_down, places = call(
         functools.partial(local_kernel, sizes),
@@ -463,8 +471,8 @@
         [VMEM] * (6 if relayed else 4),
     )(got_a, got_b, span_up, span_down, *((jets[0], got_jets) if relayed else ()))
 
-    in_b = swap(cross_b, "span", True, False)
-    in_a = swap(cross_a, "span", False, False)
+    in_b = swap_span(cross_b, True)
+    in_a = swap_span(cross_a, False)
     room_part, plen_part, inflow = call(
         functools.partial(aisle_kernel, sizes, relayed),
         [near(room_shape), near(plen_shape), near((5, ca * cs, LANES))],

time: 18.3 us -> 17.2 us (0.940)
  starting transfers between devices: 9.33 us -> 7.48 us
  waiting for transfers between devices: 4.81 us -> 5.53 us
    ppermute x4, starting transfers between devices: 5.23 us -> 3.38 us  [the longest x2 1.71 us: swap_span(): return lax.ppermute(value, ('aisle', 'span'), pairs)]
    ppermute x4, waiting for transfers between devices: 4.81 us -> 5.52 us  [the longest x2 3 us: swap_span(): return lax.ppermute(value, ('aisle', 'span'), pairs)]
  transfers between devices with their start and end apart: 5 -> 5, of which waited for: 2 -> 2; matrix products, arithmetic and copies ran while one was open for 0% -> 0% of each run, Pallas kernels for 6% -> 7%
where the time goes in v7:
time: 17.2 us; the launch traced here: 17 us
  starting transfers between devices  7.48 us (43%)
  waiting for transfers between devices  5.53 us (32%)
  Pallas kernels  3.32 us (19%)
  between operations  0.69 us (4%)
    ppermute x1, starting transfers between devices, shards(): got_jets = lax.ppermute(jets[1], 'span', [(i, i ^ 2) for i in range(4)])  4.1 us
    ppermute x2, waiting for transfers between devices, swap_span(): return lax.ppermute(value, ('aisle', 'span'), pairs)  3 us
    ppermute x2, waiting for transfers between devices, swap_aisle(): return lax.ppermute(value, 'aisle', pairs)  2.53 us
    ppermute x2, starting transfers between devices, swap_span(): return lax.ppermute(value, ('aisle', 'span'), pairs)  1.71 us
    ppermute x2, starting transfers between devices, swap_aisle(): return lax.ppermute(value, 'aisle', pairs)  1.67 us
    pallas_call x1, Pallas kernels, shards(): call(functools.partial(plenum_kernel, sizes, relayed), [near(room_shape),...  1.21 us
    pallas_call x1, Pallas kernels, shards(): call(functools.partial(finish_kernel, sizes, relayed), [near(room_shape),...  0.93 us
    pallas_call x1, Pallas kernels, shards(): call(functools.partial(local_kernel, sizes), [near(room_shape), near(plen...  0.77 us
  transfers between devices with their start and end apart: 5, of which 2 were waited for; matrix products, arithmetic and copies ran while one was open for 0% of the time, Pallas kernels for 7%

profile of v7, /device:TPU:0, one launch (start us, length us, event | category | flops | bytes accessed | tf_op | source)
XLA Modules:
  0.0 17.0 jit_solution(4309857225342554815)
XLA Ops:
  0.6 1.2 %shard_map.68 = (f32[19,4,16,128]{3,2,1,0:T(8,128)S(1)}, f32[19,16,128]{2,1,0:T(8,128)S(1)}, f32[8,1,640]{2,1,0:T(1,128)S(1)}, f32[8,1,640]{2,1,0:T(1,128)S(1)}) custom-call(f32[19,4,16,128]{3,2,1,0:T(8,128)} %bitcast.13, f32[19,16,128]{2,1,0:T(8,128)} %bitcast.14, s32[32]{0:T(128)} %cell_in.3, s32[32]{0:T(128)} %bitcast.15, s32[32]{0:T(128)} %class_in.1), custom_call_target="tpu_custom_call" | custom-call | flops 100000 | bytes 1000000 | tf_op jit(solution)/shard_map/pallas_call | solution.py:438
  1.8 4.1 %collective-permute-start.2 = (f32[8,1,640]{2,1,0:T(1,128)S(1)}, f32[8,1,640]{2,1,0:T(1,128)S(1)}, u32[]{:S(2)}, u32[]{:S(2)}) collective-permute-start(f32[8,1,640]{2,1,0:T(1,128)S(1)} %get-tuple-element.29), channel_id=1, source_target_pairs={{0,2},{1,3},{2,0},{3,1},{4,6},{5,7},{6,4},{7,5},{8,10},{9,11},{10,... | collective-permute-start | bytes 61448 | tf_op jit(solution)/shard_map/ppermute | solution.py:446
  5.9 0.3 %shard_map.69 = (f32[19,4,16,128]{3,2,1,0:T(8,128)S(1)}, f32[112,128]{1,0:T(8,128)S(1)}, f32[104,128]{1,0:T(8,128)S(1)}) custom-call(f32[19,4,16,128]{3,2,1,0:T(8,128)S(1)} %get-tuple-element.21.room_near, f32[19,16,128]{2,1,0:T(8,128)S(1)} %get-tuple-element.22.plen_post), custom_call_target="tpu_custom_call" | custom-call | flops 100000 | bytes 1000000 | tf_op jit(solution)/shard_map/pallas_call | solution.py:450
  6.3 1.7 %collective-permute-start.1 = (f32[104,128]{1,0:T(8,128)S(1)}, f32[104,128]{1,0:T(8,128)S(1)}, u32[]{:S(2)}, u32[]{:S(2)}) collective-permute-start(f32[104,128]{1,0:T(8,128)S(1)} %get-tuple-element.27), channel_id=1, source_target_pairs={{0,28},{4,8},{8,4},{12,16},{16,12},{20,24},{24,20},{28,0},{1,29},{... | collective-permute-start | bytes 159752 | tf_op jit(solution)/shard_map/ppermute | solution.py:404
  8.0 0.0 collective-permute-start
  8.0 0.8 %shard_map.70 = (f32[19,4,16,128]{3,2,1,0:T(8,128)S(1)}, f32[19,16,128]{2,1,0:T(8,128)S(1)}, f32[104,128]{1,0:T(8,128)S(1)}, f32[104,128]{1,0:T(8,128)S(1)}, f32[17,16,128]{2,1,0:T(8,128)S(1)}) custom-call(f32[19,4,16,128]{3,2,1,0:T(8,128)S(1)} %get-tuple-element.23.room_post, f32[19,16,128]{2,1,0:T(8,128)S(1)} %get-tuple-element.22.plen_post, s32[32]{0:T(128)} %cell_in.3, ...), custom_call_target="tpu_custom_call" | custom-call | flops 1000000000 | bytes 1000000 | tf_op jit(solution)/shard_map/pallas_call | solution.py:458
  8.7 0.0 collective-permute-done.2.got_jets.rest_1_
  8.7 2.5 %collective-permute-done.1.got_b = f32[104,128]{1,0:T(8,128)S(1)} collective-permute-done((f32[104,128]{1,0:T(8,128)S(1)}, f32[104,128]{1,0:T(8,128)S(1)}, u32[]{:S(2)}, u32[]{:S(2)}) %collective-permute-start.1) | collective-permute-done | bytes 53280 | tf_op jit(solution)/shard_map/ppermute | solution.py:404
  11.3 0.0 collective-permute-done.got_a
  11.3 0.1 collective-permute-start.4
  11.4 1.6 %collective-permute-start.3 = (f32[144,128]{1,0:T(8,128)S(1)}, f32[144,128]{1,0:T(8,128)S(1)}, u32[]{:S(2)}, u32[]{:S(2)}) collective-permute-start(f32[144,128]{1,0:T(8,128)S(1)} %get-tuple-element.35), channel_id=1, source_target_pairs={{0,1},{1,0},{2,3},{3,2},{4,5},{5,4},{6,7},{7,6},{8,9},{9,8},{10,11... | collective-permute-start | bytes 221192 | tf_op jit(solution)/shard_map/ppermute | solution.py:415
  13.1 0.0 collective-permute-done.4.got_b
  13.1 3.0 %collective-permute-done.3.got_a = f32[144,128]{1,0:T(8,128)S(1)} collective-permute-done((f32[144,128]{1,0:T(8,128)S(1)}, f32[144,128]{1,0:T(8,128)S(1)}, u32[]{:S(2)}, u32[]{:S(2)}) %collective-permute-start.3) | collective-permute-done | bytes 73760 | tf_op jit(solution)/shard_map/ppermute | solution.py:415
  16.1 0.9 %shard_map.73 = (f32[19,4,16,128]{3,2,1,0:T(8,128)S(1)}, f32[19,16,128]{2,1,0:T(8,128)S(1)}, f32[19,4,16,128]{3,2,1,0:T(8,128)}, f32[19,16,128]{2,1,0:T(8,128)}) custom-call(f32[19,4,16,128]{3,2,1,0:T(8,128)S(1)} %get-tuple-element.31.room_in, f32[19,16,128]{2,1,0:T(8,128)S(1)} %get-tuple-element.32.plen_in, ...), custom_call_target="tpu_custom_call", output_to_operand_aliasing={{0}: (0, {}), {1}: (1, {})} | custom-call | flops 100000 | bytes 1000000 | tf_op jit(solution)/shard_map/pallas_call | solution.py:484
  (2 shorter events, 0.1 us)
Async XLA Ops:
  1.8 6.9 %collective-permute-start.2 = (f32[8,1,640]{2,1,0:T(1,128)S(1)}, f32[8,1,640]{2,1,0:T(1,128)S(1)}, u32[]{:S(2)}, u32[]{:S(2)}) collective-permute-start(f32[8,1,640]{2,1,0:T(1,128)S(1)} %get-tuple-element.29), channel_id=1, source_target_pairs={{0,2},{1,3},{2,0},{3,1},{4,6},{5,7},{6,4},{7,5},{8,10},{9,11},{10,... | collective-permute-start | bytes 61448 | tf_op jit(solution)/shard_map/ppermute | solution.py:446
  6.3 5.0 %collective-permute-start.1 = (f32[104,128]{1,0:T(8,128)S(1)}, f32[104,128]{1,0:T(8,128)S(1)}, u32[]{:S(2)}, u32[]{:S(2)}) collective-permute-start(f32[104,128]{1,0:T(8,128)S(1)} %get-tuple-element.27), channel_id=1, source_target_pairs={{0,28},{4,8},{8,4},{12,16},{16,12},{20,24},{24,20},{28,0},{1,29},{... | collective-permute-start | bytes 159752 | tf_op jit(solution)/shard_map/ppermute | solution.py:404
  8.0 3.3 %collective-permute-start = (f32[112,128]{1,0:T(8,128)S(1)}, f32[112,128]{1,0:T(8,128)S(1)}, u32[]{:S(2)}, u32[]{:S(2)}) collective-permute-start(f32[112,128]{1,0:T(8,128)S(1)} %get-tuple-element.26), channel_id=1, source_target_pairs={{0,4},{4,0},{8,12},{12,8},{16,20},{20,16},{24,28},{28,24},{1,5},{5... | collective-permute-start | bytes 172040 | tf_op jit(solution)/shard_map/ppermute | solution.py:404
  11.3 1.8 %collective-permute-start.4 = (f32[104,128]{1,0:T(8,128)S(1)}, f32[104,128]{1,0:T(8,128)S(1)}, u32[]{:S(2)}, u32[]{:S(2)}) collective-permute-start(f32[104,128]{1,0:T(8,128)S(1)} %get-tuple-element.36), channel_id=1, source_target_pairs={{0,4},{1,2},{2,1},{3,7},{4,0},{5,6},{6,5},{7,3},{8,12},{9,10},{10,... | collective-permute-start | bytes 159752 | tf_op jit(solution)/shard_map/ppermute | solution.py:415
  11.4 4.7 %collective-permute-start.3 = (f32[144,128]{1,0:T(8,128)S(1)}, f32[144,128]{1,0:T(8,128)S(1)}, u32[]{:S(2)}, u32[]{:S(2)}) collective-permute-start(f32[144,128]{1,0:T(8,128)S(1)} %get-tuple-element.35), channel_id=1, source_target_pairs={{0,1},{1,0},{2,3},{3,2},{4,5},{5,4},{6,7},{7,6},{8,9},{9,8},{10,11... | collective-permute-start | bytes 221192 | tf_op jit(solution)/shard_map/ppermute | solution.py:415

commit v8 on v7

--- a/solution.py
+++ b/solution.py
@@ -478,7 +478,6 @@
         [near(room_shape), near(plen_shape), near((5, ca * cs, LANES))],
         [VMEM] * 7,
         aliases={0: 0, 1: 1},
-        flops=10**9,
     )(room_part, plen_part, got_a, got_b, jets[0], got_jets, places)
 
     _, _, room_next, plenum_next = call(

time: 17.2 us -> 16.8 us (0.977)
  waiting for transfers between devices: 5.53 us -> 5.26 us
    ppermute x2, waiting for transfers between devices: 3 us -> 2.73 us  [swap_span(): return lax.ppermute(value, ('aisle', 'span'), pairs)]
  transfers between devices with their start and end apart: 5 -> 5, of which waited for: 2 -> 3; matrix products, arithmetic and copies ran while one was open for 0% -> 0% of each run, Pallas kernels for 7% -> 7%
where the time goes in v8:
time: 16.8 us; the launch traced here: 16.7 us
  starting transfers between devices  7.42 us (44%)
  waiting for transfers between devices  5.26 us (31%)
  Pallas kernels  3.32 us (20%)
  between operations  0.68 us (4%)
    ppermute x1, starting transfers between devices, shards(): got_jets = lax.ppermute(jets[1], 'span', [(i, i ^ 2) for i in range(4)])  4.1 us
    ppermute x2, waiting for transfers between devices, swap_span(): return lax.ppermute(value, ('aisle', 'span'), pairs)  2.73 us
    ppermute x2, waiting for transfers between devices, swap_aisle(): return lax.ppermute(value, 'aisle', pairs)  2.53 us
    ppermute x2, starting transfers between devices, swap_aisle(): return lax.ppermute(value, 'aisle', pairs)  1.67 us
    ppermute x2, starting transfers between devices, swap_span(): return lax.ppermute(value, ('aisle', 'span'), pairs)  1.64 us
    pallas_call x1, Pallas kernels, shards(): call(functools.partial(plenum_kernel, sizes, relayed), [near(room_shape),...  1.21 us
    pallas_call x1, Pallas kernels, shards(): call(functools.partial(finish_kernel, sizes, relayed), [near(room_shape),...  0.93 us
    pallas_call x1, Pallas kernels, shards(): call(functools.partial(local_kernel, sizes), [near(room_shape), near(plen...  0.77 us
  transfers between devices with their start and end apart: 5, of which 3 were waited for; matrix products, arithmetic and copies ran while one was open for 0% of the time, Pallas kernels for 7%

profile of v8, /device:TPU:0, one launch (start us, length us, event | category | flops | bytes accessed | tf_op | source)
XLA Modules:
  0.0 16.7 jit_solution(5841050498934980664)
XLA Ops:
  0.6 1.2 %shard_map.68 = (f32[19,4,16,128]{3,2,1,0:T(8,128)S(1)}, f32[19,16,128]{2,1,0:T(8,128)S(1)}, f32[8,1,640]{2,1,0:T(1,128)S(1)}, f32[8,1,640]{2,1,0:T(1,128)S(1)}) custom-call(f32[19,4,16,128]{3,2,1,0:T(8,128)} %bitcast.13, f32[19,16,128]{2,1,0:T(8,128)} %bitcast.14, s32[32]{0:T(128)} %cell_in.3, s32[32]{0:T(128)} %bitcast.15, s32[32]{0:T(128)} %class_in.1), custom_call_target="tpu_custom_call" | custom-call | flops 100000 | bytes 1000000 | tf_op jit(solution)/shard_map/pallas_call | solution.py:438
  1.8 4.1 %collective-permute-start.2 = (f32[8,1,640]{2,1,0:T(1,128)S(1)}, f32[8,1,640]{2,1,0:T(1,128)S(1)}, u32[]{:S(2)}, u32[]{:S(2)}) collective-permute-start(f32[8,1,640]{2,1,0:T(1,128)S(1)} %get-tuple-element.29), channel_id=1, source_target_pairs={{0,2},{1,3},{2,0},{3,1},{4,6},{5,7},{6,4},{7,5},{8,10},{9,11},{10,... | collective-permute-start | bytes 61448 | tf_op jit(solution)/shard_map/ppermute | solution.py:446
  5.9 0.3 %shard_map.69 = (f32[19,4,16,128]{3,2,1,0:T(8,128)S(1)}, f32[112,128]{1,0:T(8,128)S(1)}, f32[104,128]{1,0:T(8,128)S(1)}) custom-call(f32[19,4,16,128]{3,2,1,0:T(8,128)S(1)} %get-tuple-element.21.room_near, f32[19,16,128]{2,1,0:T(8,128)S(1)} %get-tuple-element.22.plen_post), custom_call_target="tpu_custom_call" | custom-call | flops 100000 | bytes 1000000 | tf_op jit(solution)/shard_map/pallas_call | solution.py:450
  6.3 1.7 %collective-permute-start.1 = (f32[104,128]{1,0:T(8,128)S(1)}, f32[104,128]{1,0:T(8,128)S(1)}, u32[]{:S(2)}, u32[]{:S(2)}) collective-permute-start(f32[104,128]{1,0:T(8,128)S(1)} %get-tuple-element.27), channel_id=1, source_target_pairs={{0,28},{4,8},{8,4},{12,16},{16,12},{20,24},{24,20},{28,0},{1,29},{... | collective-permute-start | bytes 159752 | tf_op jit(solution)/shard_map/ppermute | solution.py:404
  8.0 0.0 collective-permute-start
  8.0 0.8 %shard_map.70 = (f32[19,4,16,128]{3,2,1,0:T(8,128)S(1)}, f32[19,16,128]{2,1,0:T(8,128)S(1)}, f32[104,128]{1,0:T(8,128)S(1)}, f32[104,128]{1,0:T(8,128)S(1)}, f32[17,16,128]{2,1,0:T(8,128)S(1)}) custom-call(f32[19,4,16,128]{3,2,1,0:T(8,128)S(1)} %get-tuple-element.23.room_post, f32[19,16,128]{2,1,0:T(8,128)S(1)} %get-tuple-element.22.plen_post, s32[32]{0:T(128)} %cell_in.3, ...), custom_call_target="tpu_custom_call" | custom-call | flops 1000000000 | bytes 1000000 | tf_op jit(solution)/shard_map/pallas_call | solution.py:458
  8.7 0.0 collective-permute-done.2.got_jets.rest_1_
  8.7 2.5 %collective-permute-done.1.got_b = f32[104,128]{1,0:T(8,128)S(1)} collective-permute-done((f32[104,128]{1,0:T(8,128)S(1)}, f32[104,128]{1,0:T(8,128)S(1)}, u32[]{:S(2)}, u32[]{:S(2)}) %collective-permute-start.1) | collective-permute-done | bytes 53280 | tf_op jit(solution)/shard_map/ppermute | solution.py:404
  11.3 0.0 collective-permute-done.got_a
  11.3 1.6 %collective-permute-start.3 = (f32[144,128]{1,0:T(8,128)S(1)}, f32[144,128]{1,0:T(8,128)S(1)}, u32[]{:S(2)}, u32[]{:S(2)}) collective-permute-start(f32[144,128]{1,0:T(8,128)S(1)} %get-tuple-element.35), channel_id=1, source_target_pairs={{0,1},{1,0},{2,3},{3,2},{4,5},{5,4},{6,7},{7,6},{8,9},{9,8},{10,11... | collective-permute-start | bytes 221192 | tf_op jit(solution)/shard_map/ppermute | solution.py:415
  13.0 0.0 collective-permute-start.4
  13.0 1.2 %collective-permute-done.4.got_b = f32[104,128]{1,0:T(8,128)S(1)} collective-permute-done((f32[104,128]{1,0:T(8,128)S(1)}, f32[104,128]{1,0:T(8,128)S(1)}, u32[]{:S(2)}, u32[]{:S(2)}) %collective-permute-start.4) | collective-permute-done | bytes 53280 | tf_op jit(solution)/shard_map/ppermute | solution.py:415
  14.2 1.5 %collective-permute-done.3.got_a = f32[144,128]{1,0:T(8,128)S(1)} collective-permute-done((f32[144,128]{1,0:T(8,128)S(1)}, f32[144,128]{1,0:T(8,128)S(1)}, u32[]{:S(2)}, u32[]{:S(2)}) %collective-permute-start.3) | collective-permute-done | bytes 73760 | tf_op jit(solution)/shard_map/ppermute | solution.py:415
  15.7 0.9 %shard_map.73 = (f32[19,4,16,128]{3,2,1,0:T(8,128)S(1)}, f32[19,16,128]{2,1,0:T(8,128)S(1)}, f32[19,4,16,128]{3,2,1,0:T(8,128)}, f32[19,16,128]{2,1,0:T(8,128)}) custom-call(f32[19,4,16,128]{3,2,1,0:T(8,128)S(1)} %get-tuple-element.31.room_in, f32[19,16,128]{2,1,0:T(8,128)S(1)} %get-tuple-element.32.plen_in, ...), custom_call_target="tpu_custom_call", output_to_operand_aliasing={{0}: (0, {}), {1}: (1, {})} | custom-call | flops 100000 | bytes 1000000 | tf_op jit(solution)/shard_map/pallas_call | solution.py:483
  (2 shorter events, 0.1 us)
Async XLA Ops:
  1.8 6.9 %collective-permute-start.2 = (f32[8,1,640]{2,1,0:T(1,128)S(1)}, f32[8,1,640]{2,1,0:T(1,128)S(1)}, u32[]{:S(2)}, u32[]{:S(2)}) collective-permute-start(f32[8,1,640]{2,1,0:T(1,128)S(1)} %get-tuple-element.29), channel_id=1, source_target_pairs={{0,2},{1,3},{2,0},{3,1},{4,6},{5,7},{6,4},{7,5},{8,10},{9,11},{10,... | collective-permute-start | bytes 61448 | tf_op jit(solution)/shard_map/ppermute | solution.py:446
  6.3 5.0 %collective-permute-start.1 = (f32[104,128]{1,0:T(8,128)S(1)}, f32[104,128]{1,0:T(8,128)S(1)}, u32[]{:S(2)}, u32[]{:S(2)}) collective-permute-start(f32[104,128]{1,0:T(8,128)S(1)} %get-tuple-element.27), channel_id=1, source_target_pairs={{0,28},{4,8},{8,4},{12,16},{16,12},{20,24},{24,20},{28,0},{1,29},{... | collective-permute-start | bytes 159752 | tf_op jit(solution)/shard_map/ppermute | solution.py:404
  8.0 3.3 %collective-permute-start = (f32[112,128]{1,0:T(8,128)S(1)}, f32[112,128]{1,0:T(8,128)S(1)}, u32[]{:S(2)}, u32[]{:S(2)}) collective-permute-start(f32[112,128]{1,0:T(8,128)S(1)} %get-tuple-element.26), channel_id=1, source_target_pairs={{0,4},{4,0},{8,12},{12,8},{16,20},{20,16},{24,28},{28,24},{1,5},{5... | collective-permute-start | bytes 172040 | tf_op jit(solution)/shard_map/ppermute | solution.py:404
  11.3 4.4 %collective-permute-start.3 = (f32[144,128]{1,0:T(8,128)S(1)}, f32[144,128]{1,0:T(8,128)S(1)}, u32[]{:S(2)}, u32[]{:S(2)}) collective-permute-start(f32[144,128]{1,0:T(8,128)S(1)} %get-tuple-element.35), channel_id=1, source_target_pairs={{0,1},{1,0},{2,3},{3,2},{4,5},{5,4},{6,7},{7,6},{8,9},{9,8},{10,11... | collective-permute-start | bytes 221192 | tf_op jit(solution)/shard_map/ppermute | solution.py:415
  13.0 1.2 %collective-permute-start.4 = (f32[104,128]{1,0:T(8,128)S(1)}, f32[104,128]{1,0:T(8,128)S(1)}, u32[]{:S(2)}, u32[]{:S(2)}) collective-permute-start(f32[104,128]{1,0:T(8,128)S(1)} %get-tuple-element.36), channel_id=1, source_target_pairs={{0,4},{1,2},{2,1},{3,7},{4,0},{5,6},{6,5},{7,3},{8,12},{9,10},{10,... | collective-permute-start | bytes 159752 | tf_op jit(solution)/shard_map/ppermute | solution.py:415

commit v9 on v8

--- a/solution.py
+++ b/solution.py
@@ -89,9 +89,12 @@
     return jnp.where(row == (0 if cy == 1 else cs - 1), value, turned)
 
 
+def shifted(value, by):
+    return pltpu.roll(value, by % value.shape[0], 0) if by else value
+
+
 def turned_to(value, source, dest):
-    shift = (dest - source) % value.shape[0]
-    return value if shift == 0 else pltpu.roll(value, shift, 0)
+    return shifted(value, dest - source)
 
 
 def repeat(count, body, start):
@@ -180,40 +183,19 @@
     return sums
 
 
-def local_kernel(sizes, room_post, plen_post, cell_in, owner_in, room_part, plen_part, span_up, span_down, places,
-                 cells, owners, sems):
+def local_kernel(sizes, room_post, plen_post, cell_in, owner_in, room_part, plen_part, places, cells, owners, sems):
     ca, cs, blocks, n_span, per_brick = sizes
     rows = blocks * cs
     copies = [pltpu.make_async_copy(src, dst, sems.at[i]) for i, (src, dst) in enumerate(
         ((cell_in, cells), (owner_in, owners)))]
     for copy in copies:
         copy.start()
-    group = lax.broadcasted_iota(jnp.int32, (rows, LANES), 0) % cs
     for q in range(19):
         cx, cy, cz = VELOCITIES[q]
-        edge = cs - 1 if cy == 1 else 0
-        span, planes = (span_up, Y_UP) if cy == 1 else (span_down, Y_DOWN)
-        packed = None
         for x in range(ca):
-            if not 0 <= x - cx < ca:
-                continue
-            value = raised(room_post[q, x - cx], cz, cs)
-            room_part[q, x] = crossed(value, cy, cs)
-            if cy:
-                ready = turned_to(value, edge, x)
-                packed = ready if packed is None else jnp.where(group == x, ready, packed)
-        value = raised(plen_post[q], cz, ca * cs)
-        if cx == 1:
-            value = pltpu.roll(value, cs, 0)
-        elif cx == -1:
-            value = pltpu.roll(value, ca * cs - cs, 0)
-        plen_part[q] = crossed(value, cy, cs)
-        if cy:
-            k = planes.index(q)
-            span[k * rows : (k + 1) * rows] = packed
-            for x in range(ca):
-                to = 5 * rows + k * ca + x
-                span[to : to + 1] = value[x * cs + edge : x * cs + edge + 1]
+            if 0 <= x - cx < ca:
+                room_part[q, x] = crossed(raised(room_post[q, x - cx], cz, cs), cy, cs)
+        plen_part[q] = crossed(shifted(raised(plen_post[q], cz, ca * cs), cx * cs), cy, cs)
     places[0 : n_span * CAP] = jnp.zeros((n_span * CAP, ca * cs, LANES), F32)
     here = lax.axis_index("span")
     row = lax.broadcasted_iota(jnp.int32, (ca * cs, LANES), 0)
@@ -233,63 +215,71 @@
     repeat(n_span, brick, 0)
 
 
-def pack_kernel(sizes, relayed, got_a, got_b, span_up, span_down, *rest):
-    ca, cs, blocks, n_span, per_brick = sizes
-    rows = blocks * cs
-    if relayed:
-        jets, got_jets, cross_a, cross_b = rest
-    else:
-        cross_a, cross_b = rest
+def cross_kernel(sizes, relayed, room_post, plen_post, jets, cross_a, cross_b):
+    ca, cs, blocks, n_span, per_brick = sizes
+    rows = blocks * cs
+    low = lax.axis_index("span") % 2 == 0
+    group = lax.broadcasted_iota(jnp.int32, (rows, LANES), 0) % cs
+    for k in range(5):
+        sides, near = [], []
+        for q, edge in ((Y_UP[k], cs - 1), (Y_DOWN[k], 0)):
+            cx, cy, cz = VELOCITIES[q]
+            packed = None
+            for x in range(max(cx, 0), ca + min(cx, 0)):
+                ready = turned_to(raised(room_post[q, x - cx], cz, cs), edge, x)
+                packed = ready if packed is None else jnp.where(group == x, ready, packed)
+            sides.append(packed)
+            near.append(shifted(raised(plen_post[q], cz, ca * cs), cx * cs - edge))
+        cross_a[k * rows : (k + 1) * rows] = jnp.where(low, sides[0], sides[1])
+        cross_b[k * rows : (k + 1) * rows] = jnp.where(low, sides[1], sides[0])
+        first, second = jnp.where(low, near[0], near[1]), jnp.where(low, near[1], near[0])
+        for x in range(ca):
+            to = 5 * rows + k * ca + x
+            cross_a[to : to + 1] = first[x * cs : x * cs + 1]
+            cross_b[to : to + 1] = second[x * cs : x * cs + 1]
+    if relayed:
+        for s in range(CAP):
+            for k in range(5):
+                to = 5 * (rows + ca) + s * 5 + k
+                cross_a[to : to + 1] = jets[CAP + s, :, k * LANES : (k + 1) * LANES]
+
+
+def corners(cs, up):
+    return [q for q in (Y_UP if up else Y_DOWN) if VELOCITIES[q][0]], cs - 1 if up else 0
+
+
+def corner_kernel(sizes, relayed, got_a, got_b, got_jets, places, cross_a, cross_b):
+    del places
+    ca, cs, blocks, n_span, per_brick = sizes
+    rows = blocks * cs
     even = lax.axis_index("aisle") % 2 == 0
     low = lax.axis_index("span") % 2 == 0
-    halo = span_up.shape[0]
     group = lax.broadcasted_iota(jnp.int32, (rows, LANES), 0) % cs
 
-    def corner(q, low, high):
+    def came(q, low, high):
         if VELOCITIES[q][0] == 1:
             k = X_UP.index(q)
             return jnp.where(even, got_b[low(k) : high(k)], got_a[low(k) : high(k)])
         k = X_DOWN.index(q)
         return jnp.where(even, got_a[low(k) : high(k)], got_b[low(k) : high(k)])
 
-    for k in range(5):
-        sides = []
-        for span, planes, edge in ((span_up, Y_UP, cs - 1), (span_down, Y_DOWN, 0)):
-            q = planes[k]
-            value = span[k * rows : (k + 1) * rows]
-            if VELOCITIES[q][0]:
-                x = 0 if VELOCITIES[q][0] == 1 else ca - 1
-                came = corner(q, lambda k: k * rows, lambda k: (k + 1) * rows)
-                value = jnp.where(group == x, turned_to(came, edge, x), value)
-            sides.append(value)
-        cross_a[k * rows : (k + 1) * rows] = jnp.where(low, sides[0], sides[1])
-        cross_b[k * rows : (k + 1) * rows] = jnp.where(low, sides[1], sides[0])
-    for r in range(5 * rows, halo, 8):
-        rising, falling = span_up[r : r + 8], span_down[r : r + 8]
-        cross_a[r : r + 8] = jnp.where(low, rising, falling)
-        cross_b[r : r + 8] = jnp.where(low, falling, rising)
-    for planes, edge in ((Y_UP, cs - 1), (Y_DOWN, 0)):
-        for k, q in enumerate(planes):
-            if VELOCITIES[q][0]:
-                x = 0 if VELOCITIES[q][0] == 1 else ca - 1
-                at = lambda k: 5 * rows + k * cs + edge
-                came = corner(q, at, lambda k: at(k) + 1)
-                to = 5 * rows + k * ca + x
-
-                @pl.when(low == (planes is Y_UP))
-                def _():
-                    cross_a[to : to + 1] = came
-
-                @pl.when(low != (planes is Y_UP))
-                def _():
-                    cross_b[to : to + 1] = came
-
-    if relayed:
-        for b, source in enumerate((jets, got_jets)):
-            for s in range(CAP):
-                for k in range(5):
-                    to = halo + (b * CAP + s) * 5 + k
-                    cross_a[to : to + 1] = source[CAP + s, :, k * LANES : (k + 1) * LANES]
+    sides, near = [], []
+    for up in (True, False):
+        two, edge = corners(cs, up)
+        parts = [turned_to(came(q, lambda k: k * rows, lambda k: (k + 1) * rows), edge, c) for c, q in enumerate(two)]
+        sides.append(jnp.where(group == 0, parts[0], parts[1]))
+        at = lambda k: 5 * rows + k * cs + edge
+        near.append([came(q, at, lambda k: at(k) + 1) for q in two])
+    cross_a[0:rows] = jnp.where(low, sides[0], sides[1])
+    cross_b[0:rows] = jnp.where(low, sides[1], sides[0])
+    for c in range(2):
+        cross_a[rows + c : rows + c + 1] = jnp.where(low, near[0][c], near[1][c])
+        cross_b[rows + c : rows + c + 1] = jnp.where(low, near[1][c], near[0][c])
+    if relayed:
+        for s in range(CAP):
+            for k in range(5):
+                to = rows + 2 + s * 5 + k
+                cross_a[to : to + 1] = got_jets[CAP + s, :, k * LANES : (k + 1) * LANES]
 
 
 def aisle_kernel(sizes, relayed, room_in, plen_in, got_a, got_b, jets, got_jets, places, room, plen, inflow):
@@ -334,14 +324,33 @@
         lax.fori_loop(0, n_span, add_brick, 0)
 
 
-def finish_kernel(sizes, relayed, room_in, plen_in, got_a, got_b, places, inflow, room, plen, room_out, plen_out, sems):
-    ca, cs, blocks, n_span, per_brick = sizes
-    rows = blocks * cs
+def entering(n_span, got_a, got_b, enter):
     here = lax.axis_index("span")
     low = here % 2 == 0
-    halo = 5 * (rows + cs)
-    halo = halo + -halo % 8
+
+    @pl.when(low)
+    def _():
+        enter(got_a, False)
+
+    @pl.when(jnp.logical_not(low))
+    def _():
+        enter(got_a, True)
+
+    @pl.when(jnp.logical_and(low, here > 0))
+    def _():
+        enter(got_b, True)
+
+    @pl.when(jnp.logical_and(jnp.logical_not(low), here < n_span - 1))
+    def _():
+        enter(got_b, False)
+
+
+def enter_kernel(sizes, relayed, room_in, plen_in, got_a, got_b, places, inflow_in, room, plen, inflow):
+    ca, cs, blocks, n_span, per_brick = sizes
+    rows = blocks * cs
+    here = lax.axis_index("span")
     group = lax.broadcasted_iota(jnp.int32, (rows, LANES), 0) % cs
+
     def enter(got, up):
         planes, y = (Y_UP, 0) if up else (Y_DOWN, cs - 1)
         for k, q in enumerate(planes):
@@ -351,30 +360,38 @@
                 at = 5 * rows + k * ca + x
                 plen[q, x * cs + y : x * cs + y + 1] = got[at : at + 1]
 
-    @pl.when(low)
-    def _():
-        enter(got_a, False)
-
-    @pl.when(jnp.logical_not(low))
-    def _():
-        enter(got_a, True)
-
-    @pl.when(jnp.logical_and(low, here > 0))
-    def _():
-        enter(got_b, True)
-
-    @pl.when(jnp.logical_and(jnp.logical_not(low), here < n_span - 1))
-    def _():
-        enter(got_b, False)
-
+    entering(n_span, got_a, got_b, enter)
+    if relayed:
+        start = 5 * (rows + ca)
+        jet = lambda s, k: got_a[start + s * 5 + k : start + s * 5 + k + 1]
+        sums = jet_sums(lambda k: inflow_in[k], places, [(here ^ 1, jet)])
+        for k in range(5):
+            inflow[k] = sums[k]
+    else:
+        inflow[...] = inflow_in[...]
+
+
+def finish_kernel(sizes, relayed, room_in, plen_in, got_a, got_b, places, inflow, room, plen, room_out, plen_out, sems):
+    ca, cs, blocks, n_span, per_brick = sizes
+    rows = blocks * cs
+    here = lax.axis_index("span")
+    group = lax.broadcasted_iota(jnp.int32, (rows, LANES), 0) % cs
+
+    def enter(got, up):
+        two, _ = corners(cs, up)
+        y = 0 if up else cs - 1
+        came = got[0:rows]
+        for c, q in enumerate(two):
+            x = 0 if VELOCITIES[q][0] == 1 else ca - 1
+            room[q, x] = jnp.where(group == y, turned_to(came, c, y), room[q, x])
+            plen[q, x * cs + y : x * cs + y + 1] = got[rows + c : rows + c + 1]
+
+    entering(n_span, got_a, got_b, enter)
     plen_copy = pltpu.make_async_copy(plen, plen_out, sems.at[0])
     plen_copy.start()
     bricks = []
     if relayed:
-        def reader(b):
-            return lambda s, k: got_a[halo + (b * CAP + s) * 5 + k : halo + (b * CAP + s) * 5 + k + 1]
-
-        bricks = [(here ^ 1, reader(0)), (here ^ 3, reader(1))]
+        bricks = [(here ^ 3, lambda s, k: got_a[rows + 2 + s * 5 + k : rows + 2 + s * 5 + k + 1])]
     sums = jet_sums(lambda k: inflow[k], places, bricks)
     for k, q in enumerate(UPWARD):
         for x in range(ca):
@@ -388,6 +405,7 @@
 def call(kernel, outs, in_specs, out_specs=None, scratch=(), aliases={}, flops=100_000, moved=1_000_000):
     return pl.pallas_call(
         kernel,
+        name=kernel.func.__name__,
         out_shape=outs,
         in_specs=in_specs,
         out_specs=[VMEM] * len(outs) if out_specs is None else out_specs,
@@ -455,30 +473,43 @@
     got_b = swap_aisle(swap_b, True)
     got_a = swap_aisle(swap_a, False)
 
-    room_part, plen_part, span_up, span_down, places = call(
+    upto8 = lambda count: count + -count % 8
+    cross_a, cross_b = call(
+        functools.partial(cross_kernel, sizes, relayed),
+        [near((upto8(5 * (rows + ca) + (5 * CAP if relayed else 0)), LANES)), near((halo, LANES))],
+        [VMEM] * 3,
+    )(room_post, plen_post, jets[0])
+    in_a = swap_span(cross_a, False)
+    in_b = swap_span(cross_b, True)
+
+    room_part, plen_part, places = call(
         functools.partial(local_kernel, sizes),
-        [near(room_shape), near(plen_shape), near((halo, LANES)), near((halo, LANES)),
-         near((n_span * CAP + 1, ca * cs, LANES))],
+        [near(room_shape), near(plen_shape), near((n_span * CAP + 1, ca * cs, LANES))],
         [VMEM, VMEM, HBM, HBM],
         scratch=[numbers, numbers, pltpu.SemaphoreType.DMA((2,))],
         flops=10**9,
     )(room_post, plen_post, tile_cell, tile_owner)
 
-    cross_shape = (halo + 2 * CAP * 5, LANES) if relayed else (halo, LANES)
-    cross_a, cross_b = call(
-        functools.partial(pack_kernel, sizes, relayed),
-        [near(cross_shape), near((halo, LANES))],
-        [VMEM] * (6 if relayed else 4),
-    )(got_a, got_b, span_up, span_down, *((jets[0], got_jets) if relayed else ()))
-
-    in_b = swap_span(cross_b, True)
-    in_a = swap_span(cross_a, False)
+    corner_a, corner_b = call(
+        functools.partial(corner_kernel, sizes, relayed),
+        [near((upto8(rows + 2 + (5 * CAP if relayed else 0)), LANES)), near((upto8(rows + 2), LANES))],
+        [VMEM] * 4,
+    )(got_a, got_b, got_jets, places)
+    last_a = swap_span(corner_a, False)
+    last_b = swap_span(corner_b, True)
+
     room_part, plen_part, inflow = call(
         functools.partial(aisle_kernel, sizes, relayed),
         [near(room_shape), near(plen_shape), near((5, ca * cs, LANES))],
         [VMEM] * 7,
         aliases={0: 0, 1: 1},
     )(room_part, plen_part, got_a, got_b, jets[0], got_jets, places)
+    room_part, plen_part, inflow = call(
+        functools.partial(enter_kernel, sizes, relayed),
+        [near(room_shape), near(plen_shape), near((5, ca * cs, LANES))],
+        [VMEM] * 6,
+        aliases={0: 0, 1: 1},
+    )(room_part, plen_part, in_a, in_b, places, inflow)
 
     _, _, room_next, plenum_next = call(
         functools.partial(finish_kernel, sizes, relayed),
@@ -488,7 +519,7 @@
         out_specs=[VMEM, VMEM, HBM, HBM],
         scratch=[pltpu.SemaphoreType.DMA((2,))],
         aliases={0: 0, 1: 1},
-    )(room_part, plen_part, in_a, in_b, places, inflow)
+    )(room_part, plen_part, last_a, last_b, places, inflow)
     room_next = room_next.reshape(19, ca, blocks, cs, LANES).transpose(0, 1, 3, 2, 4).reshape(room_pops.shape)
     return room_next, plenum_next.reshape(plenum_pops.shape)
 

time: 16.8 us -> 16.2 us (0.964)
  waiting for transfers between devices: 5.26 us -> 2.67 us
  starting transfers between devices: 7.42 us -> 9.14 us
  Pallas kernels: 3.32 us -> 3.53 us
    ppermute x2, waiting for transfers between devices: 2.53 us -> 0.6 us  [swap_aisle(): return lax.ppermute(value, 'aisle', pairs)]
    ppermute x2 -> x4, starting transfers between devices: 1.64 us -> 3.36 us  [swap_span(): return lax.ppermute(value, ('aisle', 'span'), pairs)]
    ppermute x2 -> x4, waiting for transfers between devices: 2.73 us -> 2.07 us  [swap_span(): return lax.ppermute(value, ('aisle', 'span'), pairs)]
  transfers between devices with their start and end apart: 5 -> 7, of which waited for: 3 -> 3; matrix products, arithmetic and copies ran while one was open for 0% -> 0% of each run, Pallas kernels for 7% -> 9%
where the time goes in v9:
time: 16.2 us; the launch traced here: 16.1 us
  starting transfers between devices  9.14 us (56%)
  Pallas kernels  3.53 us (22%)
  waiting for transfers between devices  2.67 us (16%)
  between operations  0.71 us (4%)
    ppermute x1, starting transfers between devices, shards(): got_jets = lax.ppermute(jets[1], 'span', [(i, i ^ 2) for i in range(4)])  4.1 us
    ppermute x4, starting transfers between devices, swap_span(): return lax.ppermute(value, ('aisle', 'span'), pairs)  3.36 us
    ppermute x4, waiting for transfers between devices, swap_span(): return lax.ppermute(value, ('aisle', 'span'), pairs)  2.07 us
    ppermute x2, starting transfers between devices, swap_aisle(): return lax.ppermute(value, 'aisle', pairs)  1.67 us
    pallas_call x1, Pallas kernels, shards(): call(functools.partial(plenum_kernel, sizes, relayed), [near(room_shape),...  1.21 us
    pallas_call x1, Pallas kernels, shards(): call(functools.partial(finish_kernel, sizes, relayed), [near(room_shape),...  0.9 us
    pallas_call x1, Pallas kernels, shards(): call(functools.partial(local_kernel, sizes), [near(room_shape), near(plen...  0.86 us
    ppermute x2, waiting for transfers between devices, swap_aisle(): return lax.ppermute(value, 'aisle', pairs)  0.6 us
  transfers between devices with their start and end apart: 7, of which 3 were waited for; matrix products, arithmetic and copies ran while one was open for 0% of the time, Pallas kernels for 9%

profile of v9, /device:TPU:0, one launch (start us, length us, event | category | flops | bytes accessed | tf_op | source)
XLA Modules:
  0.0 16.1 jit_solution(5726145847318965052)
XLA Ops:
  0.6 1.2 %plenum_kernel.1 = (f32[19,4,16,128]{3,2,1,0:T(8,128)S(1)}, f32[19,16,128]{2,1,0:T(8,128)S(1)}, f32[8,1,640]{2,1,0:T(1,128)S(1)}, f32[8,1,640]{2,1,0:T(1,128)S(1)}) custom-call(f32[19,4,16,128]{3,2,1,0:T(8,128)} %bitcast.13, f32[19,16,128]{2,1,0:T(8,128)} %bitcast.14, s32[32]{0:T(128)} %cell_in.3, s32[32]{0:T(128)} %bitcast.15, s32[32]{0:T(128)} %class_in.1), custom_call_target="tpu_custom_call" | custom-call | flops 100000 | bytes 1000000 | tf_op jit(solution)/shard_map/plenum_kernel/pallas_call | solution.py:456
  1.8 4.1 %collective-permute-start.2 = (f32[8,1,640]{2,1,0:T(1,128)S(1)}, f32[8,1,640]{2,1,0:T(1,128)S(1)}, u32[]{:S(2)}, u32[]{:S(2)}) collective-permute-start(f32[8,1,640]{2,1,0:T(1,128)S(1)} %get-tuple-element.32), channel_id=1, source_target_pairs={{0,2},{1,3},{2,0},{3,1},{4,6},{5,7},{6,4},{7,5},{8,10},{9,11},{10,... | collective-permute-start | bytes 61448 | tf_op jit(solution)/shard_map/ppermute | solution.py:464
  5.9 0.3 %room_kernel.1 = (f32[19,4,16,128]{3,2,1,0:T(8,128)S(1)}, f32[112,128]{1,0:T(8,128)S(1)}, f32[104,128]{1,0:T(8,128)S(1)}) custom-call(f32[19,4,16,128]{3,2,1,0:T(8,128)S(1)} %get-tuple-element.24.room_near, f32[19,16,128]{2,1,0:T(8,128)S(1)} %get-tuple-element.25.plen_post), custom_call_target="tpu_custom_call" | custom-call | flops 100000 | bytes 1000000 | tf_op jit(solution)/shard_map/room_kernel/pallas_call | solution.py:468
  6.3 1.7 %collective-permute-start.1 = (f32[104,128]{1,0:T(8,128)S(1)}, f32[104,128]{1,0:T(8,128)S(1)}, u32[]{:S(2)}, u32[]{:S(2)}) collective-permute-start(f32[104,128]{1,0:T(8,128)S(1)} %get-tuple-element.30), channel_id=1, source_target_pairs={{0,28},{4,8},{8,4},{12,16},{16,12},{20,24},{24,20},{28,0},{1,29},{... | collective-permute-start | bytes 159752 | tf_op jit(solution)/shard_map/ppermute | solution.py:422
  8.0 0.0 collective-permute-start
  8.0 0.1 cross_kernel.1
  8.1 0.6 %collective-permute-start.4 = (f32[104,128]{1,0:T(8,128)S(1)}, f32[104,128]{1,0:T(8,128)S(1)}, u32[]{:S(2)}, u32[]{:S(2)}) collective-permute-start(f32[104,128]{1,0:T(8,128)S(1)} %get-tuple-element.37), channel_id=1, source_target_pairs={{0,4},{1,2},{2,1},{3,7},{4,0},{5,6},{6,5},{7,3},{8,12},{9,10},{10,... | collective-permute-start | bytes 159752 | tf_op jit(solution)/shard_map/ppermute | solution.py:433
  8.6 1.1 %collective-permute-start.3 = (f32[120,128]{1,0:T(8,128)S(1)}, f32[120,128]{1,0:T(8,128)S(1)}, u32[]{:S(2)}, u32[]{:S(2)}) collective-permute-start(f32[120,128]{1,0:T(8,128)S(1)} %get-tuple-element.36), channel_id=1, source_target_pairs={{0,1},{1,0},{2,3},{3,2},{4,5},{5,4},{6,7},{7,6},{8,9},{9,8},{10,11... | collective-permute-start | bytes 184328 | tf_op jit(solution)/shard_map/ppermute | solution.py:433
  9.8 0.9 %local_kernel.1 = (f32[19,4,16,128]{3,2,1,0:T(8,128)S(1)}, f32[19,16,128]{2,1,0:T(8,128)S(1)}, f32[17,16,128]{2,1,0:T(8,128)S(1)}) custom-call(f32[19,4,16,128]{3,2,1,0:T(8,128)S(1)} %get-tuple-element.26.room_post, f32[19,16,128]{2,1,0:T(8,128)S(1)} %get-tuple-element.25.plen_post, s32[32]{0:T(128)} %cell_in.3, s32[32]{0:T(128)} %bitcast.16), custom_call_target="tpu_custom_call" | custom-call | flops 1000000000 | bytes 1000000 | tf_op jit(solution)/shard_map/local_kernel/pallas_call | solution.py:485
  10.7 0.0 collective-permute-done.2.got_jets
  10.7 0.6 %collective-permute-done.1.got_b = f32[104,128]{1,0:T(8,128)S(1)} collective-permute-done((f32[104,128]{1,0:T(8,128)S(1)}, f32[104,128]{1,0:T(8,128)S(1)}, u32[]{:S(2)}, u32[]{:S(2)}) %collective-permute-start.1) | collective-permute-done | bytes 53280 | tf_op jit(solution)/shard_map/ppermute | solution.py:422
  11.3 0.0 collective-permute-done.got_a
  11.3 1.6 %collective-permute-start.5 = (f32[40,128]{1,0:T(8,128)S(1)}, f32[40,128]{1,0:T(8,128)S(1)}, u32[]{:S(2)}, u32[]{:S(2)}) collective-permute-start(f32[40,128]{1,0:T(8,128)S(1)} %get-tuple-element.41), channel_id=1, source_target_pairs={{0,1},{1,0},{2,3},{3,2},{4,5},{5,4},{6,7},{7,6},{8,9},{9,8},{10,11... | collective-permute-start | bytes 61448 | tf_op jit(solution)/shard_map/ppermute | solution.py:433
  12.9 0.0 collective-permute-start.6
  13.0 0.0 collective-permute-done.4.got_b
  13.0 0.0 collective-permute-done.3.got_a
  13.0 0.1 enter_kernel.1
  13.1 1.0 %collective-permute-done.6.got_b = f32[24,128]{1,0:T(8,128)S(1)} collective-permute-done((f32[24,128]{1,0:T(8,128)S(1)}, f32[24,128]{1,0:T(8,128)S(1)}, u32[]{:S(2)}, u32[]{:S(2)}) %collective-permute-start.6) | collective-permute-done | bytes 12320 | tf_op jit(solution)/shard_map/ppermute | solution.py:433
  14.1 1.0 %collective-permute-done.5.got_a = f32[40,128]{1,0:T(8,128)S(1)} collective-permute-done((f32[40,128]{1,0:T(8,128)S(1)}, f32[40,128]{1,0:T(8,128)S(1)}, u32[]{:S(2)}, u32[]{:S(2)}) %collective-permute-start.5) | collective-permute-done | bytes 20512 | tf_op jit(solution)/shard_map/ppermute | solution.py:433
  15.1 0.9 %finish_kernel.1 = (f32[19,4,16,128]{3,2,1,0:T(8,128)S(1)}, f32[19,16,128]{2,1,0:T(8,128)S(1)}, f32[19,4,16,128]{3,2,1,0:T(8,128)}, f32[19,16,128]{2,1,0:T(8,128)}) custom-call(f32[19,4,16,128]{3,2,1,0:T(8,128)S(1)} %get-tuple-element.39.room_in, f32[19,16,128]{2,1,0:T(8,128)S(1)} %get-tuple-element.40.plen_in, ...), custom_call_target="tpu_custom_call", output_to_operand_aliasing={{0}: (0, {}), {1}: (1, {})} | custom-call | flops 100000 | bytes 1000000 | tf_op jit(solution)/shard_map/finish_kernel/pallas_call | solution.py:514
  (2 shorter events, 0.1 us)
Async XLA Ops:
  1.8 8.8 %collective-permute-start.2 = (f32[8,1,640]{2,1,0:T(1,128)S(1)}, f32[8,1,640]{2,1,0:T(1,128)S(1)}, u32[]{:S(2)}, u32[]{:S(2)}) collective-permute-start(f32[8,1,640]{2,1,0:T(1,128)S(1)} %get-tuple-element.32), channel_id=1, source_target_pairs={{0,2},{1,3},{2,0},{3,1},{4,6},{5,7},{6,4},{7,5},{8,10},{9,11},{10,... | collective-permute-start | bytes 61448 | tf_op jit(solution)/shard_map/ppermute | solution.py:464
  6.3 5.0 %collective-permute-start.1 = (f32[104,128]{1,0:T(8,128)S(1)}, f32[104,128]{1,0:T(8,128)S(1)}, u32[]{:S(2)}, u32[]{:S(2)}) collective-permute-start(f32[104,128]{1,0:T(8,128)S(1)} %get-tuple-element.30), channel_id=1, source_target_pairs={{0,28},{4,8},{8,4},{12,16},{16,12},{20,24},{24,20},{28,0},{1,29},{... | collective-permute-start | bytes 159752 | tf_op jit(solution)/shard_map/ppermute | solution.py:422
  8.0 3.3 %collective-permute-start = (f32[112,128]{1,0:T(8,128)S(1)}, f32[112,128]{1,0:T(8,128)S(1)}, u32[]{:S(2)}, u32[]{:S(2)}) collective-permute-start(f32[112,128]{1,0:T(8,128)S(1)} %get-tuple-element.29), channel_id=1, source_target_pairs={{0,4},{4,0},{8,12},{12,8},{16,20},{20,16},{24,28},{28,24},{1,5},{5... | collective-permute-start | bytes 172040 | tf_op jit(solution)/shard_map/ppermute | solution.py:422
  8.1 4.9 %collective-permute-start.4 = (f32[104,128]{1,0:T(8,128)S(1)}, f32[104,128]{1,0:T(8,128)S(1)}, u32[]{:S(2)}, u32[]{:S(2)}) collective-permute-start(f32[104,128]{1,0:T(8,128)S(1)} %get-tuple-element.37), channel_id=1, source_target_pairs={{0,4},{1,2},{2,1},{3,7},{4,0},{5,6},{6,5},{7,3},{8,12},{9,10},{10,... | collective-permute-start | bytes 159752 | tf_op jit(solution)/shard_map/ppermute | solution.py:433
  8.6 4.4 %collective-permute-start.3 = (f32[120,128]{1,0:T(8,128)S(1)}, f32[120,128]{1,0:T(8,128)S(1)}, u32[]{:S(2)}, u32[]{:S(2)}) collective-permute-start(f32[120,128]{1,0:T(8,128)S(1)} %get-tuple-element.36), channel_id=1, source_target_pairs={{0,1},{1,0},{2,3},{3,2},{4,5},{5,4},{6,7},{7,6},{8,9},{9,8},{10,11... | collective-permute-start | bytes 184328 | tf_op jit(solution)/shard_map/ppermute | solution.py:433
  11.3 3.8 %collective-permute-start.5 = (f32[40,128]{1,0:T(8,128)S(1)}, f32[40,128]{1,0:T(8,128)S(1)}, u32[]{:S(2)}, u32[]{:S(2)}) collective-permute-start(f32[40,128]{1,0:T(8,128)S(1)} %get-tuple-element.41), channel_id=1, source_target_pairs={{0,1},{1,0},{2,3},{3,2},{4,5},{5,4},{6,7},{7,6},{8,9},{9,8},{10,11... | collective-permute-start | bytes 61448 | tf_op jit(solution)/shard_map/ppermute | solution.py:433
  12.9 1.2 %collective-permute-start.6 = (f32[24,128]{1,0:T(8,128)S(1)}, f32[24,128]{1,0:T(8,128)S(1)}, u32[]{:S(2)}, u32[]{:S(2)}) collective-permute-start(f32[24,128]{1,0:T(8,128)S(1)} %get-tuple-element.42), channel_id=1, source_target_pairs={{0,4},{1,2},{2,1},{3,7},{4,0},{5,6},{6,5},{7,3},{8,12},{9,10},{10,... | collective-permute-start | bytes 36872 | tf_op jit(solution)/shard_map/ppermute | solution.py:433

commit v10 on v9

--- a/solution.py
+++ b/solution.py
@@ -183,7 +183,8 @@
     return sums
 
 
-def local_kernel(sizes, room_post, plen_post, cell_in, owner_in, room_part, plen_part, places, cells, owners, sems):
+def local_kernel(sizes, room_post, plen_post, corner, cell_in, owner_in, room_part, plen_part, places, cells, owners, sems):
+    del corner
     ca, cs, blocks, n_span, per_brick = sizes
     rows = blocks * cs
     copies = [pltpu.make_async_copy(src, dst, sems.at[i]) for i, (src, dst) in enumerate(
@@ -248,8 +249,7 @@
     return [q for q in (Y_UP if up else Y_DOWN) if VELOCITIES[q][0]], cs - 1 if up else 0
 
 
-def corner_kernel(sizes, relayed, got_a, got_b, got_jets, places, cross_a, cross_b):
-    del places
+def corner_kernel(sizes, relayed, got_a, got_b, got_jets, cross_a, cross_b):
     ca, cs, blocks, n_span, per_brick = sizes
     rows = blocks * cs
     even = lax.axis_index("aisle") % 2 == 0
@@ -478,25 +478,27 @@
         functools.partial(cross_kernel, sizes, relayed),
         [near((upto8(5 * (rows + ca) + (5 * CAP if relayed else 0)), LANES)), near((halo, LANES))],
         [VMEM] * 3,
+        flops=10**9,
     )(room_post, plen_post, jets[0])
     in_a = swap_span(cross_a, False)
     in_b = swap_span(cross_b, True)
 
+    last = upto8(rows + 2 + (5 * CAP if relayed else 0))
+    corner_a, corner_b = call(
+        functools.partial(corner_kernel, sizes, relayed),
+        [near((last, LANES)), near((last + 8, LANES))],
+        [VMEM] * 3,
+    )(got_a, got_b, got_jets)
+    last_a = swap_span(corner_a, False)
+    last_b = swap_span(corner_b, True)
+
     room_part, plen_part, places = call(
         functools.partial(local_kernel, sizes),
         [near(room_shape), near(plen_shape), near((n_span * CAP + 1, ca * cs, LANES))],
-        [VMEM, VMEM, HBM, HBM],
+        [VMEM, VMEM, VMEM, HBM, HBM],
         scratch=[numbers, numbers, pltpu.SemaphoreType.DMA((2,))],
         flops=10**9,
-    )(room_post, plen_post, tile_cell, tile_owner)
-
-    corner_a, corner_b = call(
-        functools.partial(corner_kernel, sizes, relayed),
-        [near((upto8(rows + 2 + (5 * CAP if relayed else 0)), LANES)), near((upto8(rows + 2), LANES))],
-        [VMEM] * 4,
-    )(got_a, got_b, got_jets, places)
-    last_a = swap_span(corner_a, False)
-    last_b = swap_span(corner_b, True)
+    )(room_post, plen_post, corner_a, tile_cell, tile_owner)
 
     room_part, plen_part, inflow = call(
         functools.partial(aisle_kernel, sizes, relayed),

time: 16.2 us -> 16.2 us (level)
    ppermute x2, waiting for transfers between devices: 0.6 us -> 1.48 us  [swap_aisle(): return lax.ppermute(value, 'aisle', pairs)]
    ppermute x4, waiting for transfers between devices: 2.07 us -> 1.2 us  [swap_span(): return lax.ppermute(value, ('aisle', 'span'), pairs)]
  transfers between devices with their start and end apart: 7 -> 7, of which waited for: 3 -> 2; matrix products, arithmetic and copies ran while one was open for 0% -> 0% of each run, Pallas kernels for 9% -> 9%
where the time goes in v10:
time: 16.2 us; the launch traced here: 16.1 us
  starting transfers between devices  9.14 us (56%)
  Pallas kernels  3.55 us (22%)
  waiting for transfers between devices  2.67 us (16%)
  between operations  0.7 us (4%)
    ppermute x1, starting transfers between devices, shards(): got_jets = lax.ppermute(jets[1], 'span', [(i, i ^ 2) for i in range(4)])  4.1 us
    ppermute x4, starting transfers between devices, swap_span(): return lax.ppermute(value, ('aisle', 'span'), pairs)  3.36 us
    ppermute x2, starting transfers between devices, swap_aisle(): return lax.ppermute(value, 'aisle', pairs)  1.67 us
    ppermute x2, waiting for transfers between devices, swap_aisle(): return lax.ppermute(value, 'aisle', pairs)  1.48 us
    pallas_call x1, Pallas kernels, shards(): call(functools.partial(plenum_kernel, sizes, relayed), [near(room_shape),...  1.21 us
    ppermute x4, waiting for transfers between devices, swap_span(): return lax.ppermute(value, ('aisle', 'span'), pairs)  1.2 us
    pallas_call x1, Pallas kernels, shards(): call(functools.partial(finish_kernel, sizes, relayed), [near(room_shape),...  0.91 us
    pallas_call x1, Pallas kernels, shards(): call(functools.partial(local_kernel, sizes), [near(room_shape), near(plen...  0.86 us
  transfers between devices with their start and end apart: 7, of which 2 were waited for; matrix products, arithmetic and copies ran while one was open for 0% of the time, Pallas kernels for 9%

profile of v10, /device:TPU:0, one launch (start us, length us, event | category | flops | bytes accessed | tf_op | source)
XLA Modules:
  0.0 16.1 jit_solution(2248991043560729126)
XLA Ops:
  0.6 1.2 %plenum_kernel.1 = (f32[19,4,16,128]{3,2,1,0:T(8,128)S(1)}, f32[19,16,128]{2,1,0:T(8,128)S(1)}, f32[8,1,640]{2,1,0:T(1,128)S(1)}, f32[8,1,640]{2,1,0:T(1,128)S(1)}) custom-call(f32[19,4,16,128]{3,2,1,0:T(8,128)} %bitcast.13, f32[19,16,128]{2,1,0:T(8,128)} %bitcast.14, s32[32]{0:T(128)} %cell_in.3, s32[32]{0:T(128)} %bitcast.15, s32[32]{0:T(128)} %class_in.1), custom_call_target="tpu_custom_call" | custom-call | flops 100000 | bytes 1000000 | tf_op jit(solution)/shard_map/plenum_kernel/pallas_call | solution.py:456
  1.8 4.1 %collective-permute-start.2 = (f32[8,1,640]{2,1,0:T(1,128)S(1)}, f32[8,1,640]{2,1,0:T(1,128)S(1)}, u32[]{:S(2)}, u32[]{:S(2)}) collective-permute-start(f32[8,1,640]{2,1,0:T(1,128)S(1)} %get-tuple-element.29), channel_id=1, source_target_pairs={{0,2},{1,3},{2,0},{3,1},{4,6},{5,7},{6,4},{7,5},{8,10},{9,11},{10,... | collective-permute-start | bytes 61448 | tf_op jit(solution)/shard_map/ppermute | solution.py:464
  5.9 0.3 %room_kernel.1 = (f32[19,4,16,128]{3,2,1,0:T(8,128)S(1)}, f32[112,128]{1,0:T(8,128)S(1)}, f32[104,128]{1,0:T(8,128)S(1)}) custom-call(f32[19,4,16,128]{3,2,1,0:T(8,128)S(1)} %get-tuple-element.24.room_near, f32[19,16,128]{2,1,0:T(8,128)S(1)} %get-tuple-element.25.plen_post), custom_call_target="tpu_custom_call" | custom-call | flops 100000 | bytes 1000000 | tf_op jit(solution)/shard_map/room_kernel/pallas_call | solution.py:468
  6.3 1.7 %collective-permute-start.1 = (f32[104,128]{1,0:T(8,128)S(1)}, f32[104,128]{1,0:T(8,128)S(1)}, u32[]{:S(2)}, u32[]{:S(2)}) collective-permute-start(f32[104,128]{1,0:T(8,128)S(1)} %get-tuple-element.28), channel_id=1, source_target_pairs={{0,28},{4,8},{8,4},{12,16},{16,12},{20,24},{24,20},{28,0},{1,29},{... | collective-permute-start | bytes 159752 | tf_op jit(solution)/shard_map/ppermute | solution.py:422
  8.0 0.0 collective-permute-start
  8.0 0.1 cross_kernel.1
  8.1 0.6 %collective-permute-start.4 = (f32[104,128]{1,0:T(8,128)S(1)}, f32[104,128]{1,0:T(8,128)S(1)}, u32[]{:S(2)}, u32[]{:S(2)}) collective-permute-start(f32[104,128]{1,0:T(8,128)S(1)} %get-tuple-element.38), channel_id=1, source_target_pairs={{0,4},{1,2},{2,1},{3,7},{4,0},{5,6},{6,5},{7,3},{8,12},{9,10},{10,... | collective-permute-start | bytes 159752 | tf_op jit(solution)/shard_map/ppermute | solution.py:433
  8.6 1.1 %collective-permute-start.3 = (f32[120,128]{1,0:T(8,128)S(1)}, f32[120,128]{1,0:T(8,128)S(1)}, u32[]{:S(2)}, u32[]{:S(2)}) collective-permute-start(f32[120,128]{1,0:T(8,128)S(1)} %get-tuple-element.37), channel_id=1, source_target_pairs={{0,1},{1,0},{2,3},{3,2},{4,5},{5,4},{6,7},{7,6},{8,9},{9,8},{10,11... | collective-permute-start | bytes 184328 | tf_op jit(solution)/shard_map/ppermute | solution.py:433
  9.8 0.0 collective-permute-done.2.got_jets
  9.8 1.5 %collective-permute-done.1.got_b = f32[104,128]{1,0:T(8,128)S(1)} collective-permute-done((f32[104,128]{1,0:T(8,128)S(1)}, f32[104,128]{1,0:T(8,128)S(1)}, u32[]{:S(2)}, u32[]{:S(2)}) %collective-permute-start.1) | collective-permute-done | bytes 53280 | tf_op jit(solution)/shard_map/ppermute | solution.py:422
  11.3 0.0 collective-permute-done.got_a
  11.3 1.6 %collective-permute-start.5 = (f32[40,128]{1,0:T(8,128)S(1)}, f32[40,128]{1,0:T(8,128)S(1)}, u32[]{:S(2)}, u32[]{:S(2)}) collective-permute-start(f32[40,128]{1,0:T(8,128)S(1)} %get-tuple-element.30.corner), channel_id=1, source_target_pairs={{0,1},{1,0},{2,3},{3,2},{4,5},{5,4},{6,7},{7,6},{8,9},{9,8},{10,11... | collective-permute-start | bytes 61448 | tf_op jit(solution)/shard_map/ppermute | solution.py:433
  12.9 0.0 collective-permute-start.6
  12.9 0.9 %local_kernel.1 = (f32[19,4,16,128]{3,2,1,0:T(8,128)S(1)}, f32[19,16,128]{2,1,0:T(8,128)S(1)}, f32[17,16,128]{2,1,0:T(8,128)S(1)}) custom-call(f32[19,4,16,128]{3,2,1,0:T(8,128)S(1)} %get-tuple-element.26.room_post, f32[19,16,128]{2,1,0:T(8,128)S(1)} %get-tuple-element.25.plen_post, f32[40,128]{1,0:T(8,128)S(1)} %get-tuple-element.30.corner, s32[32]{0:T(128)} %cell_in.3, ...), custom_call_target="tpu_custom_call" | custom-call | flops 1000000000 | bytes 1000000 | tf_op jit(solution)/shard_map/local_kernel/pallas_call | solution.py:495
  13.9 0.0 collective-permute-done.4.got_b
  13.9 0.0 collective-permute-done.3.got_a
  13.9 0.1 enter_kernel.1
  14.0 1.2 %collective-permute-done.5.got_a = f32[40,128]{1,0:T(8,128)S(1)} collective-permute-done((f32[40,128]{1,0:T(8,128)S(1)}, f32[40,128]{1,0:T(8,128)S(1)}, u32[]{:S(2)}, u32[]{:S(2)}) %collective-permute-start.5) | collective-permute-done | bytes 20512 | tf_op jit(solution)/shard_map/ppermute | solution.py:433
  15.1 0.0 collective-permute-done.6.got_b
  15.2 0.9 %finish_kernel.1 = (f32[19,4,16,128]{3,2,1,0:T(8,128)S(1)}, f32[19,16,128]{2,1,0:T(8,128)S(1)}, f32[19,4,16,128]{3,2,1,0:T(8,128)}, f32[19,16,128]{2,1,0:T(8,128)}) custom-call(f32[19,4,16,128]{3,2,1,0:T(8,128)S(1)} %get-tuple-element.40.room_in, f32[19,16,128]{2,1,0:T(8,128)S(1)} %get-tuple-element.41.plen_in, ...), custom_call_target="tpu_custom_call", output_to_operand_aliasing={{0}: (0, {}), {1}: (1, {})} | custom-call | flops 100000 | bytes 1000000 | tf_op jit(solution)/shard_map/finish_kernel/pallas_call | solution.py:516
  (2 shorter events, 0.1 us)
Async XLA Ops:
  1.8 7.9 %collective-permute-start.2 = (f32[8,1,640]{2,1,0:T(1,128)S(1)}, f32[8,1,640]{2,1,0:T(1,128)S(1)}, u32[]{:S(2)}, u32[]{:S(2)}) collective-permute-start(f32[8,1,640]{2,1,0:T(1,128)S(1)} %get-tuple-element.29), channel_id=1, source_target_pairs={{0,2},{1,3},{2,0},{3,1},{4,6},{5,7},{6,4},{7,5},{8,10},{9,11},{10,... | collective-permute-start | bytes 61448 | tf_op jit(solution)/shard_map/ppermute | solution.py:464
  6.3 5.0 %collective-permute-start.1 = (f32[104,128]{1,0:T(8,128)S(1)}, f32[104,128]{1,0:T(8,128)S(1)}, u32[]{:S(2)}, u32[]{:S(2)}) collective-permute-start(f32[104,128]{1,0:T(8,128)S(1)} %get-tuple-element.28), channel_id=1, source_target_pairs={{0,28},{4,8},{8,4},{12,16},{16,12},{20,24},{24,20},{28,0},{1,29},{... | collective-permute-start | bytes 159752 | tf_op jit(solution)/shard_map/ppermute | solution.py:422
  8.0 3.3 %collective-permute-start = (f32[112,128]{1,0:T(8,128)S(1)}, f32[112,128]{1,0:T(8,128)S(1)}, u32[]{:S(2)}, u32[]{:S(2)}) collective-permute-start(f32[112,128]{1,0:T(8,128)S(1)} %get-tuple-element.27), channel_id=1, source_target_pairs={{0,4},{4,0},{8,12},{12,8},{16,20},{20,16},{24,28},{28,24},{1,5},{5... | collective-permute-start | bytes 172040 | tf_op jit(solution)/shard_map/ppermute | solution.py:422
  8.1 5.8 %collective-permute-start.4 = (f32[104,128]{1,0:T(8,128)S(1)}, f32[104,128]{1,0:T(8,128)S(1)}, u32[]{:S(2)}, u32[]{:S(2)}) collective-permute-start(f32[104,128]{1,0:T(8,128)S(1)} %get-tuple-element.38), channel_id=1, source_target_pairs={{0,4},{1,2},{2,1},{3,7},{4,0},{5,6},{6,5},{7,3},{8,12},{9,10},{10,... | collective-permute-start | bytes 159752 | tf_op jit(solution)/shard_map/ppermute | solution.py:433
  8.6 5.2 %collective-permute-start.3 = (f32[120,128]{1,0:T(8,128)S(1)}, f32[120,128]{1,0:T(8,128)S(1)}, u32[]{:S(2)}, u32[]{:S(2)}) collective-permute-start(f32[120,128]{1,0:T(8,128)S(1)} %get-tuple-element.37), channel_id=1, source_target_pairs={{0,1},{1,0},{2,3},{3,2},{4,5},{5,4},{6,7},{7,6},{8,9},{9,8},{10,11... | collective-permute-start | bytes 184328 | tf_op jit(solution)/shard_map/ppermute | solution.py:433
  11.3 3.8 %collective-permute-start.5 = (f32[40,128]{1,0:T(8,128)S(1)}, f32[40,128]{1,0:T(8,128)S(1)}, u32[]{:S(2)}, u32[]{:S(2)}) collective-permute-start(f32[40,128]{1,0:T(8,128)S(1)} %get-tuple-element.30.corner), channel_id=1, source_target_pairs={{0,1},{1,0},{2,3},{3,2},{4,5},{5,4},{6,7},{7,6},{8,9},{9,8},{10,11... | collective-permute-start | bytes 61448 | tf_op jit(solution)/shard_map/ppermute | solution.py:433
  12.9 2.2 %collective-permute-start.6 = (f32[48,128]{1,0:T(8,128)S(1)}, f32[48,128]{1,0:T(8,128)S(1)}, u32[]{:S(2)}, u32[]{:S(2)}) collective-permute-start(f32[48,128]{1,0:T(8,128)S(1)} %get-tuple-element.42), channel_id=1, source_target_pairs={{0,4},{1,2},{2,1},{3,7},{4,0},{5,6},{6,5},{7,3},{8,12},{9,10},{10,... | collective-permute-start | bytes 73736 | tf_op jit(solution)/shard_map/ppermute | solution.py:433

commit v11 on v7

--- a/solution.py
+++ b/solution.py
@@ -102,56 +102,23 @@
     return start
 
 
-def plenum_kernel(sizes, relayed, room_in, plen_in, cell_in, owner_in, class_in, room_near, plen_post, *rest):
+def collide_kernel(sizes, room_in, plen_in, room_post, plen_post, swap_a, swap_b, room_buf, plen_buf, sems):
     ca, cs, blocks, n_span, per_brick = sizes
-    jets = rest[:-7]
-    columns, dealt, plen_buf, cells, owners, classes, sems = rest[-7:]
+    rows = blocks * cs
     copies = [pltpu.make_async_copy(src, dst, sems.at[i]) for i, (src, dst) in enumerate(
-        ((plen_in, plen_buf), (cell_in, cells), (owner_in, owners), (class_in, classes), (room_in, room_near)))]
+        ((plen_in, plen_buf), (room_in, room_buf)))]
     for copy in copies:
         copy.start()
-    dealt[...] = jnp.zeros_like(dealt)
     copies[0].wait()
     for r in range(0, ca * cs, 8):
         post = collide([plen_buf[q, r : r + 8] for q in range(19)])
         for q in range(19):
             plen_post[q, r : r + 8] = post[q]
-        for k, q in enumerate(UPWARD):
-            for y in range(8):
-                columns[r + y, :, k * LANES : (k + 1) * LANES] = post[q][y : y + 1]
-    for copy in copies[1:4]:
-        copy.wait()
-    here = lax.axis_index("span")
-    first = here * per_brick
-
-    def send_jet(i, carry):
-        t = first + i
-        owner = owners[t]
-        share = 0.15 * (classes[t].astype(F32) + 1.0)
-        same = lambda j, n: n + (owners[first + j] == owner).astype(jnp.int32)
-        slot = repeat(i, same, 0) if relayed else lax.fori_loop(0, i, same, 0)
-        to = (owner ^ here if relayed else owner) * CAP + slot
-        dealt[to] = share * columns[cells[t]]
-        return carry
-
-    if relayed:
-        for i in range(per_brick):
-            send_jet(i, 0)
-    else:
-        lax.fori_loop(0, per_brick, send_jet, 0)
-    for part, jet in enumerate(jets):
-        many = jet.shape[0]
-        jet[...] = dealt[part * many : (part + 1) * many]
-    copies[4].wait()
-
-
-def room_kernel(sizes, room_near, plen_post, room_post, swap_a, swap_b):
-    ca, cs, blocks, n_span, per_brick = sizes
-    rows = blocks * cs
+    copies[1].wait()
 
     def plane(x, carry):
         for r in range(0, rows, 8):
-            post = collide([room_near[q, x, r : r + 8] for q in range(19)])
+            post = collide([room_buf[q, x, r : r + 8] for q in range(19)])
             for q in range(19):
                 room_post[q, x, r : r + 8] = post[q]
         return carry
@@ -180,14 +147,21 @@
     return sums
 
 
-def local_kernel(sizes, room_post, plen_post, cell_in, owner_in, room_part, plen_part, span_up, span_down, places,
-                 cells, owners, sems):
+def local_kernel(sizes, direct, room_post, plen_post, cell_in, owner_in, class_in, room_part, plen_part, span_up, span_down,
+                 places, *rest):
     ca, cs, blocks, n_span, per_brick = sizes
     rows = blocks * cs
+    jets = rest[:-6]
+    columns, dealt, cells, owners, classes, sems = rest[-6:]
     copies = [pltpu.make_async_copy(src, dst, sems.at[i]) for i, (src, dst) in enumerate(
-        ((cell_in, cells), (owner_in, owners)))]
+        ((cell_in, cells), (owner_in, owners), (class_in, classes)))]
     for copy in copies:
         copy.start()
+    dealt[...] = jnp.zeros_like(dealt)
+    for k, q in enumerate(UPWARD):
+        post = plen_post[q]
+        for cell in range(ca * cs):
+            columns[cell, :, k * LANES : (k + 1) * LANES] = post[cell : cell + 1]
     group = lax.broadcasted_iota(jnp.int32, (rows, LANES), 0) % cs
     for q in range(19):
         cx, cy, cz = VELOCITIES[q]
@@ -219,6 +193,27 @@
     row = lax.broadcasted_iota(jnp.int32, (ca * cs, LANES), 0)
     for copy in copies:
         copy.wait()
+    first = here * per_brick
+
+    def send_jet(i, carry):
+        t = first + i
+        owner = owners[t]
+        share = 0.15 * (classes[t].astype(F32) + 1.0)
+        same = lambda j, n: n + (owners[first + j] == owner).astype(jnp.int32)
+        slot = repeat(i, same, 0) if direct else lax.fori_loop(0, i, same, 0)
+        to = (owner ^ here if direct else owner) * CAP + slot
+        dealt[to] = share * columns[cells[t]]
+        return carry
+
+    if direct:
+        for i in range(per_brick):
+            send_jet(i, 0)
+    else:
+        lax.fori_loop(0, per_brick, send_jet, 0)
+    start = 0
+    for jet in jets:
+        jet[...] = dealt[start : start + jet.shape[0]]
+        start = start + jet.shape[0]
 
     def brick(b, carry):
         def place(i, slot):
@@ -233,11 +228,11 @@
     repeat(n_span, brick, 0)
 
 
-def pack_kernel(sizes, relayed, got_a, got_b, span_up, span_down, *rest):
+def pack_kernel(sizes, direct, got_a, got_b, span_up, span_down, *rest):
     ca, cs, blocks, n_span, per_brick = sizes
     rows = blocks * cs
-    if relayed:
-        jets, got_jets, cross_a, cross_b = rest
+    if direct:
+        jets, cross_a, cross_b = rest
     else:
         cross_a, cross_b = rest
     even = lax.axis_index("aisle") % 2 == 0
@@ -284,15 +279,14 @@
                 def _():
                     cross_b[to : to + 1] = came
 
-    if relayed:
-        for b, source in enumerate((jets, got_jets)):
-            for s in range(CAP):
-                for k in range(5):
-                    to = halo + (b * CAP + s) * 5 + k
-                    cross_a[to : to + 1] = source[CAP + s, :, k * LANES : (k + 1) * LANES]
-
-
-def aisle_kernel(sizes, relayed, room_in, plen_in, got_a, got_b, jets, got_jets, places, room, plen, inflow):
+    if direct:
+        for s in range(CAP):
+            for k in range(5):
+                to = 5 * (rows + cs) + s * 5 + k
+                cross_a[to : to + 1] = jets[CAP + s, :, k * LANES : (k + 1) * LANES]
+
+
+def aisle_kernel(sizes, direct, room_in, plen_in, got_a, got_b, jets, places, room, plen, inflow):
     ca, cs, blocks, n_span, per_brick = sizes
     rows = blocks * cs
     even = lax.axis_index("aisle") % 2 == 0
@@ -321,27 +315,27 @@
     def reader(source, b):
         return lambda s, k: source[b * CAP + s, :, k * LANES : (k + 1) * LANES]
 
-    if relayed:
+    if direct:
         put(jet_sums(lambda k: jnp.zeros((ca * cs, LANES), F32), places,
-                     [(here, reader(jets, 0)), (here ^ 2, reader(got_jets, 0))]))
+                     [(here, reader(jets, 0))]))
     else:
         inflow[...] = jnp.zeros_like(inflow)
 
         def add_brick(b, carry):
-            put(jet_sums(lambda k: inflow[k], places, [(b, reader(got_jets, b))]))
+            put(jet_sums(lambda k: inflow[k], places, [(b, reader(jets, b))]))
             return carry
 
         lax.fori_loop(0, n_span, add_brick, 0)
 
 
-def finish_kernel(sizes, relayed, room_in, plen_in, got_a, got_b, places, inflow, room, plen, room_out, plen_out, sems):
+def finish_kernel(sizes, direct, room_in, plen_in, got_a, got_b, places, inflow, *rest):
+    *got_jets, room, plen, room_out, plen_out, sems = rest
     ca, cs, blocks, n_span, per_brick = sizes
     rows = blocks * cs
     here = lax.axis_index("span")
     low = here % 2 == 0
-    halo = 5 * (rows + cs)
-    halo = halo + -halo % 8
     group = lax.broadcasted_iota(jnp.int32, (rows, LANES), 0) % cs
+
     def enter(got, up):
         planes, y = (Y_UP, 0) if up else (Y_DOWN, cs - 1)
         for k, q in enumerate(planes):
@@ -370,11 +364,11 @@
     plen_copy = pltpu.make_async_copy(plen, plen_out, sems.at[0])
     plen_copy.start()
     bricks = []
-    if relayed:
-        def reader(b):
-            return lambda s, k: got_a[halo + (b * CAP + s) * 5 + k : halo + (b * CAP + s) * 5 + k + 1]
-
-        bricks = [(here ^ 1, reader(0)), (here ^ 3, reader(1))]
+    if direct:
+        start = 5 * (rows + cs)
+        bricks = [(here ^ 1, lambda s, k: got_a[start + s * 5 + k : start + s * 5 + k + 1])]
+        for apart, got in zip((2, 3), got_jets):
+            bricks.append((here ^ apart, lambda s, k, got=got: got[s, :, k * LANES : (k + 1) * LANES]))
     sums = jet_sums(lambda k: inflow[k], places, bricks)
     for k, q in enumerate(UPWARD):
         for x in range(ca):
@@ -388,6 +382,7 @@
 def call(kernel, outs, in_specs, out_specs=None, scratch=(), aliases={}, flops=100_000, moved=1_000_000):
     return pl.pallas_call(
         kernel,
+        name=kernel.func.__name__,
         out_shape=outs,
         in_specs=in_specs,
         out_specs=[VMEM] * len(outs) if out_specs is None else out_specs,
@@ -423,7 +418,7 @@
     rows = blocks * cs
     tiles = tile_cell.shape[0]
     sizes = (ca, cs, blocks, n_span, tiles // n_span)
-    relayed = n_span == 4
+    direct = n_span == 4
     near = lambda shape: pltpu.VMEM(shape, F32)
     far = lambda value: pltpu.with_memory_space_constraint(value, pltpu.HBM)
     room_shape, plen_shape = (19, ca, rows, LANES), (19, ca * cs, LANES)
@@ -434,62 +429,58 @@
     tile_cell, tile_owner, tile_class = far(tile_cell), far(tile_owner.reshape(tiles)), far(tile_class)
     numbers = pltpu.SMEM((tiles,), jnp.int32)
 
-    jets_shape = ((2 if relayed else n_span) * CAP, 1, 5 * hp)
-    room_near, plen_post, *jets = call(
-        functools.partial(plenum_kernel, sizes, relayed),
-        [near(room_shape), near(plen_shape)] + [near(jets_shape)] * (2 if relayed else 1),
-        [HBM] * 5,
-        scratch=[pltpu.VMEM((ca * cs, 1, 5 * hp), F32), near((n_span * CAP, 1, 5 * hp)), near(plen_shape), numbers, numbers, numbers,
-                 pltpu.SemaphoreType.DMA((5,))],
-    )(room, plen, tile_cell, tile_owner, tile_class)
-    if relayed:
-        got_jets = lax.ppermute(jets[1], "span", [(i, i ^ 2) for i in range(4)])
-    else:
-        got_jets = lax.all_to_all(jets[0], "span", 0, 0, tiled=True)
-
-    room_post, swap_a, swap_b = call(
-        functools.partial(room_kernel, sizes),
-        [near(room_shape), near((halo + 8, LANES)), near((halo, LANES))],
-        [VMEM] * 2,
-    )(room_near, plen_post)
+    jet_shapes = [(count * CAP, 1, 5 * hp) for count in ((2, 1, 1) if direct else (n_span,))]
+    room_post, plen_post, swap_a, swap_b = call(
+        functools.partial(collide_kernel, sizes),
+        [near(room_shape), near(plen_shape), near((halo + 8, LANES)), near((halo, LANES))],
+        [HBM] * 2,
+        scratch=[near(room_shape), near(plen_shape), pltpu.SemaphoreType.DMA((2,))],
+    )(room, plen)
     got_b = swap_aisle(swap_b, True)
     got_a = swap_aisle(swap_a, False)
 
-    room_part, plen_part, span_up, span_down, places = call(
-        functools.partial(local_kernel, sizes),
+    room_part, plen_part, span_up, span_down, places, *jets = call(
+        functools.partial(local_kernel, sizes, direct),
         [near(room_shape), near(plen_shape), near((halo, LANES)), near((halo, LANES)),
-         near((n_span * CAP + 1, ca * cs, LANES))],
-        [VMEM, VMEM, HBM, HBM],
-        scratch=[numbers, numbers, pltpu.SemaphoreType.DMA((2,))],
+         near((n_span * CAP + 1, ca * cs, LANES))] + [near(shape) for shape in jet_shapes],
+        [VMEM, VMEM, HBM, HBM, HBM],
+        scratch=[near((ca * cs, 1, 5 * hp)), near((n_span * CAP, 1, 5 * hp)), numbers, numbers, numbers,
+                 pltpu.SemaphoreType.DMA((3,))],
         flops=10**9,
-    )(room_post, plen_post, tile_cell, tile_owner)
-
-    cross_shape = (halo + 2 * CAP * 5, LANES) if relayed else (halo, LANES)
+    )(room_post, plen_post, tile_cell, tile_owner, tile_class)
+    if direct:
+        got_jets = [lax.ppermute(jets[apart - 1], "span", [(i, i ^ apart) for i in range(4)]) for apart in (2, 3)]
+    else:
+        jets = [lax.all_to_all(jets[0], "span", 0, 0, tiled=True)]
+        got_jets = []
+
+    upto8 = lambda count: count + -count % 8
+    cross_shape = (upto8(5 * (rows + cs) + 5 * CAP), LANES) if direct else (halo, LANES)
     cross_a, cross_b = call(
-        functools.partial(pack_kernel, sizes, relayed),
-        [near(cross_shape), near((halo, LANES))],
-        [VMEM] * (6 if relayed else 4),
-    )(got_a, got_b, span_up, span_down, *((jets[0], got_jets) if relayed else ()))
+        functools.partial(pack_kernel, sizes, direct),
+        [near(cross_shape), near((cross_shape[0] + 8, LANES))],
+        [VMEM] * (5 if direct else 4),
+    )(got_a, got_b, span_up, span_down, *(jets[:1] if direct else ()))
 
     in_b = swap_span(cross_b, True)
     in_a = swap_span(cross_a, False)
     room_part, plen_part, inflow = call(
-        functools.partial(aisle_kernel, sizes, relayed),
+        functools.partial(aisle_kernel, sizes, direct),
         [near(room_shape), near(plen_shape), near((5, ca * cs, LANES))],
-        [VMEM] * 7,
+        [VMEM] * 6,
         aliases={0: 0, 1: 1},
         flops=10**9,
-    )(room_part, plen_part, got_a, got_b, jets[0], got_jets, places)
+    )(room_part, plen_part, got_a, got_b, jets[0], places)
 
     _, _, room_next, plenum_next = call(
-        functools.partial(finish_kernel, sizes, relayed),
+        functools.partial(finish_kernel, sizes, direct),
         [near(room_shape), near(plen_shape), jax.ShapeDtypeStruct(room_shape, F32),
          jax.ShapeDtypeStruct(plen_shape, F32)],
-        [VMEM] * 6,
+        [VMEM] * (6 + len(got_jets)),
         out_specs=[VMEM, VMEM, HBM, HBM],
         scratch=[pltpu.SemaphoreType.DMA((2,))],
         aliases={0: 0, 1: 1},
-    )(room_part, plen_part, in_a, in_b, places, inflow)
+    )(room_part, plen_part, in_a, in_b, places, inflow, *got_jets)
     room_next = room_next.reshape(19, ca, blocks, cs, LANES).transpose(0, 1, 3, 2, 4).reshape(room_pops.shape)
     return room_next, plenum_next.reshape(plenum_pops.shape)
 

time: 17.2 us -> 16 us (0.930)
  waiting for transfers between devices: 5.53 us -> 4.07 us
  starting transfers between devices: 7.48 us -> 7.71 us
    ppermute x1 -> x2, waiting for transfers between devices: 0.01 us -> 3.84 us  [shards(): lax.ppermute(jets[apart - 1], 'span', [(i, i ^ apart) for i in range(4)])]
    ppermute x2, waiting for transfers between devices: 3 us -> 0.22 us  [swap_span(): return lax.ppermute(value, ('aisle', 'span'), pairs)]
    ppermute x2, waiting for transfers between devices: 2.53 us -> 0.01 us  [swap_aisle(): return lax.ppermute(value, 'aisle', pairs)]
    ppermute x2, starting transfers between devices: 1.67 us -> 3.4 us  [swap_aisle(): return lax.ppermute(value, 'aisle', pairs)]
    ppermute x2, starting transfers between devices: 1.71 us -> 0.3 us  [swap_span(): return lax.ppermute(value, ('aisle', 'span'), pairs)]
    ppermute x1 -> x2, starting transfers between devices: 4.1 us -> 4 us  [shards(): lax.ppermute(jets[apart - 1], 'span', [(i, i ^ apart) for i in range(4)])]
    pallas_call x6 -> x5, Pallas kernels: 3.32 us -> 3.38 us  [the longest x1 1.52 us: shards(): call(functools.partial(collide_kernel, sizes), [near(room_shape), near(pl...]
  transfers between devices with their start and end apart: 5 -> 6, of which waited for: 2 -> 3; matrix products, arithmetic and copies ran while one was open for 0% -> 0% of each run, Pallas kernels for 7% -> 6%
where the time goes in v11:
time: 16 us; the launch traced here: 15.8 us
  starting transfers between devices  7.71 us (48%)
  waiting for transfers between devices  4.07 us (25%)
  Pallas kernels  3.38 us (21%)
  between operations  0.66 us (4%)
    ppermute x2, starting transfers between devices, shards(): lax.ppermute(jets[apart - 1], 'span', [(i, i ^ apart) for i in range(4)])  4 us
    ppermute x2, waiting for transfers between devices, shards(): lax.ppermute(jets[apart - 1], 'span', [(i, i ^ apart) for i in range(4)])  3.84 us
    ppermute x2, starting transfers between devices, swap_aisle(): return lax.ppermute(value, 'aisle', pairs)  3.4 us
    pallas_call x1, Pallas kernels, shards(): call(functools.partial(collide_kernel, sizes), [near(room_shape), near(pl...  1.52 us
    pallas_call x1, Pallas kernels, shards(): call(functools.partial(finish_kernel, sizes, direct), [near(room_shape),...  0.93 us
    pallas_call x1, Pallas kernels, shards(): call(functools.partial(local_kernel, sizes, direct), [near(room_shape), n...  0.86 us
  transfers between devices with their start and end apart: 6, of which 3 were waited for; matrix products, arithmetic and copies ran while one was open for 0% of the time, Pallas kernels for 6%

profile of v11, /device:TPU:0, one launch (start us, length us, event | category | flops | bytes accessed | tf_op | source)
XLA Modules:
  0.0 15.8 jit_solution(11124120424040362447)
XLA Ops:
  0.6 1.5 %collide_kernel.1 = (f32[19,4,16,128]{3,2,1,0:T(8,128)S(1)}, f32[19,16,128]{2,1,0:T(8,128)S(1)}, f32[112,128]{1,0:T(8,128)S(1)}, f32[104,128]{1,0:T(8,128)S(1)}) custom-call(f32[19,4,16,128]{3,2,1,0:T(8,128)} %bitcast.13, f32[19,16,128]{2,1,0:T(8,128)} %bitcast.14), custom_call_target="tpu_custom_call" | custom-call | flops 100000 | bytes 1000000 | tf_op jit(solution)/shard_map/collide_kernel/pallas_call | solution.py:433
  2.2 3.4 %collective-permute-start.1 = (f32[104,128]{1,0:T(8,128)S(1)}, f32[104,128]{1,0:T(8,128)S(1)}, u32[]{:S(2)}, u32[]{:S(2)}) collective-permute-start(f32[104,128]{1,0:T(8,128)S(1)} %get-tuple-element.26), channel_id=1, source_target_pairs={{0,28},{4,8},{8,4},{12,16},{16,12},{20,24},{24,20},{28,0},{1,29},{... | collective-permute-start | bytes 159752 | tf_op jit(solution)/shard_map/ppermute | solution.py:399
  5.6 0.0 collective-permute-start
  5.6 0.9 %local_kernel.1 = (f32[19,4,16,128]{3,2,1,0:T(8,128)S(1)}, f32[19,16,128]{2,1,0:T(8,128)S(1)}, f32[104,128]{1,0:T(8,128)S(1)}, f32[104,128]{1,0:T(8,128)S(1)}, f...) custom-call(f32[19,4,16,128]{3,2,1,0:T(8,128)S(1)} %get-tuple-element, ...), custom_call_target="tpu_custom_call" | custom-call | flops 1000000000 | bytes 1000000 | tf_op jit(solution)/shard_map/local_kernel/pallas_call | solution.py:442
  6.4 2.7 %collective-permute-start.4 = (f32[4,1,640]{2,1,0:T(1,128)S(1)}, f32[4,1,640]{2,1,0:T(1,128)S(1)}, u32[]{:S(2)}, u32[]{:S(2)}) collective-permute-start(f32[4,1,640]{2,1,0:T(1,128)S(1)} %get-tuple-element.36), channel_id=1, source_target_pairs={{0,2},{1,3},{2,0},{3,1},{4,6},{5,7},{6,4},{7,5},{8,10},{9,11},{10,... | collective-permute-start | bytes 30728 | tf_op jit(solution)/shard_map/ppermute | solution.py:452
  9.1 1.3 %collective-permute-start.5 = (f32[4,1,640]{2,1,0:T(1,128)S(1)}, f32[4,1,640]{2,1,0:T(1,128)S(1)}, u32[]{:S(2)}, u32[]{:S(2)}) collective-permute-start(f32[4,1,640]{2,1,0:T(1,128)S(1)} %get-tuple-element.37), channel_id=1, source_target_pairs={{0,3},{1,2},{2,1},{3,0},{4,7},{5,6},{6,5},{7,4},{8,11},{9,10},{10,... | collective-permute-start | bytes 30728 | tf_op jit(solution)/shard_map/ppermute | solution.py:452
  10.4 0.0 collective-permute-done.1.got_b
  10.4 0.0 collective-permute-done.got_a
  10.5 0.3 %collective-permute-start.2 = (f32[120,128]{1,0:T(8,128)S(1)}, f32[120,128]{1,0:T(8,128)S(1)}, u32[]{:S(2)}, u32[]{:S(2)}) collective-permute-start(f32[120,128]{1,0:T(8,128)S(1)} %get-tuple-element.33), channel_id=1, source_target_pairs={{0,1},{1,0},{2,3},{3,2},{4,5},{5,4},{6,7},{7,6},{8,9},{9,8},{10,11... | collective-permute-start | bytes 184328 | tf_op jit(solution)/shard_map/ppermute | solution.py:410
  10.8 0.0 collective-permute-start.3
  10.8 0.2 %collective-permute-done.4.rest_0_ = f32[4,1,640]{2,1,0:T(1,128)S(1)} collective-permute-done((f32[4,1,640]{2,1,0:T(1,128)S(1)}, f32[4,1,640]{2,1,0:T(1,128)S(1)}, u32[]{:S(2)}, u32[]{:S(2)}) %collective-permute-start.4) | collective-permute-done | bytes 10272 | tf_op jit(solution)/shard_map/ppermute | solution.py:452
  11.1 3.6 %collective-permute-done.5.rest_1_ = f32[4,1,640]{2,1,0:T(1,128)S(1)} collective-permute-done((f32[4,1,640]{2,1,0:T(1,128)S(1)}, f32[4,1,640]{2,1,0:T(1,128)S(1)}, u32[]{:S(2)}, u32[]{:S(2)}) %collective-permute-start.5) | collective-permute-done | bytes 10272 | tf_op jit(solution)/shard_map/ppermute | solution.py:452
  14.7 0.2 %collective-permute-done.2.got_a = f32[120,128]{1,0:T(8,128)S(1)} collective-permute-done((f32[120,128]{1,0:T(8,128)S(1)}, f32[120,128]{1,0:T(8,128)S(1)}, u32[]{:S(2)}, u32[]{:S(2)}) %collective-permute-start.2) | collective-permute-done | bytes 61472 | tf_op jit(solution)/shard_map/ppermute | solution.py:410
  14.9 0.0 collective-permute-done.3.got_b
  14.9 0.9 %finish_kernel.1 = (f32[19,4,16,128]{3,2,1,0:T(8,128)S(1)}, f32[19,16,128]{2,1,0:T(8,128)S(1)}, f32[19,4,16,128]{3,2,1,0:T(8,128)}, f32[19,16,128]{2,1,0:T(8,128)}) custom-call(f32[19,4,16,128]{3,2,1,0:T(8,128)S(1)} %get-tuple-element.29.room_in, f32[19,16,128]{2,1,0:T(8,128)S(1)} %get-tuple-element.30.plen_in, ...), custom_call_target="tpu_custom_call", output_to_operand_aliasing={{0}: (0, {}), {1}: (1, {})} | custom-call | flops 100000 | bytes 1000000 | tf_op jit(solution)/shard_map/finish_kernel/pallas_call | solution.py:475
  (2 shorter events, 0.1 us)
Async XLA Ops:
  2.2 8.3 %collective-permute-start.1 = (f32[104,128]{1,0:T(8,128)S(1)}, f32[104,128]{1,0:T(8,128)S(1)}, u32[]{:S(2)}, u32[]{:S(2)}) collective-permute-start(f32[104,128]{1,0:T(8,128)S(1)} %get-tuple-element.26), channel_id=1, source_target_pairs={{0,28},{4,8},{8,4},{12,16},{16,12},{20,24},{24,20},{28,0},{1,29},{... | collective-permute-start | bytes 159752 | tf_op jit(solution)/shard_map/ppermute | solution.py:399
  5.6 4.9 %collective-permute-start = (f32[112,128]{1,0:T(8,128)S(1)}, f32[112,128]{1,0:T(8,128)S(1)}, u32[]{:S(2)}, u32[]{:S(2)}) collective-permute-start(f32[112,128]{1,0:T(8,128)S(1)} %get-tuple-element.25), channel_id=1, source_target_pairs={{0,4},{4,0},{8,12},{12,8},{16,20},{20,16},{24,28},{28,24},{1,5},{5... | collective-permute-start | bytes 172040 | tf_op jit(solution)/shard_map/ppermute | solution.py:399
  6.4 4.6 %collective-permute-start.4 = (f32[4,1,640]{2,1,0:T(1,128)S(1)}, f32[4,1,640]{2,1,0:T(1,128)S(1)}, u32[]{:S(2)}, u32[]{:S(2)}) collective-permute-start(f32[4,1,640]{2,1,0:T(1,128)S(1)} %get-tuple-element.36), channel_id=1, source_target_pairs={{0,2},{1,3},{2,0},{3,1},{4,6},{5,7},{6,4},{7,5},{8,10},{9,11},{10,... | collective-permute-start | bytes 30728 | tf_op jit(solution)/shard_map/ppermute | solution.py:452
  9.1 5.6 %collective-permute-start.5 = (f32[4,1,640]{2,1,0:T(1,128)S(1)}, f32[4,1,640]{2,1,0:T(1,128)S(1)}, u32[]{:S(2)}, u32[]{:S(2)}) collective-permute-start(f32[4,1,640]{2,1,0:T(1,128)S(1)} %get-tuple-element.37), channel_id=1, source_target_pairs={{0,3},{1,2},{2,1},{3,0},{4,7},{5,6},{6,5},{7,4},{8,11},{9,10},{10,... | collective-permute-start | bytes 30728 | tf_op jit(solution)/shard_map/ppermute | solution.py:452
  10.5 4.4 %collective-permute-start.2 = (f32[120,128]{1,0:T(8,128)S(1)}, f32[120,128]{1,0:T(8,128)S(1)}, u32[]{:S(2)}, u32[]{:S(2)}) collective-permute-start(f32[120,128]{1,0:T(8,128)S(1)} %get-tuple-element.33), channel_id=1, source_target_pairs={{0,1},{1,0},{2,3},{3,2},{4,5},{5,4},{6,7},{7,6},{8,9},{9,8},{10,11... | collective-permute-start | bytes 184328 | tf_op jit(solution)/shard_map/ppermute | solution.py:410
  10.8 4.1 %collective-permute-start.3 = (f32[128,128]{1,0:T(8,128)S(1)}, f32[128,128]{1,0:T(8,128)S(1)}, u32[]{:S(2)}, u32[]{:S(2)}) collective-permute-start(f32[128,128]{1,0:T(8,128)S(1)} %get-tuple-element.34), channel_id=1, source_target_pairs={{0,4},{1,2},{2,1},{3,7},{4,0},{5,6},{6,5},{7,3},{8,12},{9,10},{10,... | collective-permute-start | bytes 196616 | tf_op jit(solution)/shard_map/ppermute | solution.py:410

commit v12 on v9

--- a/solution.py
+++ b/solution.py
@@ -105,12 +105,14 @@
     return start
 
 
-def plenum_kernel(sizes, relayed, room_in, plen_in, cell_in, owner_in, class_in, room_near, plen_post, *rest):
+def collide_kernel(sizes, direct, room_in, plen_in, cell_in, owner_in, class_in, room_post, plen_post, swap_a, swap_b,
+                   *rest):
     ca, cs, blocks, n_span, per_brick = sizes
-    jets = rest[:-7]
-    columns, dealt, plen_buf, cells, owners, classes, sems = rest[-7:]
+    rows = blocks * cs
+    jets = rest[:-8]
+    columns, dealt, room_buf, plen_buf, cells, owners, classes, sems = rest[-8:]
     copies = [pltpu.make_async_copy(src, dst, sems.at[i]) for i, (src, dst) in enumerate(
-        ((plen_in, plen_buf), (cell_in, cells), (owner_in, owners), (class_in, classes), (room_in, room_near)))]
+        ((plen_in, plen_buf), (cell_in, cells), (owner_in, owners), (class_in, classes), (room_in, room_buf)))]
     for copy in copies:
         copy.start()
     dealt[...] = jnp.zeros_like(dealt)
@@ -132,29 +134,25 @@
         owner = owners[t]
         share = 0.15 * (classes[t].astype(F32) + 1.0)
         same = lambda j, n: n + (owners[first + j] == owner).astype(jnp.int32)
-        slot = repeat(i, same, 0) if relayed else lax.fori_loop(0, i, same, 0)
-        to = (owner ^ here if relayed else owner) * CAP + slot
+        slot = repeat(i, same, 0) if direct else lax.fori_loop(0, i, same, 0)
+        to = (owner ^ here if direct else owner) * CAP + slot
         dealt[to] = share * columns[cells[t]]
         return carry
 
-    if relayed:
+    if direct:
         for i in range(per_brick):
             send_jet(i, 0)
     else:
         lax.fori_loop(0, per_brick, send_jet, 0)
-    for part, jet in enumerate(jets):
-        many = jet.shape[0]
-        jet[...] = dealt[part * many : (part + 1) * many]
+    start = 0
+    for jet in jets:
+        jet[...] = dealt[start : start + jet.shape[0]]
+        start = start + jet.shape[0]
     copies[4].wait()
-
-
-def room_kernel(sizes, room_near, plen_post, room_post, swap_a, swap_b):
-    ca, cs, blocks, n_span, per_brick = sizes
-    rows = blocks * cs
 
     def plane(x, carry):
         for r in range(0, rows, 8):
-            post = collide([room_near[q, x, r : r + 8] for q in range(19)])
+            post = collide([room_buf[q, x, r : r + 8] for q in range(19)])
             for q in range(19):
                 room_post[q, x, r : r + 8] = post[q]
         return carry
@@ -183,7 +181,9 @@
     return sums
 
 
-def local_kernel(sizes, room_post, plen_post, cell_in, owner_in, room_part, plen_part, places, cells, owners, sems):
+def local_kernel(sizes, room_post, plen_post, crossing, cell_in, owner_in, room_part, plen_part, places, cells, owners,
+                 sems):
+    del crossing
     ca, cs, blocks, n_span, per_brick = sizes
     rows = blocks * cs
     copies = [pltpu.make_async_copy(src, dst, sems.at[i]) for i, (src, dst) in enumerate(
@@ -215,7 +215,7 @@
     repeat(n_span, brick, 0)
 
 
-def cross_kernel(sizes, relayed, room_post, plen_post, jets, cross_a, cross_b):
+def cross_kernel(sizes, direct, room_post, plen_post, jets, cross_a, cross_b):
     ca, cs, blocks, n_span, per_brick = sizes
     rows = blocks * cs
     low = lax.axis_index("span") % 2 == 0
@@ -237,7 +237,7 @@
             to = 5 * rows + k * ca + x
             cross_a[to : to + 1] = first[x * cs : x * cs + 1]
             cross_b[to : to + 1] = second[x * cs : x * cs + 1]
-    if relayed:
+    if direct:
         for s in range(CAP):
             for k in range(5):
                 to = 5 * (rows + ca) + s * 5 + k
@@ -248,41 +248,43 @@
     return [q for q in (Y_UP if up else Y_DOWN) if VELOCITIES[q][0]], cs - 1 if up else 0
 
 
-def corner_kernel(sizes, relayed, got_a, got_b, got_jets, places, cross_a, cross_b):
-    del places
+def pack_kernel(sizes, got_a, got_b, part_a, part_b, cross_a, cross_b):
     ca, cs, blocks, n_span, per_brick = sizes
     rows = blocks * cs
     even = lax.axis_index("aisle") % 2 == 0
     low = lax.axis_index("span") % 2 == 0
     group = lax.broadcasted_iota(jnp.int32, (rows, LANES), 0) % cs
+    cross_a[...] = part_a[...]
+    cross_b[...] = part_b[...]
 
     def came(q, low, high):
         if VELOCITIES[q][0] == 1:
-            k = X_UP.index(q)
-            return jnp.where(even, got_b[low(k) : high(k)], got_a[low(k) : high(k)])
-        k = X_DOWN.index(q)
-        return jnp.where(even, got_a[low(k) : high(k)], got_b[low(k) : high(k)])
-
-    sides, near = [], []
-    for up in (True, False):
+            return jnp.where(even, got_b[low:high], got_a[low:high])
+        return jnp.where(even, got_a[low:high], got_b[low:high])
+
+    def complete(cross, up):
         two, edge = corners(cs, up)
-        parts = [turned_to(came(q, lambda k: k * rows, lambda k: (k + 1) * rows), edge, c) for c, q in enumerate(two)]
-        sides.append(jnp.where(group == 0, parts[0], parts[1]))
-        at = lambda k: 5 * rows + k * cs + edge
-        near.append([came(q, at, lambda k: at(k) + 1) for q in two])
-    cross_a[0:rows] = jnp.where(low, sides[0], sides[1])
-    cross_b[0:rows] = jnp.where(low, sides[1], sides[0])
-    for c in range(2):
-        cross_a[rows + c : rows + c + 1] = jnp.where(low, near[0][c], near[1][c])
-        cross_b[rows + c : rows + c + 1] = jnp.where(low, near[1][c], near[0][c])
-    if relayed:
-        for s in range(CAP):
-            for k in range(5):
-                to = rows + 2 + s * 5 + k
-                cross_a[to : to + 1] = got_jets[CAP + s, :, k * LANES : (k + 1) * LANES]
-
-
-def aisle_kernel(sizes, relayed, room_in, plen_in, got_a, got_b, jets, got_jets, places, room, plen, inflow):
+        for q in two:
+            slot = (X_UP if VELOCITIES[q][0] == 1 else X_DOWN).index(q)
+            x = 0 if VELOCITIES[q][0] == 1 else ca - 1
+            k = (Y_UP if up else Y_DOWN).index(q)
+            column = turned_to(came(q, slot * rows, (slot + 1) * rows), edge, x)
+            cross[k * rows : (k + 1) * rows] = jnp.where(group == x, column, cross[k * rows : (k + 1) * rows])
+            at, to = 5 * rows + slot * cs + edge, 5 * rows + k * ca + x
+            cross[to : to + 1] = came(q, at, at + 1)
+
+    @pl.when(low)
+    def _():
+        complete(cross_a, True)
+        complete(cross_b, False)
+
+    @pl.when(jnp.logical_not(low))
+    def _():
+        complete(cross_a, False)
+        complete(cross_b, True)
+
+
+def aisle_kernel(sizes, direct, room_in, plen_in, got_a, got_b, jets, places, room, plen, inflow):
     ca, cs, blocks, n_span, per_brick = sizes
     rows = blocks * cs
     even = lax.axis_index("aisle") % 2 == 0
@@ -311,44 +313,25 @@
     def reader(source, b):
         return lambda s, k: source[b * CAP + s, :, k * LANES : (k + 1) * LANES]
 
-    if relayed:
+    if direct:
         put(jet_sums(lambda k: jnp.zeros((ca * cs, LANES), F32), places,
-                     [(here, reader(jets, 0)), (here ^ 2, reader(got_jets, 0))]))
+                     [(here, reader(jets, 0))]))
     else:
         inflow[...] = jnp.zeros_like(inflow)
 
         def add_brick(b, carry):
-            put(jet_sums(lambda k: inflow[k], places, [(b, reader(got_jets, b))]))
+            put(jet_sums(lambda k: inflow[k], places, [(b, reader(jets, b))]))
             return carry
 
         lax.fori_loop(0, n_span, add_brick, 0)
 
 
-def entering(n_span, got_a, got_b, enter):
+def finish_kernel(sizes, direct, room_in, plen_in, got_a, got_b, places, inflow, *rest):
+    *got_jets, room, plen, room_out, plen_out, sems = rest
+    ca, cs, blocks, n_span, per_brick = sizes
+    rows = blocks * cs
     here = lax.axis_index("span")
     low = here % 2 == 0
-
-    @pl.when(low)
-    def _():
-        enter(got_a, False)
-
-    @pl.when(jnp.logical_not(low))
-    def _():
-        enter(got_a, True)
-
-    @pl.when(jnp.logical_and(low, here > 0))
-    def _():
-        enter(got_b, True)
-
-    @pl.when(jnp.logical_and(jnp.logical_not(low), here < n_span - 1))
-    def _():
-        enter(got_b, False)
-
-
-def enter_kernel(sizes, relayed, room_in, plen_in, got_a, got_b, places, inflow_in, room, plen, inflow):
-    ca, cs, blocks, n_span, per_brick = sizes
-    rows = blocks * cs
-    here = lax.axis_index("span")
     group = lax.broadcasted_iota(jnp.int32, (rows, LANES), 0) % cs
 
     def enter(got, up):
@@ -360,38 +343,30 @@
                 at = 5 * rows + k * ca + x
                 plen[q, x * cs + y : x * cs + y + 1] = got[at : at + 1]
 
-    entering(n_span, got_a, got_b, enter)
-    if relayed:
-        start = 5 * (rows + ca)
-        jet = lambda s, k: got_a[start + s * 5 + k : start + s * 5 + k + 1]
-        sums = jet_sums(lambda k: inflow_in[k], places, [(here ^ 1, jet)])
-        for k in range(5):
-            inflow[k] = sums[k]
-    else:
-        inflow[...] = inflow_in[...]
-
-
-def finish_kernel(sizes, relayed, room_in, plen_in, got_a, got_b, places, inflow, room, plen, room_out, plen_out, sems):
-    ca, cs, blocks, n_span, per_brick = sizes
-    rows = blocks * cs
-    here = lax.axis_index("span")
-    group = lax.broadcasted_iota(jnp.int32, (rows, LANES), 0) % cs
-
-    def enter(got, up):
-        two, _ = corners(cs, up)
-        y = 0 if up else cs - 1
-        came = got[0:rows]
-        for c, q in enumerate(two):
-            x = 0 if VELOCITIES[q][0] == 1 else ca - 1
-            room[q, x] = jnp.where(group == y, turned_to(came, c, y), room[q, x])
-            plen[q, x * cs + y : x * cs + y + 1] = got[rows + c : rows + c + 1]
-
-    entering(n_span, got_a, got_b, enter)
+    @pl.when(low)
+    def _():
+        enter(got_a, False)
+
+    @pl.when(jnp.logical_not(low))
+    def _():
+        enter(got_a, True)
+
+    @pl.when(jnp.logical_and(low, here > 0))
+    def _():
+        enter(got_b, True)
+
+    @pl.when(jnp.logical_and(jnp.logical_not(low), here < n_span - 1))
+    def _():
+        enter(got_b, False)
+
     plen_copy = pltpu.make_async_copy(plen, plen_out, sems.at[0])
     plen_copy.start()
     bricks = []
-    if relayed:
-        bricks = [(here ^ 3, lambda s, k: got_a[rows + 2 + s * 5 + k : rows + 2 + s * 5 + k + 1])]
+    if direct:
+        start = 5 * (rows + cs)
+        bricks = [(here ^ 1, lambda s, k: got_a[start + s * 5 + k : start + s * 5 + k + 1])]
+        for apart, got in zip((2, 3), got_jets):
+            bricks.append((here ^ apart, lambda s, k, got=got: got[s, :, k * LANES : (k + 1) * LANES]))
     sums = jet_sums(lambda k: inflow[k], places, bricks)
     for k, q in enumerate(UPWARD):
         for x in range(ca):
@@ -441,7 +416,7 @@
     rows = blocks * cs
     tiles = tile_cell.shape[0]
     sizes = (ca, cs, blocks, n_span, tiles // n_span)
-    relayed = n_span == 4
+    direct = n_span == 4
     near = lambda shape: pltpu.VMEM(shape, F32)
     far = lambda value: pltpu.with_memory_space_constraint(value, pltpu.HBM)
     room_shape, plen_shape = (19, ca, rows, LANES), (19, ca * cs, LANES)
@@ -452,74 +427,62 @@
     tile_cell, tile_owner, tile_class = far(tile_cell), far(tile_owner.reshape(tiles)), far(tile_class)
     numbers = pltpu.SMEM((tiles,), jnp.int32)
 
-    jets_shape = ((2 if relayed else n_span) * CAP, 1, 5 * hp)
-    room_near, plen_post, *jets = call(
-        functools.partial(plenum_kernel, sizes, relayed),
-        [near(room_shape), near(plen_shape)] + [near(jets_shape)] * (2 if relayed else 1),
+    jet_shapes = [(count * CAP, 1, 5 * hp) for count in ((2, 1, 1) if direct else (n_span,))]
+    room_post, plen_post, swap_a, swap_b, *jets = call(
+        functools.partial(collide_kernel, sizes, direct),
+        [near(room_shape), near(plen_shape), near((halo, LANES)), near((halo + 8, LANES))]
+        + [near(shape) for shape in jet_shapes],
         [HBM] * 5,
-        scratch=[pltpu.VMEM((ca * cs, 1, 5 * hp), F32), near((n_span * CAP, 1, 5 * hp)), near(plen_shape), numbers, numbers, numbers,
-                 pltpu.SemaphoreType.DMA((5,))],
+        scratch=[near((ca * cs, 1, 5 * hp)), near((n_span * CAP, 1, 5 * hp)), near(room_shape), near(plen_shape),
+                 numbers, numbers, numbers, pltpu.SemaphoreType.DMA((5,))],
     )(room, plen, tile_cell, tile_owner, tile_class)
-    if relayed:
-        got_jets = lax.ppermute(jets[1], "span", [(i, i ^ 2) for i in range(4)])
-    else:
-        got_jets = lax.all_to_all(jets[0], "span", 0, 0, tiled=True)
-
-    room_post, swap_a, swap_b = call(
-        functools.partial(room_kernel, sizes),
-        [near(room_shape), near((halo + 8, LANES)), near((halo, LANES))],
-        [VMEM] * 2,
-    )(room_near, plen_post)
     got_b = swap_aisle(swap_b, True)
     got_a = swap_aisle(swap_a, False)
+    if direct:
+        got_jets = [lax.ppermute(jets[apart - 1], "span", [(i, i ^ apart) for i in range(4)]) for apart in (2, 3)]
+    else:
+        jets = [lax.all_to_all(jets[0], "span", 0, 0, tiled=True)]
+        got_jets = []
 
     upto8 = lambda count: count + -count % 8
-    cross_a, cross_b = call(
-        functools.partial(cross_kernel, sizes, relayed),
-        [near((upto8(5 * (rows + ca) + (5 * CAP if relayed else 0)), LANES)), near((halo, LANES))],
+    wide = upto8(5 * (rows + ca) + (5 * CAP if direct else 0))
+    cross_shapes = [near((wide, LANES)), near((wide + 8, LANES))]
+    part_a, part_b = call(
+        functools.partial(cross_kernel, sizes, direct),
+        cross_shapes,
         [VMEM] * 3,
     )(room_post, plen_post, jets[0])
+    cross_a, cross_b = call(
+        functools.partial(pack_kernel, sizes),
+        cross_shapes,
+        [VMEM] * 4,
+    )(got_a, got_b, part_a, part_b)
     in_a = swap_span(cross_a, False)
     in_b = swap_span(cross_b, True)
 
     room_part, plen_part, places = call(
         functools.partial(local_kernel, sizes),
         [near(room_shape), near(plen_shape), near((n_span * CAP + 1, ca * cs, LANES))],
-        [VMEM, VMEM, HBM, HBM],
+        [VMEM, VMEM, VMEM, HBM, HBM],
         scratch=[numbers, numbers, pltpu.SemaphoreType.DMA((2,))],
         flops=10**9,
-    )(room_post, plen_post, tile_cell, tile_owner)
-
-    corner_a, corner_b = call(
-        functools.partial(corner_kernel, sizes, relayed),
-        [near((upto8(rows + 2 + (5 * CAP if relayed else 0)), LANES)), near((upto8(rows + 2), LANES))],
-        [VMEM] * 4,
-    )(got_a, got_b, got_jets, places)
-    last_a = swap_span(corner_a, False)
-    last_b = swap_span(corner_b, True)
-
+    )(room_post, plen_post, cross_a, tile_cell, tile_owner)
     room_part, plen_part, inflow = call(
-        functools.partial(aisle_kernel, sizes, relayed),
-        [near(room_shape), near(plen_shape), near((5, ca * cs, LANES))],
-        [VMEM] * 7,
-        aliases={0: 0, 1: 1},
-    )(room_part, plen_part, got_a, got_b, jets[0], got_jets, places)
-    room_part, plen_part, inflow = call(
-        functools.partial(enter_kernel, sizes, relayed),
+        functools.partial(aisle_kernel, sizes, direct),
         [near(room_shape), near(plen_shape), near((5, ca * cs, LANES))],
         [VMEM] * 6,
         aliases={0: 0, 1: 1},
-    )(room_part, plen_part, in_a, in_b, places, inflow)
+    )(room_part, plen_part, got_a, got_b, jets[0], places)
 
     _, _, room_next, plenum_next = call(
-        functools.partial(finish_kernel, sizes, relayed),
+        functools.partial(finish_kernel, sizes, direct),
         [near(room_shape), near(plen_shape), jax.ShapeDtypeStruct(room_shape, F32),
          jax.ShapeDtypeStruct(plen_shape, F32)],
-        [VMEM] * 6,
+        [VMEM] * (6 + len(got_jets)),
         out_specs=[VMEM, VMEM, HBM, HBM],
         scratch=[pltpu.SemaphoreType.DMA((2,))],
         aliases={0: 0, 1: 1},
-    )(room_part, plen_part, last_a, last_b, places, inflow)
+    )(room_part, plen_part, in_a, in_b, places, inflow, *got_jets)
     room_next = room_next.reshape(19, ca, blocks, cs, LANES).transpose(0, 1, 3, 2, 4).reshape(room_pops.shape)
     return room_next, plenum_next.reshape(plenum_pops.shape)
 

time: 16.2 us -> 15.2 us (0.938)
  starting transfers between devices: 9.14 us -> 8.02 us
    ppermute x4 -> x2, starting transfers between devices: 3.36 us -> 0.68 us  [swap_span(): return lax.ppermute(value, ('aisle', 'span'), pairs)]
    ppermute x1 -> x2, waiting for transfers between devices: 0.01 us -> 2.46 us  [shards(): lax.ppermute(jets[apart - 1], 'span', [(i, i ^ apart) for i in range(4)])]
    ppermute x2, starting transfers between devices: 1.67 us -> 3.4 us  [swap_aisle(): return lax.ppermute(value, 'aisle', pairs)]
    ppermute x4 -> x2, waiting for transfers between devices: 2.07 us -> 0.34 us  [swap_span(): return lax.ppermute(value, ('aisle', 'span'), pairs)]
    ppermute x2, waiting for transfers between devices: 0.6 us -> 0.01 us  [swap_aisle(): return lax.ppermute(value, 'aisle', pairs)]
    ppermute x1 -> x2, starting transfers between devices: 4.1 us -> 3.94 us  [shards(): lax.ppermute(jets[apart - 1], 'span', [(i, i ^ apart) for i in range(4)])]
    pallas_call x7 -> x5, Pallas kernels: 2.67 us -> 2.66 us  [the longest x1 1.55 us: shards(): call(functools.partial(collide_kernel, sizes, direct), [near(room_shape),...]
  transfers between devices with their start and end apart: 7 -> 6, of which waited for: 3 -> 2; matrix products, arithmetic and copies ran while one was open for 0% -> 0% of each run, Pallas kernels for 9% -> 7%
where the time goes in v12:
time: 15.2 us; the launch traced here: 15 us
  starting transfers between devices  8.02 us (53%)
  Pallas kernels  3.52 us (23%)
  waiting for transfers between devices  2.8 us (18%)
  between operations  0.69 us (5%)
    ppermute x2, starting transfers between devices, shards(): lax.ppermute(jets[apart - 1], 'span', [(i, i ^ apart) for i in range(4)])  3.94 us
    ppermute x2, starting transfers between devices, swap_aisle(): return lax.ppermute(value, 'aisle', pairs)  3.4 us
    ppermute x2, waiting for transfers between devices, shards(): lax.ppermute(jets[apart - 1], 'span', [(i, i ^ apart) for i in range(4)])  2.46 us
    pallas_call x1, Pallas kernels, shards(): call(functools.partial(collide_kernel, sizes, direct), [near(room_shape),...  1.55 us
    pallas_call x1, Pallas kernels, shards(): call(functools.partial(finish_kernel, sizes, direct), [near(room_shape),...  0.93 us
    pallas_call x1, Pallas kernels, shards(): call(functools.partial(local_kernel, sizes), [near(room_shape), near(plen...  0.86 us
    ppermute x2, starting transfers between devices, swap_span(): return lax.ppermute(value, ('aisle', 'span'), pairs)  0.68 us
    ppermute x2, waiting for transfers between devices, swap_span(): return lax.ppermute(value, ('aisle', 'span'), pairs)  0.34 us
  transfers between devices with their start and end apart: 6, of which 2 were waited for; matrix products, arithmetic and copies ran while one was open for 0% of the time, Pallas kernels for 7%

profile of v12, /device:TPU:0, one launch (start us, length us, event | category | flops | bytes accessed | tf_op | source)
XLA Modules:
  0.0 15.0 jit_solution(11132795354855551777)
XLA Ops:
  0.6 1.5 %collide_kernel.1 = (f32[19,4,16,128]{3,2,1,0:T(8,128)S(1)}, f32[19,16,128]{2,1,0:T(8,128)S(1)}, f32[104,128]{1,0:T(8,128)S(1)}, f32[112,128]{1,0:T(8,128)S(1)},...) custom-call(f32[19,4,16,128]{3,2,1,0:T(8,128)} %bitcast.13, ...), custom_call_target="tpu_custom_call" | custom-call | flops 100000 | bytes 1000000 | tf_op jit(solution)/shard_map/collide_kernel/pallas_call | solution.py:431
  2.2 3.4 %collective-permute-start.1 = (f32[112,128]{1,0:T(8,128)S(1)}, f32[112,128]{1,0:T(8,128)S(1)}, u32[]{:S(2)}, u32[]{:S(2)}) collective-permute-start(f32[112,128]{1,0:T(8,128)S(1)} %get-tuple-element.24), channel_id=1, source_target_pairs={{0,28},{4,8},{8,4},{12,16},{16,12},{20,24},{24,20},{28,0},{1,29},{... | collective-permute-start | bytes 172040 | tf_op jit(solution)/shard_map/ppermute | solution.py:397
  5.6 0.0 collective-permute-start
  5.6 2.6 %collective-permute-start.4 = (f32[4,1,640]{2,1,0:T(1,128)S(1)}, f32[4,1,640]{2,1,0:T(1,128)S(1)}, u32[]{:S(2)}, u32[]{:S(2)}) collective-permute-start(f32[4,1,640]{2,1,0:T(1,128)S(1)} %get-tuple-element.36), channel_id=1, source_target_pairs={{0,2},{1,3},{2,0},{3,1},{4,6},{5,7},{6,4},{7,5},{8,10},{9,11},{10,... | collective-permute-start | bytes 30728 | tf_op jit(solution)/shard_map/ppermute | solution.py:442
  8.2 1.3 %collective-permute-start.5 = (f32[4,1,640]{2,1,0:T(1,128)S(1)}, f32[4,1,640]{2,1,0:T(1,128)S(1)}, u32[]{:S(2)}, u32[]{:S(2)}) collective-permute-start(f32[4,1,640]{2,1,0:T(1,128)S(1)} %get-tuple-element.37), channel_id=1, source_target_pairs={{0,3},{1,2},{2,1},{3,0},{4,7},{5,6},{6,5},{7,4},{8,11},{9,10},{10,... | collective-permute-start | bytes 30728 | tf_op jit(solution)/shard_map/ppermute | solution.py:442
  9.5 0.1 cross_kernel.1
  9.6 0.0 collective-permute-done.got_a
  9.7 0.0 collective-permute-done.1.got_b
  9.7 0.7 %collective-permute-start.2 = (f32[120,128]{1,0:T(8,128)S(1)}, f32[120,128]{1,0:T(8,128)S(1)}, u32[]{:S(2)}, u32[]{:S(2)}) collective-permute-start(f32[120,128]{1,0:T(8,128)S(1)} %get-tuple-element.28.crossing), channel_id=1, source_target_pairs={{0,1},{1,0},{2,3},{3,2},{4,5},{5,4},{6,7},{7,6},{8,9},{9,8},{10,11... | collective-permute-start | bytes 184328 | tf_op jit(solution)/shard_map/ppermute | solution.py:408
  10.4 0.0 collective-permute-start.3
  10.4 0.9 %local_kernel.1 = (f32[19,4,16,128]{3,2,1,0:T(8,128)S(1)}, f32[19,16,128]{2,1,0:T(8,128)S(1)}, f32[17,16,128]{2,1,0:T(8,128)S(1)}) custom-call(f32[19,4,16,128]{3,2,1,0:T(8,128)S(1)} %get-tuple-element.21.room_post, f32[19,16,128]{2,1,0:T(8,128)S(1)} %get-tuple-element.22.plen_post, f32[120,128]{1,0:T(8,128)S(1)} %get-tuple-element.28.crossing, s32[32]{0:T(128)} %cell_in.3, ...), custom_call_target="tpu_custom_call" | custom-call | flops 1000000000 | bytes 1000000 | tf_op jit(solution)/shard_map/local_kernel/pallas_call | solution.py:463
  11.3 0.0 collective-permute-done.4.rest_0_
  11.3 2.5 %collective-permute-done.5.rest_1_ = f32[4,1,640]{2,1,0:T(1,128)S(1)} collective-permute-done((f32[4,1,640]{2,1,0:T(1,128)S(1)}, f32[4,1,640]{2,1,0:T(1,128)S(1)}, u32[]{:S(2)}, u32[]{:S(2)}) %collective-permute-start.5) | collective-permute-done | bytes 10272 | tf_op jit(solution)/shard_map/ppermute | solution.py:442
  13.8 0.3 %collective-permute-done.2.got_a = f32[120,128]{1,0:T(8,128)S(1)} collective-permute-done((f32[120,128]{1,0:T(8,128)S(1)}, f32[120,128]{1,0:T(8,128)S(1)}, u32[]{:S(2)}, u32[]{:S(2)}) %collective-permute-start.2) | collective-permute-done | bytes 61472 | tf_op jit(solution)/shard_map/ppermute | solution.py:408
  14.1 0.0 collective-permute-done.3.got_b
  14.1 0.9 %finish_kernel.1 = (f32[19,4,16,128]{3,2,1,0:T(8,128)S(1)}, f32[19,16,128]{2,1,0:T(8,128)S(1)}, f32[19,4,16,128]{3,2,1,0:T(8,128)}, f32[19,16,128]{2,1,0:T(8,128)}) custom-call(f32[19,4,16,128]{3,2,1,0:T(8,128)S(1)} %get-tuple-element.32.room_in, f32[19,16,128]{2,1,0:T(8,128)S(1)} %get-tuple-element.33.plen_in, ...), custom_call_target="tpu_custom_call", output_to_operand_aliasing={{0}: (0, {}), {1}: (1, {})} | custom-call | flops 100000 | bytes 1000000 | tf_op jit(solution)/shard_map/finish_kernel/pallas_call | solution.py:477
  (2 shorter events, 0.1 us)
Async XLA Ops:
  2.2 7.5 %collective-permute-start.1 = (f32[112,128]{1,0:T(8,128)S(1)}, f32[112,128]{1,0:T(8,128)S(1)}, u32[]{:S(2)}, u32[]{:S(2)}) collective-permute-start(f32[112,128]{1,0:T(8,128)S(1)} %get-tuple-element.24), channel_id=1, source_target_pairs={{0,28},{4,8},{8,4},{12,16},{16,12},{20,24},{24,20},{28,0},{1,29},{... | collective-permute-start | bytes 172040 | tf_op jit(solution)/shard_map/ppermute | solution.py:397
  5.6 4.1 %collective-permute-start = (f32[104,128]{1,0:T(8,128)S(1)}, f32[104,128]{1,0:T(8,128)S(1)}, u32[]{:S(2)}, u32[]{:S(2)}) collective-permute-start(f32[104,128]{1,0:T(8,128)S(1)} %get-tuple-element.23), channel_id=1, source_target_pairs={{0,4},{4,0},{8,12},{12,8},{16,20},{20,16},{24,28},{28,24},{1,5},{5... | collective-permute-start | bytes 159752 | tf_op jit(solution)/shard_map/ppermute | solution.py:397
  5.6 5.7 %collective-permute-start.4 = (f32[4,1,640]{2,1,0:T(1,128)S(1)}, f32[4,1,640]{2,1,0:T(1,128)S(1)}, u32[]{:S(2)}, u32[]{:S(2)}) collective-permute-start(f32[4,1,640]{2,1,0:T(1,128)S(1)} %get-tuple-element.36), channel_id=1, source_target_pairs={{0,2},{1,3},{2,0},{3,1},{4,6},{5,7},{6,4},{7,5},{8,10},{9,11},{10,... | collective-permute-start | bytes 30728 | tf_op jit(solution)/shard_map/ppermute | solution.py:442
  8.2 5.6 %collective-permute-start.5 = (f32[4,1,640]{2,1,0:T(1,128)S(1)}, f32[4,1,640]{2,1,0:T(1,128)S(1)}, u32[]{:S(2)}, u32[]{:S(2)}) collective-permute-start(f32[4,1,640]{2,1,0:T(1,128)S(1)} %get-tuple-element.37), channel_id=1, source_target_pairs={{0,3},{1,2},{2,1},{3,0},{4,7},{5,6},{6,5},{7,4},{8,11},{9,10},{10,... | collective-permute-start | bytes 30728 | tf_op jit(solution)/shard_map/ppermute | solution.py:442
  9.7 4.4 %collective-permute-start.2 = (f32[120,128]{1,0:T(8,128)S(1)}, f32[120,128]{1,0:T(8,128)S(1)}, u32[]{:S(2)}, u32[]{:S(2)}) collective-permute-start(f32[120,128]{1,0:T(8,128)S(1)} %get-tuple-element.28.crossing), channel_id=1, source_target_pairs={{0,1},{1,0},{2,3},{3,2},{4,5},{5,4},{6,7},{7,6},{8,9},{9,8},{10,11... | collective-permute-start | bytes 184328 | tf_op jit(solution)/shard_map/ppermute | solution.py:408
  10.4 3.7 %collective-permute-start.3 = (f32[128,128]{1,0:T(8,128)S(1)}, f32[128,128]{1,0:T(8,128)S(1)}, u32[]{:S(2)}, u32[]{:S(2)}) collective-permute-start(f32[128,128]{1,0:T(8,128)S(1)} %get-tuple-element.34), channel_id=1, source_target_pairs={{0,4},{1,2},{2,1},{3,7},{4,0},{5,6},{6,5},{7,3},{8,12},{9,10},{10,... | collective-permute-start | bytes 196616 | tf_op jit(solution)/shard_map/ppermute | solution.py:408

commit v13 on v12

--- a/solution.py
+++ b/solution.py
@@ -112,8 +112,10 @@
     jets = rest[:-8]
     columns, dealt, room_buf, plen_buf, cells, owners, classes, sems = rest[-8:]
     copies = [pltpu.make_async_copy(src, dst, sems.at[i]) for i, (src, dst) in enumerate(
-        ((plen_in, plen_buf), (cell_in, cells), (owner_in, owners), (class_in, classes), (room_in, room_buf)))]
-    for copy in copies:
+        ((plen_in, plen_buf), (cell_in, cells), (owner_in, owners), (class_in, classes)))]
+    order = [0, ca - 1] + list(range(1, ca - 1))
+    planes = [pltpu.make_async_copy(room_in.at[:, x], room_buf.at[:, x], sems.at[4 + x]) for x in order]
+    for copy in copies[:1] + planes + copies[1:]:
         copy.start()
     dealt[...] = jnp.zeros_like(dealt)
     copies[0].wait()
@@ -148,16 +150,17 @@
     for jet in jets:
         jet[...] = dealt[start : start + jet.shape[0]]
         start = start + jet.shape[0]
-    copies[4].wait()
-
-    def plane(x, carry):
+
+    def plane(i):
+        planes[i].wait()
+        x = order[i]
         for r in range(0, rows, 8):
             post = collide([room_buf[q, x, r : r + 8] for q in range(19)])
             for q in range(19):
                 room_post[q, x, r : r + 8] = post[q]
-        return carry
-
-    lax.fori_loop(0, ca, plane, 0)
+
+    plane(0)
+    plane(1)
     even = lax.axis_index("aisle") % 2 == 0
     for k in range(5):
         up, down = X_UP[k], X_DOWN[k]
@@ -170,6 +173,8 @@
         low = 5 * rows + k * cs
         swap_a[low : low + cs] = jnp.where(even, rising, falling)
         swap_b[low : low + cs] = jnp.where(even, falling, rising)
+    for i in range(2, ca):
+        plane(i)
 
 
 def jet_sums(start, places, bricks):
@@ -434,7 +439,7 @@
         + [near(shape) for shape in jet_shapes],
         [HBM] * 5,
         scratch=[near((ca * cs, 1, 5 * hp)), near((n_span * CAP, 1, 5 * hp)), near(room_shape), near(plen_shape),
-                 numbers, numbers, numbers, pltpu.SemaphoreType.DMA((5,))],
+                 numbers, numbers, numbers, pltpu.SemaphoreType.DMA((4 + ca,))],
     )(room, plen, tile_cell, tile_owner, tile_class)
     got_b = swap_aisle(swap_b, True)
     got_a = swap_aisle(swap_a, False)

time: 15.2 us -> 15.1 us (level)
  no operation moved by 1% of the time
where the time goes in v13:
time: 15.1 us; the launch traced here: 15 us
  starting transfers between devices  8.02 us (53%)
  Pallas kernels  3.47 us (23%)
  waiting for transfers between devices  2.8 us (19%)
  between operations  0.69 us (5%)
    ppermute x2, starting transfers between devices, shards(): lax.ppermute(jets[apart - 1], 'span', [(i, i ^ apart) for i in range(4)])  3.94 us
    ppermute x2, starting transfers between devices, swap_aisle(): return lax.ppermute(value, 'aisle', pairs)  3.4 us
    ppermute x2, waiting for transfers between devices, shards(): lax.ppermute(jets[apart - 1], 'span', [(i, i ^ apart) for i in range(4)])  2.46 us
    pallas_call x1, Pallas kernels, shards(): call(functools.partial(collide_kernel, sizes, direct), [near(room_shape),...  1.5 us
    pallas_call x1, Pallas kernels, shards(): call(functools.partial(finish_kernel, sizes, direct), [near(room_shape),...  0.93 us
    pallas_call x1, Pallas kernels, shards(): call(functools.partial(local_kernel, sizes), [near(room_shape), near(plen...  0.86 us
    ppermute x2, starting transfers between devices, swap_span(): return lax.ppermute(value, ('aisle', 'span'), pairs)  0.69 us
    ppermute x2, waiting for transfers between devices, swap_span(): return lax.ppermute(value, ('aisle', 'span'), pairs)  0.34 us
  transfers between devices with their start and end apart: 6, of which 2 were waited for; matrix products, arithmetic and copies ran while one was open for 0% of the time, Pallas kernels for 7%

profile of v13, /device:TPU:0, one launch (start us, length us, event | category | flops | bytes accessed | tf_op | source)
XLA Modules:
  0.0 15.0 jit_solution(16995413202501958446)
XLA Ops:
  0.6 1.5 %collide_kernel.1 = (f32[19,4,16,128]{3,2,1,0:T(8,128)S(1)}, f32[19,16,128]{2,1,0:T(8,128)S(1)}, f32[104,128]{1,0:T(8,128)S(1)}, f32[112,128]{1,0:T(8,128)S(1)},...) custom-call(f32[19,4,16,128]{3,2,1,0:T(8,128)} %bitcast.13, ...), custom_call_target="tpu_custom_call" | custom-call | flops 100000 | bytes 1000000 | tf_op jit(solution)/shard_map/collide_kernel/pallas_call | solution.py:436
  2.1 3.4 %collective-permute-start.1 = (f32[112,128]{1,0:T(8,128)S(1)}, f32[112,128]{1,0:T(8,128)S(1)}, u32[]{:S(2)}, u32[]{:S(2)}) collective-permute-start(f32[112,128]{1,0:T(8,128)S(1)} %get-tuple-element.24), channel_id=1, source_target_pairs={{0,28},{4,8},{8,4},{12,16},{16,12},{20,24},{24,20},{28,0},{1,29},{... | collective-permute-start | bytes 172040 | tf_op jit(solution)/shard_map/ppermute | solution.py:402
  5.5 0.0 collective-permute-start
  5.5 2.6 %collective-permute-start.4 = (f32[4,1,640]{2,1,0:T(1,128)S(1)}, f32[4,1,640]{2,1,0:T(1,128)S(1)}, u32[]{:S(2)}, u32[]{:S(2)}) collective-permute-start(f32[4,1,640]{2,1,0:T(1,128)S(1)} %get-tuple-element.36), channel_id=1, source_target_pairs={{0,2},{1,3},{2,0},{3,1},{4,6},{5,7},{6,4},{7,5},{8,10},{9,11},{10,... | collective-permute-start | bytes 30728 | tf_op jit(solution)/shard_map/ppermute | solution.py:447
  8.1 1.3 %collective-permute-start.5 = (f32[4,1,640]{2,1,0:T(1,128)S(1)}, f32[4,1,640]{2,1,0:T(1,128)S(1)}, u32[]{:S(2)}, u32[]{:S(2)}) collective-permute-start(f32[4,1,640]{2,1,0:T(1,128)S(1)} %get-tuple-element.37), channel_id=1, source_target_pairs={{0,3},{1,2},{2,1},{3,0},{4,7},{5,6},{6,5},{7,4},{8,11},{9,10},{10,... | collective-permute-start | bytes 30728 | tf_op jit(solution)/shard_map/ppermute | solution.py:447
  9.5 0.1 cross_kernel.1
  9.6 0.0 collective-permute-done.got_a
  9.6 0.0 collective-permute-done.1.got_b
  9.7 0.7 %collective-permute-start.2 = (f32[120,128]{1,0:T(8,128)S(1)}, f32[120,128]{1,0:T(8,128)S(1)}, u32[]{:S(2)}, u32[]{:S(2)}) collective-permute-start(f32[120,128]{1,0:T(8,128)S(1)} %get-tuple-element.28.crossing), channel_id=1, source_target_pairs={{0,1},{1,0},{2,3},{3,2},{4,5},{5,4},{6,7},{7,6},{8,9},{9,8},{10,11... | collective-permute-start | bytes 184328 | tf_op jit(solution)/shard_map/ppermute | solution.py:413
  10.3 0.0 collective-permute-start.3
  10.3 0.9 %local_kernel.1 = (f32[19,4,16,128]{3,2,1,0:T(8,128)S(1)}, f32[19,16,128]{2,1,0:T(8,128)S(1)}, f32[17,16,128]{2,1,0:T(8,128)S(1)}) custom-call(f32[19,4,16,128]{3,2,1,0:T(8,128)S(1)} %get-tuple-element.21.room_post, f32[19,16,128]{2,1,0:T(8,128)S(1)} %get-tuple-element.22.plen_post, f32[120,128]{1,0:T(8,128)S(1)} %get-tuple-element.28.crossing, s32[32]{0:T(128)} %cell_in.3, ...), custom_call_target="tpu_custom_call" | custom-call | flops 1000000000 | bytes 1000000 | tf_op jit(solution)/shard_map/local_kernel/pallas_call | solution.py:468
  11.2 0.0 collective-permute-done.4.rest_0_
  11.3 2.5 %collective-permute-done.5.rest_1_ = f32[4,1,640]{2,1,0:T(1,128)S(1)} collective-permute-done((f32[4,1,640]{2,1,0:T(1,128)S(1)}, f32[4,1,640]{2,1,0:T(1,128)S(1)}, u32[]{:S(2)}, u32[]{:S(2)}) %collective-permute-start.5) | collective-permute-done | bytes 10272 | tf_op jit(solution)/shard_map/ppermute | solution.py:447
  13.7 0.3 %collective-permute-done.2.got_a = f32[120,128]{1,0:T(8,128)S(1)} collective-permute-done((f32[120,128]{1,0:T(8,128)S(1)}, f32[120,128]{1,0:T(8,128)S(1)}, u32[]{:S(2)}, u32[]{:S(2)}) %collective-permute-start.2) | collective-permute-done | bytes 61472 | tf_op jit(solution)/shard_map/ppermute | solution.py:413
  14.1 0.0 collective-permute-done.3.got_b
  14.1 0.9 %finish_kernel.1 = (f32[19,4,16,128]{3,2,1,0:T(8,128)S(1)}, f32[19,16,128]{2,1,0:T(8,128)S(1)}, f32[19,4,16,128]{3,2,1,0:T(8,128)}, f32[19,16,128]{2,1,0:T(8,128)}) custom-call(f32[19,4,16,128]{3,2,1,0:T(8,128)S(1)} %get-tuple-element.32.room_in, f32[19,16,128]{2,1,0:T(8,128)S(1)} %get-tuple-element.33.plen_in, ...), custom_call_target="tpu_custom_call", output_to_operand_aliasing={{0}: (0, {}), {1}: (1, {})} | custom-call | flops 100000 | bytes 1000000 | tf_op jit(solution)/shard_map/finish_kernel/pallas_call | solution.py:482
  (2 shorter events, 0.1 us)
Async XLA Ops:
  2.1 7.5 %collective-permute-start.1 = (f32[112,128]{1,0:T(8,128)S(1)}, f32[112,128]{1,0:T(8,128)S(1)}, u32[]{:S(2)}, u32[]{:S(2)}) collective-permute-start(f32[112,128]{1,0:T(8,128)S(1)} %get-tuple-element.24), channel_id=1, source_target_pairs={{0,28},{4,8},{8,4},{12,16},{16,12},{20,24},{24,20},{28,0},{1,29},{... | collective-permute-start | bytes 172040 | tf_op jit(solution)/shard_map/ppermute | solution.py:402
  5.5 4.1 %collective-permute-start = (f32[104,128]{1,0:T(8,128)S(1)}, f32[104,128]{1,0:T(8,128)S(1)}, u32[]{:S(2)}, u32[]{:S(2)}) collective-permute-start(f32[104,128]{1,0:T(8,128)S(1)} %get-tuple-element.23), channel_id=1, source_target_pairs={{0,4},{4,0},{8,12},{12,8},{16,20},{20,16},{24,28},{28,24},{1,5},{5... | collective-permute-start | bytes 159752 | tf_op jit(solution)/shard_map/ppermute | solution.py:402
  5.5 5.7 %collective-permute-start.4 = (f32[4,1,640]{2,1,0:T(1,128)S(1)}, f32[4,1,640]{2,1,0:T(1,128)S(1)}, u32[]{:S(2)}, u32[]{:S(2)}) collective-permute-start(f32[4,1,640]{2,1,0:T(1,128)S(1)} %get-tuple-element.36), channel_id=1, source_target_pairs={{0,2},{1,3},{2,0},{3,1},{4,6},{5,7},{6,4},{7,5},{8,10},{9,11},{10,... | collective-permute-start | bytes 30728 | tf_op jit(solution)/shard_map/ppermute | solution.py:447
  8.1 5.6 %collective-permute-start.5 = (f32[4,1,640]{2,1,0:T(1,128)S(1)}, f32[4,1,640]{2,1,0:T(1,128)S(1)}, u32[]{:S(2)}, u32[]{:S(2)}) collective-permute-start(f32[4,1,640]{2,1,0:T(1,128)S(1)} %get-tuple-element.37), channel_id=1, source_target_pairs={{0,3},{1,2},{2,1},{3,0},{4,7},{5,6},{6,5},{7,4},{8,11},{9,10},{10,... | collective-permute-start | bytes 30728 | tf_op jit(solution)/shard_map/ppermute | solution.py:447
  9.7 4.4 %collective-permute-start.2 = (f32[120,128]{1,0:T(8,128)S(1)}, f32[120,128]{1,0:T(8,128)S(1)}, u32[]{:S(2)}, u32[]{:S(2)}) collective-permute-start(f32[120,128]{1,0:T(8,128)S(1)} %get-tuple-element.28.crossing), channel_id=1, source_target_pairs={{0,1},{1,0},{2,3},{3,2},{4,5},{5,4},{6,7},{7,6},{8,9},{9,8},{10,11... | collective-permute-start | bytes 184328 | tf_op jit(solution)/shard_map/ppermute | solution.py:413
  10.3 3.7 %collective-permute-start.3 = (f32[128,128]{1,0:T(8,128)S(1)}, f32[128,128]{1,0:T(8,128)S(1)}, u32[]{:S(2)}, u32[]{:S(2)}) collective-permute-start(f32[128,128]{1,0:T(8,128)S(1)} %get-tuple-element.34), channel_id=1, source_target_pairs={{0,4},{1,2},{2,1},{3,7},{4,0},{5,6},{6,5},{7,3},{8,12},{9,10},{10,... | collective-permute-start | bytes 196616 | tf_op jit(solution)/shard_map/ppermute | solution.py:413

commit v14 on v13

--- a/solution.py
+++ b/solution.py
@@ -105,16 +105,21 @@
     return start
 
 
+def collide_plane(room, x):
+    for r in range(0, room.shape[2], 8):
+        post = collide([room[q, x, r : r + 8] for q in range(19)])
+        for q in range(19):
+            room[q, x, r : r + 8] = post[q]
+
+
 def collide_kernel(sizes, direct, room_in, plen_in, cell_in, owner_in, class_in, room_post, plen_post, swap_a, swap_b,
-                   *rest):
+                   dealt, columns, plen_buf, cells, owners, classes, sems):
     ca, cs, blocks, n_span, per_brick = sizes
     rows = blocks * cs
-    jets = rest[:-8]
-    columns, dealt, room_buf, plen_buf, cells, owners, classes, sems = rest[-8:]
     copies = [pltpu.make_async_copy(src, dst, sems.at[i]) for i, (src, dst) in enumerate(
         ((plen_in, plen_buf), (cell_in, cells), (owner_in, owners), (class_in, classes)))]
     order = [0, ca - 1] + list(range(1, ca - 1))
-    planes = [pltpu.make_async_copy(room_in.at[:, x], room_buf.at[:, x], sems.at[4 + x]) for x in order]
+    planes = [pltpu.make_async_copy(room_in.at[:, x], room_post.at[:, x], sems.at[4 + x]) for x in order]
     for copy in copies[:1] + planes + copies[1:]:
         copy.start()
     dealt[...] = jnp.zeros_like(dealt)
@@ -146,21 +151,9 @@
             send_jet(i, 0)
     else:
         lax.fori_loop(0, per_brick, send_jet, 0)
-    start = 0
-    for jet in jets:
-        jet[...] = dealt[start : start + jet.shape[0]]
-        start = start + jet.shape[0]
-
-    def plane(i):
+    for i in range(2):
         planes[i].wait()
-        x = order[i]
-        for r in range(0, rows, 8):
-            post = collide([room_buf[q, x, r : r + 8] for q in range(19)])
-            for q in range(19):
-                room_post[q, x, r : r + 8] = post[q]
-
-    plane(0)
-    plane(1)
+        collide_plane(room_post, order[i])
     even = lax.axis_index("aisle") % 2 == 0
     for k in range(5):
         up, down = X_UP[k], X_DOWN[k]
@@ -174,7 +167,7 @@
         swap_a[low : low + cs] = jnp.where(even, rising, falling)
         swap_b[low : low + cs] = jnp.where(even, falling, rising)
     for i in range(2, ca):
-        plane(i)
+        planes[i].wait()
 
 
 def jet_sums(start, places, bricks):
@@ -220,11 +213,13 @@
     repeat(n_span, brick, 0)
 
 
-def cross_kernel(sizes, direct, room_post, plen_post, jets, cross_a, cross_b):
+def inner(sizes, direct, room_post, plen_post, jets, cross_a, cross_b):
     ca, cs, blocks, n_span, per_brick = sizes
     rows = blocks * cs
     low = lax.axis_index("span") % 2 == 0
     group = lax.broadcasted_iota(jnp.int32, (rows, LANES), 0) % cs
+    for x in range(1, ca - 1):
+        collide_plane(room_post, x)
     for k in range(5):
         sides, near = [], []
         for q, edge in ((Y_UP[k], cs - 1), (Y_DOWN[k], 0)):
@@ -249,6 +244,23 @@
                 cross_a[to : to + 1] = jets[CAP + s, :, k * LANES : (k + 1) * LANES]
 
 
+def early_kernel(sizes, direct, room_in, plen_post, dealt, room_post, cross_a, cross_b, *jets):
+    start = 2 * CAP
+    for jet in jets:
+        jet[...] = dealt[start : start + CAP]
+        start = start + CAP
+
+    @pl.when(lax.axis_index("span") < sizes[3] // 2)
+    def _():
+        inner(sizes, direct, room_post, plen_post, dealt, cross_a, cross_b)
+
+
+def late_kernel(sizes, direct, room_in, plen_post, dealt, a_in, b_in, room_post, cross_a, cross_b):
+    @pl.when(lax.axis_index("span") >= sizes[3] // 2)
+    def _():
+        inner(sizes, direct, room_post, plen_post, dealt, cross_a, cross_b)
+
+
 def corners(cs, up):
     return [q for q in (Y_UP if up else Y_DOWN) if VELOCITIES[q][0]], cs - 1 if up else 0
 
@@ -432,31 +444,39 @@
     tile_cell, tile_owner, tile_class = far(tile_cell), far(tile_owner.reshape(tiles)), far(tile_class)
     numbers = pltpu.SMEM((tiles,), jnp.int32)
 
-    jet_shapes = [(count * CAP, 1, 5 * hp) for count in ((2, 1, 1) if direct else (n_span,))]
-    room_post, plen_post, swap_a, swap_b, *jets = call(
+    dealt_shape, jet_shape = (n_span * CAP, 1, 5 * hp), (CAP, 1, 5 * hp)
+    room_post, plen_post, swap_a, swap_b, dealt = call(
         functools.partial(collide_kernel, sizes, direct),
-        [near(room_shape), near(plen_shape), near((halo, LANES)), near((halo + 8, LANES))]
-        + [near(shape) for shape in jet_shapes],
+        [near(room_shape), near(plen_shape), near((halo, LANES)), near((halo + 8, LANES)),
+         near(dealt_shape)],
         [HBM] * 5,
-        scratch=[near((ca * cs, 1, 5 * hp)), near((n_span * CAP, 1, 5 * hp)), near(room_shape), near(plen_shape),
-                 numbers, numbers, numbers, pltpu.SemaphoreType.DMA((4 + ca,))],
+        scratch=[near((ca * cs, 1, 5 * hp)), near(plen_shape), numbers, numbers, numbers,
+                 pltpu.SemaphoreType.DMA((4 + ca,))],
     )(room, plen, tile_cell, tile_owner, tile_class)
     got_b = swap_aisle(swap_b, True)
     got_a = swap_aisle(swap_a, False)
-    if direct:
-        got_jets = [lax.ppermute(jets[apart - 1], "span", [(i, i ^ apart) for i in range(4)]) for apart in (2, 3)]
-    else:
-        jets = [lax.all_to_all(jets[0], "span", 0, 0, tiled=True)]
-        got_jets = []
 
     upto8 = lambda count: count + -count % 8
     wide = upto8(5 * (rows + ca) + (5 * CAP if direct else 0))
     cross_shapes = [near((wide, LANES)), near((wide + 8, LANES))]
-    part_a, part_b = call(
-        functools.partial(cross_kernel, sizes, direct),
-        cross_shapes,
+    room_post, part_a, part_b, *jets = call(
+        functools.partial(early_kernel, sizes, direct),
+        [near(room_shape)] + cross_shapes + [near(jet_shape)] * (2 if direct else 0),
         [VMEM] * 3,
-    )(room_post, plen_post, jets[0])
+        aliases={0: 0},
+    )(room_post, plen_post, dealt)
+    if direct:
+        own_jets = dealt
+        got_jets = [lax.ppermute(jets[apart - 2], "span", [(i, i ^ apart) for i in range(4)]) for apart in (2, 3)]
+    else:
+        own_jets = lax.all_to_all(dealt, "span", 0, 0, tiled=True)
+        got_jets = []
+    room_post, part_a, part_b = call(
+        functools.partial(late_kernel, sizes, direct),
+        [near(room_shape)] + cross_shapes,
+        [VMEM] * 5,
+        aliases={0: 0, 3: 1, 4: 2},
+    )(room_post, plen_post, dealt, part_a, part_b)
     cross_a, cross_b = call(
         functools.partial(pack_kernel, sizes),
         cross_shapes,
@@ -477,7 +497,7 @@
         [near(room_shape), near(plen_shape), near((5, ca * cs, LANES))],
         [VMEM] * 6,
         aliases={0: 0, 1: 1},
-    )(room_part, plen_part, got_a, got_b, jets[0], places)
+    )(room_part, plen_part, got_a, got_b, own_jets, places)
 
     _, _, room_next, plenum_next = call(
         functools.partial(finish_kernel, sizes, direct),

time: 15.1 us -> 15.2 us (level)
  waiting for transfers between devices: 2.8 us -> 2.96 us
    ppermute x2, starting transfers between devices: 0.69 us -> 0.53 us  [swap_span(): return lax.ppermute(value, ('aisle', 'span'), pairs)]
  transfers between devices with their start and end apart: 6 -> 6, of which waited for: 2 -> 2; matrix products, arithmetic and copies ran while one was open for 0% -> 0% of each run, Pallas kernels for 7% -> 8%
where the time goes in v14:
time: 15.2 us; the launch traced here: 15 us
  starting transfers between devices  7.94 us (52%)
  Pallas kernels  3.43 us (23%)
  waiting for transfers between devices  2.96 us (19%)
  between operations  0.68 us (4%)
    ppermute x2, starting transfers between devices, shards(): lax.ppermute(jets[apart - 2], 'span', [(i, i ^ apart) for i in range(4)])  4 us
    ppermute x2, starting transfers between devices, swap_aisle(): return lax.ppermute(value, 'aisle', pairs)  3.4 us
    ppermute x2, waiting for transfers between devices, shards(): lax.ppermute(jets[apart - 2], 'span', [(i, i ^ apart) for i in range(4)])  2.52 us
    pallas_call x1, Pallas kernels, shards(): call(functools.partial(collide_kernel, sizes, direct), [near(room_shape),...  1.37 us
    pallas_call x1, Pallas kernels, shards(): call(functools.partial(finish_kernel, sizes, direct), [near(room_shape),...  0.93 us
    pallas_call x1, Pallas kernels, shards(): call(functools.partial(local_kernel, sizes), [near(room_shape), near(plen...  0.86 us
    ppermute x2, starting transfers between devices, swap_span(): return lax.ppermute(value, ('aisle', 'span'), pairs)  0.53 us
    ppermute x2, waiting for transfers between devices, swap_span(): return lax.ppermute(value, ('aisle', 'span'), pairs)  0.43 us
  transfers between devices with their start and end apart: 6, of which 2 were waited for; matrix products, arithmetic and copies ran while one was open for 0% of the time, Pallas kernels for 8%

profile of v14, /device:TPU:0, one launch (start us, length us, event | category | flops | bytes accessed | tf_op | source)
XLA Modules:
  0.0 15.0 jit_solution(1058825307113572169)
XLA Ops:
  0.6 1.4 %collide_kernel.1 = (f32[19,4,16,128]{3,2,1,0:T(8,128)S(1)}, f32[19,16,128]{2,1,0:T(8,128)S(1)}, f32[104,128]{1,0:T(8,128)S(1)}, f32[112,128]{1,0:T(8,128)S(1)}, f32[16,1,640]{2,1,0:T(1,128)S(1)}) custom-call(f32[19,4,16,128]{3,2,1,0:T(8,128)} %bitcast.13, f32[19,16,128]{2,1,0:T(8,128)} %bitcast.14, s32[32]{0:T(128)} %cell_in.3, s32[32]{0:T(128)} %bitcast.15, ...), custom_call_target="tpu_custom_call" | custom-call | flops 100000 | bytes 1000000 | tf_op jit(solution)/shard_map/collide_kernel/pallas_call | solution.py:448
  2.0 3.4 %collective-permute-start.1 = (f32[112,128]{1,0:T(8,128)S(1)}, f32[112,128]{1,0:T(8,128)S(1)}, u32[]{:S(2)}, u32[]{:S(2)}) collective-permute-start(f32[112,128]{1,0:T(8,128)S(1)} %get-tuple-element.33), channel_id=1, source_target_pairs={{0,28},{4,8},{8,4},{12,16},{16,12},{20,24},{24,20},{28,0},{1,29},{... | collective-permute-start | bytes 172040 | tf_op jit(solution)/shard_map/ppermute | solution.py:414
  5.4 0.0 collective-permute-start
  5.4 0.2 %early_kernel.1 = (f32[19,4,16,128]{3,2,1,0:T(8,128)S(1)}, f32[120,128]{1,0:T(8,128)S(1)}, f32[128,128]{1,0:T(8,128)S(1)}, f32[4,1,640]{2,1,0:T(1,128)S(1)}, f32[4,1,640]{2,1,0:T(1,128)S(1)}) custom-call(f32[19,4,16,128]{3,2,1,0:T(8,128)S(1)} %get-tuple-element.25.room_in, ...), custom_call_target="tpu_custom_call", output_to_operand_aliasing={{0}: (0, {})} | custom-call | flops 100000 | bytes 1000000 | tf_op jit(solution)/shard_map/early_kernel/pallas_call | solution.py:462
  5.6 2.4 %collective-permute-start.4 = (f32[4,1,640]{2,1,0:T(1,128)S(1)}, f32[4,1,640]{2,1,0:T(1,128)S(1)}, u32[]{:S(2)}, u32[]{:S(2)}) collective-permute-start(f32[4,1,640]{2,1,0:T(1,128)S(1)} %get-tuple-element.44), channel_id=1, source_target_pairs={{0,2},{1,3},{2,0},{3,1},{4,6},{5,7},{6,4},{7,5},{8,10},{9,11},{10,... | collective-permute-start | bytes 30728 | tf_op jit(solution)/shard_map/ppermute | solution.py:470
  8.1 1.6 %collective-permute-start.5 = (f32[4,1,640]{2,1,0:T(1,128)S(1)}, f32[4,1,640]{2,1,0:T(1,128)S(1)}, u32[]{:S(2)}, u32[]{:S(2)}) collective-permute-start(f32[4,1,640]{2,1,0:T(1,128)S(1)} %get-tuple-element.45), channel_id=1, source_target_pairs={{0,3},{1,2},{2,1},{3,0},{4,7},{5,6},{6,5},{7,4},{8,11},{9,10},{10,... | collective-permute-start | bytes 30728 | tf_op jit(solution)/shard_map/ppermute | solution.py:470
  9.6 0.0 collective-permute-done.got_a
  9.6 0.0 collective-permute-done.1.got_b
  9.7 0.5 %collective-permute-start.2 = (f32[120,128]{1,0:T(8,128)S(1)}, f32[120,128]{1,0:T(8,128)S(1)}, u32[]{:S(2)}, u32[]{:S(2)}) collective-permute-start(f32[120,128]{1,0:T(8,128)S(1)} %get-tuple-element.36.crossing), channel_id=1, source_target_pairs={{0,1},{1,0},{2,3},{3,2},{4,5},{5,4},{6,7},{7,6},{8,9},{9,8},{10,11... | collective-permute-start | bytes 184328 | tf_op jit(solution)/shard_map/ppermute | solution.py:425
  10.2 0.0 collective-permute-start.3
  10.2 0.9 %local_kernel.1 = (f32[19,4,16,128]{3,2,1,0:T(8,128)S(1)}, f32[19,16,128]{2,1,0:T(8,128)S(1)}, f32[17,16,128]{2,1,0:T(8,128)S(1)}) custom-call(f32[19,4,16,128]{3,2,1,0:T(8,128)S(1)} %get-tuple-element.31.room_post, f32[19,16,128]{2,1,0:T(8,128)S(1)} %get-tuple-element.26.plen_post, f32[120,128]{1,0:T(8,128)S(1)} %get-tuple-element.36.crossing, s32[32]{0:T(128)} %cell_in.3, ...), custom_call_target="tpu_custom_call" | custom-call | flops 1000000000 | bytes 1000000 | tf_op jit(solution)/shard_map/local_kernel/pallas_call | solution.py:488
  11.1 0.0 collective-permute-done.4.rest_0_
  11.1 2.5 %collective-permute-done.5.rest_1_ = f32[4,1,640]{2,1,0:T(1,128)S(1)} collective-permute-done((f32[4,1,640]{2,1,0:T(1,128)S(1)}, f32[4,1,640]{2,1,0:T(1,128)S(1)}, u32[]{:S(2)}, u32[]{:S(2)}) %collective-permute-start.5) | collective-permute-done | bytes 10272 | tf_op jit(solution)/shard_map/ppermute | solution.py:470
  13.6 0.4 %collective-permute-done.2.got_a = f32[120,128]{1,0:T(8,128)S(1)} collective-permute-done((f32[120,128]{1,0:T(8,128)S(1)}, f32[120,128]{1,0:T(8,128)S(1)}, u32[]{:S(2)}, u32[]{:S(2)}) %collective-permute-start.2) | collective-permute-done | bytes 61472 | tf_op jit(solution)/shard_map/ppermute | solution.py:425
  14.1 0.0 collective-permute-done.3.got_b
  14.1 0.9 %finish_kernel.1 = (f32[19,4,16,128]{3,2,1,0:T(8,128)S(1)}, f32[19,16,128]{2,1,0:T(8,128)S(1)}, f32[19,4,16,128]{3,2,1,0:T(8,128)}, f32[19,16,128]{2,1,0:T(8,128)}) custom-call(f32[19,4,16,128]{3,2,1,0:T(8,128)S(1)} %get-tuple-element.40.room_in, f32[19,16,128]{2,1,0:T(8,128)S(1)} %get-tuple-element.41.plen_in, ...), custom_call_target="tpu_custom_call", output_to_operand_aliasing={{0}: (0, {}), {1}: (1, {})} | custom-call | flops 100000 | bytes 1000000 | tf_op jit(solution)/shard_map/finish_kernel/pallas_call | solution.py:502
  (3 shorter events, 0.1 us)
Async XLA Ops:
  2.0 7.6 %collective-permute-start.1 = (f32[112,128]{1,0:T(8,128)S(1)}, f32[112,128]{1,0:T(8,128)S(1)}, u32[]{:S(2)}, u32[]{:S(2)}) collective-permute-start(f32[112,128]{1,0:T(8,128)S(1)} %get-tuple-element.33), channel_id=1, source_target_pairs={{0,28},{4,8},{8,4},{12,16},{16,12},{20,24},{24,20},{28,0},{1,29},{... | collective-permute-start | bytes 172040 | tf_op jit(solution)/shard_map/ppermute | solution.py:414
  5.4 4.2 %collective-permute-start = (f32[104,128]{1,0:T(8,128)S(1)}, f32[104,128]{1,0:T(8,128)S(1)}, u32[]{:S(2)}, u32[]{:S(2)}) collective-permute-start(f32[104,128]{1,0:T(8,128)S(1)} %get-tuple-element.32), channel_id=1, source_target_pairs={{0,4},{4,0},{8,12},{12,8},{16,20},{20,16},{24,28},{28,24},{1,5},{5... | collective-permute-start | bytes 159752 | tf_op jit(solution)/shard_map/ppermute | solution.py:414
  5.6 5.5 %collective-permute-start.4 = (f32[4,1,640]{2,1,0:T(1,128)S(1)}, f32[4,1,640]{2,1,0:T(1,128)S(1)}, u32[]{:S(2)}, u32[]{:S(2)}) collective-permute-start(f32[4,1,640]{2,1,0:T(1,128)S(1)} %get-tuple-element.44), channel_id=1, source_target_pairs={{0,2},{1,3},{2,0},{3,1},{4,6},{5,7},{6,4},{7,5},{8,10},{9,11},{10,... | collective-permute-start | bytes 30728 | tf_op jit(solution)/shard_map/ppermute | solution.py:470
  8.1 5.6 %collective-permute-start.5 = (f32[4,1,640]{2,1,0:T(1,128)S(1)}, f32[4,1,640]{2,1,0:T(1,128)S(1)}, u32[]{:S(2)}, u32[]{:S(2)}) collective-permute-start(f32[4,1,640]{2,1,0:T(1,128)S(1)} %get-tuple-element.45), channel_id=1, source_target_pairs={{0,3},{1,2},{2,1},{3,0},{4,7},{5,6},{6,5},{7,4},{8,11},{9,10},{10,... | collective-permute-start | bytes 30728 | tf_op jit(solution)/shard_map/ppermute | solution.py:470
  9.7 4.4 %collective-permute-start.2 = (f32[120,128]{1,0:T(8,128)S(1)}, f32[120,128]{1,0:T(8,128)S(1)}, u32[]{:S(2)}, u32[]{:S(2)}) collective-permute-start(f32[120,128]{1,0:T(8,128)S(1)} %get-tuple-element.36.crossing), channel_id=1, source_target_pairs={{0,1},{1,0},{2,3},{3,2},{4,5},{5,4},{6,7},{7,6},{8,9},{9,8},{10,11... | collective-permute-start | bytes 184328 | tf_op jit(solution)/shard_map/ppermute | solution.py:425
  10.2 3.9 %collective-permute-start.3 = (f32[128,128]{1,0:T(8,128)S(1)}, f32[128,128]{1,0:T(8,128)S(1)}, u32[]{:S(2)}, u32[]{:S(2)}) collective-permute-start(f32[128,128]{1,0:T(8,128)S(1)} %get-tuple-element.42), channel_id=1, source_target_pairs={{0,4},{1,2},{2,1},{3,7},{4,0},{5,6},{6,5},{7,3},{8,12},{9,10},{10,... | collective-permute-start | bytes 196616 | tf_op jit(solution)/shard_map/ppermute | solution.py:425

commit v15 on v14

--- a/solution.py
+++ b/solution.py
@@ -250,13 +250,13 @@
         jet[...] = dealt[start : start + CAP]
         start = start + CAP
 
-    @pl.when(lax.axis_index("span") < sizes[3] // 2)
+    @pl.when(lax.axis_index("span") == 0)
     def _():
         inner(sizes, direct, room_post, plen_post, dealt, cross_a, cross_b)
 
 
 def late_kernel(sizes, direct, room_in, plen_post, dealt, a_in, b_in, room_post, cross_a, cross_b):
-    @pl.when(lax.axis_index("span") >= sizes[3] // 2)
+    @pl.when(lax.axis_index("span") > 0)
     def _():
         inner(sizes, direct, room_post, plen_post, dealt, cross_a, cross_b)
 

time: 15.2 us -> 14.9 us (0.980)
  waiting for transfers between devices: 2.96 us -> 2.74 us
    ppermute x2, waiting for transfers between devices: 0.43 us -> 0.21 us  [swap_span(): return lax.ppermute(value, ('aisle', 'span'), pairs)]
    ppermute x2, starting transfers between devices: 4 us -> 3.78 us  [shards(): lax.ppermute(jets[apart - 2], 'span', [(i, i ^ apart) for i in range(4)])]
    ppermute x2, starting transfers between devices: 0.53 us -> 0.75 us  [swap_span(): return lax.ppermute(value, ('aisle', 'span'), pairs)]
where the time goes in v15:
time: 14.9 us; the launch traced here: 14.8 us
  starting transfers between devices  7.94 us (53%)
  Pallas kernels  3.43 us (23%)
  waiting for transfers between devices  2.74 us (18%)
  between operations  0.68 us (5%)
    ppermute x2, starting transfers between devices, shards(): lax.ppermute(jets[apart - 2], 'span', [(i, i ^ apart) for i in range(4)])  3.78 us
    ppermute x2, starting transfers between devices, swap_aisle(): return lax.ppermute(value, 'aisle', pairs)  3.4 us
    ppermute x2, waiting for transfers between devices, shards(): lax.ppermute(jets[apart - 2], 'span', [(i, i ^ apart) for i in range(4)])  2.53 us
    pallas_call x1, Pallas kernels, shards(): call(functools.partial(collide_kernel, sizes, direct), [near(room_shape),...  1.37 us
    pallas_call x1, Pallas kernels, shards(): call(functools.partial(finish_kernel, sizes, direct), [near(room_shape),...  0.93 us
    pallas_call x1, Pallas kernels, shards(): call(functools.partial(local_kernel, sizes), [near(room_shape), near(plen...  0.86 us
    ppermute x2, starting transfers between devices, swap_span(): return lax.ppermute(value, ('aisle', 'span'), pairs)  0.75 us
  transfers between devices with their start and end apart: 6, of which 2 were waited for; matrix products, arithmetic and copies ran while one was open for 0% of the time, Pallas kernels for 8%

profile of v15, /device:TPU:0, one launch (start us, length us, event | category | flops | bytes accessed | tf_op | source)
XLA Modules:
  0.0 14.8 jit_solution(14114530042212302319)
XLA Ops:
  0.6 1.4 %collide_kernel.1 = (f32[19,4,16,128]{3,2,1,0:T(8,128)S(1)}, f32[19,16,128]{2,1,0:T(8,128)S(1)}, f32[104,128]{1,0:T(8,128)S(1)}, f32[112,128]{1,0:T(8,128)S(1)}, f32[16,1,640]{2,1,0:T(1,128)S(1)}) custom-call(f32[19,4,16,128]{3,2,1,0:T(8,128)} %bitcast.13, f32[19,16,128]{2,1,0:T(8,128)} %bitcast.14, s32[32]{0:T(128)} %cell_in.3, s32[32]{0:T(128)} %bitcast.15, ...), custom_call_target="tpu_custom_call" | custom-call | flops 100000 | bytes 1000000 | tf_op jit(solution)/shard_map/collide_kernel/pallas_call | solution.py:448
  2.0 3.4 %collective-permute-start.1 = (f32[112,128]{1,0:T(8,128)S(1)}, f32[112,128]{1,0:T(8,128)S(1)}, u32[]{:S(2)}, u32[]{:S(2)}) collective-permute-start(f32[112,128]{1,0:T(8,128)S(1)} %get-tuple-element.33), channel_id=1, source_target_pairs={{0,28},{4,8},{8,4},{12,16},{16,12},{20,24},{24,20},{28,0},{1,29},{... | collective-permute-start | bytes 172040 | tf_op jit(solution)/shard_map/ppermute | solution.py:414
  5.4 0.0 collective-permute-start
  5.4 0.2 %early_kernel.1 = (f32[19,4,16,128]{3,2,1,0:T(8,128)S(1)}, f32[120,128]{1,0:T(8,128)S(1)}, f32[128,128]{1,0:T(8,128)S(1)}, f32[4,1,640]{2,1,0:T(1,128)S(1)}, f32[4,1,640]{2,1,0:T(1,128)S(1)}) custom-call(f32[19,4,16,128]{3,2,1,0:T(8,128)S(1)} %get-tuple-element.25.room_in, ...), custom_call_target="tpu_custom_call", output_to_operand_aliasing={{0}: (0, {})} | custom-call | flops 100000 | bytes 1000000 | tf_op jit(solution)/shard_map/early_kernel/pallas_call | solution.py:462
  5.6 2.4 %collective-permute-start.4 = (f32[4,1,640]{2,1,0:T(1,128)S(1)}, f32[4,1,640]{2,1,0:T(1,128)S(1)}, u32[]{:S(2)}, u32[]{:S(2)}) collective-permute-start(f32[4,1,640]{2,1,0:T(1,128)S(1)} %get-tuple-element.44), channel_id=1, source_target_pairs={{0,2},{1,3},{2,0},{3,1},{4,6},{5,7},{6,4},{7,5},{8,10},{9,11},{10,... | collective-permute-start | bytes 30728 | tf_op jit(solution)/shard_map/ppermute | solution.py:470
  8.1 1.3 %collective-permute-start.5 = (f32[4,1,640]{2,1,0:T(1,128)S(1)}, f32[4,1,640]{2,1,0:T(1,128)S(1)}, u32[]{:S(2)}, u32[]{:S(2)}) collective-permute-start(f32[4,1,640]{2,1,0:T(1,128)S(1)} %get-tuple-element.45), channel_id=1, source_target_pairs={{0,3},{1,2},{2,1},{3,0},{4,7},{5,6},{6,5},{7,4},{8,11},{9,10},{10,... | collective-permute-start | bytes 30728 | tf_op jit(solution)/shard_map/ppermute | solution.py:470
  9.4 0.0 collective-permute-done.got_a
  9.4 0.0 collective-permute-done.1.got_b
  9.5 0.8 %collective-permute-start.2 = (f32[120,128]{1,0:T(8,128)S(1)}, f32[120,128]{1,0:T(8,128)S(1)}, u32[]{:S(2)}, u32[]{:S(2)}) collective-permute-start(f32[120,128]{1,0:T(8,128)S(1)} %get-tuple-element.36.crossing), channel_id=1, source_target_pairs={{0,1},{1,0},{2,3},{3,2},{4,5},{5,4},{6,7},{7,6},{8,9},{9,8},{10,11... | collective-permute-start | bytes 184328 | tf_op jit(solution)/shard_map/ppermute | solution.py:425
  10.2 0.0 collective-permute-start.3
  10.2 0.9 %local_kernel.1 = (f32[19,4,16,128]{3,2,1,0:T(8,128)S(1)}, f32[19,16,128]{2,1,0:T(8,128)S(1)}, f32[17,16,128]{2,1,0:T(8,128)S(1)}) custom-call(f32[19,4,16,128]{3,2,1,0:T(8,128)S(1)} %get-tuple-element.31.room_post, f32[19,16,128]{2,1,0:T(8,128)S(1)} %get-tuple-element.26.plen_post, f32[120,128]{1,0:T(8,128)S(1)} %get-tuple-element.36.crossing, s32[32]{0:T(128)} %cell_in.3, ...), custom_call_target="tpu_custom_call" | custom-call | flops 1000000000 | bytes 1000000 | tf_op jit(solution)/shard_map/local_kernel/pallas_call | solution.py:488
  11.1 0.0 collective-permute-done.4.rest_0_
  11.1 2.5 %collective-permute-done.5.rest_1_ = f32[4,1,640]{2,1,0:T(1,128)S(1)} collective-permute-done((f32[4,1,640]{2,1,0:T(1,128)S(1)}, f32[4,1,640]{2,1,0:T(1,128)S(1)}, u32[]{:S(2)}, u32[]{:S(2)}) %collective-permute-start.5) | collective-permute-done | bytes 10272 | tf_op jit(solution)/shard_map/ppermute | solution.py:470
  13.6 0.2 %collective-permute-done.2.got_a = f32[120,128]{1,0:T(8,128)S(1)} collective-permute-done((f32[120,128]{1,0:T(8,128)S(1)}, f32[120,128]{1,0:T(8,128)S(1)}, u32[]{:S(2)}, u32[]{:S(2)}) %collective-permute-start.2) | collective-permute-done | bytes 61472 | tf_op jit(solution)/shard_map/ppermute | solution.py:425
  13.9 0.0 collective-permute-done.3.got_b
  13.9 0.9 %finish_kernel.1 = (f32[19,4,16,128]{3,2,1,0:T(8,128)S(1)}, f32[19,16,128]{2,1,0:T(8,128)S(1)}, f32[19,4,16,128]{3,2,1,0:T(8,128)}, f32[19,16,128]{2,1,0:T(8,128)}) custom-call(f32[19,4,16,128]{3,2,1,0:T(8,128)S(1)} %get-tuple-element.40.room_in, f32[19,16,128]{2,1,0:T(8,128)S(1)} %get-tuple-element.41.plen_in, ...), custom_call_target="tpu_custom_call", output_to_operand_aliasing={{0}: (0, {}), {1}: (1, {})} | custom-call | flops 100000 | bytes 1000000 | tf_op jit(solution)/shard_map/finish_kernel/pallas_call | solution.py:502
  (3 shorter events, 0.1 us)
Async XLA Ops:
  2.0 7.4 %collective-permute-start.1 = (f32[112,128]{1,0:T(8,128)S(1)}, f32[112,128]{1,0:T(8,128)S(1)}, u32[]{:S(2)}, u32[]{:S(2)}) collective-permute-start(f32[112,128]{1,0:T(8,128)S(1)} %get-tuple-element.33), channel_id=1, source_target_pairs={{0,28},{4,8},{8,4},{12,16},{16,12},{20,24},{24,20},{28,0},{1,29},{... | collective-permute-start | bytes 172040 | tf_op jit(solution)/shard_map/ppermute | solution.py:414
  5.4 4.0 %collective-permute-start = (f32[104,128]{1,0:T(8,128)S(1)}, f32[104,128]{1,0:T(8,128)S(1)}, u32[]{:S(2)}, u32[]{:S(2)}) collective-permute-start(f32[104,128]{1,0:T(8,128)S(1)} %get-tuple-element.32), channel_id=1, source_target_pairs={{0,4},{4,0},{8,12},{12,8},{16,20},{20,16},{24,28},{28,24},{1,5},{5... | collective-permute-start | bytes 159752 | tf_op jit(solution)/shard_map/ppermute | solution.py:414
  5.6 5.5 %collective-permute-start.4 = (f32[4,1,640]{2,1,0:T(1,128)S(1)}, f32[4,1,640]{2,1,0:T(1,128)S(1)}, u32[]{:S(2)}, u32[]{:S(2)}) collective-permute-start(f32[4,1,640]{2,1,0:T(1,128)S(1)} %get-tuple-element.44), channel_id=1, source_target_pairs={{0,2},{1,3},{2,0},{3,1},{4,6},{5,7},{6,4},{7,5},{8,10},{9,11},{10,... | collective-permute-start | bytes 30728 | tf_op jit(solution)/shard_map/ppermute | solution.py:470
  8.1 5.6 %collective-permute-start.5 = (f32[4,1,640]{2,1,0:T(1,128)S(1)}, f32[4,1,640]{2,1,0:T(1,128)S(1)}, u32[]{:S(2)}, u32[]{:S(2)}) collective-permute-start(f32[4,1,640]{2,1,0:T(1,128)S(1)} %get-tuple-element.45), channel_id=1, source_target_pairs={{0,3},{1,2},{2,1},{3,0},{4,7},{5,6},{6,5},{7,4},{8,11},{9,10},{10,... | collective-permute-start | bytes 30728 | tf_op jit(solution)/shard_map/ppermute | solution.py:470
  9.5 4.4 %collective-permute-start.2 = (f32[120,128]{1,0:T(8,128)S(1)}, f32[120,128]{1,0:T(8,128)S(1)}, u32[]{:S(2)}, u32[]{:S(2)}) collective-permute-start(f32[120,128]{1,0:T(8,128)S(1)} %get-tuple-element.36.crossing), channel_id=1, source_target_pairs={{0,1},{1,0},{2,3},{3,2},{4,5},{5,4},{6,7},{7,6},{8,9},{9,8},{10,11... | collective-permute-start | bytes 184328 | tf_op jit(solution)/shard_map/ppermute | solution.py:425
  10.2 3.6 %collective-permute-start.3 = (f32[128,128]{1,0:T(8,128)S(1)}, f32[128,128]{1,0:T(8,128)S(1)}, u32[]{:S(2)}, u32[]{:S(2)}) collective-permute-start(f32[128,128]{1,0:T(8,128)S(1)} %get-tuple-element.42), channel_id=1, source_target_pairs={{0,4},{1,2},{2,1},{3,7},{4,0},{5,6},{6,5},{7,3},{8,12},{9,10},{10,... | collective-permute-start | bytes 196616 | tf_op jit(solution)/shard_map/ppermute | solution.py:425

commit v16 on v15

--- a/solution.py
+++ b/solution.py
@@ -120,7 +120,7 @@
         ((plen_in, plen_buf), (cell_in, cells), (owner_in, owners), (class_in, classes)))]
     order = [0, ca - 1] + list(range(1, ca - 1))
     planes = [pltpu.make_async_copy(room_in.at[:, x], room_post.at[:, x], sems.at[4 + x]) for x in order]
-    for copy in copies[:1] + planes + copies[1:]:
+    for copy in copies[1:] + copies[:1] + planes:
         copy.start()
     dealt[...] = jnp.zeros_like(dealt)
     copies[0].wait()
@@ -376,8 +376,11 @@
     def _():
         enter(got_b, False)
 
-    plen_copy = pltpu.make_async_copy(plen, plen_out, sems.at[0])
-    plen_copy.start()
+    parts = [pltpu.make_async_copy(room.at[low_q:high_q], room_out.at[low_q:high_q], sems.at[1 + i])
+             for i, (low_q, high_q) in enumerate(((0, 5), (6, 11), (11, 19), (5, 6)))]
+    parts.append(pltpu.make_async_copy(plen, plen_out, sems.at[0]))
+    for part in parts[:2] + parts[4:]:
+        part.start()
     bricks = []
     if direct:
         start = 5 * (rows + cs)
@@ -388,10 +391,10 @@
     for k, q in enumerate(UPWARD):
         for x in range(ca):
             room[q, x, 0:cs] = room[q, x, 0:cs] + sums[k][x * cs : (x + 1) * cs]
-    room_copy = pltpu.make_async_copy(room, room_out, sems.at[1])
-    room_copy.start()
-    plen_copy.wait()
-    room_copy.wait()
+    for part in parts[2:4]:
+        part.start()
+    for part in parts:
+        part.wait()
 
 
 def call(kernel, outs, in_specs, out_specs=None, scratch=(), aliases={}, flops=100_000, moved=1_000_000):
@@ -505,7 +508,7 @@
          jax.ShapeDtypeStruct(plen_shape, F32)],
         [VMEM] * (6 + len(got_jets)),
         out_specs=[VMEM, VMEM, HBM, HBM],
-        scratch=[pltpu.SemaphoreType.DMA((2,))],
+        scratch=[pltpu.SemaphoreType.DMA((5,))],
         aliases={0: 0, 1: 1},
     )(room_part, plen_part, in_a, in_b, places, inflow, *got_jets)
     room_next = room_next.reshape(19, ca, blocks, cs, LANES).transpose(0, 1, 3, 2, 4).reshape(room_pops.shape)

time: 14.9 us -> 15 us (level)
  no operation moved by 1% of the time
where the time goes in v16:
time: 15 us; the launch traced here: 14.8 us
  starting transfers between devices  7.94 us (53%)
  Pallas kernels  3.45 us (23%)
  waiting for transfers between devices  2.74 us (18%)
  between operations  0.68 us (5%)
    ppermute x2, starting transfers between devices, shards(): lax.ppermute(jets[apart - 2], 'span', [(i, i ^ apart) for i in range(4)])  3.78 us
    ppermute x2, starting transfers between devices, swap_aisle(): return lax.ppermute(value, 'aisle', pairs)  3.4 us
    ppermute x2, waiting for transfers between devices, shards(): lax.ppermute(jets[apart - 2], 'span', [(i, i ^ apart) for i in range(4)])  2.53 us
    pallas_call x1, Pallas kernels, shards(): call(functools.partial(collide_kernel, sizes, direct), [near(room_shape),...  1.37 us
    pallas_call x1, Pallas kernels, shards(): call(functools.partial(finish_kernel, sizes, direct), [near(room_shape),...  0.94 us
    pallas_call x1, Pallas kernels, shards(): call(functools.partial(local_kernel, sizes), [near(room_shape), near(plen...  0.86 us
    ppermute x2, starting transfers between devices, swap_span(): return lax.ppermute(value, ('aisle', 'span'), pairs)  0.75 us
  transfers between devices with their start and end apart: 6, of which 2 were waited for; matrix products, arithmetic and copies ran while one was open for 0% of the time, Pallas kernels for 8%

profile of v16, /device:TPU:0, one launch (start us, length us, event | category | flops | bytes accessed | tf_op | source)
XLA Modules:
  0.0 14.8 jit_solution(17339383190368380513)
XLA Ops:
  0.6 1.4 %collide_kernel.1 = (f32[19,4,16,128]{3,2,1,0:T(8,128)S(1)}, f32[19,16,128]{2,1,0:T(8,128)S(1)}, f32[104,128]{1,0:T(8,128)S(1)}, f32[112,128]{1,0:T(8,128)S(1)}, f32[16,1,640]{2,1,0:T(1,128)S(1)}) custom-call(f32[19,4,16,128]{3,2,1,0:T(8,128)} %bitcast.13, f32[19,16,128]{2,1,0:T(8,128)} %bitcast.14, s32[32]{0:T(128)} %cell_in.3, s32[32]{0:T(128)} %bitcast.15, ...), custom_call_target="tpu_custom_call" | custom-call | flops 100000 | bytes 1000000 | tf_op jit(solution)/shard_map/collide_kernel/pallas_call | solution.py:451
  2.0 3.4 %collective-permute-start.1 = (f32[112,128]{1,0:T(8,128)S(1)}, f32[112,128]{1,0:T(8,128)S(1)}, u32[]{:S(2)}, u32[]{:S(2)}) collective-permute-start(f32[112,128]{1,0:T(8,128)S(1)} %get-tuple-element.33), channel_id=1, source_target_pairs={{0,28},{4,8},{8,4},{12,16},{16,12},{20,24},{24,20},{28,0},{1,29},{... | collective-permute-start | bytes 172040 | tf_op jit(solution)/shard_map/ppermute | solution.py:417
  5.4 0.0 collective-permute-start
  5.4 0.2 %early_kernel.1 = (f32[19,4,16,128]{3,2,1,0:T(8,128)S(1)}, f32[120,128]{1,0:T(8,128)S(1)}, f32[128,128]{1,0:T(8,128)S(1)}, f32[4,1,640]{2,1,0:T(1,128)S(1)}, f32[4,1,640]{2,1,0:T(1,128)S(1)}) custom-call(f32[19,4,16,128]{3,2,1,0:T(8,128)S(1)} %get-tuple-element.25.room_in, ...), custom_call_target="tpu_custom_call", output_to_operand_aliasing={{0}: (0, {})} | custom-call | flops 100000 | bytes 1000000 | tf_op jit(solution)/shard_map/early_kernel/pallas_call | solution.py:465
  5.6 2.4 %collective-permute-start.4 = (f32[4,1,640]{2,1,0:T(1,128)S(1)}, f32[4,1,640]{2,1,0:T(1,128)S(1)}, u32[]{:S(2)}, u32[]{:S(2)}) collective-permute-start(f32[4,1,640]{2,1,0:T(1,128)S(1)} %get-tuple-element.44), channel_id=1, source_target_pairs={{0,2},{1,3},{2,0},{3,1},{4,6},{5,7},{6,4},{7,5},{8,10},{9,11},{10,... | collective-permute-start | bytes 30728 | tf_op jit(solution)/shard_map/ppermute | solution.py:473
  8.1 1.3 %collective-permute-start.5 = (f32[4,1,640]{2,1,0:T(1,128)S(1)}, f32[4,1,640]{2,1,0:T(1,128)S(1)}, u32[]{:S(2)}, u32[]{:S(2)}) collective-permute-start(f32[4,1,640]{2,1,0:T(1,128)S(1)} %get-tuple-element.45), channel_id=1, source_target_pairs={{0,3},{1,2},{2,1},{3,0},{4,7},{5,6},{6,5},{7,4},{8,11},{9,10},{10,... | collective-permute-start | bytes 30728 | tf_op jit(solution)/shard_map/ppermute | solution.py:473
  9.4 0.0 collective-permute-done.got_a
  9.4 0.0 collective-permute-done.1.got_b
  9.5 0.8 %collective-permute-start.2 = (f32[120,128]{1,0:T(8,128)S(1)}, f32[120,128]{1,0:T(8,128)S(1)}, u32[]{:S(2)}, u32[]{:S(2)}) collective-permute-start(f32[120,128]{1,0:T(8,128)S(1)} %get-tuple-element.36.crossing), channel_id=1, source_target_pairs={{0,1},{1,0},{2,3},{3,2},{4,5},{5,4},{6,7},{7,6},{8,9},{9,8},{10,11... | collective-permute-start | bytes 184328 | tf_op jit(solution)/shard_map/ppermute | solution.py:428
  10.2 0.0 collective-permute-start.3
  10.2 0.9 %local_kernel.1 = (f32[19,4,16,128]{3,2,1,0:T(8,128)S(1)}, f32[19,16,128]{2,1,0:T(8,128)S(1)}, f32[17,16,128]{2,1,0:T(8,128)S(1)}) custom-call(f32[19,4,16,128]{3,2,1,0:T(8,128)S(1)} %get-tuple-element.31.room_post, f32[19,16,128]{2,1,0:T(8,128)S(1)} %get-tuple-element.26.plen_post, f32[120,128]{1,0:T(8,128)S(1)} %get-tuple-element.36.crossing, s32[32]{0:T(128)} %cell_in.3, ...), custom_call_target="tpu_custom_call" | custom-call | flops 1000000000 | bytes 1000000 | tf_op jit(solution)/shard_map/local_kernel/pallas_call | solution.py:491
  11.1 0.0 collective-permute-done.4.rest_0_
  11.1 2.5 %collective-permute-done.5.rest_1_ = f32[4,1,640]{2,1,0:T(1,128)S(1)} collective-permute-done((f32[4,1,640]{2,1,0:T(1,128)S(1)}, f32[4,1,640]{2,1,0:T(1,128)S(1)}, u32[]{:S(2)}, u32[]{:S(2)}) %collective-permute-start.5) | collective-permute-done | bytes 10272 | tf_op jit(solution)/shard_map/ppermute | solution.py:473
  13.7 0.2 %collective-permute-done.2.got_a = f32[120,128]{1,0:T(8,128)S(1)} collective-permute-done((f32[120,128]{1,0:T(8,128)S(1)}, f32[120,128]{1,0:T(8,128)S(1)}, u32[]{:S(2)}, u32[]{:S(2)}) %collective-permute-start.2) | collective-permute-done | bytes 61472 | tf_op jit(solution)/shard_map/ppermute | solution.py:428
  13.9 0.0 collective-permute-done.3.got_b
  13.9 0.9 %finish_kernel.1 = (f32[19,4,16,128]{3,2,1,0:T(8,128)S(1)}, f32[19,16,128]{2,1,0:T(8,128)S(1)}, f32[19,4,16,128]{3,2,1,0:T(8,128)}, f32[19,16,128]{2,1,0:T(8,128)}) custom-call(f32[19,4,16,128]{3,2,1,0:T(8,128)S(1)} %get-tuple-element.40.room_in, f32[19,16,128]{2,1,0:T(8,128)S(1)} %get-tuple-element.41.plen_in, ...), custom_call_target="tpu_custom_call", output_to_operand_aliasing={{0}: (0, {}), {1}: (1, {})} | custom-call | flops 100000 | bytes 1000000 | tf_op jit(solution)/shard_map/finish_kernel/pallas_call | solution.py:505
  (3 shorter events, 0.1 us)
Async XLA Ops:
  2.0 7.4 %collective-permute-start.1 = (f32[112,128]{1,0:T(8,128)S(1)}, f32[112,128]{1,0:T(8,128)S(1)}, u32[]{:S(2)}, u32[]{:S(2)}) collective-permute-start(f32[112,128]{1,0:T(8,128)S(1)} %get-tuple-element.33), channel_id=1, source_target_pairs={{0,28},{4,8},{8,4},{12,16},{16,12},{20,24},{24,20},{28,0},{1,29},{... | collective-permute-start | bytes 172040 | tf_op jit(solution)/shard_map/ppermute | solution.py:417
  5.4 4.0 %collective-permute-start = (f32[104,128]{1,0:T(8,128)S(1)}, f32[104,128]{1,0:T(8,128)S(1)}, u32[]{:S(2)}, u32[]{:S(2)}) collective-permute-start(f32[104,128]{1,0:T(8,128)S(1)} %get-tuple-element.32), channel_id=1, source_target_pairs={{0,4},{4,0},{8,12},{12,8},{16,20},{20,16},{24,28},{28,24},{1,5},{5... | collective-permute-start | bytes 159752 | tf_op jit(solution)/shard_map/ppermute | solution.py:417
  5.6 5.5 %collective-permute-start.4 = (f32[4,1,640]{2,1,0:T(1,128)S(1)}, f32[4,1,640]{2,1,0:T(1,128)S(1)}, u32[]{:S(2)}, u32[]{:S(2)}) collective-permute-start(f32[4,1,640]{2,1,0:T(1,128)S(1)} %get-tuple-element.44), channel_id=1, source_target_pairs={{0,2},{1,3},{2,0},{3,1},{4,6},{5,7},{6,4},{7,5},{8,10},{9,11},{10,... | collective-permute-start | bytes 30728 | tf_op jit(solution)/shard_map/ppermute | solution.py:473
  8.1 5.6 %collective-permute-start.5 = (f32[4,1,640]{2,1,0:T(1,128)S(1)}, f32[4,1,640]{2,1,0:T(1,128)S(1)}, u32[]{:S(2)}, u32[]{:S(2)}) collective-permute-start(f32[4,1,640]{2,1,0:T(1,128)S(1)} %get-tuple-element.45), channel_id=1, source_target_pairs={{0,3},{1,2},{2,1},{3,0},{4,7},{5,6},{6,5},{7,4},{8,11},{9,10},{10,... | collective-permute-start | bytes 30728 | tf_op jit(solution)/shard_map/ppermute | solution.py:473
  9.5 4.4 %collective-permute-start.2 = (f32[120,128]{1,0:T(8,128)S(1)}, f32[120,128]{1,0:T(8,128)S(1)}, u32[]{:S(2)}, u32[]{:S(2)}) collective-permute-start(f32[120,128]{1,0:T(8,128)S(1)} %get-tuple-element.36.crossing), channel_id=1, source_target_pairs={{0,1},{1,0},{2,3},{3,2},{4,5},{5,4},{6,7},{7,6},{8,9},{9,8},{10,11... | collective-permute-start | bytes 184328 | tf_op jit(solution)/shard_map/ppermute | solution.py:428
  10.2 3.6 %collective-permute-start.3 = (f32[128,128]{1,0:T(8,128)S(1)}, f32[128,128]{1,0:T(8,128)S(1)}, u32[]{:S(2)}, u32[]{:S(2)}) collective-permute-start(f32[128,128]{1,0:T(8,128)S(1)} %get-tuple-element.42), channel_id=1, source_target_pairs={{0,4},{1,2},{2,1},{3,7},{4,0},{5,6},{6,5},{7,3},{8,12},{9,10},{10,... | collective-permute-start | bytes 196616 | tf_op jit(solution)/shard_map/ppermute | solution.py:428

commit v17 on v15

--- a/solution.py
+++ b/solution.py
@@ -105,6 +105,10 @@
     return start
 
 
+def first_up(n_span):
+    return (lax.axis_index("aisle") % 2 == 0) == (lax.axis_index("span") == n_span - 1)
+
+
 def collide_plane(room, x):
     for r in range(0, room.shape[2], 8):
         post = collide([room[q, x, r : r + 8] for q in range(19)])
@@ -154,7 +158,7 @@
     for i in range(2):
         planes[i].wait()
         collide_plane(room_post, order[i])
-    even = lax.axis_index("aisle") % 2 == 0
+    even = first_up(n_span)
     for k in range(5):
         up, down = X_UP[k], X_DOWN[k]
         rising = raised(room_post[up, ca - 1], VELOCITIES[up][2], cs)
@@ -179,8 +183,8 @@
     return sums
 
 
-def local_kernel(sizes, room_post, plen_post, crossing, cell_in, owner_in, room_part, plen_part, places, cells, owners,
-                 sems):
+def local_kernel(sizes, room_post, plen_post, crossing, *rest):
+    cell_in, owner_in, room_part, plen_part, places, cells, owners, sems = rest[-8:]
     del crossing
     ca, cs, blocks, n_span, per_brick = sizes
     rows = blocks * cs
@@ -247,7 +251,7 @@
 def early_kernel(sizes, direct, room_in, plen_post, dealt, room_post, cross_a, cross_b, *jets):
     start = 2 * CAP
     for jet in jets:
-        jet[...] = dealt[start : start + CAP]
+        jet[0:CAP] = dealt[start : start + CAP]
         start = start + CAP
 
     @pl.when(lax.axis_index("span") == 0)
@@ -268,7 +272,7 @@
 def pack_kernel(sizes, got_a, got_b, part_a, part_b, cross_a, cross_b):
     ca, cs, blocks, n_span, per_brick = sizes
     rows = blocks * cs
-    even = lax.axis_index("aisle") % 2 == 0
+    even = first_up(n_span)
     low = lax.axis_index("span") % 2 == 0
     group = lax.broadcasted_iota(jnp.int32, (rows, LANES), 0) % cs
     cross_a[...] = part_a[...]
@@ -304,7 +308,7 @@
 def aisle_kernel(sizes, direct, room_in, plen_in, got_a, got_b, jets, places, room, plen, inflow):
     ca, cs, blocks, n_span, per_brick = sizes
     rows = blocks * cs
-    even = lax.axis_index("aisle") % 2 == 0
+    even = first_up(n_span)
     for k in range(5):
         for q, x, first, second in ((X_UP[k], 0, got_b, got_a), (X_DOWN[k], ca - 1, got_a, got_b)):
             cy = VELOCITIES[q][1]
@@ -408,10 +412,14 @@
     )
 
 
-def swap_aisle(value, odd):
-    count = lax.axis_size("aisle")
-    pairs = [(i, (i ^ 1 if not odd else i + 1 if i % 2 else i - 1) % count) for i in range(count)]
-    return lax.ppermute(value, "aisle", pairs)
+def swap_aisle(value, second):
+    count, across = lax.axis_size("aisle"), lax.axis_size("span")
+    pairs = []
+    for a in range(count):
+        for s in range(across):
+            b = a ^ 1 if second != (s == across - 1) else (a + 1 if a % 2 else a - 1) % count
+            pairs.append((a * across + s, b * across + s))
+    return lax.ppermute(value, ("aisle", "span"), pairs)
 
 
 def swap_span(value, odd):
@@ -444,24 +452,26 @@
     tile_cell, tile_owner, tile_class = far(tile_cell), far(tile_owner.reshape(tiles)), far(tile_class)
     numbers = pltpu.SMEM((tiles,), jnp.int32)
 
-    dealt_shape, jet_shape = (n_span * CAP, 1, 5 * hp), (CAP, 1, 5 * hp)
+    dealt_shape = (n_span * CAP, 1, 5 * hp)
+    between = -(-(halo + 4) * LANES // (5 * hp))
+    jet_shapes = [near((CAP, 1, 5 * hp)), near((between, 1, 5 * hp))] if direct else []
     room_post, plen_post, swap_a, swap_b, dealt = call(
         functools.partial(collide_kernel, sizes, direct),
-        [near(room_shape), near(plen_shape), near((halo, LANES)), near((halo + 8, LANES)),
+        [near(room_shape), near(plen_shape), near((halo + 8, LANES)), near((halo, LANES)),
          near(dealt_shape)],
         [HBM] * 5,
         scratch=[near((ca * cs, 1, 5 * hp)), near(plen_shape), numbers, numbers, numbers,
                  pltpu.SemaphoreType.DMA((4 + ca,))],
     )(room, plen, tile_cell, tile_owner, tile_class)
+    got_a = swap_aisle(swap_a, False)
     got_b = swap_aisle(swap_b, True)
-    got_a = swap_aisle(swap_a, False)
 
     upto8 = lambda count: count + -count % 8
     wide = upto8(5 * (rows + ca) + (5 * CAP if direct else 0))
-    cross_shapes = [near((wide, LANES)), near((wide + 8, LANES))]
+    cross_shapes = [near((wide + 8, LANES)), near((wide, LANES))]
     room_post, part_a, part_b, *jets = call(
         functools.partial(early_kernel, sizes, direct),
-        [near(room_shape)] + cross_shapes + [near(jet_shape)] * (2 if direct else 0),
+        [near(room_shape)] + cross_shapes + jet_shapes,
         [VMEM] * 3,
         aliases={0: 0},
     )(room_post, plen_post, dealt)
@@ -488,10 +498,10 @@
     room_part, plen_part, places = call(
         functools.partial(local_kernel, sizes),
         [near(room_shape), near(plen_shape), near((n_span * CAP + 1, ca * cs, LANES))],
-        [VMEM, VMEM, VMEM, HBM, HBM],
+        [VMEM] * (3 + len(got_jets[1:])) + [HBM, HBM],
         scratch=[numbers, numbers, pltpu.SemaphoreType.DMA((2,))],
         flops=10**9,
-    )(room_post, plen_post, cross_a, tile_cell, tile_owner)
+    )(room_post, plen_post, cross_a, *got_jets[1:], tile_cell, tile_owner)
     room_part, plen_part, inflow = call(
         functools.partial(aisle_kernel, sizes, direct),
         [near(room_shape), near(plen_shape), near((5, ca * cs, LANES))],

time: 14.9 us -> 15.1 us (1.013)
  starting transfers between devices: 7.94 us -> 9.51 us
  waiting for transfers between devices: 2.74 us -> 1.32 us
    ppermute x2, starting transfers between devices: 0.75 us -> 3.29 us  [swap_span(): return lax.ppermute(value, ('aisle', 'span'), pairs)]
    ppermute x2, waiting for transfers between devices: 2.53 us -> 0.01 us  [shards(): lax.ppermute(jets[apart - 2], 'span', [(i, i ^ apart) for i in range(4)])]
    ppermute x2, starting transfers between devices: 3.78 us -> 2.68 us  [shards(): lax.ppermute(jets[apart - 2], 'span', [(i, i ^ apart) for i in range(4)])]
    ppermute x2, waiting for transfers between devices: 0.21 us -> 1.31 us  [swap_span(): return lax.ppermute(value, ('aisle', 'span'), pairs)]
  transfers between devices with their start and end apart: 6 -> 6, of which waited for: 2 -> 1; matrix products, arithmetic and copies ran while one was open for 0% -> 0% of each run, Pallas kernels for 8% -> 8%
where the time goes in v17:
time: 15.1 us; the launch traced here: 15 us
  starting transfers between devices  9.51 us (63%)
  Pallas kernels  3.44 us (23%)
  waiting for transfers between devices  1.32 us (9%)
  between operations  0.69 us (5%)
    ppermute x2, starting transfers between devices, swap_aisle(): return lax.ppermute(value, ('aisle', 'span'), pairs)  3.55 us
    ppermute x2, starting transfers between devices, swap_span(): return lax.ppermute(value, ('aisle', 'span'), pairs)  3.29 us
    ppermute x2, starting transfers between devices, shards(): lax.ppermute(jets[apart - 2], 'span', [(i, i ^ apart) for i in range(4)])  2.68 us
    pallas_call x1, Pallas kernels, shards(): call(functools.partial(collide_kernel, sizes, direct), [near(room_shape),...  1.37 us
    ppermute x2, waiting for transfers between devices, swap_span(): return lax.ppermute(value, ('aisle', 'span'), pairs)  1.31 us
    pallas_call x1, Pallas kernels, shards(): call(functools.partial(finish_kernel, sizes, direct), [near(room_shape),...  0.93 us
    pallas_call x1, Pallas kernels, shards(): call(functools.partial(local_kernel, sizes), [near(room_shape), near(plen...  0.86 us
  transfers between devices with their start and end apart: 6, of which 1 were waited for; matrix products, arithmetic and copies ran while one was open for 0% of the time, Pallas kernels for 8%

profile of v17, /device:TPU:0, one launch (start us, length us, event | category | flops | bytes accessed | tf_op | source)
XLA Modules:
  0.0 15.0 jit_solution(8926803826069167085)
XLA Ops:
  0.6 1.4 %collide_kernel.1 = (f32[19,4,16,128]{3,2,1,0:T(8,128)S(1)}, f32[19,16,128]{2,1,0:T(8,128)S(1)}, f32[112,128]{1,0:T(8,128)S(1)}, f32[104,128]{1,0:T(8,128)S(1)}, f32[16,1,640]{2,1,0:T(1,128)S(1)}) custom-call(f32[19,4,16,128]{3,2,1,0:T(8,128)} %bitcast.13, f32[19,16,128]{2,1,0:T(8,128)} %bitcast.14, s32[32]{0:T(128)} %rest_1_.1, s32[32]{0:T(128)} %bitcast.15, ...), custom_call_target="tpu_custom_call" | custom-call | flops 100000 | bytes 1000000 | tf_op jit(solution)/shard_map/collide_kernel/pallas_call | solution.py:458
  2.0 3.4 %collective-permute-start = (f32[112,128]{1,0:T(8,128)S(1)}, f32[112,128]{1,0:T(8,128)S(1)}, u32[]{:S(2)}, u32[]{:S(2)}) collective-permute-start(f32[112,128]{1,0:T(8,128)S(1)} %get-tuple-element.32), channel_id=1, source_target_pairs={{0,28},{1,29},{2,30},{3,7},{4,8},{5,9},{6,10},{7,3},{8,4},{9,5},{1... | collective-permute-start | bytes 172040 | tf_op jit(solution)/shard_map/ppermute | solution.py:422
  5.4 0.2 %early_kernel.1 = (f32[19,4,16,128]{3,2,1,0:T(8,128)S(1)}, f32[128,128]{1,0:T(8,128)S(1)}, f32[120,128]{1,0:T(8,128)S(1)}, f32[4,1,640]{2,1,0:T(1,128)S(1)}, f32[22,1,640]{2,1,0:T(1,128)S(1)}) custom-call(f32[19,4,16,128]{3,2,1,0:T(8,128)S(1)} %get-tuple-element.25.room_in, ...), custom_call_target="tpu_custom_call", output_to_operand_aliasing={{0}: (0, {})} | custom-call | flops 100000 | bytes 1000000 | tf_op jit(solution)/shard_map/early_kernel/pallas_call | solution.py:472
  5.6 1.6 %collective-permute-start.2 = (f32[22,1,640]{2,1,0:T(1,128)S(1)}, f32[22,1,640]{2,1,0:T(1,128)S(1)}, u32[]{:S(2)}, u32[]{:S(2)}) collective-permute-start(f32[22,1,640]{2,1,0:T(1,128)S(1)} %get-tuple-element.37), channel_id=1, source_target_pairs={{0,3},{1,2},{2,1},{3,0},{4,7},{5,6},{6,5},{7,4},{8,11},{9,10},{10,... | collective-permute-start | bytes 168968 | tf_op jit(solution)/shard_map/ppermute | solution.py:480
  7.2 0.1 collective-permute-start.1
  7.4 1.1 %collective-permute-start.5 = (f32[4,1,640]{2,1,0:T(1,128)S(1)}, f32[4,1,640]{2,1,0:T(1,128)S(1)}, u32[]{:S(2)}, u32[]{:S(2)}) collective-permute-start(f32[4,1,640]{2,1,0:T(1,128)S(1)} %get-tuple-element.45), channel_id=1, source_target_pairs={{0,2},{1,3},{2,0},{3,1},{4,6},{5,7},{6,4},{7,5},{8,10},{9,11},{10,... | collective-permute-start | bytes 30728 | tf_op jit(solution)/shard_map/ppermute | solution.py:480
  8.5 0.0 collective-permute-done.1.got_b
  8.5 0.0 collective-permute-done.got_a
  8.5 0.3 %collective-permute-start.4 = (f32[120,128]{1,0:T(8,128)S(1)}, f32[120,128]{1,0:T(8,128)S(1)}, u32[]{:S(2)}, u32[]{:S(2)}) collective-permute-start(f32[120,128]{1,0:T(8,128)S(1)} %get-tuple-element.43), channel_id=1, source_target_pairs={{0,4},{1,2},{2,1},{3,7},{4,0},{5,6},{6,5},{7,3},{8,12},{9,10},{10,... | collective-permute-start | bytes 184328 | tf_op jit(solution)/shard_map/ppermute | solution.py:433
  8.8 3.0 %collective-permute-start.3 = (f32[128,128]{1,0:T(8,128)S(1)}, f32[128,128]{1,0:T(8,128)S(1)}, u32[]{:S(2)}, u32[]{:S(2)}) collective-permute-start(f32[128,128]{1,0:T(8,128)S(1)} %get-tuple-element.36.crossing), channel_id=1, source_target_pairs={{0,1},{1,0},{2,3},{3,2},{4,5},{5,4},{6,7},{7,6},{8,9},{9,8},{10,11... | collective-permute-start | bytes 196616 | tf_op jit(solution)/shard_map/ppermute | solution.py:433
  11.8 0.0 collective-permute-done.2.rest_0_.rest_1_
  11.8 0.9 %local_kernel.1 = (f32[19,4,16,128]{3,2,1,0:T(8,128)S(1)}, f32[19,16,128]{2,1,0:T(8,128)S(1)}, f32[17,16,128]{2,1,0:T(8,128)S(1)}) custom-call(f32[19,4,16,128]{3,2,1,0:T(8,128)S(1)} %get-tuple-element.31.room_post, f32[19,16,128]{2,1,0:T(8,128)S(1)} %get-tuple-element.26.plen_post, f32[128,128]{1,0:T(8,128)S(1)} %get-tuple-element.36.crossing, ...), custom_call_target="tpu_custom_call" | custom-call | flops 1000000000 | bytes 1000000 | tf_op jit(solution)/shard_map/local_kernel/pallas_call | solution.py:498
  12.7 0.0 collective-permute-done.5.rest_0_
  12.7 0.0 collective-permute-done.4.got_b
  12.7 1.3 %collective-permute-done.3.got_a = f32[128,128]{1,0:T(8,128)S(1)} collective-permute-done((f32[128,128]{1,0:T(8,128)S(1)}, f32[128,128]{1,0:T(8,128)S(1)}, u32[]{:S(2)}, u32[]{:S(2)}) %collective-permute-start.3) | collective-permute-done | bytes 65568 | tf_op jit(solution)/shard_map/ppermute | solution.py:433
  14.0 0.9 %finish_kernel.1 = (f32[19,4,16,128]{3,2,1,0:T(8,128)S(1)}, f32[19,16,128]{2,1,0:T(8,128)S(1)}, f32[19,4,16,128]{3,2,1,0:T(8,128)}, f32[19,16,128]{2,1,0:T(8,128)}) custom-call(f32[19,4,16,128]{3,2,1,0:T(8,128)S(1)} %get-tuple-element.41.room_in, f32[19,16,128]{2,1,0:T(8,128)S(1)} %get-tuple-element.42.plen_in, ...), custom_call_target="tpu_custom_call", output_to_operand_aliasing={{0}: (0, {}), {1}: (1, {})} | custom-call | flops 100000 | bytes 1000000 | tf_op jit(solution)/shard_map/finish_kernel/pallas_call | solution.py:512
  (3 shorter events, 0.1 us)
Async XLA Ops:
  2.0 6.5 %collective-permute-start = (f32[112,128]{1,0:T(8,128)S(1)}, f32[112,128]{1,0:T(8,128)S(1)}, u32[]{:S(2)}, u32[]{:S(2)}) collective-permute-start(f32[112,128]{1,0:T(8,128)S(1)} %get-tuple-element.32), channel_id=1, source_target_pairs={{0,28},{1,29},{2,30},{3,7},{4,8},{5,9},{6,10},{7,3},{8,4},{9,5},{1... | collective-permute-start | bytes 172040 | tf_op jit(solution)/shard_map/ppermute | solution.py:422
  5.6 6.2 %collective-permute-start.2 = (f32[22,1,640]{2,1,0:T(1,128)S(1)}, f32[22,1,640]{2,1,0:T(1,128)S(1)}, u32[]{:S(2)}, u32[]{:S(2)}) collective-permute-start(f32[22,1,640]{2,1,0:T(1,128)S(1)} %get-tuple-element.37), channel_id=1, source_target_pairs={{0,3},{1,2},{2,1},{3,0},{4,7},{5,6},{6,5},{7,4},{8,11},{9,10},{10,... | collective-permute-start | bytes 168968 | tf_op jit(solution)/shard_map/ppermute | solution.py:480
  7.2 1.2 %collective-permute-start.1 = (f32[104,128]{1,0:T(8,128)S(1)}, f32[104,128]{1,0:T(8,128)S(1)}, u32[]{:S(2)}, u32[]{:S(2)}) collective-permute-start(f32[104,128]{1,0:T(8,128)S(1)} %get-tuple-element.33), channel_id=1, source_target_pairs={{0,4},{1,5},{2,6},{3,31},{4,0},{5,1},{6,2},{7,11},{8,12},{9,13},{1... | collective-permute-start | bytes 159752 | tf_op jit(solution)/shard_map/ppermute | solution.py:422
  7.4 5.3 %collective-permute-start.5 = (f32[4,1,640]{2,1,0:T(1,128)S(1)}, f32[4,1,640]{2,1,0:T(1,128)S(1)}, u32[]{:S(2)}, u32[]{:S(2)}) collective-permute-start(f32[4,1,640]{2,1,0:T(1,128)S(1)} %get-tuple-element.45), channel_id=1, source_target_pairs={{0,2},{1,3},{2,0},{3,1},{4,6},{5,7},{6,4},{7,5},{8,10},{9,11},{10,... | collective-permute-start | bytes 30728 | tf_op jit(solution)/shard_map/ppermute | solution.py:480
  8.5 4.2 %collective-permute-start.4 = (f32[120,128]{1,0:T(8,128)S(1)}, f32[120,128]{1,0:T(8,128)S(1)}, u32[]{:S(2)}, u32[]{:S(2)}) collective-permute-start(f32[120,128]{1,0:T(8,128)S(1)} %get-tuple-element.43), channel_id=1, source_target_pairs={{0,4},{1,2},{2,1},{3,7},{4,0},{5,6},{6,5},{7,3},{8,12},{9,10},{10,... | collective-permute-start | bytes 184328 | tf_op jit(solution)/shard_map/ppermute | solution.py:433
  8.8 5.2 %collective-permute-start.3 = (f32[128,128]{1,0:T(8,128)S(1)}, f32[128,128]{1,0:T(8,128)S(1)}, u32[]{:S(2)}, u32[]{:S(2)}) collective-permute-start(f32[128,128]{1,0:T(8,128)S(1)} %get-tuple-element.36.crossing), channel_id=1, source_target_pairs={{0,1},{1,0},{2,3},{3,2},{4,5},{5,4},{6,7},{7,6},{8,9},{9,8},{10,11... | collective-permute-start | bytes 196616 | tf_op jit(solution)/shard_map/ppermute | solution.py:433

commit v18 on v17

--- a/solution.py
+++ b/solution.py
@@ -269,7 +269,7 @@
     return [q for q in (Y_UP if up else Y_DOWN) if VELOCITIES[q][0]], cs - 1 if up else 0
 
 
-def pack_kernel(sizes, got_a, got_b, part_a, part_b, cross_a, cross_b):
+def pack_kernel(sizes, got_a, got_b, part_a, part_b, cross_a, cross_b, *copies):
     ca, cs, blocks, n_span, per_brick = sizes
     rows = blocks * cs
     even = first_up(n_span)
@@ -303,6 +303,9 @@
     def _():
         complete(cross_a, False)
         complete(cross_b, True)
+
+    for copy in copies:
+        copy[0 : cross_a.shape[0]] = cross_a[...]
 
 
 def aisle_kernel(sizes, direct, room_in, plen_in, got_a, got_b, jets, places, room, plen, inflow):
@@ -347,8 +350,10 @@
         lax.fori_loop(0, n_span, add_brick, 0)
 
 
-def finish_kernel(sizes, direct, room_in, plen_in, got_a, got_b, places, inflow, *rest):
+def finish_kernel(sizes, direct, room_in, plen_in, got_b, places, inflow, *rest):
     *got_jets, room, plen, room_out, plen_out, sems = rest
+    many = 2 if direct else 1
+    got_a, got_jets = got_jets[:many], got_jets[many:]
     ca, cs, blocks, n_span, per_brick = sizes
     rows = blocks * cs
     here = lax.axis_index("span")
@@ -364,13 +369,16 @@
                 at = 5 * rows + k * ca + x
                 plen[q, x * cs + y : x * cs + y + 1] = got[at : at + 1]
 
-    @pl.when(low)
-    def _():
-        enter(got_a, False)
-
-    @pl.when(jnp.logical_not(low))
-    def _():
-        enter(got_a, True)
+    for half, got in enumerate(got_a):
+        inside = jnp.logical_and(here >= 2 * half, here < (2 * half + 2 if direct else n_span))
+
+        @pl.when(jnp.logical_and(low, inside))
+        def _(got=got):
+            enter(got, False)
+
+        @pl.when(jnp.logical_and(jnp.logical_not(low), inside))
+        def _(got=got):
+            enter(got, True)
 
     @pl.when(jnp.logical_and(low, here > 0))
     def _():
@@ -385,7 +393,8 @@
     bricks = []
     if direct:
         start = 5 * (rows + cs)
-        bricks = [(here ^ 1, lambda s, k: got_a[start + s * 5 + k : start + s * 5 + k + 1])]
+        near_jet = lambda s, k: jnp.where(here < 2, *[got[start + s * 5 + k : start + s * 5 + k + 1] for got in got_a])
+        bricks = [(here ^ 1, near_jet)]
         for apart, got in zip((2, 3), got_jets):
             bricks.append((here ^ apart, lambda s, k, got=got: got[s, :, k * LANES : (k + 1) * LANES]))
     sums = jet_sums(lambda k: inflow[k], places, bricks)
@@ -422,13 +431,13 @@
     return lax.ppermute(value, ("aisle", "span"), pairs)
 
 
-def swap_span(value, odd):
+def swap_span(value, odd, bricks):
     count = lax.axis_size("span")
     pairs = []
     for a in range(lax.axis_size("aisle")):
         for s in range(count):
             t = s ^ 1 if not odd else s + 1 if s % 2 else s - 1
-            b, t = (a, t) if 0 <= t < count else (a ^ 1, s)
+            b, t = (a, t) if 0 <= t < count and s in bricks else (a ^ 1, s)
             pairs.append((a * count + s, b * count + t))
     return lax.ppermute(value, ("aisle", "span"), pairs)
 
@@ -468,7 +477,7 @@
 
     upto8 = lambda count: count + -count % 8
     wide = upto8(5 * (rows + ca) + (5 * CAP if direct else 0))
-    cross_shapes = [near((wide + 8, LANES)), near((wide, LANES))]
+    cross_shapes = [near((wide, LANES)), near((wide + 8, LANES))]
     room_post, part_a, part_b, *jets = call(
         functools.partial(early_kernel, sizes, direct),
         [near(room_shape)] + cross_shapes + jet_shapes,
@@ -487,13 +496,14 @@
         [VMEM] * 5,
         aliases={0: 0, 3: 1, 4: 2},
     )(room_post, plen_post, dealt, part_a, part_b)
-    cross_a, cross_b = call(
+    cross_a, cross_b, *cross_c = call(
         functools.partial(pack_kernel, sizes),
-        cross_shapes,
+        cross_shapes + [near((wide + 16, LANES))] * (1 if direct else 0),
         [VMEM] * 4,
     )(got_a, got_b, part_a, part_b)
-    in_a = swap_span(cross_a, False)
-    in_b = swap_span(cross_b, True)
+    halves = (range(2), range(2, 4)) if direct else (range(n_span),)
+    in_a = [swap_span(value, False, half) for value, half in zip((cross_a, *cross_c), halves)]
+    in_b = swap_span(cross_b, True, range(n_span))
 
     room_part, plen_part, places = call(
         functools.partial(local_kernel, sizes),
@@ -513,11 +523,11 @@
         functools.partial(finish_kernel, sizes, direct),
         [near(room_shape), near(plen_shape), jax.ShapeDtypeStruct(room_shape, F32),
          jax.ShapeDtypeStruct(plen_shape, F32)],
-        [VMEM] * (6 + len(got_jets)),
+        [VMEM] * (5 + len(in_a) + len(got_jets)),
         out_specs=[VMEM, VMEM, HBM, HBM],
         scratch=[pltpu.SemaphoreType.DMA((2,))],
         aliases={0: 0, 1: 1},
-    )(room_part, plen_part, in_a, in_b, places, inflow, *got_jets)
+    )(room_part, plen_part, in_b, places, inflow, *in_a, *got_jets)
     room_next = room_next.reshape(19, ca, blocks, cs, LANES).transpose(0, 1, 3, 2, 4).reshape(room_pops.shape)
     return room_next, plenum_next.reshape(plenum_pops.shape)
 

time: 15.1 us -> 15.2 us (level)
  the two profiles are of different devices: /device:TPU:0 before, /device:TPU:24 now
where the time goes in v18:
time: 15.2 us; the launch traced here: 15 us
  waiting for transfers between devices  6.45 us (42%)
  starting transfers between devices  4.41 us (29%)
  Pallas kernels  3.46 us (23%)
  between operations  0.72 us (5%)
    ppermute x2, starting transfers between devices, shards(): lax.ppermute(jets[apart - 2], 'span', [(i, i ^ apart) for i in range(4)])  3.53 us
    ppermute x3, waiting for transfers between devices, swap_span(): return lax.ppermute(value, ('aisle', 'span'), pairs)  3.37 us
    ppermute x2, waiting for transfers between devices, swap_aisle(): return lax.ppermute(value, ('aisle', 'span'), pairs)  3.08 us
    pallas_call x1, Pallas kernels, shards(): call(functools.partial(collide_kernel, sizes, direct), [near(room_shape),...  1.37 us
    pallas_call x1, Pallas kernels, shards(): call(functools.partial(finish_kernel, sizes, direct), [near(room_shape),...  0.93 us
    pallas_call x1, Pallas kernels, shards(): call(functools.partial(local_kernel, sizes), [near(room_shape), near(plen...  0.86 us
    ppermute x3, starting transfers between devices, swap_span(): return lax.ppermute(value, ('aisle', 'span'), pairs)  0.57 us
    ppermute x2, starting transfers between devices, swap_aisle(): return lax.ppermute(value, ('aisle', 'span'), pairs)  0.31 us
  transfers between devices with their start and end apart: 7, of which 2 were waited for; matrix products, arithmetic and copies ran while one was open for 0% of the time, Pallas kernels for 8%

profile of v18, /device:TPU:24, one launch (start us, length us, event | category | flops | bytes accessed | tf_op | source)
XLA Modules:
  0.0 15.0 jit_solution(17178519703119693899)
XLA Ops:
  0.6 1.4 %collide_kernel.1 = (f32[19,4,16,128]{3,2,1,0:T(8,128)S(1)}, f32[19,16,128]{2,1,0:T(8,128)S(1)}, f32[112,128]{1,0:T(8,128)S(1)}, f32[104,128]{1,0:T(8,128)S(1)}, f32[16,1,640]{2,1,0:T(1,128)S(1)}) custom-call(f32[19,4,16,128]{3,2,1,0:T(8,128)} %bitcast.13, f32[19,16,128]{2,1,0:T(8,128)} %bitcast.14, s32[32]{0:T(128)} %rest_1_.1, s32[32]{0:T(128)} %bitcast.15, ...), custom_call_target="tpu_custom_call" | custom-call | flops 100000 | bytes 1000000 | tf_op jit(solution)/shard_map/collide_kernel/pallas_call | solution.py:467
  2.0 0.1 collective-permute-start
  2.1 2.4 %collective-permute-start.2 = (f32[22,1,640]{2,1,0:T(1,128)S(1)}, f32[22,1,640]{2,1,0:T(1,128)S(1)}, u32[]{:S(2)}, u32[]{:S(2)}) collective-permute-start(f32[22,1,640]{2,1,0:T(1,128)S(1)} %get-tuple-element.38), channel_id=1, source_target_pairs={{0,3},{1,2},{2,1},{3,0},{4,7},{5,6},{6,5},{7,4},{8,11},{9,10},{10,... | collective-permute-start | bytes 168968 | tf_op jit(solution)/shard_map/ppermute | solution.py:489
  4.5 0.2 %collective-permute-start.1 = (f32[104,128]{1,0:T(8,128)S(1)}, f32[104,128]{1,0:T(8,128)S(1)}, u32[]{:S(2)}, u32[]{:S(2)}) collective-permute-start(f32[104,128]{1,0:T(8,128)S(1)} %get-tuple-element.34), channel_id=1, source_target_pairs={{0,4},{1,5},{2,6},{3,31},{4,0},{5,1},{6,2},{7,11},{8,12},{9,13},{1... | collective-permute-start | bytes 159752 | tf_op jit(solution)/shard_map/ppermute | solution.py:431
  4.7 1.2 %collective-permute-start.6 = (f32[4,1,640]{2,1,0:T(1,128)S(1)}, f32[4,1,640]{2,1,0:T(1,128)S(1)}, u32[]{:S(2)}, u32[]{:S(2)}) collective-permute-start(f32[4,1,640]{2,1,0:T(1,128)S(1)} %get-tuple-element.47), channel_id=1, source_target_pairs={{0,2},{1,3},{2,0},{3,1},{4,6},{5,7},{6,4},{7,5},{8,10},{9,11},{10,... | collective-permute-start | bytes 30728 | tf_op jit(solution)/shard_map/ppermute | solution.py:489
  5.9 0.2 %late_kernel.1 = (f32[19,4,16,128]{3,2,1,0:T(8,128)S(1)}, f32[120,128]{1,0:T(8,128)S(1)}, f32[128,128]{1,0:T(8,128)S(1)}) custom-call(f32[19,4,16,128]{3,2,1,0:T(8,128)S(1)} %get-tuple-element.29.room_in, f32[19,16,128]{2,1,0:T(8,128)S(1)} %get-tuple-element.27.plen_post, ...), custom_call_target="tpu_custom_call", output_to_operand_aliasing={{0}: (0, {}), {1}: (3, {}), {2}: (4, {})} | custom-call | flops 100000 | bytes 1000000 | tf_op jit(solution)/shard_map/late_kernel/pallas_call | solution.py:493
  6.1 3.1 %collective-permute-done.1.got_b = f32[104,128]{1,0:T(8,128)S(1)} collective-permute-done((f32[104,128]{1,0:T(8,128)S(1)}, f32[104,128]{1,0:T(8,128)S(1)}, u32[]{:S(2)}, u32[]{:S(2)}) %collective-permute-start.1) | collective-permute-done | bytes 53280 | tf_op jit(solution)/shard_map/ppermute | solution.py:431
  9.2 0.0 collective-permute-done.got_a
  9.2 0.1 collective-permute-start.4
  9.3 0.5 %collective-permute-start.3 = (f32[128,128]{1,0:T(8,128)S(1)}, f32[128,128]{1,0:T(8,128)S(1)}, u32[]{:S(2)}, u32[]{:S(2)}) collective-permute-start(f32[128,128]{1,0:T(8,128)S(1)} %get-tuple-element.44), channel_id=1, source_target_pairs={{0,4},{1,2},{2,1},{3,7},{4,0},{5,6},{6,5},{7,3},{8,12},{9,10},{10,... | collective-permute-start | bytes 196616 | tf_op jit(solution)/shard_map/ppermute | solution.py:442
  9.8 0.0 collective-permute-start.5
  9.8 0.0 collective-permute-done.2.rest_0_.rest_3_
  9.8 0.9 %local_kernel.1 = (f32[19,4,16,128]{3,2,1,0:T(8,128)S(1)}, f32[19,16,128]{2,1,0:T(8,128)S(1)}, f32[17,16,128]{2,1,0:T(8,128)S(1)}) custom-call(f32[19,4,16,128]{3,2,1,0:T(8,128)S(1)} %get-tuple-element.32.room_post, f32[19,16,128]{2,1,0:T(8,128)S(1)} %get-tuple-element.27.plen_post, f32[120,128]{1,0:T(8,128)S(1)} %get-tuple-element.37.crossing, ...), custom_call_target="tpu_custom_call" | custom-call | flops 1000000000 | bytes 1000000 | tf_op jit(solution)/shard_map/local_kernel/pallas_call | solution.py:508
  10.7 0.0 collective-permute-done.6.rest_2_
  10.7 0.0 collective-permute-done.4.rest_0_
  10.7 0.0 collective-permute-done.3.got_b
  10.7 3.4 %collective-permute-done.5.rest_1_ = f32[136,128]{1,0:T(8,128)S(1)} collective-permute-done((f32[136,128]{1,0:T(8,128)S(1)}, f32[136,128]{1,0:T(8,128)S(1)}, u32[]{:S(2)}, u32[]{:S(2)}) %collective-permute-start.5) | collective-permute-done | bytes 69664 | tf_op jit(solution)/shard_map/ppermute | solution.py:442
  14.1 0.9 %finish_kernel.1 = (f32[19,4,16,128]{3,2,1,0:T(8,128)S(1)}, f32[19,16,128]{2,1,0:T(8,128)S(1)}, f32[19,4,16,128]{3,2,1,0:T(8,128)}, f32[19,16,128]{2,1,0:T(8,128)}) custom-call(f32[19,4,16,128]{3,2,1,0:T(8,128)S(1)} %get-tuple-element.42.room_in, f32[19,16,128]{2,1,0:T(8,128)S(1)} %get-tuple-element.43.plen_in, ...), custom_call_target="tpu_custom_call", output_to_operand_aliasing={{0}: (0, {}), {1}: (1, {})} | custom-call | flops 100000 | bytes 1000000 | tf_op jit(solution)/shard_map/finish_kernel/pallas_call | solution.py:522
  (3 shorter events, 0.1 us)
Async XLA Ops:
  2.0 7.2 %collective-permute-start = (f32[112,128]{1,0:T(8,128)S(1)}, f32[112,128]{1,0:T(8,128)S(1)}, u32[]{:S(2)}, u32[]{:S(2)}) collective-permute-start(f32[112,128]{1,0:T(8,128)S(1)} %get-tuple-element.33), channel_id=1, source_target_pairs={{0,28},{1,29},{2,30},{3,7},{4,8},{5,9},{6,10},{7,3},{8,4},{9,5},{1... | collective-permute-start | bytes 172040 | tf_op jit(solution)/shard_map/ppermute | solution.py:431
  2.1 7.7 %collective-permute-start.2 = (f32[22,1,640]{2,1,0:T(1,128)S(1)}, f32[22,1,640]{2,1,0:T(1,128)S(1)}, u32[]{:S(2)}, u32[]{:S(2)}) collective-permute-start(f32[22,1,640]{2,1,0:T(1,128)S(1)} %get-tuple-element.38), channel_id=1, source_target_pairs={{0,3},{1,2},{2,1},{3,0},{4,7},{5,6},{6,5},{7,4},{8,11},{9,10},{10,... | collective-permute-start | bytes 168968 | tf_op jit(solution)/shard_map/ppermute | solution.py:489
  4.5 4.7 %collective-permute-start.1 = (f32[104,128]{1,0:T(8,128)S(1)}, f32[104,128]{1,0:T(8,128)S(1)}, u32[]{:S(2)}, u32[]{:S(2)}) collective-permute-start(f32[104,128]{1,0:T(8,128)S(1)} %get-tuple-element.34), channel_id=1, source_target_pairs={{0,4},{1,5},{2,6},{3,31},{4,0},{5,1},{6,2},{7,11},{8,12},{9,13},{1... | collective-permute-start | bytes 159752 | tf_op jit(solution)/shard_map/ppermute | solution.py:431
  4.7 6.0 %collective-permute-start.6 = (f32[4,1,640]{2,1,0:T(1,128)S(1)}, f32[4,1,640]{2,1,0:T(1,128)S(1)}, u32[]{:S(2)}, u32[]{:S(2)}) collective-permute-start(f32[4,1,640]{2,1,0:T(1,128)S(1)} %get-tuple-element.47), channel_id=1, source_target_pairs={{0,2},{1,3},{2,0},{3,1},{4,6},{5,7},{6,4},{7,5},{8,10},{9,11},{10,... | collective-permute-start | bytes 30728 | tf_op jit(solution)/shard_map/ppermute | solution.py:489
  9.2 1.5 %collective-permute-start.4 = (f32[120,128]{1,0:T(8,128)S(1)}, f32[120,128]{1,0:T(8,128)S(1)}, u32[]{:S(2)}, u32[]{:S(2)}) collective-permute-start(f32[120,128]{1,0:T(8,128)S(1)} %get-tuple-element.37.crossing), channel_id=1, source_target_pairs={{0,1},{1,0},{2,6},{3,7},{4,5},{5,4},{6,2},{7,3},{8,9},{9,8},{10,14... | collective-permute-start | bytes 184328 | tf_op jit(solution)/shard_map/ppermute | solution.py:442
  9.3 1.4 %collective-permute-start.3 = (f32[128,128]{1,0:T(8,128)S(1)}, f32[128,128]{1,0:T(8,128)S(1)}, u32[]{:S(2)}, u32[]{:S(2)}) collective-permute-start(f32[128,128]{1,0:T(8,128)S(1)} %get-tuple-element.44), channel_id=1, source_target_pairs={{0,4},{1,2},{2,1},{3,7},{4,0},{5,6},{6,5},{7,3},{8,12},{9,10},{10,... | collective-permute-start | bytes 196616 | tf_op jit(solution)/shard_map/ppermute | solution.py:442
  9.8 4.3 %collective-permute-start.5 = (f32[136,128]{1,0:T(8,128)S(1)}, f32[136,128]{1,0:T(8,128)S(1)}, u32[]{:S(2)}, u32[]{:S(2)}) collective-permute-start(f32[136,128]{1,0:T(8,128)S(1)} %get-tuple-element.46), channel_id=1, source_target_pairs={{0,4},{1,5},{2,3},{3,2},{4,0},{5,1},{6,7},{7,6},{8,12},{9,13},{10,... | collective-permute-start | bytes 208904 | tf_op jit(solution)/shard_map/ppermute | solution.py:442

commit v19 on v15

--- a/solution.py
+++ b/solution.py
@@ -247,7 +247,7 @@
 def early_kernel(sizes, direct, room_in, plen_post, dealt, room_post, cross_a, cross_b, *jets):
     start = 2 * CAP
     for jet in jets:
-        jet[...] = dealt[start : start + CAP]
+        jet[0:CAP] = dealt[start : start + CAP]
         start = start + CAP
 
     @pl.when(lax.axis_index("span") == 0)
@@ -444,7 +444,8 @@
     tile_cell, tile_owner, tile_class = far(tile_cell), far(tile_owner.reshape(tiles)), far(tile_class)
     numbers = pltpu.SMEM((tiles,), jnp.int32)
 
-    dealt_shape, jet_shape = (n_span * CAP, 1, 5 * hp), (CAP, 1, 5 * hp)
+    dealt_shape = (n_span * CAP, 1, 5 * hp)
+    jet_shapes = [near((count, 1, 5 * hp)) for count in ((CAP + 1, CAP) if direct else ())]
     room_post, plen_post, swap_a, swap_b, dealt = call(
         functools.partial(collide_kernel, sizes, direct),
         [near(room_shape), near(plen_shape), near((halo, LANES)), near((halo + 8, LANES)),
@@ -461,7 +462,7 @@
     cross_shapes = [near((wide, LANES)), near((wide + 8, LANES))]
     room_post, part_a, part_b, *jets = call(
         functools.partial(early_kernel, sizes, direct),
-        [near(room_shape)] + cross_shapes + [near(jet_shape)] * (2 if direct else 0),
+        [near(room_shape)] + cross_shapes + jet_shapes,
         [VMEM] * 3,
         aliases={0: 0},
     )(room_post, plen_post, dealt)

time: 14.9 us -> 14.8 us (level)
  waiting for transfers between devices: 2.74 us -> 2.39 us
  starting transfers between devices: 7.94 us -> 8.15 us
    ppermute x2, starting transfers between devices: 0.75 us -> 1.3 us  [swap_span(): return lax.ppermute(value, ('aisle', 'span'), pairs)]
    ppermute x2, starting transfers between devices: 3.78 us -> 3.45 us  [shards(): lax.ppermute(jets[apart - 2], 'span', [(i, i ^ apart) for i in range(4)])]
    ppermute x2, waiting for transfers between devices: 0.21 us -> 0.01 us  [swap_span(): return lax.ppermute(value, ('aisle', 'span'), pairs)]
  transfers between devices with their start and end apart: 6 -> 6, of which waited for: 2 -> 1; matrix products, arithmetic and copies ran while one was open for 0% -> 0% of each run, Pallas kernels for 8% -> 8%
where the time goes in v19:
time: 14.8 us; the launch traced here: 14.7 us
  starting transfers between devices  8.15 us (55%)
  Pallas kernels  3.44 us (23%)
  waiting for transfers between devices  2.39 us (16%)
  between operations  0.69 us (5%)
    ppermute x2, starting transfers between devices, shards(): lax.ppermute(jets[apart - 2], 'span', [(i, i ^ apart) for i in range(4)])  3.45 us
    ppermute x2, starting transfers between devices, swap_aisle(): return lax.ppermute(value, 'aisle', pairs)  3.4 us
    ppermute x2, waiting for transfers between devices, shards(): lax.ppermute(jets[apart - 2], 'span', [(i, i ^ apart) for i in range(4)])  2.38 us
    pallas_call x1, Pallas kernels, shards(): call(functools.partial(collide_kernel, sizes, direct), [near(room_shape),...  1.37 us
    ppermute x2, starting transfers between devices, swap_span(): return lax.ppermute(value, ('aisle', 'span'), pairs)  1.3 us
    pallas_call x1, Pallas kernels, shards(): call(functools.partial(finish_kernel, sizes, direct), [near(room_shape),...  0.94 us
    pallas_call x1, Pallas kernels, shards(): call(functools.partial(local_kernel, sizes), [near(room_shape), near(plen...  0.86 us
  transfers between devices with their start and end apart: 6, of which 1 were waited for; matrix products, arithmetic and copies ran while one was open for 0% of the time, Pallas kernels for 8%

profile of v19, /device:TPU:0, one launch (start us, length us, event | category | flops | bytes accessed | tf_op | source)
XLA Modules:
  0.0 14.7 jit_solution(8078155155550951756)
XLA Ops:
  0.6 1.4 %collide_kernel.1 = (f32[19,4,16,128]{3,2,1,0:T(8,128)S(1)}, f32[19,16,128]{2,1,0:T(8,128)S(1)}, f32[104,128]{1,0:T(8,128)S(1)}, f32[112,128]{1,0:T(8,128)S(1)}, f32[16,1,640]{2,1,0:T(1,128)S(1)}) custom-call(f32[19,4,16,128]{3,2,1,0:T(8,128)} %bitcast.13, f32[19,16,128]{2,1,0:T(8,128)} %bitcast.14, s32[32]{0:T(128)} %cell_in.3, s32[32]{0:T(128)} %bitcast.15, ...), custom_call_target="tpu_custom_call" | custom-call | flops 100000 | bytes 1000000 | tf_op jit(solution)/shard_map/collide_kernel/pallas_call | solution.py:449
  2.0 3.4 %collective-permute-start.1 = (f32[112,128]{1,0:T(8,128)S(1)}, f32[112,128]{1,0:T(8,128)S(1)}, u32[]{:S(2)}, u32[]{:S(2)}) collective-permute-start(f32[112,128]{1,0:T(8,128)S(1)} %get-tuple-element.33), channel_id=1, source_target_pairs={{0,28},{4,8},{8,4},{12,16},{16,12},{20,24},{24,20},{28,0},{1,29},{... | collective-permute-start | bytes 172040 | tf_op jit(solution)/shard_map/ppermute | solution.py:414
  5.4 0.0 collective-permute-start
  5.4 0.2 %early_kernel.1 = (f32[19,4,16,128]{3,2,1,0:T(8,128)S(1)}, f32[120,128]{1,0:T(8,128)S(1)}, f32[128,128]{1,0:T(8,128)S(1)}, f32[5,1,640]{2,1,0:T(1,128)S(1)}, f32[4,1,640]{2,1,0:T(1,128)S(1)}) custom-call(f32[19,4,16,128]{3,2,1,0:T(8,128)S(1)} %get-tuple-element.25.room_in, ...), custom_call_target="tpu_custom_call", output_to_operand_aliasing={{0}: (0, {})} | custom-call | flops 100000 | bytes 1000000 | tf_op jit(solution)/shard_map/early_kernel/pallas_call | solution.py:463
  5.6 3.4 %collective-permute-start.5 = (f32[4,1,640]{2,1,0:T(1,128)S(1)}, f32[4,1,640]{2,1,0:T(1,128)S(1)}, u32[]{:S(2)}, u32[]{:S(2)}) collective-permute-start(f32[4,1,640]{2,1,0:T(1,128)S(1)} %get-tuple-element.45), channel_id=1, source_target_pairs={{0,3},{1,2},{2,1},{3,0},{4,7},{5,6},{6,5},{7,4},{8,11},{9,10},{10,... | collective-permute-start | bytes 30728 | tf_op jit(solution)/shard_map/ppermute | solution.py:471
  9.1 0.0 collective-permute-start.4
  9.1 0.0 collective-permute-done.got_a
  9.1 0.0 collective-permute-done.1.got_b
  9.1 1.3 %collective-permute-start.2 = (f32[120,128]{1,0:T(8,128)S(1)}, f32[120,128]{1,0:T(8,128)S(1)}, u32[]{:S(2)}, u32[]{:S(2)}) collective-permute-start(f32[120,128]{1,0:T(8,128)S(1)} %get-tuple-element.36.crossing), channel_id=1, source_target_pairs={{0,1},{1,0},{2,3},{3,2},{4,5},{5,4},{6,7},{7,6},{8,9},{9,8},{10,11... | collective-permute-start | bytes 184328 | tf_op jit(solution)/shard_map/ppermute | solution.py:425
  10.4 0.0 collective-permute-start.3
  10.4 0.9 %local_kernel.1 = (f32[19,4,16,128]{3,2,1,0:T(8,128)S(1)}, f32[19,16,128]{2,1,0:T(8,128)S(1)}, f32[17,16,128]{2,1,0:T(8,128)S(1)}) custom-call(f32[19,4,16,128]{3,2,1,0:T(8,128)S(1)} %get-tuple-element.31.room_post, f32[19,16,128]{2,1,0:T(8,128)S(1)} %get-tuple-element.26.plen_post, f32[120,128]{1,0:T(8,128)S(1)} %get-tuple-element.36.crossing, s32[32]{0:T(128)} %cell_in.3, ...), custom_call_target="tpu_custom_call" | custom-call | flops 1000000000 | bytes 1000000 | tf_op jit(solution)/shard_map/local_kernel/pallas_call | solution.py:489
  11.3 0.0 collective-permute-done.5.rest_1_
  11.3 2.4 %collective-permute-done.4.rest_0_ = f32[5,1,640]{2,1,0:T(1,128)S(1)} collective-permute-done((f32[5,1,640]{2,1,0:T(1,128)S(1)}, f32[5,1,640]{2,1,0:T(1,128)S(1)}, u32[]{:S(2)}, u32[]{:S(2)}) %collective-permute-start.4) | collective-permute-done | bytes 12832 | tf_op jit(solution)/shard_map/ppermute | solution.py:471
  13.7 0.0 collective-permute-done.2.got_a
  13.7 0.0 collective-permute-done.3.got_b
  13.7 0.9 %finish_kernel.1 = (f32[19,4,16,128]{3,2,1,0:T(8,128)S(1)}, f32[19,16,128]{2,1,0:T(8,128)S(1)}, f32[19,4,16,128]{3,2,1,0:T(8,128)}, f32[19,16,128]{2,1,0:T(8,128)}) custom-call(f32[19,4,16,128]{3,2,1,0:T(8,128)S(1)} %get-tuple-element.40.room_in, f32[19,16,128]{2,1,0:T(8,128)S(1)} %get-tuple-element.41.plen_in, ...), custom_call_target="tpu_custom_call", output_to_operand_aliasing={{0}: (0, {}), {1}: (1, {})} | custom-call | flops 100000 | bytes 1000000 | tf_op jit(solution)/shard_map/finish_kernel/pallas_call | solution.py:503
  (3 shorter events, 0.1 us)
Async XLA Ops:
  2.0 7.1 %collective-permute-start.1 = (f32[112,128]{1,0:T(8,128)S(1)}, f32[112,128]{1,0:T(8,128)S(1)}, u32[]{:S(2)}, u32[]{:S(2)}) collective-permute-start(f32[112,128]{1,0:T(8,128)S(1)} %get-tuple-element.33), channel_id=1, source_target_pairs={{0,28},{4,8},{8,4},{12,16},{16,12},{20,24},{24,20},{28,0},{1,29},{... | collective-permute-start | bytes 172040 | tf_op jit(solution)/shard_map/ppermute | solution.py:414
  5.4 3.7 %collective-permute-start = (f32[104,128]{1,0:T(8,128)S(1)}, f32[104,128]{1,0:T(8,128)S(1)}, u32[]{:S(2)}, u32[]{:S(2)}) collective-permute-start(f32[104,128]{1,0:T(8,128)S(1)} %get-tuple-element.32), channel_id=1, source_target_pairs={{0,4},{4,0},{8,12},{12,8},{16,20},{20,16},{24,28},{28,24},{1,5},{5... | collective-permute-start | bytes 159752 | tf_op jit(solution)/shard_map/ppermute | solution.py:414
  5.6 5.7 %collective-permute-start.5 = (f32[4,1,640]{2,1,0:T(1,128)S(1)}, f32[4,1,640]{2,1,0:T(1,128)S(1)}, u32[]{:S(2)}, u32[]{:S(2)}) collective-permute-start(f32[4,1,640]{2,1,0:T(1,128)S(1)} %get-tuple-element.45), channel_id=1, source_target_pairs={{0,3},{1,2},{2,1},{3,0},{4,7},{5,6},{6,5},{7,4},{8,11},{9,10},{10,... | collective-permute-start | bytes 30728 | tf_op jit(solution)/shard_map/ppermute | solution.py:471
  9.1 4.6 %collective-permute-start.4 = (f32[5,1,640]{2,1,0:T(1,128)S(1)}, f32[5,1,640]{2,1,0:T(1,128)S(1)}, u32[]{:S(2)}, u32[]{:S(2)}) collective-permute-start(f32[5,1,640]{2,1,0:T(1,128)S(1)} %get-tuple-element.44), channel_id=1, source_target_pairs={{0,2},{1,3},{2,0},{3,1},{4,6},{5,7},{6,4},{7,5},{8,10},{9,11},{10,... | collective-permute-start | bytes 38408 | tf_op jit(solution)/shard_map/ppermute | solution.py:471
  9.1 4.6 %collective-permute-start.2 = (f32[120,128]{1,0:T(8,128)S(1)}, f32[120,128]{1,0:T(8,128)S(1)}, u32[]{:S(2)}, u32[]{:S(2)}) collective-permute-start(f32[120,128]{1,0:T(8,128)S(1)} %get-tuple-element.36.crossing), channel_id=1, source_target_pairs={{0,1},{1,0},{2,3},{3,2},{4,5},{5,4},{6,7},{7,6},{8,9},{9,8},{10,11... | collective-permute-start | bytes 184328 | tf_op jit(solution)/shard_map/ppermute | solution.py:425
  10.4 3.3 %collective-permute-start.3 = (f32[128,128]{1,0:T(8,128)S(1)}, f32[128,128]{1,0:T(8,128)S(1)}, u32[]{:S(2)}, u32[]{:S(2)}) collective-permute-start(f32[128,128]{1,0:T(8,128)S(1)} %get-tuple-element.42), channel_id=1, source_target_pairs={{0,4},{1,2},{2,1},{3,7},{4,0},{5,6},{6,5},{7,3},{8,12},{9,10},{10,... | collective-permute-start | bytes 196616 | tf_op jit(solution)/shard_map/ppermute | solution.py:425

commit v20 on v19

--- a/solution.py
+++ b/solution.py
@@ -120,9 +120,24 @@
         ((plen_in, plen_buf), (cell_in, cells), (owner_in, owners), (class_in, classes)))]
     order = [0, ca - 1] + list(range(1, ca - 1))
     planes = [pltpu.make_async_copy(room_in.at[:, x], room_post.at[:, x], sems.at[4 + x]) for x in order]
-    for copy in copies[:1] + planes + copies[1:]:
+    for copy in copies[1:] + copies[:1] + planes:
         copy.start()
     dealt[...] = jnp.zeros_like(dealt)
+    for copy in copies[1:4]:
+        copy.wait()
+    here = lax.axis_index("span")
+    first = here * per_brick
+
+    def deal(i, slot):
+        owner = owners[first + i]
+        to = (owner ^ here if direct else owner) * CAP + slot
+        return to, 0.15 * (classes[first + i].astype(F32) + 1.0), cells[first + i]
+
+    tiles = []
+    if direct:
+        named = [owners[first + i] for i in range(per_brick)]
+        for i in range(per_brick):
+            tiles.append(deal(i, sum([(named[j] == named[i]).astype(jnp.int32) for j in range(i)], jnp.int32(0))))
     copies[0].wait()
     for r in range(0, ca * cs, 8):
         post = collide([plen_buf[q, r : r + 8] for q in range(19)])
@@ -131,26 +146,18 @@
         for k, q in enumerate(UPWARD):
             for y in range(8):
                 columns[r + y, :, k * LANES : (k + 1) * LANES] = post[q][y : y + 1]
-    for copy in copies[1:4]:
-        copy.wait()
-    here = lax.axis_index("span")
-    first = here * per_brick
+    for to, share, cell in tiles:
+        dealt[to] = share * columns[cell]
 
     def send_jet(i, carry):
-        t = first + i
-        owner = owners[t]
-        share = 0.15 * (classes[t].astype(F32) + 1.0)
-        same = lambda j, n: n + (owners[first + j] == owner).astype(jnp.int32)
-        slot = repeat(i, same, 0) if direct else lax.fori_loop(0, i, same, 0)
-        to = (owner ^ here if direct else owner) * CAP + slot
-        dealt[to] = share * columns[cells[t]]
+        same = lambda j, n: n + (owners[first + j] == owners[first + i]).astype(jnp.int32)
+        to, share, cell = deal(i, lax.fori_loop(0, i, same, 0))
+        dealt[to] = share * columns[cell]
         return carry
 
-    if direct:
-        for i in range(per_brick):
-            send_jet(i, 0)
-    else:
+    if not direct:
         lax.fori_loop(0, per_brick, send_jet, 0)
+
     for i in range(2):
         planes[i].wait()
         collide_plane(room_post, order[i])

time: 14.8 us -> 14.8 us (level)
  no operation moved by 1% of the time
where the time goes in v20:
time: 14.8 us; the launch traced here: 14.6 us
  starting transfers between devices  8.15 us (55%)
  Pallas kernels  3.37 us (23%)
  waiting for transfers between devices  2.39 us (16%)
  between operations  0.69 us (5%)
    ppermute x2, starting transfers between devices, shards(): lax.ppermute(jets[apart - 2], 'span', [(i, i ^ apart) for i in range(4)])  3.45 us
    ppermute x2, starting transfers between devices, swap_aisle(): return lax.ppermute(value, 'aisle', pairs)  3.4 us
    ppermute x2, waiting for transfers between devices, shards(): lax.ppermute(jets[apart - 2], 'span', [(i, i ^ apart) for i in range(4)])  2.38 us
    ppermute x2, starting transfers between devices, swap_span(): return lax.ppermute(value, ('aisle', 'span'), pairs)  1.3 us
    pallas_call x1, Pallas kernels, shards(): call(functools.partial(collide_kernel, sizes, direct), [near(room_shape),...  1.3 us
    pallas_call x1, Pallas kernels, shards(): call(functools.partial(finish_kernel, sizes, direct), [near(room_shape),...  0.94 us
    pallas_call x1, Pallas kernels, shards(): call(functools.partial(local_kernel, sizes), [near(room_shape), near(plen...  0.86 us
  transfers between devices with their start and end apart: 6, of which 1 were waited for; matrix products, arithmetic and copies ran while one was open for 0% of the time, Pallas kernels for 8%

profile of v20, /device:TPU:0, one launch (start us, length us, event | category | flops | bytes accessed | tf_op | source)
XLA Modules:
  0.0 14.6 jit_solution(2609057205796506477)
XLA Ops:
  0.6 1.3 %collide_kernel.1 = (f32[19,4,16,128]{3,2,1,0:T(8,128)S(1)}, f32[19,16,128]{2,1,0:T(8,128)S(1)}, f32[104,128]{1,0:T(8,128)S(1)}, f32[112,128]{1,0:T(8,128)S(1)}, f32[16,1,640]{2,1,0:T(1,128)S(1)}) custom-call(f32[19,4,16,128]{3,2,1,0:T(8,128)} %bitcast.13, f32[19,16,128]{2,1,0:T(8,128)} %bitcast.14, s32[32]{0:T(128)} %cell_in.3, s32[32]{0:T(128)} %bitcast.15, ...), custom_call_target="tpu_custom_call" | custom-call | flops 100000 | bytes 1000000 | tf_op jit(solution)/shard_map/collide_kernel/pallas_call | solution.py:456
  1.9 3.4 %collective-permute-start.1 = (f32[112,128]{1,0:T(8,128)S(1)}, f32[112,128]{1,0:T(8,128)S(1)}, u32[]{:S(2)}, u32[]{:S(2)}) collective-permute-start(f32[112,128]{1,0:T(8,128)S(1)} %get-tuple-element.33), channel_id=1, source_target_pairs={{0,28},{4,8},{8,4},{12,16},{16,12},{20,24},{24,20},{28,0},{1,29},{... | collective-permute-start | bytes 172040 | tf_op jit(solution)/shard_map/ppermute | solution.py:421
  5.3 0.0 collective-permute-start
  5.3 0.2 %early_kernel.1 = (f32[19,4,16,128]{3,2,1,0:T(8,128)S(1)}, f32[120,128]{1,0:T(8,128)S(1)}, f32[128,128]{1,0:T(8,128)S(1)}, f32[5,1,640]{2,1,0:T(1,128)S(1)}, f32[4,1,640]{2,1,0:T(1,128)S(1)}) custom-call(f32[19,4,16,128]{3,2,1,0:T(8,128)S(1)} %get-tuple-element.25.room_in, ...), custom_call_target="tpu_custom_call", output_to_operand_aliasing={{0}: (0, {})} | custom-call | flops 100000 | bytes 1000000 | tf_op jit(solution)/shard_map/early_kernel/pallas_call | solution.py:470
  5.6 3.4 %collective-permute-start.5 = (f32[4,1,640]{2,1,0:T(1,128)S(1)}, f32[4,1,640]{2,1,0:T(1,128)S(1)}, u32[]{:S(2)}, u32[]{:S(2)}) collective-permute-start(f32[4,1,640]{2,1,0:T(1,128)S(1)} %get-tuple-element.45), channel_id=1, source_target_pairs={{0,3},{1,2},{2,1},{3,0},{4,7},{5,6},{6,5},{7,4},{8,11},{9,10},{10,... | collective-permute-start | bytes 30728 | tf_op jit(solution)/shard_map/ppermute | solution.py:478
  9.0 0.0 collective-permute-start.4
  9.0 0.0 collective-permute-done.got_a
  9.0 0.0 collective-permute-done.1.got_b
  9.1 1.3 %collective-permute-start.2 = (f32[120,128]{1,0:T(8,128)S(1)}, f32[120,128]{1,0:T(8,128)S(1)}, u32[]{:S(2)}, u32[]{:S(2)}) collective-permute-start(f32[120,128]{1,0:T(8,128)S(1)} %get-tuple-element.36.crossing), channel_id=1, source_target_pairs={{0,1},{1,0},{2,3},{3,2},{4,5},{5,4},{6,7},{7,6},{8,9},{9,8},{10,11... | collective-permute-start | bytes 184328 | tf_op jit(solution)/shard_map/ppermute | solution.py:432
  10.4 0.0 collective-permute-start.3
  10.4 0.9 %local_kernel.1 = (f32[19,4,16,128]{3,2,1,0:T(8,128)S(1)}, f32[19,16,128]{2,1,0:T(8,128)S(1)}, f32[17,16,128]{2,1,0:T(8,128)S(1)}) custom-call(f32[19,4,16,128]{3,2,1,0:T(8,128)S(1)} %get-tuple-element.31.room_post, f32[19,16,128]{2,1,0:T(8,128)S(1)} %get-tuple-element.26.plen_post, f32[120,128]{1,0:T(8,128)S(1)} %get-tuple-element.36.crossing, s32[32]{0:T(128)} %cell_in.3, ...), custom_call_target="tpu_custom_call" | custom-call | flops 1000000000 | bytes 1000000 | tf_op jit(solution)/shard_map/local_kernel/pallas_call | solution.py:496
  11.3 0.0 collective-permute-done.5.rest_1_
  11.3 2.4 %collective-permute-done.4.rest_0_ = f32[5,1,640]{2,1,0:T(1,128)S(1)} collective-permute-done((f32[5,1,640]{2,1,0:T(1,128)S(1)}, f32[5,1,640]{2,1,0:T(1,128)S(1)}, u32[]{:S(2)}, u32[]{:S(2)}) %collective-permute-start.4) | collective-permute-done | bytes 12832 | tf_op jit(solution)/shard_map/ppermute | solution.py:478
  13.7 0.0 collective-permute-done.2.got_a
  13.7 0.0 collective-permute-done.3.got_b
  13.7 0.9 %finish_kernel.1 = (f32[19,4,16,128]{3,2,1,0:T(8,128)S(1)}, f32[19,16,128]{2,1,0:T(8,128)S(1)}, f32[19,4,16,128]{3,2,1,0:T(8,128)}, f32[19,16,128]{2,1,0:T(8,128)}) custom-call(f32[19,4,16,128]{3,2,1,0:T(8,128)S(1)} %get-tuple-element.40.room_in, f32[19,16,128]{2,1,0:T(8,128)S(1)} %get-tuple-element.41.plen_in, ...), custom_call_target="tpu_custom_call", output_to_operand_aliasing={{0}: (0, {}), {1}: (1, {})} | custom-call | flops 100000 | bytes 1000000 | tf_op jit(solution)/shard_map/finish_kernel/pallas_call | solution.py:510
  (3 shorter events, 0.1 us)
Async XLA Ops:
  1.9 7.1 %collective-permute-start.1 = (f32[112,128]{1,0:T(8,128)S(1)}, f32[112,128]{1,0:T(8,128)S(1)}, u32[]{:S(2)}, u32[]{:S(2)}) collective-permute-start(f32[112,128]{1,0:T(8,128)S(1)} %get-tuple-element.33), channel_id=1, source_target_pairs={{0,28},{4,8},{8,4},{12,16},{16,12},{20,24},{24,20},{28,0},{1,29},{... | collective-permute-start | bytes 172040 | tf_op jit(solution)/shard_map/ppermute | solution.py:421
  5.3 3.7 %collective-permute-start = (f32[104,128]{1,0:T(8,128)S(1)}, f32[104,128]{1,0:T(8,128)S(1)}, u32[]{:S(2)}, u32[]{:S(2)}) collective-permute-start(f32[104,128]{1,0:T(8,128)S(1)} %get-tuple-element.32), channel_id=1, source_target_pairs={{0,4},{4,0},{8,12},{12,8},{16,20},{20,16},{24,28},{28,24},{1,5},{5... | collective-permute-start | bytes 159752 | tf_op jit(solution)/shard_map/ppermute | solution.py:421
  5.6 5.7 %collective-permute-start.5 = (f32[4,1,640]{2,1,0:T(1,128)S(1)}, f32[4,1,640]{2,1,0:T(1,128)S(1)}, u32[]{:S(2)}, u32[]{:S(2)}) collective-permute-start(f32[4,1,640]{2,1,0:T(1,128)S(1)} %get-tuple-element.45), channel_id=1, source_target_pairs={{0,3},{1,2},{2,1},{3,0},{4,7},{5,6},{6,5},{7,4},{8,11},{9,10},{10,... | collective-permute-start | bytes 30728 | tf_op jit(solution)/shard_map/ppermute | solution.py:478
  9.0 4.6 %collective-permute-start.4 = (f32[5,1,640]{2,1,0:T(1,128)S(1)}, f32[5,1,640]{2,1,0:T(1,128)S(1)}, u32[]{:S(2)}, u32[]{:S(2)}) collective-permute-start(f32[5,1,640]{2,1,0:T(1,128)S(1)} %get-tuple-element.44), channel_id=1, source_target_pairs={{0,2},{1,3},{2,0},{3,1},{4,6},{5,7},{6,4},{7,5},{8,10},{9,11},{10,... | collective-permute-start | bytes 38408 | tf_op jit(solution)/shard_map/ppermute | solution.py:478
  9.1 4.6 %collective-permute-start.2 = (f32[120,128]{1,0:T(8,128)S(1)}, f32[120,128]{1,0:T(8,128)S(1)}, u32[]{:S(2)}, u32[]{:S(2)}) collective-permute-start(f32[120,128]{1,0:T(8,128)S(1)} %get-tuple-element.36.crossing), channel_id=1, source_target_pairs={{0,1},{1,0},{2,3},{3,2},{4,5},{5,4},{6,7},{7,6},{8,9},{9,8},{10,11... | collective-permute-start | bytes 184328 | tf_op jit(solution)/shard_map/ppermute | solution.py:432
  10.4 3.3 %collective-permute-start.3 = (f32[128,128]{1,0:T(8,128)S(1)}, f32[128,128]{1,0:T(8,128)S(1)}, u32[]{:S(2)}, u32[]{:S(2)}) collective-permute-start(f32[128,128]{1,0:T(8,128)S(1)} %get-tuple-element.42), channel_id=1, source_target_pairs={{0,4},{1,2},{2,1},{3,7},{4,0},{5,6},{6,5},{7,3},{8,12},{9,10},{10,... | collective-permute-start | bytes 196616 | tf_op jit(solution)/shard_map/ppermute | solution.py:432

commit v21 on v20

--- a/solution.py
+++ b/solution.py
@@ -113,7 +113,7 @@
 
 
 def collide_kernel(sizes, direct, room_in, plen_in, cell_in, owner_in, class_in, room_post, plen_post, swap_a, swap_b,
-                   dealt, columns, plen_buf, cells, owners, classes, sems):
+                   dealt, plen_buf, cells, owners, classes, sems):
     ca, cs, blocks, n_span, per_brick = sizes
     rows = blocks * cs
     copies = [pltpu.make_async_copy(src, dst, sems.at[i]) for i, (src, dst) in enumerate(
@@ -143,16 +143,17 @@
         post = collide([plen_buf[q, r : r + 8] for q in range(19)])
         for q in range(19):
             plen_post[q, r : r + 8] = post[q]
+
+    def put(to, share, cell):
         for k, q in enumerate(UPWARD):
-            for y in range(8):
-                columns[r + y, :, k * LANES : (k + 1) * LANES] = post[q][y : y + 1]
-    for to, share, cell in tiles:
-        dealt[to] = share * columns[cell]
+            dealt[to, :, k * LANES : (k + 1) * LANES] = share * plen_post[q, pl.ds(cell, 1), :]
+
+    for tile in tiles:
+        put(*tile)
 
     def send_jet(i, carry):
         same = lambda j, n: n + (owners[first + j] == owners[first + i]).astype(jnp.int32)
-        to, share, cell = deal(i, lax.fori_loop(0, i, same, 0))
-        dealt[to] = share * columns[cell]
+        put(*deal(i, lax.fori_loop(0, i, same, 0)))
         return carry
 
     if not direct:
@@ -458,7 +459,7 @@
         [near(room_shape), near(plen_shape), near((halo, LANES)), near((halo + 8, LANES)),
          near(dealt_shape)],
         [HBM] * 5,
-        scratch=[near((ca * cs, 1, 5 * hp)), near(plen_shape), numbers, numbers, numbers,
+        scratch=[near(plen_shape), numbers, numbers, numbers,
                  pltpu.SemaphoreType.DMA((4 + ca,))],
     )(room, plen, tile_cell, tile_owner, tile_class)
     got_b = swap_aisle(swap_b, True)

time: 14.8 us -> 14.8 us (level)
  no operation moved by 1% of the time
where the time goes in v21:
time: 14.8 us; the launch traced here: 14.6 us
  starting transfers between devices  8.15 us (55%)
  Pallas kernels  3.37 us (23%)
  waiting for transfers between devices  2.39 us (16%)
  between operations  0.69 us (5%)
    ppermute x2, starting transfers between devices, shards(): lax.ppermute(jets[apart - 2], 'span', [(i, i ^ apart) for i in range(4)])  3.45 us
    ppermute x2, starting transfers between devices, swap_aisle(): return lax.ppermute(value, 'aisle', pairs)  3.4 us
    ppermute x2, waiting for transfers between devices, shards(): lax.ppermute(jets[apart - 2], 'span', [(i, i ^ apart) for i in range(4)])  2.38 us
    ppermute x2, starting transfers between devices, swap_span(): return lax.ppermute(value, ('aisle', 'span'), pairs)  1.3 us
    pallas_call x1, Pallas kernels, shards(): call(functools.partial(collide_kernel, sizes, direct), [near(room_shape),...  1.3 us
    pallas_call x1, Pallas kernels, shards(): call(functools.partial(finish_kernel, sizes, direct), [near(room_shape),...  0.94 us
    pallas_call x1, Pallas kernels, shards(): call(functools.partial(local_kernel, sizes), [near(room_shape), near(plen...  0.86 us
  transfers between devices with their start and end apart: 6, of which 1 were waited for; matrix products, arithmetic and copies ran while one was open for 0% of the time, Pallas kernels for 8%

profile of v21, /device:TPU:0, one launch (start us, length us, event | category | flops | bytes accessed | tf_op | source)
XLA Modules:
  0.0 14.6 jit_solution(13200480502399601454)
XLA Ops:
  0.6 1.3 %collide_kernel.1 = (f32[19,4,16,128]{3,2,1,0:T(8,128)S(1)}, f32[19,16,128]{2,1,0:T(8,128)S(1)}, f32[104,128]{1,0:T(8,128)S(1)}, f32[112,128]{1,0:T(8,128)S(1)}, f32[16,1,640]{2,1,0:T(1,128)S(1)}) custom-call(f32[19,4,16,128]{3,2,1,0:T(8,128)} %bitcast.13, f32[19,16,128]{2,1,0:T(8,128)} %bitcast.14, s32[32]{0:T(128)} %cell_in.3, s32[32]{0:T(128)} %bitcast.15, ...), custom_call_target="tpu_custom_call" | custom-call | flops 100000 | bytes 1000000 | tf_op jit(solution)/shard_map/collide_kernel/pallas_call | solution.py:457
  1.9 3.4 %collective-permute-start.1 = (f32[112,128]{1,0:T(8,128)S(1)}, f32[112,128]{1,0:T(8,128)S(1)}, u32[]{:S(2)}, u32[]{:S(2)}) collective-permute-start(f32[112,128]{1,0:T(8,128)S(1)} %get-tuple-element.33), channel_id=1, source_target_pairs={{0,28},{4,8},{8,4},{12,16},{16,12},{20,24},{24,20},{28,0},{1,29},{... | collective-permute-start | bytes 172040 | tf_op jit(solution)/shard_map/ppermute | solution.py:422
  5.3 0.0 collective-permute-start
  5.3 0.2 %early_kernel.1 = (f32[19,4,16,128]{3,2,1,0:T(8,128)S(1)}, f32[120,128]{1,0:T(8,128)S(1)}, f32[128,128]{1,0:T(8,128)S(1)}, f32[5,1,640]{2,1,0:T(1,128)S(1)}, f32[4,1,640]{2,1,0:T(1,128)S(1)}) custom-call(f32[19,4,16,128]{3,2,1,0:T(8,128)S(1)} %get-tuple-element.25.room_in, ...), custom_call_target="tpu_custom_call", output_to_operand_aliasing={{0}: (0, {})} | custom-call | flops 100000 | bytes 1000000 | tf_op jit(solution)/shard_map/early_kernel/pallas_call | solution.py:471
  5.6 3.4 %collective-permute-start.5 = (f32[4,1,640]{2,1,0:T(1,128)S(1)}, f32[4,1,640]{2,1,0:T(1,128)S(1)}, u32[]{:S(2)}, u32[]{:S(2)}) collective-permute-start(f32[4,1,640]{2,1,0:T(1,128)S(1)} %get-tuple-element.45), channel_id=1, source_target_pairs={{0,3},{1,2},{2,1},{3,0},{4,7},{5,6},{6,5},{7,4},{8,11},{9,10},{10,... | collective-permute-start | bytes 30728 | tf_op jit(solution)/shard_map/ppermute | solution.py:479
  9.0 0.0 collective-permute-start.4
  9.0 0.0 collective-permute-done.got_a
  9.0 0.0 collective-permute-done.1.got_b
  9.1 1.3 %collective-permute-start.2 = (f32[120,128]{1,0:T(8,128)S(1)}, f32[120,128]{1,0:T(8,128)S(1)}, u32[]{:S(2)}, u32[]{:S(2)}) collective-permute-start(f32[120,128]{1,0:T(8,128)S(1)} %get-tuple-element.36.crossing), channel_id=1, source_target_pairs={{0,1},{1,0},{2,3},{3,2},{4,5},{5,4},{6,7},{7,6},{8,9},{9,8},{10,11... | collective-permute-start | bytes 184328 | tf_op jit(solution)/shard_map/ppermute | solution.py:433
  10.4 0.0 collective-permute-start.3
  10.4 0.9 %local_kernel.1 = (f32[19,4,16,128]{3,2,1,0:T(8,128)S(1)}, f32[19,16,128]{2,1,0:T(8,128)S(1)}, f32[17,16,128]{2,1,0:T(8,128)S(1)}) custom-call(f32[19,4,16,128]{3,2,1,0:T(8,128)S(1)} %get-tuple-element.31.room_post, f32[19,16,128]{2,1,0:T(8,128)S(1)} %get-tuple-element.26.plen_post, f32[120,128]{1,0:T(8,128)S(1)} %get-tuple-element.36.crossing, s32[32]{0:T(128)} %cell_in.3, ...), custom_call_target="tpu_custom_call" | custom-call | flops 1000000000 | bytes 1000000 | tf_op jit(solution)/shard_map/local_kernel/pallas_call | solution.py:497
  11.3 0.0 collective-permute-done.5.rest_1_
  11.3 2.4 %collective-permute-done.4.rest_0_ = f32[5,1,640]{2,1,0:T(1,128)S(1)} collective-permute-done((f32[5,1,640]{2,1,0:T(1,128)S(1)}, f32[5,1,640]{2,1,0:T(1,128)S(1)}, u32[]{:S(2)}, u32[]{:S(2)}) %collective-permute-start.4) | collective-permute-done | bytes 12832 | tf_op jit(solution)/shard_map/ppermute | solution.py:479
  13.7 0.0 collective-permute-done.2.got_a
  13.7 0.0 collective-permute-done.3.got_b
  13.7 0.9 %finish_kernel.1 = (f32[19,4,16,128]{3,2,1,0:T(8,128)S(1)}, f32[19,16,128]{2,1,0:T(8,128)S(1)}, f32[19,4,16,128]{3,2,1,0:T(8,128)}, f32[19,16,128]{2,1,0:T(8,128)}) custom-call(f32[19,4,16,128]{3,2,1,0:T(8,128)S(1)} %get-tuple-element.40.room_in, f32[19,16,128]{2,1,0:T(8,128)S(1)} %get-tuple-element.41.plen_in, ...), custom_call_target="tpu_custom_call", output_to_operand_aliasing={{0}: (0, {}), {1}: (1, {})} | custom-call | flops 100000 | bytes 1000000 | tf_op jit(solution)/shard_map/finish_kernel/pallas_call | solution.py:511
  (3 shorter events, 0.1 us)
Async XLA Ops:
  1.9 7.1 %collective-permute-start.1 = (f32[112,128]{1,0:T(8,128)S(1)}, f32[112,128]{1,0:T(8,128)S(1)}, u32[]{:S(2)}, u32[]{:S(2)}) collective-permute-start(f32[112,128]{1,0:T(8,128)S(1)} %get-tuple-element.33), channel_id=1, source_target_pairs={{0,28},{4,8},{8,4},{12,16},{16,12},{20,24},{24,20},{28,0},{1,29},{... | collective-permute-start | bytes 172040 | tf_op jit(solution)/shard_map/ppermute | solution.py:422
  5.3 3.7 %collective-permute-start = (f32[104,128]{1,0:T(8,128)S(1)}, f32[104,128]{1,0:T(8,128)S(1)}, u32[]{:S(2)}, u32[]{:S(2)}) collective-permute-start(f32[104,128]{1,0:T(8,128)S(1)} %get-tuple-element.32), channel_id=1, source_target_pairs={{0,4},{4,0},{8,12},{12,8},{16,20},{20,16},{24,28},{28,24},{1,5},{5... | collective-permute-start | bytes 159752 | tf_op jit(solution)/shard_map/ppermute | solution.py:422
  5.6 5.7 %collective-permute-start.5 = (f32[4,1,640]{2,1,0:T(1,128)S(1)}, f32[4,1,640]{2,1,0:T(1,128)S(1)}, u32[]{:S(2)}, u32[]{:S(2)}) collective-permute-start(f32[4,1,640]{2,1,0:T(1,128)S(1)} %get-tuple-element.45), channel_id=1, source_target_pairs={{0,3},{1,2},{2,1},{3,0},{4,7},{5,6},{6,5},{7,4},{8,11},{9,10},{10,... | collective-permute-start | bytes 30728 | tf_op jit(solution)/shard_map/ppermute | solution.py:479
  9.0 4.6 %collective-permute-start.4 = (f32[5,1,640]{2,1,0:T(1,128)S(1)}, f32[5,1,640]{2,1,0:T(1,128)S(1)}, u32[]{:S(2)}, u32[]{:S(2)}) collective-permute-start(f32[5,1,640]{2,1,0:T(1,128)S(1)} %get-tuple-element.44), channel_id=1, source_target_pairs={{0,2},{1,3},{2,0},{3,1},{4,6},{5,7},{6,4},{7,5},{8,10},{9,11},{10,... | collective-permute-start | bytes 38408 | tf_op jit(solution)/shard_map/ppermute | solution.py:479
  9.1 4.6 %collective-permute-start.2 = (f32[120,128]{1,0:T(8,128)S(1)}, f32[120,128]{1,0:T(8,128)S(1)}, u32[]{:S(2)}, u32[]{:S(2)}) collective-permute-start(f32[120,128]{1,0:T(8,128)S(1)} %get-tuple-element.36.crossing), channel_id=1, source_target_pairs={{0,1},{1,0},{2,3},{3,2},{4,5},{5,4},{6,7},{7,6},{8,9},{9,8},{10,11... | collective-permute-start | bytes 184328 | tf_op jit(solution)/shard_map/ppermute | solution.py:433
  10.4 3.3 %collective-permute-start.3 = (f32[128,128]{1,0:T(8,128)S(1)}, f32[128,128]{1,0:T(8,128)S(1)}, u32[]{:S(2)}, u32[]{:S(2)}) collective-permute-start(f32[128,128]{1,0:T(8,128)S(1)} %get-tuple-element.42), channel_id=1, source_target_pairs={{0,4},{1,2},{2,1},{3,7},{4,0},{5,6},{6,5},{7,3},{8,12},{9,10},{10,... | collective-permute-start | bytes 196616 | tf_op jit(solution)/shard_map/ppermute | solution.py:433

commit v22 on v21

--- a/solution.py
+++ b/solution.py
@@ -263,24 +263,20 @@
         inner(sizes, direct, room_post, plen_post, dealt, cross_a, cross_b)
 
 
-def late_kernel(sizes, direct, room_in, plen_post, dealt, a_in, b_in, room_post, cross_a, cross_b):
-    @pl.when(lax.axis_index("span") > 0)
-    def _():
-        inner(sizes, direct, room_post, plen_post, dealt, cross_a, cross_b)
-
-
 def corners(cs, up):
     return [q for q in (Y_UP if up else Y_DOWN) if VELOCITIES[q][0]], cs - 1 if up else 0
 
 
-def pack_kernel(sizes, got_a, got_b, part_a, part_b, cross_a, cross_b):
+def late_kernel(sizes, direct, room_in, plen_post, dealt, a_in, b_in, got_a, got_b, room_post, cross_a, cross_b):
+    @pl.when(lax.axis_index("span") > 0)
+    def _():
+        inner(sizes, direct, room_post, plen_post, dealt, cross_a, cross_b)
+
     ca, cs, blocks, n_span, per_brick = sizes
     rows = blocks * cs
     even = lax.axis_index("aisle") % 2 == 0
     low = lax.axis_index("span") % 2 == 0
     group = lax.broadcasted_iota(jnp.int32, (rows, LANES), 0) % cs
-    cross_a[...] = part_a[...]
-    cross_b[...] = part_b[...]
 
     def came(q, low, high):
         if VELOCITIES[q][0] == 1:
@@ -480,17 +476,12 @@
     else:
         own_jets = lax.all_to_all(dealt, "span", 0, 0, tiled=True)
         got_jets = []
-    room_post, part_a, part_b = call(
+    room_post, cross_a, cross_b = call(
         functools.partial(late_kernel, sizes, direct),
         [near(room_shape)] + cross_shapes,
-        [VMEM] * 5,
+        [VMEM] * 7,
         aliases={0: 0, 3: 1, 4: 2},
-    )(room_post, plen_post, dealt, part_a, part_b)
-    cross_a, cross_b = call(
-        functools.partial(pack_kernel, sizes),
-        cross_shapes,
-        [VMEM] * 4,
-    )(got_a, got_b, part_a, part_b)
+    )(room_post, plen_post, dealt, part_a, part_b, got_a, got_b)
     in_a = swap_span(cross_a, False)
     in_b = swap_span(cross_b, True)
 

time: 14.8 us -> 14.8 us (level)
  no operation moved by 1% of the time
where the time goes in v22:
time: 14.8 us; the launch traced here: 14.6 us
  starting transfers between devices  8.13 us (55%)
  Pallas kernels  3.38 us (23%)
  waiting for transfers between devices  2.4 us (16%)
  between operations  0.68 us (5%)
    ppermute x2, starting transfers between devices, shards(): lax.ppermute(jets[apart - 2], 'span', [(i, i ^ apart) for i in range(4)])  3.45 us
    ppermute x2, starting transfers between devices, swap_aisle(): return lax.ppermute(value, 'aisle', pairs)  3.4 us
    ppermute x2, waiting for transfers between devices, shards(): lax.ppermute(jets[apart - 2], 'span', [(i, i ^ apart) for i in range(4)])  2.39 us
    pallas_call x1, Pallas kernels, shards(): call(functools.partial(collide_kernel, sizes, direct), [near(room_shape),...  1.3 us
    ppermute x2, starting transfers between devices, swap_span(): return lax.ppermute(value, ('aisle', 'span'), pairs)  1.28 us
    pallas_call x1, Pallas kernels, shards(): call(functools.partial(finish_kernel, sizes, direct), [near(room_shape),...  0.94 us
    pallas_call x1, Pallas kernels, shards(): call(functools.partial(local_kernel, sizes), [near(room_shape), near(plen...  0.86 us
  transfers between devices with their start and end apart: 6, of which 1 were waited for; matrix products, arithmetic and copies ran while one was open for 0% of the time, Pallas kernels for 8%

profile of v22, /device:TPU:0, one launch (start us, length us, event | category | flops | bytes accessed | tf_op | source)
XLA Modules:
  0.0 14.6 jit_solution(490074690041175561)
XLA Ops:
  0.6 1.3 %collide_kernel.1 = (f32[19,4,16,128]{3,2,1,0:T(8,128)S(1)}, f32[19,16,128]{2,1,0:T(8,128)S(1)}, f32[104,128]{1,0:T(8,128)S(1)}, f32[112,128]{1,0:T(8,128)S(1)}, f32[16,1,640]{2,1,0:T(1,128)S(1)}) custom-call(f32[19,4,16,128]{3,2,1,0:T(8,128)} %bitcast.13, f32[19,16,128]{2,1,0:T(8,128)} %bitcast.14, s32[32]{0:T(128)} %cell_in.3, s32[32]{0:T(128)} %bitcast.15, ...), custom_call_target="tpu_custom_call" | custom-call | flops 100000 | bytes 1000000 | tf_op jit(solution)/shard_map/collide_kernel/pallas_call | solution.py:453
  1.9 3.4 %collective-permute-start.1 = (f32[112,128]{1,0:T(8,128)S(1)}, f32[112,128]{1,0:T(8,128)S(1)}, u32[]{:S(2)}, u32[]{:S(2)}) collective-permute-start(f32[112,128]{1,0:T(8,128)S(1)} %get-tuple-element.30), channel_id=1, source_target_pairs={{0,28},{4,8},{8,4},{12,16},{16,12},{20,24},{24,20},{28,0},{1,29},{... | collective-permute-start | bytes 172040 | tf_op jit(solution)/shard_map/ppermute | solution.py:418
  5.3 0.0 collective-permute-start
  5.3 0.2 %early_kernel.1 = (f32[19,4,16,128]{3,2,1,0:T(8,128)S(1)}, f32[120,128]{1,0:T(8,128)S(1)}, f32[128,128]{1,0:T(8,128)S(1)}, f32[5,1,640]{2,1,0:T(1,128)S(1)}, f32[4,1,640]{2,1,0:T(1,128)S(1)}) custom-call(f32[19,4,16,128]{3,2,1,0:T(8,128)S(1)} %get-tuple-element.23.room_in, ...), custom_call_target="tpu_custom_call", output_to_operand_aliasing={{0}: (0, {})} | custom-call | flops 100000 | bytes 1000000 | tf_op jit(solution)/shard_map/early_kernel/pallas_call | solution.py:467
  5.6 3.4 %collective-permute-start.5 = (f32[4,1,640]{2,1,0:T(1,128)S(1)}, f32[4,1,640]{2,1,0:T(1,128)S(1)}, u32[]{:S(2)}, u32[]{:S(2)}) collective-permute-start(f32[4,1,640]{2,1,0:T(1,128)S(1)} %get-tuple-element.41), channel_id=1, source_target_pairs={{0,3},{1,2},{2,1},{3,0},{4,7},{5,6},{6,5},{7,4},{8,11},{9,10},{10,... | collective-permute-start | bytes 30728 | tf_op jit(solution)/shard_map/ppermute | solution.py:475
  9.0 0.0 collective-permute-start.4
  9.0 0.0 collective-permute-done.got_a
  9.0 0.0 collective-permute-done.1.got_b
  9.1 1.3 %collective-permute-start.2 = (f32[120,128]{1,0:T(8,128)S(1)}, f32[120,128]{1,0:T(8,128)S(1)}, u32[]{:S(2)}, u32[]{:S(2)}) collective-permute-start(f32[120,128]{1,0:T(8,128)S(1)} %get-tuple-element.32.crossing), channel_id=1, source_target_pairs={{0,1},{1,0},{2,3},{3,2},{4,5},{5,4},{6,7},{7,6},{8,9},{9,8},{10,11... | collective-permute-start | bytes 184328 | tf_op jit(solution)/shard_map/ppermute | solution.py:429
  10.3 0.0 collective-permute-start.3
  10.3 0.9 %local_kernel.1 = (f32[19,4,16,128]{3,2,1,0:T(8,128)S(1)}, f32[19,16,128]{2,1,0:T(8,128)S(1)}, f32[17,16,128]{2,1,0:T(8,128)S(1)}) custom-call(f32[19,4,16,128]{3,2,1,0:T(8,128)S(1)} %get-tuple-element.31.room_post, f32[19,16,128]{2,1,0:T(8,128)S(1)} %get-tuple-element.24.plen_post, f32[120,128]{1,0:T(8,128)S(1)} %get-tuple-element.32.crossing, s32[32]{0:T(128)} %cell_in.3, ...), custom_call_target="tpu_custom_call" | custom-call | flops 1000000000 | bytes 1000000 | tf_op jit(solution)/shard_map/local_kernel/pallas_call | solution.py:488
  11.3 0.0 collective-permute-done.5.rest_1_
  11.3 2.4 %collective-permute-done.4.rest_0_ = f32[5,1,640]{2,1,0:T(1,128)S(1)} collective-permute-done((f32[5,1,640]{2,1,0:T(1,128)S(1)}, f32[5,1,640]{2,1,0:T(1,128)S(1)}, u32[]{:S(2)}, u32[]{:S(2)}) %collective-permute-start.4) | collective-permute-done | bytes 12832 | tf_op jit(solution)/shard_map/ppermute | solution.py:475
  13.7 0.0 collective-permute-done.2.got_a
  13.7 0.0 collective-permute-done.3.got_b
  13.7 0.9 %finish_kernel.1 = (f32[19,4,16,128]{3,2,1,0:T(8,128)S(1)}, f32[19,16,128]{2,1,0:T(8,128)S(1)}, f32[19,4,16,128]{3,2,1,0:T(8,128)}, f32[19,16,128]{2,1,0:T(8,128)}) custom-call(f32[19,4,16,128]{3,2,1,0:T(8,128)S(1)} %get-tuple-element.36.room_in, f32[19,16,128]{2,1,0:T(8,128)S(1)} %get-tuple-element.37.plen_in, ...), custom_call_target="tpu_custom_call", output_to_operand_aliasing={{0}: (0, {}), {1}: (1, {})} | custom-call | flops 100000 | bytes 1000000 | tf_op jit(solution)/shard_map/finish_kernel/pallas_call | solution.py:502
  (2 shorter events, 0.1 us)
Async XLA Ops:
  1.9 7.1 %collective-permute-start.1 = (f32[112,128]{1,0:T(8,128)S(1)}, f32[112,128]{1,0:T(8,128)S(1)}, u32[]{:S(2)}, u32[]{:S(2)}) collective-permute-start(f32[112,128]{1,0:T(8,128)S(1)} %get-tuple-element.30), channel_id=1, source_target_pairs={{0,28},{4,8},{8,4},{12,16},{16,12},{20,24},{24,20},{28,0},{1,29},{... | collective-permute-start | bytes 172040 | tf_op jit(solution)/shard_map/ppermute | solution.py:418
  5.3 3.7 %collective-permute-start = (f32[104,128]{1,0:T(8,128)S(1)}, f32[104,128]{1,0:T(8,128)S(1)}, u32[]{:S(2)}, u32[]{:S(2)}) collective-permute-start(f32[104,128]{1,0:T(8,128)S(1)} %get-tuple-element.29), channel_id=1, source_target_pairs={{0,4},{4,0},{8,12},{12,8},{16,20},{20,16},{24,28},{28,24},{1,5},{5... | collective-permute-start | bytes 159752 | tf_op jit(solution)/shard_map/ppermute | solution.py:418
  5.6 5.7 %collective-permute-start.5 = (f32[4,1,640]{2,1,0:T(1,128)S(1)}, f32[4,1,640]{2,1,0:T(1,128)S(1)}, u32[]{:S(2)}, u32[]{:S(2)}) collective-permute-start(f32[4,1,640]{2,1,0:T(1,128)S(1)} %get-tuple-element.41), channel_id=1, source_target_pairs={{0,3},{1,2},{2,1},{3,0},{4,7},{5,6},{6,5},{7,4},{8,11},{9,10},{10,... | collective-permute-start | bytes 30728 | tf_op jit(solution)/shard_map/ppermute | solution.py:475
  9.0 4.6 %collective-permute-start.4 = (f32[5,1,640]{2,1,0:T(1,128)S(1)}, f32[5,1,640]{2,1,0:T(1,128)S(1)}, u32[]{:S(2)}, u32[]{:S(2)}) collective-permute-start(f32[5,1,640]{2,1,0:T(1,128)S(1)} %get-tuple-element.40), channel_id=1, source_target_pairs={{0,2},{1,3},{2,0},{3,1},{4,6},{5,7},{6,4},{7,5},{8,10},{9,11},{10,... | collective-permute-start | bytes 38408 | tf_op jit(solution)/shard_map/ppermute | solution.py:475
  9.1 4.6 %collective-permute-start.2 = (f32[120,128]{1,0:T(8,128)S(1)}, f32[120,128]{1,0:T(8,128)S(1)}, u32[]{:S(2)}, u32[]{:S(2)}) collective-permute-start(f32[120,128]{1,0:T(8,128)S(1)} %get-tuple-element.32.crossing), channel_id=1, source_target_pairs={{0,1},{1,0},{2,3},{3,2},{4,5},{5,4},{6,7},{7,6},{8,9},{9,8},{10,11... | collective-permute-start | bytes 184328 | tf_op jit(solution)/shard_map/ppermute | solution.py:429
  10.3 3.3 %collective-permute-start.3 = (f32[128,128]{1,0:T(8,128)S(1)}, f32[128,128]{1,0:T(8,128)S(1)}, u32[]{:S(2)}, u32[]{:S(2)}) collective-permute-start(f32[128,128]{1,0:T(8,128)S(1)} %get-tuple-element.38), channel_id=1, source_target_pairs={{0,4},{1,2},{2,1},{3,7},{4,0},{5,6},{6,5},{7,3},{8,12},{9,10},{10,... | collective-permute-start | bytes 196616 | tf_op jit(solution)/shard_map/ppermute | solution.py:429

commit v23 on v21

--- a/solution.py
+++ b/solution.py
@@ -365,27 +365,32 @@
             came = got[k * rows : (k + 1) * rows]
             for x in range(ca):
                 room[q, x] = jnp.where(group == y, turned_to(came, x, y), room[q, x])
+
+    def enter_plenum(got, up):
+        planes, y = (Y_UP, 0) if up else (Y_DOWN, cs - 1)
+        for k, q in enumerate(planes):
+            for x in range(ca):
                 at = 5 * rows + k * ca + x
                 plen[q, x * cs + y : x * cs + y + 1] = got[at : at + 1]
 
-    @pl.when(low)
-    def _():
-        enter(got_a, False)
-
-    @pl.when(jnp.logical_not(low))
-    def _():
-        enter(got_a, True)
-
-    @pl.when(jnp.logical_and(low, here > 0))
-    def _():
-        enter(got_b, True)
-
-    @pl.when(jnp.logical_and(jnp.logical_not(low), here < n_span - 1))
-    def _():
-        enter(got_b, False)
-
-    plen_copy = pltpu.make_async_copy(plen, plen_out, sems.at[0])
-    plen_copy.start()
+    def entering(enter):
+        @pl.when(low)
+        def _():
+            enter(got_a, False)
+
+        @pl.when(jnp.logical_not(low))
+        def _():
+            enter(got_a, True)
+
+        @pl.when(jnp.logical_and(low, here > 0))
+        def _():
+            enter(got_b, True)
+
+        @pl.when(jnp.logical_and(jnp.logical_not(low), here < n_span - 1))
+        def _():
+            enter(got_b, False)
+
+    entering(enter)
     bricks = []
     if direct:
         start = 5 * (rows + cs)
@@ -398,6 +403,9 @@
             room[q, x, 0:cs] = room[q, x, 0:cs] + sums[k][x * cs : (x + 1) * cs]
     room_copy = pltpu.make_async_copy(room, room_out, sems.at[1])
     room_copy.start()
+    entering(enter_plenum)
+    plen_copy = pltpu.make_async_copy(plen, plen_out, sems.at[0])
+    plen_copy.start()
     plen_copy.wait()
     room_copy.wait()
 

time: 14.8 us -> 14.8 us (level)
  no operation moved by 1% of the time
where the time goes in v23:
time: 14.8 us; the launch traced here: 14.6 us
  starting transfers between devices  8.15 us (55%)
  Pallas kernels  3.41 us (23%)
  waiting for transfers between devices  2.39 us (16%)
  between operations  0.69 us (5%)
    ppermute x2, starting transfers between devices, shards(): lax.ppermute(jets[apart - 2], 'span', [(i, i ^ apart) for i in range(4)])  3.45 us
    ppermute x2, starting transfers between devices, swap_aisle(): return lax.ppermute(value, 'aisle', pairs)  3.4 us
    ppermute x2, waiting for transfers between devices, shards(): lax.ppermute(jets[apart - 2], 'span', [(i, i ^ apart) for i in range(4)])  2.38 us
    pallas_call x1, Pallas kernels, shards(): call(functools.partial(collide_kernel, sizes, direct), [near(room_shape),...  1.3 us
    ppermute x2, starting transfers between devices, swap_span(): return lax.ppermute(value, ('aisle', 'span'), pairs)  1.3 us
    pallas_call x1, Pallas kernels, shards(): call(functools.partial(finish_kernel, sizes, direct), [near(room_shape),...  0.97 us
    pallas_call x1, Pallas kernels, shards(): call(functools.partial(local_kernel, sizes), [near(room_shape), near(plen...  0.86 us
  transfers between devices with their start and end apart: 6, of which 1 were waited for; matrix products, arithmetic and copies ran while one was open for 0% of the time, Pallas kernels for 8%

profile of v23, /device:TPU:0, one launch (start us, length us, event | category | flops | bytes accessed | tf_op | source)
XLA Modules:
  0.0 14.6 jit_solution(2709741958191547754)
XLA Ops:
  0.6 1.3 %collide_kernel.1 = (f32[19,4,16,128]{3,2,1,0:T(8,128)S(1)}, f32[19,16,128]{2,1,0:T(8,128)S(1)}, f32[104,128]{1,0:T(8,128)S(1)}, f32[112,128]{1,0:T(8,128)S(1)}, f32[16,1,640]{2,1,0:T(1,128)S(1)}) custom-call(f32[19,4,16,128]{3,2,1,0:T(8,128)} %bitcast.13, f32[19,16,128]{2,1,0:T(8,128)} %bitcast.14, s32[32]{0:T(128)} %cell_in.3, s32[32]{0:T(128)} %bitcast.15, ...), custom_call_target="tpu_custom_call" | custom-call | flops 100000 | bytes 1000000 | tf_op jit(solution)/shard_map/collide_kernel/pallas_call | solution.py:465
  1.9 3.4 %collective-permute-start.1 = (f32[112,128]{1,0:T(8,128)S(1)}, f32[112,128]{1,0:T(8,128)S(1)}, u32[]{:S(2)}, u32[]{:S(2)}) collective-permute-start(f32[112,128]{1,0:T(8,128)S(1)} %get-tuple-element.33), channel_id=1, source_target_pairs={{0,28},{4,8},{8,4},{12,16},{16,12},{20,24},{24,20},{28,0},{1,29},{... | collective-permute-start | bytes 172040 | tf_op jit(solution)/shard_map/ppermute | solution.py:430
  5.3 0.0 collective-permute-start
  5.3 0.2 %early_kernel.1 = (f32[19,4,16,128]{3,2,1,0:T(8,128)S(1)}, f32[120,128]{1,0:T(8,128)S(1)}, f32[128,128]{1,0:T(8,128)S(1)}, f32[5,1,640]{2,1,0:T(1,128)S(1)}, f32[4,1,640]{2,1,0:T(1,128)S(1)}) custom-call(f32[19,4,16,128]{3,2,1,0:T(8,128)S(1)} %get-tuple-element.25.room_in, ...), custom_call_target="tpu_custom_call", output_to_operand_aliasing={{0}: (0, {})} | custom-call | flops 100000 | bytes 1000000 | tf_op jit(solution)/shard_map/early_kernel/pallas_call | solution.py:479
  5.6 3.4 %collective-permute-start.5 = (f32[4,1,640]{2,1,0:T(1,128)S(1)}, f32[4,1,640]{2,1,0:T(1,128)S(1)}, u32[]{:S(2)}, u32[]{:S(2)}) collective-permute-start(f32[4,1,640]{2,1,0:T(1,128)S(1)} %get-tuple-element.45), channel_id=1, source_target_pairs={{0,3},{1,2},{2,1},{3,0},{4,7},{5,6},{6,5},{7,4},{8,11},{9,10},{10,... | collective-permute-start | bytes 30728 | tf_op jit(solution)/shard_map/ppermute | solution.py:487
  9.0 0.0 collective-permute-start.4
  9.0 0.0 collective-permute-done.got_a
  9.0 0.0 collective-permute-done.1.got_b
  9.1 1.3 %collective-permute-start.2 = (f32[120,128]{1,0:T(8,128)S(1)}, f32[120,128]{1,0:T(8,128)S(1)}, u32[]{:S(2)}, u32[]{:S(2)}) collective-permute-start(f32[120,128]{1,0:T(8,128)S(1)} %get-tuple-element.36.crossing), channel_id=1, source_target_pairs={{0,1},{1,0},{2,3},{3,2},{4,5},{5,4},{6,7},{7,6},{8,9},{9,8},{10,11... | collective-permute-start | bytes 184328 | tf_op jit(solution)/shard_map/ppermute | solution.py:441
  10.4 0.0 collective-permute-start.3
  10.4 0.9 %local_kernel.1 = (f32[19,4,16,128]{3,2,1,0:T(8,128)S(1)}, f32[19,16,128]{2,1,0:T(8,128)S(1)}, f32[17,16,128]{2,1,0:T(8,128)S(1)}) custom-call(f32[19,4,16,128]{3,2,1,0:T(8,128)S(1)} %get-tuple-element.31.room_post, f32[19,16,128]{2,1,0:T(8,128)S(1)} %get-tuple-element.26.plen_post, f32[120,128]{1,0:T(8,128)S(1)} %get-tuple-element.36.crossing, s32[32]{0:T(128)} %cell_in.3, ...), custom_call_target="tpu_custom_call" | custom-call | flops 1000000000 | bytes 1000000 | tf_op jit(solution)/shard_map/local_kernel/pallas_call | solution.py:505
  11.3 0.0 collective-permute-done.5.rest_1_
  11.3 2.4 %collective-permute-done.4.rest_0_ = f32[5,1,640]{2,1,0:T(1,128)S(1)} collective-permute-done((f32[5,1,640]{2,1,0:T(1,128)S(1)}, f32[5,1,640]{2,1,0:T(1,128)S(1)}, u32[]{:S(2)}, u32[]{:S(2)}) %collective-permute-start.4) | collective-permute-done | bytes 12832 | tf_op jit(solution)/shard_map/ppermute | solution.py:487
  13.7 0.0 collective-permute-done.2.got_a
  13.7 0.0 collective-permute-done.3.got_b
  13.7 1.0 %finish_kernel.1 = (f32[19,4,16,128]{3,2,1,0:T(8,128)S(1)}, f32[19,16,128]{2,1,0:T(8,128)S(1)}, f32[19,4,16,128]{3,2,1,0:T(8,128)}, f32[19,16,128]{2,1,0:T(8,128)}) custom-call(f32[19,4,16,128]{3,2,1,0:T(8,128)S(1)} %get-tuple-element.40.room_in, f32[19,16,128]{2,1,0:T(8,128)S(1)} %get-tuple-element.41.plen_in, ...), custom_call_target="tpu_custom_call", output_to_operand_aliasing={{0}: (0, {}), {1}: (1, {})} | custom-call | flops 100000 | bytes 1000000 | tf_op jit(solution)/shard_map/finish_kernel/pallas_call | solution.py:519
  (3 shorter events, 0.1 us)
Async XLA Ops:
  1.9 7.1 %collective-permute-start.1 = (f32[112,128]{1,0:T(8,128)S(1)}, f32[112,128]{1,0:T(8,128)S(1)}, u32[]{:S(2)}, u32[]{:S(2)}) collective-permute-start(f32[112,128]{1,0:T(8,128)S(1)} %get-tuple-element.33), channel_id=1, source_target_pairs={{0,28},{4,8},{8,4},{12,16},{16,12},{20,24},{24,20},{28,0},{1,29},{... | collective-permute-start | bytes 172040 | tf_op jit(solution)/shard_map/ppermute | solution.py:430
  5.3 3.7 %collective-permute-start = (f32[104,128]{1,0:T(8,128)S(1)}, f32[104,128]{1,0:T(8,128)S(1)}, u32[]{:S(2)}, u32[]{:S(2)}) collective-permute-start(f32[104,128]{1,0:T(8,128)S(1)} %get-tuple-element.32), channel_id=1, source_target_pairs={{0,4},{4,0},{8,12},{12,8},{16,20},{20,16},{24,28},{28,24},{1,5},{5... | collective-permute-start | bytes 159752 | tf_op jit(solution)/shard_map/ppermute | solution.py:430
  5.6 5.7 %collective-permute-start.5 = (f32[4,1,640]{2,1,0:T(1,128)S(1)}, f32[4,1,640]{2,1,0:T(1,128)S(1)}, u32[]{:S(2)}, u32[]{:S(2)}) collective-permute-start(f32[4,1,640]{2,1,0:T(1,128)S(1)} %get-tuple-element.45), channel_id=1, source_target_pairs={{0,3},{1,2},{2,1},{3,0},{4,7},{5,6},{6,5},{7,4},{8,11},{9,10},{10,... | collective-permute-start | bytes 30728 | tf_op jit(solution)/shard_map/ppermute | solution.py:487
  9.0 4.6 %collective-permute-start.4 = (f32[5,1,640]{2,1,0:T(1,128)S(1)}, f32[5,1,640]{2,1,0:T(1,128)S(1)}, u32[]{:S(2)}, u32[]{:S(2)}) collective-permute-start(f32[5,1,640]{2,1,0:T(1,128)S(1)} %get-tuple-element.44), channel_id=1, source_target_pairs={{0,2},{1,3},{2,0},{3,1},{4,6},{5,7},{6,4},{7,5},{8,10},{9,11},{10,... | collective-permute-start | bytes 38408 | tf_op jit(solution)/shard_map/ppermute | solution.py:487
  9.1 4.6 %collective-permute-start.2 = (f32[120,128]{1,0:T(8,128)S(1)}, f32[120,128]{1,0:T(8,128)S(1)}, u32[]{:S(2)}, u32[]{:S(2)}) collective-permute-start(f32[120,128]{1,0:T(8,128)S(1)} %get-tuple-element.36.crossing), channel_id=1, source_target_pairs={{0,1},{1,0},{2,3},{3,2},{4,5},{5,4},{6,7},{7,6},{8,9},{9,8},{10,11... | collective-permute-start | bytes 184328 | tf_op jit(solution)/shard_map/ppermute | solution.py:441
  10.4 3.3 %collective-permute-start.3 = (f32[128,128]{1,0:T(8,128)S(1)}, f32[128,128]{1,0:T(8,128)S(1)}, u32[]{:S(2)}, u32[]{:S(2)}) collective-permute-start(f32[128,128]{1,0:T(8,128)S(1)} %get-tuple-element.42), channel_id=1, source_target_pairs={{0,4},{1,2},{2,1},{3,7},{4,0},{5,6},{6,5},{7,3},{8,12},{9,10},{10,... | collective-permute-start | bytes 196616 | tf_op jit(solution)/shard_map/ppermute | solution.py:441
